TPU v7x, 32 devices: a whole 2x2x4 slice. The times are simulated.
32 devices in a mesh: segment: 4 (over y, x), dp: 8 (over z, core).
Axes of the slice: x: 2, y: 2, z: 4, core: 2. Of those that a mesh axis runs over, the one named last changes fastest.
Arguments:
- layer_input: bfloat16 [4, 48, 49, 2048], P(None, 'dp'), may hold values from -12 to 12
- output_grad: bfloat16 [4, 48, 49, 2048], P(None, 'dp'), may hold values from -12 to 12
- resolution: int32 [4, 48], P(None, 'dp'), may hold values from 0 to 2
- tile_order: int32 [4, 48, 9], P(None, 'dp'), may hold values from 0 to 8, each once within a row
- proj_weight: bfloat16 [4, 2048, 512], P('segment'), may hold values from -0.125 to 0.125
- spatial_weight: bfloat16 [4, 4608, 512], P('segment'), may hold values from -0.09375 to 0.09375
- shortcut_weight: bfloat16 [4, 2048, 2048], P('segment'), may hold values from -0.125 to 0.125
- bn_gain: float32 [4, 2048], P('segment'), may hold values from 0.1 to 1.9
- bn_bias: float32 [4, 2048], P('segment'), may hold values from -2.5 to 2.5
Outputs:
- section_maps: bfloat16 [4, 4, 48, 49, 2048], P('segment', None, 'dp')
- proj_grad: float32 [4, 2048, 512], P('segment')
- spatial_grad: float32 [4, 4608, 512], P('segment')
- shortcut_grad: float32 [4, 2048, 2048], P('segment')
- gain_grad: float32 [4, 2048], P('segment')
- bias_grad: float32 [4, 2048], P('segment')
All inputs are finite; a program needn't handle non-finite values.
Results may differ from a plain program's by a relative error of at most 0.018.
Values may be sent and summed in bfloat16 or wider, within the bound.
A program may use at most 320 MiB of HBM per device.

v0:
```python
import jax
import jax.numpy as jnp
from jax import lax
from jax.sharding import PartitionSpec as P

MAP = 7


EPSILON = 1e-05
OFFSETS = ((-1, -1), (-1, 0), (-1, 1), (0, -1), (0, 0), (0, 1), (1, -1), (1, 0), (1, 1))


def shortened(value):
    return jax.tree.map(lambda a: a.astype(jnp.bfloat16) if a.dtype == jnp.float32 else a, value)


def from_behind(block, axis, distance):
    devices = range(lax.axis_size(axis))
    route = [(i - distance, i) for i in devices if i - distance in devices]
    return lax.ppermute(block, axis, route)


def silu_slope(values):
    sigmoid = jax.nn.sigmoid(values)
    return sigmoid * (1.0 + values * (1.0 - sigmoid))


def widen(values, width):
    extra = width - values.shape[-1]
    pads = [(0, 0)] * (values.ndim - 1) + [(0, extra)]
    return jnp.pad(values, pads)


def layout(resolution_ids, order_ids, tiled):
    pixels = jnp.arange(MAP * MAP, dtype=jnp.int32)
    row_of = pixels // MAP
    column_of = pixels % MAP
    extent = 5 + resolution_ids[:, None]
    image_mask = ((row_of[None, :] < extent) & (column_of[None, :] < extent)).astype(jnp.float32)
    inside = (row_of < 6) & (column_of < 6)
    position = jnp.where(inside, row_of // 2 * 3 + column_of // 2, 0)
    tile_ids = jnp.arange(9, dtype=jnp.int32)
    matches = (order_ids[:, :, None] == tile_ids[None, None, :]).astype(jnp.int32)
    inverse_order = jnp.sum(matches * tile_ids[None, :, None], axis=1)

    def pixel_of(chosen):
        picked = chosen[:, position]
        target = (2 * (picked // 3) + row_of % 2) * MAP + 2 * (picked % 3) + column_of % 2
        return jnp.where(inside[None, :] & tiled, target, pixels[None, :])

    source = pixel_of(order_ids)
    back = pixel_of(inverse_order)
    tile_mask = inside.astype(jnp.float32)[None, :] * jnp.take_along_axis(
        image_mask, source, axis=1
    )
    weight_mask = jnp.where(tiled, tile_mask, image_mask)
    retained = jnp.where(tiled, inside, True)
    lattice = jnp.arange(MAP, dtype=jnp.int32)
    tables = []
    for vertical, lateral in OFFSETS:
        same_row = (lattice + vertical) // 2 == lattice // 2
        same_column = (lattice + lateral) // 2 == lattice // 2
        within = same_row[:, None] & same_column[None, :]
        tables.append(jnp.where(tiled, within, True))
    return (weight_mask.reshape(-1), source, back, retained, jnp.stack(tables))


def gather_rows(values, indices, retained):
    moved = jnp.take_along_axis(values, indices[:, :, None], axis=1)
    return jnp.where(retained[None, :, None], moved, jnp.zeros_like(moved))


def columns(activation, taps):
    images = activation.shape[0]
    narrow = activation.shape[-1]
    lattice = activation.reshape(images, MAP, MAP, narrow)
    padded = jnp.pad(lattice, ((0, 0), (1, 1), (1, 1), (0, 0)))
    pieces = []
    for number, (vertical, lateral) in enumerate(OFFSETS):
        window = padded[:, 1 + vertical : 1 + vertical + MAP, 1 + lateral : 1 + lateral + MAP, :]
        pieces.append(jnp.where(taps[number][None, :, :, None], window, jnp.zeros_like(window)))
    return jnp.concatenate(pieces, axis=-1).reshape(images * MAP * MAP, 9 * narrow)


def uncolumns(gradient, taps, images):
    narrow = gradient.shape[-1] // 9
    pieces = gradient.reshape(images, MAP, MAP, 9, narrow)
    padded = jnp.zeros((images, MAP + 2, MAP + 2, narrow), jnp.float32)
    for number, (vertical, lateral) in enumerate(OFFSETS):
        window = jnp.where(taps[number][None, :, :, None], pieces[:, :, :, number, :], 0.0)
        padded = padded + jnp.pad(
            window, ((0, 0), (1 + vertical, 1 - vertical), (1 + lateral, 1 - lateral), (0, 0))
        )
    return padded[:, 1 : 1 + MAP, 1 : 1 + MAP, :].reshape(images * MAP * MAP, narrow)


def norm_forward(hidden, weight_mask, gamma_part, beta_part):
    sums = (
        jnp.sum(weight_mask[:, None] * hidden, axis=0),
        jnp.sum(weight_mask[:, None] * hidden * hidden, axis=0),
        jnp.sum(weight_mask),
    )
    totals, squares, counts = lax.psum((sums[0], sums[1], sums[2]), "dp")
    average = totals / counts
    inverse = lax.rsqrt(squares / counts - average * average + EPSILON)
    return (gamma_part * (hidden - average) * inverse + beta_part, average, inverse)


def norm_backward(grad_out, hidden, average, inverse, weight_mask, gamma_part):
    normed = (hidden - average) * inverse
    sums = (jnp.sum(grad_out, axis=0), jnp.sum(grad_out * normed, axis=0), jnp.sum(weight_mask))
    offset_sum, scale_sum, counts = lax.psum((sums[0], sums[1], sums[2]), "dp")
    grad_hidden = (
        weight_mask[:, None]
        * gamma_part
        * inverse
        * (grad_out - (offset_sum + normed * scale_sum) / counts)
    )
    return (grad_hidden, scale_sum, offset_sum)


def spread(terms):
    return tuple(
        (
            lax.psum_scatter(terms[0], "dp", scatter_dimension=0, tiled=True),
            lax.psum_scatter(terms[1], "dp", scatter_dimension=0, tiled=True),
            lax.psum_scatter(terms[2], "dp", scatter_dimension=0, tiled=True),
        )
    )


def collect(terms):
    return tuple(
        (
            lax.all_gather(terms[0].astype(jnp.bfloat16), "dp", axis=0, tiled=True).astype(
                jnp.float32
            ),
            lax.all_gather(terms[1].astype(jnp.bfloat16), "dp", axis=0, tiled=True).astype(
                jnp.float32
            ),
            lax.all_gather(terms[2].astype(jnp.bfloat16), "dp", axis=0, tiled=True).astype(
                jnp.float32
            ),
        )
    )


def store(stash, batch, pairs):
    items = list(stash)
    for place, value in pairs:
        items[place] = items[place].at[batch].set(value)
    return tuple(items)


def body(
    layer_input,
    output_grad,
    resolution,
    tile_order,
    proj_weight,
    spatial_weight,
    shortcut_weight,
    bn_gain,
    bn_bias,
):
    micro_count, images, pixels, channels = layer_input.shape
    narrow = proj_weight.shape[2]
    row_count = images * pixels
    sections = lax.axis_size("segment")
    section = lax.axis_index("segment")
    parity = section % 2
    tiled = section >= 2
    even = parity == 0
    projection = proj_weight[0]
    spatial = spatial_weight[0]
    shortcut = shortcut_weight[0]
    gamma = bn_gain[0]
    beta = bn_bias[0]
    message = jnp.zeros((row_count, channels + narrow), jnp.bfloat16)
    empty_narrow = jnp.zeros((row_count, narrow), jnp.bfloat16)
    zero_wide = jnp.zeros((row_count, channels), jnp.float32)
    zero_flat = jnp.zeros((row_count, channels), jnp.bfloat16)
    zero_vector = jnp.zeros((channels,), jnp.float32)
    zero_proj = jnp.zeros((channels, narrow), jnp.float32)
    zero_spat = jnp.zeros((9 * narrow, narrow), jnp.float32)
    zero_short = jnp.zeros((channels, channels), jnp.float32)
    gamma_first = jnp.where(even, widen(gamma[:narrow], channels), gamma)
    beta_first = jnp.where(even, widen(beta[:narrow], channels), beta)
    gamma_second = widen(gamma[narrow : 2 * narrow], channels)
    beta_second = widen(beta[narrow : 2 * narrow], channels)

    def geometry(batch):
        return layout(resolution[batch], tile_order[batch], tiled)

    stash = (
        jnp.zeros((micro_count, images, pixels, channels), jnp.bfloat16),
        jnp.zeros((micro_count, row_count, narrow), jnp.float32),
        jnp.zeros((micro_count, row_count, narrow), jnp.bfloat16),
        jnp.zeros((micro_count, row_count, narrow), jnp.float32),
        jnp.zeros((micro_count, 2, narrow), jnp.float32),
        jnp.zeros((micro_count, 2, narrow), jnp.float32),
        jnp.zeros((micro_count, row_count, narrow), jnp.bfloat16),
        jnp.zeros((micro_count, row_count, channels), jnp.float32),
        jnp.zeros((micro_count, row_count, channels), jnp.float32),
        jnp.zeros((micro_count, 2, channels), jnp.float32),
        jnp.zeros((micro_count, images, pixels, channels), jnp.bfloat16),
    )

    def forward_turn(moment, carried):
        incoming, stash = carried
        batch = moment - section
        active = (batch >= 0) & (batch < micro_count)
        clipped = jnp.clip(batch, 0, micro_count - 1)
        branch = jnp.where(active, 1 + parity, 0)
        weight_mask, source, back, retained, taps = geometry(clipped)

        def forward_first_spare():
            return (zero_flat, zero_wide)

        def forward_first_even():
            received = incoming[:, :channels].reshape(images, pixels, channels)
            entering = jnp.where(section == 0, layer_input[clipped], received)
            flat = gather_rows(entering, source, retained).reshape(row_count, channels)
            return (
                flat,
                widen(jnp.dot(flat, projection, preferred_element_type=jnp.float32), channels),
            )

        def forward_first_odd():
            hidden_three = jnp.einsum(
                "rk,dk->rd", incoming[:, channels:], projection, preferred_element_type=jnp.float32
            )
            return (incoming[:, :channels], hidden_three)

        flat, hidden_a = lax.switch(
            branch, (forward_first_spare, forward_first_even, forward_first_odd)
        )
        normed_a, average_a, inverse_a = norm_forward(
            hidden_a, weight_mask, gamma_first, beta_first
        )

        def second_other():
            return (zero_wide, stash)

        def forward_second_even():
            act_one = (weight_mask[:, None] * jax.nn.silu(normed_a[:, :narrow])).astype(
                jnp.bfloat16
            )
            hidden_two = jnp.dot(
                columns(act_one.reshape(images, pixels, narrow), taps),
                spatial,
                preferred_element_type=jnp.float32,
            )
            kept = store(
                stash,
                clipped,
                (
                    (0, flat.reshape(images, pixels, channels)),
                    (1, hidden_a[:, :narrow]),
                    (2, act_one),
                    (4, jnp.stack([average_a[:narrow], inverse_a[:narrow]])),
                ),
            )
            return (widen(hidden_two, channels), kept)

        second_branch = jnp.where(active & even, 1, 0).astype(jnp.int32)
        hidden_b, stash = lax.switch(second_branch, (second_other, forward_second_even))
        normed_b, average_b, inverse_b = norm_forward(
            hidden_b, weight_mask, gamma_second, beta_second
        )

        def third_spare():
            return (message, stash)

        def forward_third_even():
            act_two = (weight_mask[:, None] * jax.nn.silu(normed_b[:, :narrow])).astype(
                jnp.bfloat16
            )
            residual = lax.cond(
                tiled,
                lambda: flat,
                lambda: jnp.dot(flat, shortcut, preferred_element_type=jnp.float32).astype(
                    jnp.bfloat16
                ),
            )
            kept = store(
                stash,
                clipped,
                (
                    (3, hidden_b[:, :narrow]),
                    (5, jnp.stack([average_b[:narrow], inverse_b[:narrow]])),
                ),
            )
            return (jnp.concatenate([residual, act_two], axis=1), kept)

        def third_odd():
            summed = normed_a + flat.astype(jnp.float32)
            result = (weight_mask[:, None] * jax.nn.silu(summed)).astype(jnp.bfloat16)
            kept = store(
                stash,
                clipped,
                (
                    (6, incoming[:, channels:]),
                    (7, hidden_a),
                    (8, summed),
                    (9, jnp.stack([average_a, inverse_a])),
                    (10, result.reshape(images, pixels, channels)),
                ),
            )
            return (jnp.concatenate([result, empty_narrow], axis=1), kept)

        outgoing, stash = lax.switch(branch, (third_spare, forward_third_even, third_odd))
        incoming = jax.tree.map(
            lambda part, own: part.astype(own.dtype),
            from_behind(shortened(outgoing), "segment", 1),
            outgoing,
        )
        return (incoming, stash)

    unused, stash = lax.fori_loop(0, micro_count + sections - 1, forward_turn, (message, stash))
    (
        kept_moved,
        kept_one,
        kept_act,
        kept_two,
        stats_one,
        stats_two,
        kept_narrow,
        kept_three,
        kept_summed,
        stats_three,
        maps,
    ) = stash
    rows_spatial = 9 * narrow
    gamma_back_first = jnp.where(even, widen(gamma[narrow : 2 * narrow], channels), gamma)
    gamma_back_second = widen(gamma[:narrow], channels)

    def backward_turn(moment, carried):
        incoming, accum = carried
        grad_projection, grad_spatial, grad_shortcut, grad_gamma, grad_beta, grad_maps = accum
        batch = moment - (sections - 1 - section)
        active = (batch >= 0) & (batch < micro_count)
        clipped = jnp.clip(batch, 0, micro_count - 1)
        branch = jnp.where(active, 1 + parity, 0)
        weight_mask, source, back, retained, taps = geometry(clipped)

        def backward_first_spare():
            return (zero_wide, zero_wide, zero_vector, zero_vector)

        def backward_first_even():
            grad_act_two = incoming[:, channels:].astype(jnp.float32)
            hidden_two = kept_two[clipped]
            average = stats_two[clipped, 0]
            inverse = stats_two[clipped, 1]
            normed_two = (
                gamma[narrow : 2 * narrow] * (hidden_two - average) * inverse
                + beta[narrow : 2 * narrow]
            )
            grad_normed_two = grad_act_two * weight_mask[:, None] * silu_slope(normed_two)
            return (
                widen(grad_normed_two, channels),
                widen(hidden_two, channels),
                widen(average, channels),
                widen(inverse, channels),
            )

        def backward_first_odd():
            grad_result = jnp.where(
                section == sections - 1,
                output_grad[clipped].reshape(row_count, channels),
                incoming[:, :channels],
            )
            summed = kept_summed[clipped]
            grad_summed = (
                grad_result.astype(jnp.float32) * weight_mask[:, None] * silu_slope(summed)
            ).astype(jnp.bfloat16)
            return (
                grad_summed.astype(jnp.float32),
                kept_three[clipped],
                stats_three[clipped, 0],
                stats_three[clipped, 1],
            )

        grad_out_a, hidden_a, average_a, inverse_a = lax.switch(
            branch, (backward_first_spare, backward_first_even, backward_first_odd)
        )
        grad_hidden_a, scale_a, offset_a = norm_backward(
            grad_out_a, hidden_a, average_a, inverse_a, weight_mask, gamma_back_first
        )

        def second_spare():
            return (zero_wide, zero_wide, zero_vector, zero_vector, zero_proj, zero_spat, message)

        def backward_second_even():
            grad_hidden_two = grad_hidden_a[:, :narrow].astype(jnp.bfloat16)
            unfolded = columns(kept_act[clipped].reshape(images, pixels, narrow), taps)
            spatial_term = jnp.einsum(
                "rk,rn->kn", unfolded, grad_hidden_two, preferred_element_type=jnp.float32
            )
            grad_act_one = uncolumns(
                jnp.einsum(
                    "rn,kn->rk", grad_hidden_two, spatial, preferred_element_type=jnp.float32
                ),
                taps,
                images,
            )
            hidden_one = kept_one[clipped]
            average = stats_one[clipped, 0]
            inverse = stats_one[clipped, 1]
            normed_one = gamma[:narrow] * (hidden_one - average) * inverse + beta[:narrow]
            grad_normed_one = grad_act_one * weight_mask[:, None] * silu_slope(normed_one)
            return (
                widen(grad_normed_one, channels),
                widen(hidden_one, channels),
                widen(average, channels),
                widen(inverse, channels),
                zero_proj,
                spatial_term,
                message,
            )

        def second_odd():
            grad_hidden_three = grad_hidden_a.astype(jnp.bfloat16)
            projection_term = jnp.einsum(
                "rd,rk->dk",
                grad_hidden_three,
                kept_narrow[clipped],
                preferred_element_type=jnp.float32,
            )
            grad_act_two = jnp.dot(
                grad_hidden_three, projection, preferred_element_type=jnp.float32
            ).astype(jnp.bfloat16)
            outgoing = jnp.concatenate([grad_out_a.astype(jnp.bfloat16), grad_act_two], axis=1)
            return (
                zero_wide,
                zero_wide,
                zero_vector,
                zero_vector,
                projection_term,
                zero_spat,
                outgoing,
            )

        grad_out_b, hidden_b, average_b, inverse_b, proj_second, spatial_term, outgoing_second = (
            lax.switch(branch, (second_spare, backward_second_even, second_odd))
        )
        grad_hidden_b, scale_b, offset_b = norm_backward(
            grad_out_b, hidden_b, average_b, inverse_b, weight_mask, gamma_back_second
        )

        def third_other():
            return (zero_proj, zero_short, outgoing_second, grad_maps)

        def backward_third_even():
            grad_hidden_one = grad_hidden_b[:, :narrow].astype(jnp.bfloat16)
            flat = kept_moved[clipped].reshape(row_count, channels)
            grad_residual = incoming[:, :channels]
            projection_term = jnp.einsum(
                "rc,rn->cn", flat, grad_hidden_one, preferred_element_type=jnp.float32
            )
            grad_moved = jnp.einsum(
                "rn,cn->rc", grad_hidden_one, projection, preferred_element_type=jnp.float32
            )
            grad_moved, shortcut_term = lax.cond(
                tiled,
                lambda: (grad_moved + grad_residual.astype(jnp.float32), zero_short),
                lambda: (
                    grad_moved
                    + jnp.einsum(
                        "rd,cd->rc", grad_residual, shortcut, preferred_element_type=jnp.float32
                    ),
                    jnp.einsum(
                        "rc,rd->cd", flat, grad_residual, preferred_element_type=jnp.float32
                    ),
                ),
            )
            grad_entering = gather_rows(
                grad_moved.reshape(images, pixels, channels), back, retained
            ).astype(jnp.bfloat16)
            outgoing = jnp.concatenate(
                [grad_entering.reshape(row_count, channels), empty_narrow], axis=1
            )
            return (
                projection_term,
                shortcut_term,
                outgoing,
                grad_maps.at[clipped].set(grad_entering),
            )

        third_branch = jnp.where(active & even, 1, 0).astype(jnp.int32)
        proj_third, shortcut_term, outgoing, grad_maps = lax.switch(
            third_branch, (third_other, backward_third_even)
        )
        terms = (proj_second + proj_third, spatial_term, shortcut_term)
        moved_scale = jnp.concatenate(
            [jnp.zeros((narrow,), jnp.float32), scale_a[: channels - narrow]]
        )
        moved_offset = jnp.concatenate(
            [jnp.zeros((narrow,), jnp.float32), offset_a[: channels - narrow]]
        )
        grad_gamma = grad_gamma + jnp.where(even, moved_scale, scale_a) + scale_b
        grad_beta = grad_beta + jnp.where(even, moved_offset, offset_a) + offset_b
        accum = (
            grad_projection + terms[0],
            grad_spatial + terms[1],
            grad_shortcut + terms[2],
            grad_gamma,
            grad_beta,
            grad_maps,
        )
        incoming = jax.tree.map(
            lambda part, own: part.astype(own.dtype),
            from_behind(shortened(outgoing), "segment", -1),
            outgoing,
        )
        return (incoming, accum)

    accum = (
        jnp.zeros((channels, narrow), jnp.float32),
        jnp.zeros((rows_spatial, narrow), jnp.float32),
        jnp.zeros((channels, channels), jnp.float32),
        zero_vector,
        zero_vector,
        maps,
    )
    unused, accum = lax.fori_loop(0, micro_count + sections - 1, backward_turn, (message, accum))
    grad_projection, grad_spatial, grad_shortcut, grad_gamma, grad_beta, maps = accum
    slices = spread((grad_projection, grad_spatial, grad_shortcut))
    whole = collect((slices[0], slices[1], slices[2]))
    return (
        maps[None],
        whole[0][None],
        whole[1][None],
        whole[2][None],
        grad_gamma[None],
        grad_beta[None],
    )


def solution(mesh):
    return jax.shard_map(
        body,
        mesh=mesh,
        in_specs=(
            P(None, "dp", None, None),
            P(None, "dp", None, None),
            P(None, "dp"),
            P(None, "dp", None),
            P("segment", None, None),
            P("segment", None, None),
            P("segment", None, None),
            P("segment", None),
            P("segment", None),
        ),
        out_specs=(
            P("segment", None, "dp", None, None),
            P("segment", None, None),
            P("segment", None, None),
            P("segment", None, None),
            P("segment", None),
            P("segment", None),
        ),
        check_vma=False,
    )
```

profile of v0, /device:TPU:0, one launch (start us, length us, event | category | flops | bytes accessed | tf_op | source)
XLA Modules:
  0.0 3116.5 jit_solution(5361597849964519094)
XLA Ops:
  44.7 1090.2 %while.79 = (s32[]{:T(128)}, bf16[294,2560]{1,0:T(8,128)(2,1)S(1)}, bf16[4,6,49,2048]{3,2,1,0:T(8,128)(2,1)}, f32[4,294,512]{2,1,0:T(8,128)}, bf16[4,294,512]{2,...) while((s32[]{:T(128)}, bf16[294,2560]{1,0:T(8,128)(2,1)S(1)}, ...), condition=%wide.region_26.28_spmd, body=%wide.region_0.27_spmd.sunk | while | flops 4487440896 | bytes 114896136 | solution.py:320
  71.7 31.5 %all-reduce.37 = (f32[]{:T(128)}, f32[2048]{0:T(1024)S(1)}, f32[2048]{0:T(1024)S(1)}) all-reduce(f32[]{:T(128)} %get-tuple-element.5733, f32[2048]{0:T(1024)S(1)} %get-tuple-element.5735, f32[2048]{0:T(1024)S(1)} %get-tuple-element.5736), channel_id=1, replica_groups=mesh['segment'=4,'dp'=8] {'dp'}, use_global_device_ids=true, to_apply=%region_7.8 | all-reduce | flops 4097 | bytes 32776 | tf_op jit(solution)/shard_map/while/body/eval_jaxpr/psum | solution.py:103
  105.9 34.9 %conditional.18 = (f32[294,2048]{1,0:T(8,128)}, bf16[4,6,49,2048]{3,2,1,0:T(8,128)(2,1)}, f32[4,294,512]{2,1,0:T(8,128)}, bf16[4,294,512]{2,1,0:T(8,128)(2,1)}, f32[4,2,512]{2,1,0:T(2,128)S(1)}) conditional(s32[]{:T(128)} %clamp.92, (bf16[4,6,49,2048]{3,2,1,0:T(8,128)(2,1)}, f32[4,294,512]{2,1,0:T(8,128)}, ...), branch_computations={%region_10.11_spmd, %region_11.14_spmd.clone.clone} | conditional | flops 1390280064 | bytes 37409572 | solution.py:267
  142.9 25.9 all-reduce.38
  188.2 29.5 collective-permute-done
  224.3 18.1 conditional.17
  244.5 29.0 all-reduce.37
  276.2 35.0 %conditional.18 = (f32[294,2048]{1,0:T(8,128)}, bf16[4,6,49,2048]{3,2,1,0:T(8,128)(2,1)}, f32[4,294,512]{2,1,0:T(8,128)}, bf16[4,294,512]{2,1,0:T(8,128)(2,1)}, f32[4,2,512]{2,1,0:T(2,128)S(1)}) conditional(s32[]{:T(128)} %clamp.92, (bf16[4,6,49,2048]{3,2,1,0:T(8,128)(2,1)}, f32[4,294,512]{2,1,0:T(8,128)}, ...), branch_computations={%region_10.11_spmd, %region_11.14_spmd.clone.clone} | conditional | flops 1390280064 | bytes 37409572 | solution.py:267
  313.3 25.9 all-reduce.38
  358.6 29.5 collective-permute-done
  414.9 29.0 all-reduce.37
  446.7 34.9 %conditional.18 = (f32[294,2048]{1,0:T(8,128)}, bf16[4,6,49,2048]{3,2,1,0:T(8,128)(2,1)}, f32[4,294,512]{2,1,0:T(8,128)}, bf16[4,294,512]{2,1,0:T(8,128)(2,1)}, f32[4,2,512]{2,1,0:T(2,128)S(1)}) conditional(s32[]{:T(128)} %clamp.92, (bf16[4,6,49,2048]{3,2,1,0:T(8,128)(2,1)}, f32[4,294,512]{2,1,0:T(8,128)}, ...), branch_computations={%region_10.11_spmd, %region_11.14_spmd.clone.clone} | conditional | flops 1390280064 | bytes 37409572 | solution.py:267
  483.7 25.9 all-reduce.38
  529.0 29.5 collective-permute-done
  565.1 18.1 conditional.17
  585.3 29.0 all-reduce.37
  617.1 35.0 %conditional.18 = (f32[294,2048]{1,0:T(8,128)}, bf16[4,6,49,2048]{3,2,1,0:T(8,128)(2,1)}, f32[4,294,512]{2,1,0:T(8,128)}, bf16[4,294,512]{2,1,0:T(8,128)(2,1)}, f32[4,2,512]{2,1,0:T(2,128)S(1)}) conditional(s32[]{:T(128)} %clamp.92, (bf16[4,6,49,2048]{3,2,1,0:T(8,128)(2,1)}, f32[4,294,512]{2,1,0:T(8,128)}, ...), branch_computations={%region_10.11_spmd, %region_11.14_spmd.clone.clone} | conditional | flops 1390280064 | bytes 37409572 | solution.py:267
  654.2 25.9 all-reduce.38
  699.4 29.5 collective-permute-done
  740.6 29.0 all-reduce.37
  776.1 25.9 all-reduce.38
  803.3 30.8 collective-permute-start
  834.1 29.2 collective-permute-done
  875.0 29.3 all-reduce.37
  910.8 25.9 all-reduce.38
  942.1 29.2 collective-permute-done
  983.0 29.3 all-reduce.37
  1018.8 25.9 all-reduce.38
  1046.0 59.6 %collective-permute-start = (bf16[294,2560]{1,0:T(8,128)(2,1)}, bf16[294,2560]{1,0:T(8,128)(2,1)S(1)}, u32[]{:S(2)}, u32[]{:S(2)}) collective-permute-start(bf16[294,2560]{1,0:T(8,128)(2,1)} %get-tuple-element.5751), channel_id=1, source_target_pairs={{0,8},{8,16},{16,24},{1,9},{9,17},{17,25},{2,10},{10,18},{18,26},{... | collective-permute-start | bytes 4515848 | tf_op jit(solution)/shard_map/while/body/eval_jaxpr/ppermute | solution.py:20
  1105.6 29.2 collective-permute-done
  1136.0 1477.2 %while.80 = (s32[]{:T(128)}, bf16[294,2560]{1,0:T(8,128)(2,1)}, f32[2048,512]{1,0:T(8,128)}, f32[4608,512]{1,0:T(8,128)}, f32[2048,2048]{1,0:T(8,128)}, /*index=...) while((s32[]{:T(128)}, bf16[294,2560]{1,0:T(8,128)(2,1)}, ...), condition=%wide.region_50.52_spmd.clone, body=%wide.region_27.51_spmd.clone.sunk | while | flops 8986916864 | bytes 380267936 | solution.py:526
  1148.6 29.3 all-reduce.39
  1201.6 25.9 all-reduce.40
  1297.9 28.7 all-reduce.39
  1350.4 25.9 all-reduce.40
  1469.7 28.7 all-reduce.39
  1522.0 25.9 all-reduce.40
  1609.9 83.6 %collective-permute-done.1 = bf16[294,2560]{1,0:T(8,128)(2,1)S(1)} collective-permute-done((bf16[294,2560]{1,0:T(8,128)(2,1)}, bf16[294,2560]{1,0:T(8,128)(2,1)S(1)}, u32[]{:S(2)}, u32[]{:S(2)}) %collective-permute-start.1) | collective-permute-done | bytes 1505312 | tf_op jit(solution)/shard_map/while/body/eval_jaxpr/ppermute | solution.py:20
  1710.1 28.7 all-reduce.39
  1743.1 55.4 %conditional.21 = (f32[294,2048]{1,0:T(8,128)S(1)}, f32[294,2048]{1,0:T(8,128)S(1)}, f32[2048]{0:T(1024)S(1)}, f32[2048]{0:T(1024)S(1)}, f32[2048,512]{1,0:T(8,1...) conditional(s32[]{:T(128)} %clamp.97, () %tuple.484, (pred[]{:T(512)}, ...), branch_computations={%region_37.38_spmd, %region_38.39_spmd.clone.clone, %region_39.40_... | conditional | flops 2780299776 | bytes 104434512 | solution.py:445
  1764.0 18.6 fusion.151
  1800.7 25.9 all-reduce.40
  1832.8 50.1 %conditional.22 = (f32[2048,512]{1,0:T(8,128)}, f32[2048,2048]{1,0:T(8,128)}, bf16[294,2560]{1,0:T(8,128)(2,1)}, bf16[4,6,49,2048]{3,2,1,0:T(8,128)(2,1)}) conditional(s32[]{:T(128)} %clamp.96, (bf16[294,2560]{1,0:T(8,128)(2,1)}, bf16[4,6,49,2048]{3,2,1,0:T(8,128)(2,1)}) %tuple.490, (s32[]{:T(128)}, bf16[4,6,49,2048]{3,2,1,0:T(8,128)(2,1)}, ...), branch_computations={%region_44.45_spmd, %region_45.50_spmd} | conditional | flops 6170456064 | bytes 74607800 | solution.py:491
  1939.8 27.1 all-reduce.39
  1971.1 55.2 %conditional.21 = (f32[294,2048]{1,0:T(8,128)S(1)}, f32[294,2048]{1,0:T(8,128)S(1)}, f32[2048]{0:T(1024)S(1)}, f32[2048]{0:T(1024)S(1)}, f32[2048,512]{1,0:T(8,1...) conditional(s32[]{:T(128)} %clamp.97, () %tuple.484, (pred[]{:T(512)}, ...), branch_computations={%region_37.38_spmd, %region_38.39_spmd.clone.clone, %region_39.40_... | conditional | flops 2780299776 | bytes 104434512 | solution.py:445
  1991.8 18.6 fusion.151
  2028.5 25.9 all-reduce.40
  2060.7 50.2 %conditional.22 = (f32[2048,512]{1,0:T(8,128)}, f32[2048,2048]{1,0:T(8,128)}, bf16[294,2560]{1,0:T(8,128)(2,1)}, bf16[4,6,49,2048]{3,2,1,0:T(8,128)(2,1)}) conditional(s32[]{:T(128)} %clamp.96, (bf16[294,2560]{1,0:T(8,128)(2,1)}, bf16[4,6,49,2048]{3,2,1,0:T(8,128)(2,1)}) %tuple.490, (s32[]{:T(128)}, bf16[4,6,49,2048]{3,2,1,0:T(8,128)(2,1)}, ...), branch_computations={%region_44.45_spmd, %region_45.50_spmd} | conditional | flops 6170456064 | bytes 74607800 | solution.py:491
  2167.5 27.1 all-reduce.39
  2198.7 55.4 %conditional.21 = (f32[294,2048]{1,0:T(8,128)S(1)}, f32[294,2048]{1,0:T(8,128)S(1)}, f32[2048]{0:T(1024)S(1)}, f32[2048]{0:T(1024)S(1)}, f32[2048,512]{1,0:T(8,1...) conditional(s32[]{:T(128)} %clamp.97, () %tuple.484, (pred[]{:T(512)}, ...), branch_computations={%region_37.38_spmd, %region_38.39_spmd.clone.clone, %region_39.40_... | conditional | flops 2780299776 | bytes 104434512 | solution.py:445
  2219.6 18.6 fusion.151
  2256.4 25.9 all-reduce.40
  2288.5 50.1 %conditional.22 = (f32[2048,512]{1,0:T(8,128)}, f32[2048,2048]{1,0:T(8,128)}, bf16[294,2560]{1,0:T(8,128)(2,1)}, bf16[4,6,49,2048]{3,2,1,0:T(8,128)(2,1)}) conditional(s32[]{:T(128)} %clamp.96, (bf16[294,2560]{1,0:T(8,128)(2,1)}, bf16[4,6,49,2048]{3,2,1,0:T(8,128)(2,1)}) %tuple.490, (s32[]{:T(128)}, bf16[4,6,49,2048]{3,2,1,0:T(8,128)(2,1)}, ...), branch_computations={%region_44.45_spmd, %region_45.50_spmd} | conditional | flops 6170456064 | bytes 74607800 | solution.py:491
  2395.4 27.1 all-reduce.39
  2426.7 55.2 %conditional.21 = (f32[294,2048]{1,0:T(8,128)S(1)}, f32[294,2048]{1,0:T(8,128)S(1)}, f32[2048]{0:T(1024)S(1)}, f32[2048]{0:T(1024)S(1)}, f32[2048,512]{1,0:T(8,1...) conditional(s32[]{:T(128)} %clamp.97, () %tuple.484, (pred[]{:T(512)}, ...), branch_computations={%region_37.38_spmd, %region_38.39_spmd.clone.clone, %region_39.40_... | conditional | flops 2780299776 | bytes 104434512 | solution.py:445
  2447.4 18.6 fusion.151
  2484.2 25.9 all-reduce.40
  2516.3 50.2 %conditional.22 = (f32[2048,512]{1,0:T(8,128)}, f32[2048,2048]{1,0:T(8,128)}, bf16[294,2560]{1,0:T(8,128)(2,1)}, bf16[4,6,49,2048]{3,2,1,0:T(8,128)(2,1)}) conditional(s32[]{:T(128)} %clamp.96, (bf16[294,2560]{1,0:T(8,128)(2,1)}, bf16[4,6,49,2048]{3,2,1,0:T(8,128)(2,1)}) %tuple.490, (s32[]{:T(128)}, bf16[4,6,49,2048]{3,2,1,0:T(8,128)(2,1)}, ...), branch_computations={%region_44.45_spmd, %region_45.50_spmd} | conditional | flops 6170456064 | bytes 74607800 | solution.py:491
  2614.8 47.0 %reduce-scatter.4.cloned.1.call-done = f32[256,512]{1,0:T(8,128)} async-done(((f32[2048,512]{1,0:T(8,128)}), f32[256,512]{1,0:T(8,128)}) %reduce-scatter.4.cloned.1.call-update) | async-done | bytes 524304 | tf_op jit(solution)/shard_map/reduce_scatter | solution.py:125
  2663.7 98.7 %reduce-scatter.6.cloned.1.call-done = f32[576,512]{1,0:T(8,128)} async-done(((f32[4608,512]{1,0:T(8,128)}), f32[576,512]{1,0:T(8,128)}) %reduce-scatter.6.cloned.1.call-update) | async-done | bytes 1179664 | tf_op jit(solution)/shard_map/reduce_scatter | solution.py:126
  2764.6 167.3 %reduce-scatter.8.cloned.1.call-done = f32[256,2048]{1,0:T(8,128)} async-done(((f32[2048,2048]{1,0:T(8,128)}), f32[256,2048]{1,0:T(8,128)}) %reduce-scatter.8.cloned.1.call-update) | async-done | bytes 2097168 | tf_op jit(solution)/shard_map/reduce_scatter | solution.py:127
  2943.3 18.2 all-gather.4.cloned.1.call-done
  2965.7 49.1 %all-gather.6.cloned.1.call-done = bf16[4608,512]{1,0:T(8,128)(2,1)} async-done(((bf16[576,512]{1,0:T(8,128)(2,1)}), bf16[4608,512]{1,0:T(8,128)(2,1)}) %all-gather.6.cloned.1.call-update) | async-done | bytes 4718608 | tf_op jit(solution)/shard_map/all_gather | solution.py:138
  3022.2 75.5 %all-gather.8.cloned.1.call-done = bf16[2048,2048]{1,0:T(8,128)(2,1)} async-done(((bf16[256,2048]{1,0:T(8,128)(2,1)}), bf16[2048,2048]{1,0:T(8,128)(2,1)}) %all-gather.8.cloned.1.call-update) | async-done | bytes 8388624 | tf_op jit(solution)/shard_map/all_gather | solution.py:141
  (1758 shorter events, 1707.3 us)
Async XLA Ops:
  7.2 2654.7 %reduce-scatter.4.cloned.1.call-start = ((), (), s32[]{:S(2)}) async-start(), calls=%async_computation.3 | async-start | bytes 4718592 | tf_op jit(solution)/shard_map/reduce_scatter | solution.py:125
  44.7 1091.4 %copy-start.13 = (f32[2048]{0:T(1024)S(1)}, f32[2048]{0:T(1024)}, u32[]{:S(2)}) copy-start(f32[2048]{0:T(1024)} %get-tuple-element.6038) | copy-start | bytes 24580
  186.8 30.9 collective-permute-start
  357.3 30.9 collective-permute-start
  527.6 30.9 collective-permute-start
  698.0 30.9 collective-permute-start
  803.3 60.0 %collective-permute-start = (bf16[294,2560]{1,0:T(8,128)(2,1)}, bf16[294,2560]{1,0:T(8,128)(2,1)S(1)}, u32[]{:S(2)}, u32[]{:S(2)}) collective-permute-start(bf16[294,2560]{1,0:T(8,128)(2,1)} %get-tuple-element.5751), channel_id=1, source_target_pairs={{0,8},{8,16},{16,24},{1,9},{9,17},{17,25},{2,10},{10,18},{18,26},{... | collective-permute-start | bytes 4515848 | tf_op jit(solution)/shard_map/while/body/eval_jaxpr/ppermute | solution.py:20
  938.0 33.3 %collective-permute-start = (bf16[294,2560]{1,0:T(8,128)(2,1)}, bf16[294,2560]{1,0:T(8,128)(2,1)S(1)}, u32[]{:S(2)}, u32[]{:S(2)}) collective-permute-start(bf16[294,2560]{1,0:T(8,128)(2,1)} %get-tuple-element.5751), channel_id=1, source_target_pairs={{0,8},{8,16},{16,24},{1,9},{9,17},{17,25},{2,10},{10,18},{18,26},{... | collective-permute-start | bytes 4515848 | tf_op jit(solution)/shard_map/while/body/eval_jaxpr/ppermute | solution.py:20
  1046.0 88.8 %collective-permute-start = (bf16[294,2560]{1,0:T(8,128)(2,1)}, bf16[294,2560]{1,0:T(8,128)(2,1)S(1)}, u32[]{:S(2)}, u32[]{:S(2)}) collective-permute-start(bf16[294,2560]{1,0:T(8,128)(2,1)} %get-tuple-element.5751), channel_id=1, source_target_pairs={{0,8},{8,16},{16,24},{1,9},{9,17},{17,25},{2,10},{10,18},{18,26},{... | collective-permute-start | bytes 4515848 | tf_op jit(solution)/shard_map/while/body/eval_jaxpr/ppermute | solution.py:20
  1136.5 45.7 %copy-start.22 = (f32[4,2,512]{2,1,0:T(2,128)}, f32[4,2,512]{2,1,0:T(2,128)S(1)}, u32[]{:S(2)}) copy-start(f32[4,2,512]{2,1,0:T(2,128)S(1)} %get-tuple-element.6132) | copy-start | bytes 49156 | tf_op jit(solution)/shard_map/while
  1199.3 28.1 copy-start.31
  1199.3 28.2 copy-start.29
  1199.4 28.3 copy-start.27
  1249.5 34.8 %collective-permute-start.1 = (bf16[294,2560]{1,0:T(8,128)(2,1)}, bf16[294,2560]{1,0:T(8,128)(2,1)S(1)}, u32[]{:S(2)}, u32[]{:S(2)}) collective-permute-start(bf16[294,2560]{1,0:T(8,128)(2,1)} %get-tuple-element.5821), channel_id=1, source_target_pairs={{8,0},{16,8},{24,16},{9,1},{17,9},{25,17},{10,2},{18,10},{26,18},{... | collective-permute-start | bytes 4515848 | tf_op jit(solution)/shard_map/while/body/eval_jaxpr/ppermute | solution.py:20
  1285.7 45.1 %copy-start.22 = (f32[4,2,512]{2,1,0:T(2,128)}, f32[4,2,512]{2,1,0:T(2,128)S(1)}, u32[]{:S(2)}) copy-start(f32[4,2,512]{2,1,0:T(2,128)S(1)} %get-tuple-element.6132) | copy-start | bytes 49156 | tf_op jit(solution)/shard_map/while
  1348.2 28.1 copy-start.31
  1348.2 28.2 copy-start.29
  1348.2 28.3 copy-start.27
  1398.2 57.7 %collective-permute-start.1 = (bf16[294,2560]{1,0:T(8,128)(2,1)}, bf16[294,2560]{1,0:T(8,128)(2,1)S(1)}, u32[]{:S(2)}, u32[]{:S(2)}) collective-permute-start(bf16[294,2560]{1,0:T(8,128)(2,1)} %get-tuple-element.5821), channel_id=1, source_target_pairs={{8,0},{16,8},{24,16},{9,1},{17,9},{25,17},{10,2},{18,10},{26,18},{... | collective-permute-start | bytes 4515848 | tf_op jit(solution)/shard_map/while/body/eval_jaxpr/ppermute | solution.py:20
  1399.5 19.1 copy-start.5
  1425.6 31.4 %copy-start.12 = (f32[4,2,2048]{2,1,0:T(2,128)S(1)}, f32[4,2,2048]{2,1,0:T(2,128)}, u32[]{:S(2)}) copy-start(f32[4,2,2048]{2,1,0:T(2,128)} %copy-done.11) | copy-start | bytes 196612 | tf_op jit(solution)/shard_map/while
  1425.6 31.4 %copy-start.19 = (s32[4,6,9]{2,1,0:T(8,128)S(1)}, s32[4,6,9]{2,1,0:T(8,128)}, u32[]{:S(2)}) copy-start(s32[4,6,9]{2,1,0:T(8,128)} %copy-done.18) | copy-start | bytes 2596 | tf_op jit(solution)/shard_map/while
  1425.6 31.4 %copy-start.21 = (f32[4,2,512]{2,1,0:T(2,128)S(1)}, f32[4,2,512]{2,1,0:T(2,128)}, u32[]{:S(2)}) copy-start(f32[4,2,512]{2,1,0:T(2,128)} %copy-done.20) | copy-start | bytes 49156 | tf_op jit(solution)/shard_map/while
  1425.6 31.4 %copy-start.23 = (f32[4,2,512]{2,1,0:T(2,128)S(1)}, f32[4,2,512]{2,1,0:T(2,128)}, u32[]{:S(2)}) copy-start(f32[4,2,512]{2,1,0:T(2,128)} %copy-done.22) | copy-start | bytes 49156 | tf_op jit(solution)/shard_map/while
  1457.5 45.1 %copy-start.22 = (f32[4,2,512]{2,1,0:T(2,128)}, f32[4,2,512]{2,1,0:T(2,128)S(1)}, u32[]{:S(2)}) copy-start(f32[4,2,512]{2,1,0:T(2,128)S(1)} %get-tuple-element.6132) | copy-start | bytes 49156 | tf_op jit(solution)/shard_map/while
  1519.8 28.1 copy-start.31
  1519.8 28.2 copy-start.29
  1519.8 28.3 copy-start.27
  1570.0 123.5 %collective-permute-start.1 = (bf16[294,2560]{1,0:T(8,128)(2,1)}, bf16[294,2560]{1,0:T(8,128)(2,1)S(1)}, u32[]{:S(2)}, u32[]{:S(2)}) collective-permute-start(bf16[294,2560]{1,0:T(8,128)(2,1)} %get-tuple-element.5821), channel_id=1, source_target_pairs={{8,0},{16,8},{24,16},{9,1},{17,9},{25,17},{10,2},{18,10},{26,18},{... | collective-permute-start | bytes 4515848 | tf_op jit(solution)/shard_map/while/body/eval_jaxpr/ppermute | solution.py:20
  1571.3 17.9 copy-start
  1571.3 19.1 copy-start.5
  1597.4 97.3 %copy-start.12 = (f32[4,2,2048]{2,1,0:T(2,128)S(1)}, f32[4,2,2048]{2,1,0:T(2,128)}, u32[]{:S(2)}) copy-start(f32[4,2,2048]{2,1,0:T(2,128)} %copy-done.11) | copy-start | bytes 196612 | tf_op jit(solution)/shard_map/while
  1597.4 97.3 %copy-start.19 = (s32[4,6,9]{2,1,0:T(8,128)S(1)}, s32[4,6,9]{2,1,0:T(8,128)}, u32[]{:S(2)}) copy-start(s32[4,6,9]{2,1,0:T(8,128)} %copy-done.18) | copy-start | bytes 2596 | tf_op jit(solution)/shard_map/while
  1597.4 97.2 %copy-start.21 = (f32[4,2,512]{2,1,0:T(2,128)S(1)}, f32[4,2,512]{2,1,0:T(2,128)}, u32[]{:S(2)}) copy-start(f32[4,2,512]{2,1,0:T(2,128)} %copy-done.20) | copy-start | bytes 49156 | tf_op jit(solution)/shard_map/while
  1597.4 97.2 %copy-start.23 = (f32[4,2,512]{2,1,0:T(2,128)S(1)}, f32[4,2,512]{2,1,0:T(2,128)}, u32[]{:S(2)}) copy-start(f32[4,2,512]{2,1,0:T(2,128)} %copy-done.22) | copy-start | bytes 49156 | tf_op jit(solution)/shard_map/while
  1694.9 48.2 %copy-start.22 = (f32[4,2,512]{2,1,0:T(2,128)}, f32[4,2,512]{2,1,0:T(2,128)S(1)}, u32[]{:S(2)}) copy-start(f32[4,2,512]{2,1,0:T(2,128)S(1)} %get-tuple-element.6132) | copy-start | bytes 49156 | tf_op jit(solution)/shard_map/while
  1798.5 28.1 copy-start.31
  1798.5 28.2 copy-start.29
  1798.5 28.3 copy-start.27
  1882.9 40.0 %collective-permute-start.1 = (bf16[294,2560]{1,0:T(8,128)(2,1)}, bf16[294,2560]{1,0:T(8,128)(2,1)S(1)}, u32[]{:S(2)}, u32[]{:S(2)}) collective-permute-start(bf16[294,2560]{1,0:T(8,128)(2,1)} %get-tuple-element.5821), channel_id=1, source_target_pairs={{8,0},{16,8},{24,16},{9,1},{17,9},{25,17},{10,2},{18,10},{26,18},{... | collective-permute-start | bytes 4515848 | tf_op jit(solution)/shard_map/while/body/eval_jaxpr/ppermute | solution.py:20
  1884.2 19.1 copy-start.5
  1924.6 46.5 %copy-start.22 = (f32[4,2,512]{2,1,0:T(2,128)}, f32[4,2,512]{2,1,0:T(2,128)S(1)}, u32[]{:S(2)}) copy-start(f32[4,2,512]{2,1,0:T(2,128)S(1)} %get-tuple-element.6132) | copy-start | bytes 49156 | tf_op jit(solution)/shard_map/while
  2026.3 28.1 copy-start.31
  2026.3 28.2 copy-start.29
  2026.3 28.3 copy-start.27
  2110.8 40.0 %collective-permute-start.1 = (bf16[294,2560]{1,0:T(8,128)(2,1)}, bf16[294,2560]{1,0:T(8,128)(2,1)S(1)}, u32[]{:S(2)}, u32[]{:S(2)}) collective-permute-start(bf16[294,2560]{1,0:T(8,128)(2,1)} %get-tuple-element.5821), channel_id=1, source_target_pairs={{8,0},{16,8},{24,16},{9,1},{17,9},{25,17},{10,2},{18,10},{26,18},{... | collective-permute-start | bytes 4515848 | tf_op jit(solution)/shard_map/while/body/eval_jaxpr/ppermute | solution.py:20
  2112.1 19.1 copy-start.5
  2152.2 46.5 %copy-start.22 = (f32[4,2,512]{2,1,0:T(2,128)}, f32[4,2,512]{2,1,0:T(2,128)S(1)}, u32[]{:S(2)}) copy-start(f32[4,2,512]{2,1,0:T(2,128)S(1)} %get-tuple-element.6132) | copy-start | bytes 49156 | tf_op jit(solution)/shard_map/while
  2254.1 28.1 copy-start.31
  2254.2 28.2 copy-start.29
  2254.2 28.3 copy-start.27
  2338.6 40.0 %collective-permute-start.1 = (bf16[294,2560]{1,0:T(8,128)(2,1)}, bf16[294,2560]{1,0:T(8,128)(2,1)S(1)}, u32[]{:S(2)}, u32[]{:S(2)}) collective-permute-start(bf16[294,2560]{1,0:T(8,128)(2,1)} %get-tuple-element.5821), channel_id=1, source_target_pairs={{8,0},{16,8},{24,16},{9,1},{17,9},{25,17},{10,2},{18,10},{26,18},{... | collective-permute-start | bytes 4515848 | tf_op jit(solution)/shard_map/while/body/eval_jaxpr/ppermute | solution.py:20
  2339.9 19.1 copy-start.5
  2380.2 46.5 %copy-start.22 = (f32[4,2,512]{2,1,0:T(2,128)}, f32[4,2,512]{2,1,0:T(2,128)S(1)}, u32[]{:S(2)}) copy-start(f32[4,2,512]{2,1,0:T(2,128)S(1)} %get-tuple-element.6132) | copy-start | bytes 49156 | tf_op jit(solution)/shard_map/while
  2481.9 28.1 copy-start.31
  2481.9 28.2 copy-start.29
  2482.0 28.3 copy-start.27
  2566.5 40.0 %collective-permute-start.1 = (bf16[294,2560]{1,0:T(8,128)(2,1)}, bf16[294,2560]{1,0:T(8,128)(2,1)S(1)}, u32[]{:S(2)}, u32[]{:S(2)}) collective-permute-start(bf16[294,2560]{1,0:T(8,128)(2,1)} %get-tuple-element.5821), channel_id=1, source_target_pairs={{8,0},{16,8},{24,16},{9,1},{17,9},{25,17},{10,2},{18,10},{26,18},{... | collective-permute-start | bytes 4515848 | tf_op jit(solution)/shard_map/while/body/eval_jaxpr/ppermute | solution.py:20
  2567.8 19.1 copy-start.5
  2613.3 149.2 %reduce-scatter.6.cloned.1.call-start = ((), (), s32[]{:S(2)}) async-start(), calls=%async_computation.5 | async-start | bytes 10616832 | tf_op jit(solution)/shard_map/reduce_scatter | solution.py:126
  2614.0 318.0 %reduce-scatter.8.cloned.1.call-start = ((), (), s32[]{:S(2)}) async-start(), calls=%async_computation.7 | async-start | bytes 18874368 | tf_op jit(solution)/shard_map/reduce_scatter | solution.py:127
  2614.7 346.7 %all-gather.4.cloned.1.call-start = ((), (), s32[]{:S(2)}) async-start(), calls=%async_computation.4 | async-start | bytes 2359296 | tf_op jit(solution)/shard_map/all_gather | solution.py:135
  2663.6 351.2 %all-gather.6.cloned.1.call-start = ((), (), s32[]{:S(2)}) async-start(), calls=%async_computation.6 | async-start | bytes 5308416 | tf_op jit(solution)/shard_map/all_gather | solution.py:138
  2764.6 333.1 %all-gather.8.cloned.1.call-start = ((), (), s32[]{:S(2)}) async-start(), calls=%async_computation.8 | async-start | bytes 9437184 | tf_op jit(solution)/shard_map/all_gather | solution.py:141
  (154 other events, 1102.6 us)
Sparse Core Ops, SparseCore 0:
  2613.4 48.4 reduce-scatter.3
  2664.7 97.6 reduce-scatter.5
  2765.3 166.5 reduce-scatter.7
  2934.0 27.4 all-gather.3
  2963.5 51.1 all-gather.5
  3016.8 80.8 all-gather.7
where the time goes:
time: 3130 us; the launch traced here: 3120 us
  waiting for transfers between devices  766 us (24%)
  blocking collectives  765 us (24%)
  local copies, waits for them, and re-layouts  615 us (20%)
  other arithmetic  603 us (19%)
  matrix products  185 us (6%)
  starting transfers between devices  109 us (3%)
  loops' own time  59.4 us (2%)
    psum x14, blocking collectives, norm_forward(): totals, squares, counts = lax.psum((sums[0], sums[1], sums[2]), 'dp')  387 us
    psum x14, blocking collectives, norm_backward(): offset_sum, scale_sum, counts = lax.psum((sums[0], sums[1], sums[2]), 'dp')  378 us
    ppermute x14, waiting for transfers between devices, from_behind(): return lax.ppermute(block, axis, route)  309 us
    reduce_scatter x1, waiting for transfers between devices, spread(): lax.psum_scatter(terms[2], 'dp', scatter_dimension=0, tiled=True)  167 us
    add x7, other arithmetic, backward_turn(): grad_shortcut + terms[2]  122 us
    ppermute x14, starting transfers between devices, from_behind(): return lax.ppermute(block, axis, route)  109 us
    reduce_scatter x1, waiting for transfers between devices, spread(): lax.psum_scatter(terms[1], 'dp', scatter_dimension=0, tiled=True)  98.7 us
    another operation x117, local copies, waits for them, and re-layouts  98.1 us
  transfers between devices with their start and end apart: 20, of which 16 were waited for; matrix products, arithmetic and copies ran while one was open for 9% of the time, Pallas kernels for 0%

commit v1 on v0

v1 whole, which is shorter than its diff:
```python
import functools

import jax
import jax.numpy as jnp
import numpy as np
from jax import lax
from jax.experimental import pallas as pl
from jax.experimental.pallas import tpu as pltpu
from jax.sharding import PartitionSpec as P

MAP = 7
EPSILON = 1e-05
OFFSETS = ((-1, -1), (-1, 0), (-1, 1), (0, -1), (0, 0), (0, 1), (1, -1), (1, 0), (1, 1))
MESH = pl.DeviceIdType.MESH
F32 = jnp.float32
BF16 = jnp.bfloat16


def dp_sum_kernel(count, x_ref, o_ref, slots, own_sem, send_sem, recv_sem):
    segment = lax.axis_index("segment")
    me = lax.axis_index("dp")
    barrier = pltpu.get_barrier_semaphore()

    def greet(k, carry):
        pl.semaphore_signal(
            barrier, inc=1, device_id=(segment, lax.rem(me + k, count)), device_id_type=MESH
        )
        return carry

    lax.fori_loop(1, count, greet, 0)
    pl.semaphore_wait(barrier, count - 1)

    def copy(k):
        return pltpu.make_async_remote_copy(
            src_ref=x_ref,
            dst_ref=slots.at[me],
            send_sem=send_sem.at[k],
            recv_sem=recv_sem.at[k],
            device_id=(segment, lax.rem(me + k, count)),
            device_id_type=MESH,
        )

    def start(k, carry):
        copy(k).start()
        return carry

    lax.fori_loop(1, count, start, 0)
    own = pltpu.make_async_copy(x_ref, slots.at[me], own_sem)
    own.start()
    own.wait()

    def finish(k, carry):
        copy(k).wait_recv()
        copy(k).wait_send()
        return carry

    lax.fori_loop(1, count, finish, 0)
    total = slots[0]
    for k in range(1, count):
        total = total + slots[k]
    o_ref[...] = total


def dp_sum(values, ident):
    count = lax.axis_size("dp")
    return pl.pallas_call(
        functools.partial(dp_sum_kernel, count),
        out_shape=jax.ShapeDtypeStruct(values.shape, values.dtype),
        in_specs=[pl.BlockSpec(memory_space=pltpu.VMEM)],
        out_specs=pl.BlockSpec(memory_space=pltpu.VMEM),
        scratch_shapes=[
            pltpu.VMEM((count,) + values.shape, values.dtype),
            pltpu.SemaphoreType.DMA,
            pltpu.SemaphoreType.DMA((count,)),
            pltpu.SemaphoreType.DMA((count,)),
        ],
        compiler_params=pltpu.CompilerParams(collective_id=ident, has_side_effects=True),
    )(values)


def silu_slope(values):
    sigmoid = jax.nn.sigmoid(values)
    return sigmoid * (1.0 + values * (1.0 - sigmoid))


def layouts(resolution_ids, order_ids):
    pixels = jnp.arange(MAP * MAP, dtype=jnp.int32)
    row_of = pixels // MAP
    column_of = pixels % MAP
    extent = 5 + resolution_ids[:, None]
    image_mask = ((row_of[None, :] < extent) & (column_of[None, :] < extent)).astype(F32)
    inside = (row_of < 6) & (column_of < 6)
    position = jnp.where(inside, row_of // 2 * 3 + column_of // 2, 0)
    onehot_tile = (position[:, None] == jnp.arange(9)[None, :]).astype(jnp.int32)
    picked = jnp.sum(onehot_tile[None] * order_ids[:, None, :], axis=2)
    target = (2 * (picked // 3) + row_of % 2) * MAP + 2 * (picked % 3) + column_of % 2
    moves = (inside[None, :, None] & (target[:, :, None] == pixels[None, None, :])).astype(BF16)
    tile_mask = jnp.einsum("ipq,iq->ip", moves.astype(F32), image_mask)
    return image_mask, tile_mask, moves


def tap_tables(tiled):
    lattice = np.arange(MAP)
    tables = []
    for vertical, lateral in OFFSETS:
        same_row = (lattice + vertical) // 2 == lattice // 2
        same_column = (lattice + lateral) // 2 == lattice // 2
        within = same_row[:, None] & same_column[None, :]
        tables.append(within if tiled else np.ones_like(within))
    return np.stack(tables)


def columns(activation, tiled):
    images, pixels, narrow = activation.shape
    taps = tap_tables(tiled)
    padded = jnp.pad(
        activation.reshape(images, MAP, MAP, narrow), ((0, 0), (1, 1), (1, 1), (0, 0))
    )
    pieces = []
    for number, (vertical, lateral) in enumerate(OFFSETS):
        window = padded[:, 1 + vertical : 1 + vertical + MAP, 1 + lateral : 1 + lateral + MAP, :]
        pieces.append(jnp.where(taps[number][None, :, :, None], window, jnp.zeros_like(window)))
    return jnp.concatenate(pieces, axis=-1).reshape(images * pixels, 9 * narrow)


def uncolumns(gradient, images, tiled):
    narrow = gradient.shape[-1] // 9
    taps = tap_tables(tiled)
    pieces = gradient.reshape(images, MAP, MAP, 9, narrow)
    padded = jnp.zeros((images, MAP + 2, MAP + 2, narrow), F32)
    for number, (vertical, lateral) in enumerate(OFFSETS):
        window = jnp.where(taps[number][None, :, :, None], pieces[:, :, :, number, :], 0.0)
        padded = padded + jnp.pad(
            window, ((0, 0), (1 + vertical, 1 - vertical), (1 + lateral, 1 - lateral), (0, 0))
        )
    return padded[:, 1 : 1 + MAP, 1 : 1 + MAP, :].reshape(images * MAP * MAP, narrow)


def batched(values, batches):
    return values.reshape((batches, values.shape[0] // batches) + values.shape[1:])


def norm_stats(hidden, mask, batches, ident):
    h = batched(hidden, batches)
    m = batched(mask, batches)
    width = hidden.shape[1]
    sums = jnp.concatenate(
        [
            jnp.sum(m * h, axis=1),
            jnp.sum(m * h * h, axis=1),
            jnp.broadcast_to(jnp.sum(m, axis=1), (batches, width)),
        ]
    )
    sums = dp_sum(sums, ident)
    counts = sums[2 * batches :]
    average = sums[:batches] / counts
    inverse = lax.rsqrt(sums[batches : 2 * batches] / counts - average * average + EPSILON)
    return average[:, None, :], inverse[:, None, :], counts[:, None, :]


def norm_apply(hidden, stats, gain, bias, batches):
    average, inverse, _ = stats
    out = gain * (batched(hidden, batches) - average) * inverse + bias
    return out.reshape(hidden.shape)


def norm_back(grad_out, hidden, stats, mask, gain, batches, ident):
    average, inverse, counts = stats
    g = batched(grad_out, batches)
    normed = (batched(hidden, batches) - average) * inverse
    sums = dp_sum(jnp.concatenate([jnp.sum(g, axis=1), jnp.sum(g * normed, axis=1)]), ident)
    offset, scale = sums[:batches, None, :], sums[batches:, None, :]
    out = batched(mask, batches) * gain * inverse * (g - (offset + normed * scale) / counts)
    return (
        out.reshape(hidden.shape).astype(BF16),
        jnp.sum(scale, axis=(0, 1)),
        jnp.sum(offset, axis=(0, 1)),
    )


def mm(a, b, dims="rk,kn->rn"):
    return jnp.einsum(dims, a, b, preferred_element_type=F32)


def to_section_zero(value):
    sections = lax.axis_size("segment")
    parts = [value] + [lax.ppermute(value, "segment", [(t, 0)]) for t in range(1, sections)]
    return jnp.stack(parts)


def core_swap(value):
    count = lax.axis_size("dp")
    return lax.ppermute(value, "dp", [(d, d ^ 1) for d in range(count)])


def body(
    layer_input,
    output_grad,
    resolution,
    tile_order,
    proj_weight,
    spatial_weight,
    shortcut_weight,
    bn_gain,
    bn_bias,
):
    micro, images, pixels, wide = layer_input.shape
    narrow = proj_weight.shape[2]
    rows = images * pixels
    sections = lax.axis_size("segment")
    count = lax.axis_size("dp")
    section = lax.axis_index("segment")
    place = lax.axis_index("dp")
    core = place % 2
    first = section == 0
    proj, spatial, shortcut = proj_weight[0], spatial_weight[0], shortcut_weight[0]

    slice_rows = wide // count
    tap_rows = spatial.shape[0] // count
    own_proj = lax.dynamic_slice_in_dim(proj, place * slice_rows, slice_rows)
    own_taps = lax.dynamic_slice_in_dim(spatial, place * tap_rows, tap_rows)
    fine = tap_rows // sections
    taps_piece = lax.dynamic_slice_in_dim(own_taps, 2 * fine, fine)
    for t in range(sections):
        if t != 2:
            got = lax.ppermute(own_taps[t * fine : (t + 1) * fine], "segment", [(2, t)])
            taps_piece = jnp.where(section == t, got, taps_piece)
    packed = jnp.concatenate([own_proj, taps_piece])
    everyone = lax.all_gather(packed, ("segment", "dp"), axis=0, tiled=True)
    everyone = everyone.reshape(sections, count, slice_rows + fine, narrow)
    proj_of = [everyone[k, :, :slice_rows].reshape(wide, narrow) for k in range(sections)]
    taps_two = jnp.swapaxes(everyone[:, :, slice_rows:], 0, 1).reshape(9 * narrow, narrow)

    quarter = wide // sections
    half = wide // 2
    own_half = lax.dynamic_slice_in_dim(shortcut, core * half, half)
    short_half = own_half[:, :quarter]
    for t in range(1, sections):
        got = lax.ppermute(own_half[:, t * quarter : (t + 1) * quarter], "segment", [(0, t)])
        short_half = jnp.where(section == t, got, short_half)
    short_other = core_swap(short_half)
    short_quarter = jnp.where(
        core == 0,
        jnp.concatenate([short_half, short_other]),
        jnp.concatenate([short_other, short_half]),
    )

    stats_gain = jnp.concatenate([bn_gain[0], bn_bias[0]])
    gains = lax.all_gather(stats_gain, "segment", axis=0)
    gain, bias = gains[:, :wide], gains[:, wide:]

    image_mask_all, tile_mask_all, moves_all = layouts(
        resolution.reshape(-1), tile_order.reshape(micro * images, -1)
    )
    mask_all = image_mask_all.reshape(micro * rows, 1)
    pick = lambda a: lax.dynamic_index_in_dim(a, section, 0, keepdims=False)
    image_mask = pick(image_mask_all.reshape(micro, rows, 1))
    tile_mask = pick(tile_mask_all.reshape(micro, rows, 1))
    moves = pick(moves_all.reshape(micro, images, pixels, pixels))

    flat_all = layer_input.reshape(micro * rows, wide)
    gain_a, bias_a = bn_gain[0, :narrow], bn_bias[0, :narrow]
    gain_b, bias_b = bn_gain[0, narrow : 2 * narrow], bn_bias[0, narrow : 2 * narrow]
    hidden_one = mm(flat_all, proj)
    stats_one = norm_stats(hidden_one, mask_all, micro, 0)
    normed_one = norm_apply(hidden_one, stats_one, gain_a, bias_a, micro)
    act_one = (mask_all * jax.nn.silu(normed_one)).astype(BF16)
    hidden_two = mm(columns(act_one.reshape(micro * images, pixels, narrow), False), spatial)
    stats_two = norm_stats(hidden_two, mask_all, micro, 1)
    normed_two = norm_apply(hidden_two, stats_two, gain_b, bias_b, micro)
    act_two_all = (mask_all * jax.nn.silu(normed_two)).astype(BF16)
    act_two_parts = act_two_all.reshape(micro, rows, narrow)
    act_two = act_two_parts[0]
    for t in range(1, sections):
        got = lax.ppermute(act_two_parts[t], "segment", [(0, t)])
        act_two = jnp.where(section == t, got, act_two)

    residual_quarter = mm(flat_all, short_quarter).astype(BF16).reshape(micro, rows, quarter)
    residual = lax.all_to_all(residual_quarter, "segment", 0, 2, tiled=True).reshape(rows, wide)

    hidden_three = mm(act_two, proj_of[1], "rk,dk->rd")
    stats_three = norm_stats(hidden_three, image_mask, 1, 2)
    summed = norm_apply(hidden_three, stats_three, gain[1], bias[1], 1) + residual.astype(F32)
    first_out = (image_mask * jax.nn.silu(summed)).astype(BF16)

    moved = mm(moves, first_out.reshape(images, pixels, wide), "ipq,iqd->ipd").astype(BF16)
    moved = moved.reshape(rows, wide)
    tile_gain_a, tile_bias_a = gain[2, :narrow], bias[2, :narrow]
    tile_gain_b, tile_bias_b = gain[2, narrow : 2 * narrow], bias[2, narrow : 2 * narrow]
    tile_one = mm(moved, proj_of[2])
    tile_stats_one = norm_stats(tile_one, tile_mask, 1, 3)
    tile_normed_one = norm_apply(tile_one, tile_stats_one, tile_gain_a, tile_bias_a, 1)
    tile_act_one = (tile_mask * jax.nn.silu(tile_normed_one)).astype(BF16)
    tile_columns = columns(tile_act_one.reshape(images, pixels, narrow), True)
    tile_two = mm(tile_columns, taps_two)
    tile_stats_two = norm_stats(tile_two, tile_mask, 1, 4)
    tile_normed_two = norm_apply(tile_two, tile_stats_two, tile_gain_b, tile_bias_b, 1)
    tile_act_two = (tile_mask * jax.nn.silu(tile_normed_two)).astype(BF16)
    tile_three = mm(tile_act_two, proj_of[3], "rk,dk->rd")
    tile_stats_three = norm_stats(tile_three, tile_mask, 1, 5)
    tile_summed = norm_apply(tile_three, tile_stats_three, gain[3], bias[3], 1) + moved.astype(F32)
    second_out = (tile_mask * jax.nn.silu(tile_summed)).astype(BF16)

    grad = pick(output_grad).reshape(rows, wide)
    grad_summed = (grad.astype(F32) * tile_mask * silu_slope(tile_summed)).astype(BF16)
    grad_three, scale_3, offset_3 = norm_back(
        grad_summed.astype(F32), tile_three, tile_stats_three, tile_mask, gain[3], 1, 6
    )
    proj_term_3 = mm(grad_three, tile_act_two, "rd,rk->dk")
    grad_act_two = mm(grad_three, proj_of[3]).astype(BF16)
    grad_normed = grad_act_two.astype(F32) * tile_mask * silu_slope(tile_normed_two)
    grad_two, scale_2b, offset_2b = norm_back(
        grad_normed, tile_two, tile_stats_two, tile_mask, tile_gain_b, 1, 7
    )
    taps_term_2 = mm(tile_columns, grad_two, "rk,rn->kn")
    grad_act_one = uncolumns(mm(grad_two, taps_two, "rn,kn->rk"), images, True)
    grad_normed = grad_act_one * tile_mask * silu_slope(tile_normed_one)
    grad_one, scale_2a, offset_2a = norm_back(
        grad_normed, tile_one, tile_stats_one, tile_mask, tile_gain_a, 1, 8
    )
    proj_term_2 = mm(moved, grad_one, "rc,rn->cn")
    grad_moved = (mm(grad_one, proj_of[2], "rn,cn->rc") + grad_summed.astype(F32)).astype(BF16)
    grad_first = mm(moves, grad_moved.reshape(images, pixels, wide), "ipq,ipd->iqd").astype(BF16)
    grad_first = grad_first.reshape(rows, wide)

    grad_sum_one = (grad_first.astype(F32) * image_mask * silu_slope(summed)).astype(BF16)
    grad_sum_all = to_section_zero(grad_sum_one).reshape(micro * rows, wide)
    grad_sum_quarter = lax.all_to_all(
        grad_sum_one.reshape(rows, sections, quarter), "segment", 1, 0, tiled=True
    ).reshape(micro * rows, quarter)
    short_term = mm(flat_all, grad_sum_quarter, "rc,rd->cd")
    grad_hidden_three, scale_1, offset_1 = norm_back(
        grad_sum_one.astype(F32), hidden_three, stats_three, image_mask, gain[1], 1, 9
    )
    proj_term_1 = mm(grad_hidden_three, act_two, "rd,rk->dk")
    grad_act_two = to_section_zero(mm(grad_hidden_three, proj_of[1]).astype(BF16))
    grad_act_two = grad_act_two.reshape(micro * rows, narrow)

    grad_normed = grad_act_two.astype(F32) * mask_all * silu_slope(normed_two)
    grad_hidden_two, scale_0b, offset_0b = norm_back(
        grad_normed, hidden_two, stats_two, mask_all, gain_b, micro, 10
    )
    taps_term_0 = mm(
        columns(act_one.reshape(micro * images, pixels, narrow), False),
        grad_hidden_two,
        "rk,rn->kn",
    )
    grad_act_one = uncolumns(mm(grad_hidden_two, spatial, "rn,kn->rk"), micro * images, False)
    grad_normed = grad_act_one * mask_all * silu_slope(normed_one)
    grad_hidden_one, scale_0a, offset_0a = norm_back(
        grad_normed, hidden_one, stats_one, mask_all, gain_a, micro, 11
    )
    proj_term_0 = mm(flat_all, grad_hidden_one, "rc,rn->cn")
    grad_input = (
        mm(grad_hidden_one, proj, "rn,cn->rc") + mm(grad_sum_all, shortcut, "rd,cd->rc")
    ).astype(BF16)

    as_map = lambda a: a.reshape(images, pixels, wide)
    exchanged = lax.all_to_all(
        jnp.stack([as_map(first_out), as_map(first_out), as_map(grad_first), as_map(second_out)]),
        "segment",
        0,
        0,
        tiled=True,
    )
    maps = jnp.where(first, grad_input.reshape(micro, images, pixels, wide), exchanged)

    blank = jnp.zeros((wide,), F32)
    pad = jnp.zeros((wide - 2 * narrow,), F32)
    zero_gain = jnp.where(first, jnp.concatenate([scale_0a, scale_0b, pad]), blank)
    zero_bias = jnp.where(first, jnp.concatenate([offset_0a, offset_0b, pad]), blank)
    vectors = jnp.stack(
        [
            zero_gain,
            zero_bias,
            scale_1,
            offset_1,
            jnp.concatenate([scale_2a, scale_2b, pad]),
            jnp.concatenate([offset_2a, offset_2b, pad]),
            scale_3,
            offset_3,
        ]
    )
    vectors = pick(lax.psum(vectors, "segment").reshape(sections, 2, wide))

    def halved(term):
        rows_half = term.shape[0] // 2
        mine = lax.dynamic_slice_in_dim(term, core * rows_half, rows_half)
        theirs = lax.dynamic_slice_in_dim(term, (1 - core) * rows_half, rows_half)
        return mine + core_swap(theirs.astype(BF16)).astype(F32)

    def planar(term):
        part = halved(term).astype(BF16)
        part = lax.all_to_all(
            part.reshape((sections, part.shape[0] // sections) + part.shape[1:]),
            "segment",
            0,
            0,
        )
        return jnp.sum(part.astype(F32), axis=0)

    keep = lambda term: jnp.where(first, term, jnp.zeros_like(term))
    stacked = [
        planar(keep(proj_term_0)),
        planar(keep(taps_term_0)),
        planar(proj_term_1),
        planar(proj_term_2),
        planar(taps_term_2),
        planar(proj_term_3),
        halved(short_term),
    ]
    heights = [a.shape[0] for a in stacked]
    groups = [[d for d in range(count) if d % 2 == c] for c in range(2)]
    depth = count // 2
    joined = jnp.concatenate(
        [a.astype(BF16).reshape(depth, a.shape[0] // depth, narrow) for a in stacked], axis=1
    )
    summed_up = lax.psum_scatter(
        joined, "dp", scatter_dimension=0, tiled=False, axis_index_groups=groups
    )
    whole = lax.all_gather(summed_up.astype(BF16), "dp", axis=0, axis_index_groups=groups)
    pieces, at = [], 0
    for h in heights:
        pieces.append(whole[:, at : at + h // depth].reshape(h, narrow))
        at += h // depth
    none_taps, none_short = jnp.zeros_like(pieces[1]), jnp.zeros_like(pieces[6])
    parcels = jnp.stack(
        [
            jnp.concatenate([pieces[0], pieces[1], pieces[6]]),
            jnp.concatenate([pieces[2], none_taps, none_short]),
            jnp.concatenate([pieces[3], pieces[4], none_short]),
            jnp.concatenate([pieces[5], none_taps, none_short]),
        ]
    )
    parcels = lax.all_to_all(parcels, "segment", 0, 0)
    other = core_swap(parcels)
    both = jnp.where(core == 0, jnp.stack([parcels, other]), jnp.stack([other, parcels]))
    hp, ht = heights[0], heights[1]
    proj_grad = both[:, :, :hp].reshape(wide, narrow).astype(F32)
    spatial_grad = both[:, :, hp : hp + ht].reshape(9 * narrow, narrow).astype(F32)
    short_grad = jnp.swapaxes(both[:, :, hp + ht :], 1, 2).reshape(wide, wide).astype(F32)
    return (
        maps[None],
        proj_grad[None],
        spatial_grad[None],
        short_grad[None],
        vectors[:1],
        vectors[1:],
    )


def solution(mesh):
    return jax.shard_map(
        body,
        mesh=mesh,
        in_specs=(
            P(None, "dp", None, None),
            P(None, "dp", None, None),
            P(None, "dp"),
            P(None, "dp", None),
            P("segment", None, None),
            P("segment", None, None),
            P("segment", None, None),
            P("segment", None),
            P("segment", None),
        ),
        out_specs=(
            P("segment", None, "dp", None, None),
            P("segment", None, None),
            P("segment", None, None),
            P("segment", None, None),
            P("segment", None),
            P("segment", None),
        ),
        check_vma=False,
    )
```

time: 3130 us -> 1200 us (0.38)
  blocking collectives: 765 us -> 95.4 us
  waiting for transfers between devices: 766 us -> 252 us
  other arithmetic: 603 us -> 212 us
  local copies, waits for them, and re-layouts: 615 us -> 289 us
  Pallas kernels: 0 us -> 115 us
  loops' own time: 59.4 us -> 0 us
  matrix products: 185 us -> 134 us
  starting transfers between devices: 109 us -> 72.9 us
    psum x28 -> x0, blocking collectives: 765 us -> none  [the longest x14 387 us: norm_forward(): totals, squares, counts = lax.psum((sums[0], sums[1], sums[2]), 'dp')]
    ppermute x14 -> x24, waiting for transfers between devices: 309 us -> 5.45 us  [the longest x3 5.39 us: body(): got = lax.ppermute(own_taps[t * fine:(t + 1) * fine], 'segment', [(2, t)])]
    add x74 -> x7, other arithmetic: 267 us -> 11.9 us  [the longest x4 11.9 us: norm_apply(): out = gain * (batched(hidden, batches) - average) * inverse + bias]
    reduce_scatter x3 -> x1, waiting for transfers between devices: 313 us -> 64 us  [body(): lax.psum_scatter(joined, 'dp', scatter_dimension=0, tiled=False, axis_ind...]
    gather x112 -> x0, local copies, waits for them, and re-layouts: 147 us -> none  [the longest x24 81.1 us: gather_rows(): moved = jnp.take_along_axis(values, indices[:, :, None], axis=1)]
    pallas_call x0 -> x12, Pallas kernels: none -> 115 us  [dp_sum(): pl.pallas_call(functools.partial(dp_sum_kernel, count), out_shape=jax.Sha...]
    another operation x117 -> x1, local copies, waits for them, and re-layouts: 98.1 us -> 0.11 us  [body(): jnp.stack([zero_gain, zero_bias, scale_1, offset_1, jnp.concatenate([scal...]
    convert_element_type x0 -> x22, local copies, waits for them, and re-layouts: none -> 93.8 us  [the longest x2 41.4 us: body(): jnp.swapaxes(both[:, :, hp + ht:], 1, 2).reshape(wide, wide).astype(F32)]
  transfers between devices with their start and end apart: 20 -> 37, of which waited for: 16 -> 8; matrix products, arithmetic and copies ran while one was open for 9% -> 33% of each run, Pallas kernels for 0% -> 4%
where the time goes in v1:
time: 1200 us; the launch traced here: 1190 us
  local copies, waits for them, and re-layouts  289 us (24%)
  waiting for transfers between devices  252 us (21%)
  other arithmetic  212 us (18%)
  matrix products  134 us (11%)
  Pallas kernels  115 us (10%)
  blocking collectives  95.4 us (8%)
  starting transfers between devices  72.9 us (6%)
  between operations  16 us (1%)
    dot_general x23, matrix products, mm(): return jnp.einsum(dims, a, b, preferred_element_type=F32)  134 us
    pallas_call x12, Pallas kernels, dp_sum(): pl.pallas_call(functools.partial(dp_sum_kernel, count), out_shape=jax.Sha...  115 us
    all_to_all x1, blocking collectives, body(): parcels = lax.all_to_all(parcels, 'segment', 0, 0)  88.3 us
    psum x1, waiting for transfers between devices, body(): vectors = pick(lax.psum(vectors, 'segment').reshape(sections, 2, wide))  78.1 us
    all_gather x1, waiting for transfers between devices, body(): lax.all_gather(summed_up.astype(BF16), 'dp', axis=0, axis_index_groups=gr...  67.2 us
    reduce_scatter x1, waiting for transfers between devices, body(): lax.psum_scatter(joined, 'dp', scatter_dimension=0, tiled=False, axis_ind...  64 us
    unnamed x242, local copies, waits for them, and re-layouts  48.3 us
    convert_element_type x2, local copies, waits for them, and re-layouts, body(): jnp.swapaxes(both[:, :, hp + ht:], 1, 2).reshape(wide, wide).astype(F32)  41.4 us
  transfers between devices with their start and end apart: 37, of which 8 were waited for; matrix products, arithmetic and copies ran while one was open for 33% of the time, Pallas kernels for 4%

profile of v1, /device:TPU:0, one launch (start us, length us, event | category | flops | bytes accessed | tf_op | source)
XLA Modules:
  0.0 1186.1 jit_solution(6920546056046724484)
XLA Ops:
  11.2 5.4 collective-permute-done.5
  23.8 7.0 collective-permute-start.8
  37.1 9.6 multiply_reduce_fusion.3
  47.4 12.0 %shard_map.541 = f32[12,512]{1,0:T(8,128)} custom-call(f32[12,512]{1,0:T(8,128)} %maximum_maximum_fusion.x_ref), custom_call_target="tpu_custom_call" | custom-call | tf_op jit(solution)/shard_map/pallas_call | solution.py:66
  83.1 10.1 dot_general.82
  93.2 12.5 %multiply_reduce_fusion.2 = (f32[4,512]{1,0:T(4,128)S(1)}, f32[4,512]{1,0:T(4,128)S(1)}, f32[4,294,512]{2,1,0:T(8,128)}) fusion(f32[4,294]{1,0:T(4,128)S(1)} %and_convert_fusion.2, bf16[4,294,4608]{2,1,0:T(8,128)(2,1)} %dot_general.82, bf16[1,4608,512]{2,1,0:T(8,128)(2,1)} %param.59), kind=kOutput, calls=%fused_computation.40 | convolution fusion | flops 5551468544 | bytes 17986144 | tf_op jit(solution)/shard_map/rk,kn->rn/dot_general | solution.py:182
  106.4 15.7 %shard_map.542 = f32[12,512]{1,0:T(8,128)} custom-call(f32[12,512]{1,0:T(8,128)} %maximum_maximum_fusion.1.x_ref), custom_call_target="tpu_custom_call" | custom-call | tf_op jit(solution)/shard_map/pallas_call | solution.py:66
  143.7 7.5 copy.200
  151.4 7.1 all-gather
  158.6 6.4 reshape.1174
  165.0 11.0 convert_reduce_fusion.2
  176.7 6.3 fusion.5
  188.5 17.1 %reshape.1189 = bf16[1176,4608]{1,0:T(8,128)(2,1)} reshape(bf16[24,7,7,4608]{3,2,1,0:T(8,128)(2,1)} %fusion.38) | data formatting | bytes 21676032 | tf_op jit(solution)/shard_map/reshape | solution.py:123
  227.9 4.9 slice_bitcast_fusion
  232.9 5.5 fusion.129
  241.4 14.1 %shard_map.543 = f32[3,2048]{1,0:T(4,128)} custom-call(f32[3,2048]{1,0:T(4,128)} %maximum_maximum_fusion.2.x_ref), custom_call_target="tpu_custom_call" | custom-call | tf_op jit(solution)/shard_map/pallas_call | solution.py:66
  268.3 5.1 copy.202
  280.6 8.1 shard_map.544
  299.4 5.4 reshape.1178
  304.8 4.8 multiply_reduce_fusion.6
  310.3 7.4 shard_map.545
  323.7 9.9 shard_map.546
  334.6 6.2 convert_reduce_fusion
  341.5 8.8 shard_map.547
  356.6 7.6 shard_map.548
  366.7 4.8 fusion.78
  379.1 7.0 shard_map.549
  407.0 5.8 convert_reduce_fusion.1
  413.4 8.1 shard_map.550
  434.6 5.2 fusion.143
  448.8 5.9 all-to-all-start.8
  467.0 8.1 shard_map.551
  482.7 12.7 %fusion.43 = f32[24,7,7,9,512]{4,0,3,2,1:T(8,128)} fusion(bf16[9,512,512,1,1]{2,1,0,4,3:T(8,128)(2,1)} %bitcast.393, bf16[24,7,7,512,1]{3,2,1,0,4:T(8,128)(2,1)} %bitcast.369), kind=kOutput, calls=%fused_computation.147 | convolution fusion | flops 5549064192 | bytes 27598848 | tf_op jit(solution)/shard_map/rn,kn->rk/dot_general | solution.py:182
  495.4 13.3 %slice_bitcast_fusion.9 = (f32[24,7,7,512]{3,0,2,1:T(8,128)}, f32[24,7,7,512]{3,0,2,1:T(8,128)S(1)}, f32[24,7,7,512]{3,0,2,1:T(8,128)S(1)}, f32[24,7,7,512]{3,0,...) fusion(f32[24,7,7,9,512]{4,0,3,2,1:T(8,128)} %fusion.43), kind=kLoop, calls=%fused_computation.95 | loop fusion | bytes 43352064 | tf_op jit(solution)/shard_map/squeeze | solution.py:132
  512.8 6.0 pad_add_fusion.1
  518.8 4.6 copy.223
  526.4 4.7 fusion.125
  531.7 8.2 shard_map.552
  558.0 5.3 convolution_select_fusion.1
  576.9 11.8 convolution_select_fusion
  603.0 6.4 all-to-all-done.4
  613.6 5.3 add_convert_fusion.1
  618.8 7.9 all-to-all-done.2
  633.9 5.3 add_convert_fusion.2
  639.1 19.3 %all-to-all-done.6 = bf16[4,576,512]{2,1,0:T(8,128)(2,1)} async-done(((bf16[4,576,512]{2,1,0:T(8,128)(2,1)}), bf16[4,576,512]{2,1,0:T(8,128)(2,1)}, u32[]{:S(2)}, u32[]{:S(2)}) %all-to-all-start.6) | async-done | bytes 2359328 | tf_op jit(solution)/shard_map/all_to_all | solution.py:394
  658.4 4.5 all-to-all-start.3
  663.0 5.3 fusion.144
  703.2 64.0 %reduce-scatter.2.cloned.1.call-done = bf16[1,800,512]{2,1,0:T(8,128)(2,1)} async-done(((bf16[4,800,512]{2,1,0:T(8,128)(2,1)}), bf16[1,800,512]{2,1,0:T(8,128)(2,1)}) %reduce-scatter.2.cloned.1.call-update) | async-done | bytes 819216 | tf_op jit(solution)/shard_map/reduce_scatter | solution.py:418
  767.3 67.2 %all-gather.6.cloned.1.call-done = bf16[4,800,512]{2,1,0:T(8,128)(2,1)} async-done(((bf16[1,800,512]{2,1,0:T(8,128)(2,1)}), bf16[4,800,512]{2,1,0:T(8,128)(2,1)}) %all-gather.6.cloned.1.call-update) | async-done | bytes 3276816 | tf_op jit(solution)/shard_map/all_gather | solution.py:421
  840.9 88.3 %all_to_all.64 = bf16[4,1856,512]{2,1,0:T(8,128)(2,1)} all-to-all(bf16[4,1856,512]{2,1,0:T(8,128)(2,1)S(1)} %pad_maximum_fusion), channel_id=1, replica_groups=mesh['segment'=4,'dp'=8] {'segment'}, dimensions={0} | all-to-all | bytes 15204352 | tf_op jit(solution)/shard_map/all_to_all | solution.py:435
  929.3 4.7 copy.224
  956.9 6.8 all-to-all-start.1
  964.6 6.6 fusion.28
  971.3 78.1 %all-reduce.22.cloned.1.call-done = f32[4,2,2048]{2,1,0:T(2,128)} async-done(((f32[4,2,2048]{2,1,0:T(2,128)}), f32[4,2,2048]{2,1,0:T(2,128)}) %all-reduce.22.cloned.1.call-update) | async-done | bytes 65552 | tf_op jit(solution)/shard_map/psum | solution.py:384
  1054.7 5.8 reshape.1183
  1060.6 17.0 %add_convert_fusion = bf16[1176,2048]{1,0:T(8,128)(2,1)} fusion(f32[1176,2048]{1,0:T(8,128)} %fusion.28, bf16[1176,2048]{1,0:T(8,128)(2,1)} %reshape.1183, bf16[1,2048,2048]{2,1,0:T(8,128)(2,1)} %param.60), kind=kOutput, calls=%fused_computation.2 | convolution fusion | flops 9869819904 | bytes 27656192 | tf_op jit(solution)/shard_map/rd,cd->rc/dot_general | solution.py:182
  1077.5 6.5 reshape.1184
  1087.2 6.0 copy.233
  1093.2 14.7 %maximum_select_fusion = bf16[2,4,1856,512]{3,2,1,0:T(8,128)(2,1)S(1)} fusion(bf16[1,4,1856,512]{3,2,1,0:T(8,128)(2,1)} %bitcast.144, bf16[1,4,1856,512]{3,2,1,0:T(8,128)(2,1)} %bitcast.143, pred[]{:T(512)S(6)} %eq.80), kind=kLoop, calls=%fused_computation.1 | loop fusion | flops 22806528 | bytes 30408704 | tf_op jit(solution)/shard_map/jit(_where)/select_n | solution.py:437
  1108.0 5.2 copy-done.1
  1115.7 12.0 %convert_bitcast_fusion = f32[2,1024,4,512]{3,1,2,0:T(8,128)} fusion(bf16[2,4,1856,512]{3,2,1,0:T(8,128)(2,1)} %copy-done.1), kind=kLoop, calls=%fused_computation | loop fusion | flops 4194304 | bytes 25165824 | tf_op jit(solution)/shard_map/convert_element_type | solution.py:441
  1130.3 20.9 %copy.232 = f32[2,1024,4,512]{3,2,1,0:T(4,128)} copy(f32[2,1024,4,512]{3,1,2,0:T(8,128)} %convert_bitcast_fusion) | data formatting | bytes 33554432 | tf_op jit(solution)/shard_map/convert_element_type | solution.py:441
  1151.2 20.5 %reshape.1221 = f32[1,2048,2048]{2,1,0:T(8,128)} reshape(f32[2,1024,4,512]{3,2,1,0:T(4,128)} %copy.232) | data formatting | bytes 33554432 | tf_op jit(solution)/shard_map/convert_element_type | solution.py:441
  1171.7 7.4 convert.28
  (498 shorter events, 357.5 us)
Async XLA Ops:
  7.2 220.8 %all-gather.4.cloned.1.call-start = ((), (), s32[]{:S(2)}) async-start(), calls=%async_computation.11 | async-start | bytes 13516800 | tf_op jit(solution)/shard_map/all_gather | solution.py:229
  8.5 8.1 collective-permute-start.5
  9.8 6.8 collective-permute-start.4
  10.4 6.1 collective-permute-start.3
  20.9 15.3 %copy-start.107 = (s32[4,6]{1,0:T(4,128)S(1)}, s32[4,6]{1,0:T(4,128)}, u32[]{:S(2)}) copy-start(s32[4,6]{1,0:T(4,128)} %param.56) | copy-start | bytes 292
  23.8 115.1 %collective-permute-start.8 = (bf16[1024,512]{1,0:T(8,128)(2,1)}, bf16[1024,512]{1,0:T(8,128)(2,1)S(1)}, u32[]{:S(2)}, u32[]{:S(2)}) collective-permute-start(bf16[1024,512]{1,0:T(8,128)(2,1)} %get-tuple-element.112), channel_id=1, source_target_pairs={{0,8},{1,9},{2,10},{3,11},{4,12},{5,13},{6,14},{7,15}} | collective-permute-start | bytes 3145736 | tf_op jit(solution)/shard_map/ppermute | solution.py:239
  30.8 110.1 %collective-permute-start.7 = (bf16[1024,512]{1,0:T(8,128)(2,1)}, bf16[1024,512]{1,0:T(8,128)(2,1)}, u32[]{:S(2)}, u32[]{:S(2)}) collective-permute-start(bf16[1024,512]{1,0:T(8,128)(2,1)} %get-tuple-element.113), channel_id=1, source_target_pairs={{0,16},{1,17},{2,18},{3,19},{4,20},{5,21},{6,22},{7,23}} | collective-permute-start | bytes 3145736 | tf_op jit(solution)/shard_map/ppermute | solution.py:239
  33.2 107.8 %collective-permute-start.6 = (bf16[1024,512]{1,0:T(8,128)(2,1)}, bf16[1024,512]{1,0:T(8,128)(2,1)}, u32[]{:S(2)}, u32[]{:S(2)}) collective-permute-start(bf16[1024,512]{1,0:T(8,128)(2,1)} %get-tuple-element.114), channel_id=1, source_target_pairs={{0,24},{1,25},{2,26},{3,27},{4,28},{5,29},{6,30},{7,31}} | collective-permute-start | bytes 3145736 | tf_op jit(solution)/shard_map/ppermute | solution.py:239
  37.1 22.2 %copy-start.74 = (f32[1,2048]{1,0:T(1,128)S(1)}, f32[1,2048]{1,0:T(1,128)}, u32[]{:S(2)}) copy-start(f32[1,2048]{1,0:T(1,128)} %param.61) | copy-start | bytes 24580
  37.1 22.2 %copy-start.73 = (f32[1,2048]{1,0:T(1,128)S(1)}, f32[1,2048]{1,0:T(1,128)}, u32[]{:S(2)}) copy-start(f32[1,2048]{1,0:T(1,128)} %param.62) | copy-start | bytes 24580
  59.4 64.1 %copy-start.57 = (f32[1,512]{1,0:T(1,128)}, f32[1,512]{1,0:T(1,128)S(1)}, u32[]{:S(2)}) copy-start(f32[1,512]{1,0:T(1,128)S(1)} %get-tuple-element.154) | copy-start | bytes 6148
  59.4 64.1 %copy-start.65 = (f32[1,512]{1,0:T(1,128)}, f32[1,512]{1,0:T(1,128)S(1)}, u32[]{:S(2)}) copy-start(f32[1,512]{1,0:T(1,128)S(1)} %get-tuple-element.156) | copy-start | bytes 6148
  134.9 79.5 %collective-permute-start.2 = (bf16[294,512]{1,0:T(8,128)(2,1)}, bf16[294,512]{1,0:T(8,128)(2,1)}, u32[]{:S(2)}, u32[]{:S(2)}) collective-permute-start(bf16[294,512]{1,0:T(8,128)(2,1)} %get-tuple-element.121), channel_id=1, source_target_pairs={{0,8},{1,9},{2,10},{3,11},{4,12},{5,13},{6,14},{7,15}} | collective-permute-start | bytes 903176 | tf_op jit(solution)/shard_map/ppermute | solution.py:275
  136.9 77.5 %collective-permute-start.1 = (bf16[294,512]{1,0:T(8,128)(2,1)}, bf16[294,512]{1,0:T(8,128)(2,1)}, u32[]{:S(2)}, u32[]{:S(2)}) collective-permute-start(bf16[294,512]{1,0:T(8,128)(2,1)} %get-tuple-element.122), channel_id=1, source_target_pairs={{0,16},{1,17},{2,18},{3,19},{4,20},{5,21},{6,22},{7,23}} | collective-permute-start | bytes 903176 | tf_op jit(solution)/shard_map/ppermute | solution.py:275
  139.0 75.4 %collective-permute-start = (bf16[294,512]{1,0:T(8,128)(2,1)}, bf16[294,512]{1,0:T(8,128)(2,1)}, u32[]{:S(2)}, u32[]{:S(2)}) collective-permute-start(bf16[294,512]{1,0:T(8,128)(2,1)} %get-tuple-element.123), channel_id=1, source_target_pairs={{0,24},{1,25},{2,26},{3,27},{4,28},{5,29},{6,30},{7,31}} | collective-permute-start | bytes 903176 | tf_op jit(solution)/shard_map/ppermute | solution.py:275
  143.4 33.4 %collective-permute-start.9 = (bf16[1024,512]{1,0:T(8,128)(2,1)}, bf16[1024,512]{1,0:T(8,128)(2,1)}, u32[]{:S(2)}, u32[]{:S(2)}) collective-permute-start(bf16[1024,512]{1,0:T(8,128)(2,1)} %fusion.48), channel_id=1, source_target_pairs={{0,1},{1,0},{2,3},{3,2},{4,5},{5,4},{6,7},{7,6},{8,9},{9,8},{10,11... | collective-permute-start | bytes 3145736 | tf_op jit(solution)/shard_map/ppermute | solution.py:193
  143.7 44.4 %copy-start.109 = (pred[49]{0:T(512)(128)(4,1)}, pred[49]{0:T(512)(128)(4,1)S(1)}, u32[]{:S(2)}) copy-start(pred[49]{0:T(512)(128)(4,1)S(1)} %compare_and_fusion.1) | copy-start | bytes 151
  176.7 80.2 %copy-start.46 = (f32[1,2048]{1,0:T(1,128)}, f32[1,2048]{1,0:T(1,128)S(1)}, u32[]{:S(2)}) copy-start(f32[1,2048]{1,0:T(1,128)S(1)} %get-tuple-element.128) | copy-start | bytes 24580
  184.4 31.7 %all-to-all-start = ((bf16[4,294,512]{2,1,0:T(8,128)(2,1)}), bf16[4,294,512]{2,1,0:T(8,128)(2,1)S(1)}, u32[]{:S(2)}, u32[]{:S(2)}) async-start(bf16[4,294,512]{2,1,0:T(8,128)(2,1)} %reshape.1175), calls=%async_computation | async-start | bytes 2424832 | tf_op jit(solution)/shard_map/all_to_all | solution.py:279
  279.9 11.7 copy-start.91
  279.9 12.6 %copy-start.93 = (pred[7,7]{1,0:T(8,128)(4,1)S(1)}, pred[7,7]{1,0:T(8,128)(4,1)}, u32[]{:S(2)}) copy-start(pred[7,7]{1,0:T(8,128)(4,1)} %constant.241) | copy-start | bytes 151
  304.7 14.3 %copy-start.75 = (f32[1,512]{1,0:T(1,128)S(1)}, f32[1,512]{1,0:T(1,128)}, u32[]{:S(2)}) copy-start(f32[1,512]{1,0:T(1,128)} %get-tuple-element.130) | copy-start | bytes 6148
  304.7 14.3 %copy-start.87 = (f32[1,512]{1,0:T(1,128)S(1)}, f32[1,512]{1,0:T(1,128)}, u32[]{:S(2)}) copy-start(f32[1,512]{1,0:T(1,128)} %get-tuple-element.131) | copy-start | bytes 6148
  309.5 44.6 %copy-start.30 = (f32[294,512]{1,0:T(8,128)}, f32[294,512]{1,0:T(8,128)S(1)}, u32[]{:S(2)}) copy-start(f32[294,512]{1,0:T(8,128)S(1)} %get-tuple-element.172) | copy-start | bytes 1806340
  319.0 15.5 %copy-start.54 = (f32[1,2048]{1,0:T(1,128)S(1)}, f32[1,2048]{1,0:T(1,128)}, u32[]{:S(2)}) copy-start(f32[1,2048]{1,0:T(1,128)} %get-tuple-element.126) | copy-start | bytes 24580
  319.0 15.6 %copy-start.62 = (f32[1,2048]{1,0:T(1,128)S(1)}, f32[1,2048]{1,0:T(1,128)}, u32[]{:S(2)}) copy-start(f32[1,2048]{1,0:T(1,128)} %get-tuple-element.127) | copy-start | bytes 24580
  354.2 10.9 copy-start.76
  354.2 10.9 copy-start.82
  374.7 12.2 %copy-start.23 = (bf16[294,2048]{1,0:T(8,128)(2,1)S(1)}, bf16[294,2048]{1,0:T(8,128)(2,1)}, u32[]{:S(2)}) copy-start(bf16[294,2048]{1,0:T(8,128)(2,1)} %get-tuple-element.71) | copy-start | bytes 3612676
  374.7 12.2 %copy-start.108 = (f32[1,512]{1,0:T(1,128)S(1)}, f32[1,512]{1,0:T(1,128)}, u32[]{:S(2)}) copy-start(f32[1,512]{1,0:T(1,128)} %get-tuple-element.153) | copy-start | bytes 6148
  407.0 15.4 %copy-start.61 = (f32[1,2048]{1,0:T(1,128)S(1)}, f32[1,2048]{1,0:T(1,128)}, u32[]{:S(2)}) copy-start(f32[1,2048]{1,0:T(1,128)} %get-tuple-element.136) | copy-start | bytes 24580
  427.0 7.6 copy-start.29
  427.0 34.7 %collective-permute-start.12 = (bf16[294,512]{1,0:T(8,128)(2,1)}, bf16[294,512]{1,0:T(8,128)(2,1)}, u32[]{:S(2)}, u32[]{:S(2)}) collective-permute-start(bf16[294,512]{1,0:T(8,128)(2,1)} %convolution_convert_fusion.3), channel_id=1, source_target_pairs={{24,0},{25,1},{26,2},{27,3},{28,4},{29,5},{30,6},{31,7}} | collective-permute-start | bytes 903176 | tf_op jit(solution)/shard_map/ppermute | solution.py:187
  428.5 33.1 %collective-permute-start.11 = (bf16[294,512]{1,0:T(8,128)(2,1)}, bf16[294,512]{1,0:T(8,128)(2,1)}, u32[]{:S(2)}, u32[]{:S(2)}) collective-permute-start(bf16[294,512]{1,0:T(8,128)(2,1)} %convolution_convert_fusion.3), channel_id=1, source_target_pairs={{16,0},{17,1},{18,2},{19,3},{20,4},{21,5},{22,6},{23,7}} | collective-permute-start | bytes 903176 | tf_op jit(solution)/shard_map/ppermute | solution.py:187
  429.8 32.3 %collective-permute-start.10 = (bf16[294,512]{1,0:T(8,128)(2,1)}, bf16[294,512]{1,0:T(8,128)(2,1)}, u32[]{:S(2)}, u32[]{:S(2)}) collective-permute-start(bf16[294,512]{1,0:T(8,128)(2,1)} %convolution_convert_fusion.3), channel_id=1, source_target_pairs={{8,0},{9,1},{10,2},{11,3},{12,4},{13,5},{14,6},{15,7}} | collective-permute-start | bytes 903176 | tf_op jit(solution)/shard_map/ppermute | solution.py:187
  434.5 11.3 copy-start.17
  442.6 107.8 %collective-permute-start.19 = (bf16[1024,512]{1,0:T(8,128)(2,1)}, bf16[1024,512]{1,0:T(8,128)(2,1)}, u32[]{:S(2)}, u32[]{:S(2)}) collective-permute-start(bf16[1024,512]{1,0:T(8,128)(2,1)} %dynamic-slice_convert_fusion.4), channel_id=1, source_target_pairs={{0,1},{1,0},{2,3},{3,2},{4,5},{5,4},{6,7},{7,6},{8,9},{9,8},{10,11... | collective-permute-start | bytes 3145736 | tf_op jit(solution)/shard_map/ppermute | solution.py:193
  445.5 121.1 %collective-permute-start.21 = (bf16[1024,512]{1,0:T(8,128)(2,1)}, bf16[1024,512]{1,0:T(8,128)(2,1)}, u32[]{:S(2)}, u32[]{:S(2)}) collective-permute-start(bf16[1024,512]{1,0:T(8,128)(2,1)} %dynamic-slice_convert_fusion.3), channel_id=1, source_target_pairs={{0,1},{1,0},{2,3},{3,2},{4,5},{5,4},{6,7},{7,6},{8,9},{9,8},{10,11... | collective-permute-start | bytes 3145736 | tf_op jit(solution)/shard_map/ppermute | solution.py:193
  448.8 105.0 %all-to-all-start.8 = ((bf16[294,4,512]{2,0,1:T(8,128)(2,1)}), bf16[294,4,512]{2,0,1:T(8,128)(2,1)}, u32[]{:S(2)}, u32[]{:S(2)}) async-start(bf16[294,4,512]{2,0,1:T(8,128)(2,1)} %fusion.19), calls=%async_computation.8 | async-start | bytes 2424832 | tf_op jit(solution)/shard_map/all_to_all | solution.py:328
  461.7 127.0 %collective-permute-start.18 = (bf16[1024,512]{1,0:T(8,128)(2,1)}, bf16[1024,512]{1,0:T(8,128)(2,1)}, u32[]{:S(2)}, u32[]{:S(2)}) collective-permute-start(bf16[1024,512]{1,0:T(8,128)(2,1)} %dynamic-slice_convert_fusion.5), channel_id=1, source_target_pairs={{0,1},{1,0},{2,3},{3,2},{4,5},{5,4},{6,7},{7,6},{8,9},{9,8},{10,11... | collective-permute-start | bytes 3145736 | tf_op jit(solution)/shard_map/ppermute | solution.py:193
  461.7 151.9 %collective-permute-start.20 = (bf16[2304,512]{1,0:T(8,128)(2,1)}, bf16[2304,512]{1,0:T(8,128)(2,1)}, u32[]{:S(2)}, u32[]{:S(2)}) collective-permute-start(bf16[2304,512]{1,0:T(8,128)(2,1)} %dynamic-slice_convert_fusion), channel_id=1, source_target_pairs={{0,1},{1,0},{2,3},{3,2},{4,5},{5,4},{6,7},{7,6},{8,9},{9,8},{10,11... | collective-permute-start | bytes 7077896 | tf_op jit(solution)/shard_map/ppermute | solution.py:193
  462.2 13.7 %copy-start.60 = (f32[4,512]{1,0:T(4,128)S(1)}, f32[4,512]{1,0:T(4,128)}, u32[]{:S(2)}) copy-start(f32[4,512]{1,0:T(4,128)} %get-tuple-element.135) | copy-start | bytes 24580
  531.1 12.3 %copy-start.59 = (f32[4,512]{1,0:T(4,128)S(1)}, f32[4,512]{1,0:T(4,128)}, u32[]{:S(2)}) copy-start(f32[4,512]{1,0:T(4,128)} %get-tuple-element.134) | copy-start | bytes 24580
  553.7 18.8 %all-to-all-start.5 = ((bf16[4,256,512]{2,1,0:T(8,128)(2,1)}), bf16[4,256,512]{2,1,0:T(8,128)(2,1)}, u32[]{:S(2)}, u32[]{:S(2)}) async-start(bf16[4,256,512]{2,1,0:T(8,128)(2,1)} %bitcast.353), calls=%async_computation.5 | async-start | bytes 2097152 | tf_op jit(solution)/shard_map/all_to_all | solution.py:394
  558.0 8.7 copy-start.3
  566.5 33.2 %collective-permute-start.16 = (bf16[1024,512]{0,1:T(8,128)(2,1)}, bf16[1024,512]{0,1:T(8,128)(2,1)}, u32[]{:S(2)}, u32[]{:S(2)}) collective-permute-start(bf16[1024,512]{0,1:T(8,128)(2,1)} %fusion.45), channel_id=1, source_target_pairs={{0,1},{1,0},{2,3},{3,2},{4,5},{5,4},{6,7},{7,6},{8,9},{9,8},{10,11... | collective-permute-start | bytes 3145736 | tf_op jit(solution)/shard_map/ppermute | solution.py:193
  572.6 18.7 %all-to-all-start.7 = ((bf16[4,256,512]{2,1,0:T(8,128)(2,1)}), bf16[4,256,512]{2,1,0:T(8,128)(2,1)}, u32[]{:S(2)}, u32[]{:S(2)}) async-start(bf16[4,256,512]{2,1,0:T(8,128)(2,1)} %bitcast.354), calls=%async_computation.7 | async-start | bytes 2097152 | tf_op jit(solution)/shard_map/all_to_all | solution.py:394
  576.8 11.9 %copy-start.5 = (f32[2048,512]{1,0:T(8,128)S(1)}, f32[2048,512]{1,0:T(8,128)}, u32[]{:S(2)}) copy-start(f32[2048,512]{1,0:T(8,128)} %fusion.142) | copy-start | bytes 12582916
  591.3 18.0 %all-to-all-start.4 = ((bf16[4,256,512]{2,1,0:T(8,128)(2,1)}), bf16[4,256,512]{2,1,0:T(8,128)(2,1)}, u32[]{:S(2)}, u32[]{:S(2)}) async-start(bf16[4,256,512]{2,1,0:T(8,128)(2,1)} %bitcast.352), calls=%async_computation.4 | async-start | bytes 2097152 | tf_op jit(solution)/shard_map/all_to_all | solution.py:394
  599.6 34.2 %collective-permute-start.17 = (bf16[2304,512]{1,0:T(8,128)(2,1)}, bf16[2304,512]{1,0:T(8,128)(2,1)}, u32[]{:S(2)}, u32[]{:S(2)}) collective-permute-start(bf16[2304,512]{1,0:T(8,128)(2,1)} %dynamic-slice_convert_fusion.1), channel_id=1, source_target_pairs={{0,1},{1,0},{2,3},{3,2},{4,5},{5,4},{6,7},{7,6},{8,9},{9,8},{10,11... | collective-permute-start | bytes 7077896 | tf_op jit(solution)/shard_map/ppermute | solution.py:193
  609.3 17.4 %all-to-all-start.2 = ((bf16[4,256,512]{1,2,0:T(8,128)(2,1)}), bf16[4,256,512]{1,2,0:T(8,128)(2,1)}, u32[]{:S(2)}, u32[]{:S(2)}) async-start(bf16[4,256,512]{1,2,0:T(8,128)(2,1)} %bitcast.357), calls=%async_computation.2 | async-start | bytes 2097152 | tf_op jit(solution)/shard_map/all_to_all | solution.py:394
  626.7 31.7 %all-to-all-start.6 = ((bf16[4,576,512]{2,1,0:T(8,128)(2,1)}), bf16[4,576,512]{2,1,0:T(8,128)(2,1)}, u32[]{:S(2)}, u32[]{:S(2)}) async-start(bf16[4,576,512]{2,1,0:T(8,128)(2,1)} %bitcast.346), calls=%async_computation.6 | async-start | bytes 4718592 | tf_op jit(solution)/shard_map/all_to_all | solution.py:394
  658.4 33.7 %all-to-all-start.3 = ((bf16[4,576,512]{2,1,0:T(8,128)(2,1)}), bf16[4,576,512]{2,1,0:T(8,128)(2,1)}, u32[]{:S(2)}, u32[]{:S(2)}) async-start(bf16[4,576,512]{2,1,0:T(8,128)(2,1)} %bitcast.345), calls=%async_computation.3 | async-start | bytes 4718592 | tf_op jit(solution)/shard_map/all_to_all | solution.py:394
  662.9 104.3 %reduce-scatter.2.cloned.1.call-start = ((), (), s32[]{:S(2)}) async-start(), calls=%async_computation.12 | async-start | bytes 4096000 | tf_op jit(solution)/shard_map/reduce_scatter | solution.py:418
  671.5 6.5 collective-permute-start.22
  703.1 131.4 %all-gather.6.cloned.1.call-start = ((), (), s32[]{:S(2)}) async-start(), calls=%async_computation.13 | async-start | bytes 4096000 | tf_op jit(solution)/shard_map/all_gather | solution.py:421
  929.2 164.0 %collective-permute-start.23 = (bf16[4,1856,512]{2,1,0:T(8,128)(2,1)}, bf16[4,1856,512]{2,1,0:T(8,128)(2,1)}, u32[]{:S(2)}, u32[]{:S(2)}) collective-permute-start(bf16[4,1856,512]{2,1,0:T(8,128)(2,1)} %all_to_all.64), channel_id=1, source_target_pairs={{0,1},{1,0},{2,3},{3,2},{4,5},{5,4},{6,7},{7,6},{8,9},{9,8},{10,11... | collective-permute-start | bytes 22806536 | tf_op jit(solution)/shard_map/ppermute | solution.py:193
  941.5 109.3 %collective-permute-start.15 = (bf16[294,2048]{1,0:T(8,128)(2,1)}, bf16[294,2048]{1,0:T(8,128)(2,1)}, u32[]{:S(2)}, u32[]{:S(2)}) collective-permute-start(bf16[294,2048]{1,0:T(8,128)(2,1)} %get-tuple-element.68), channel_id=1, source_target_pairs={{24,0},{25,1},{26,2},{27,3},{28,4},{29,5},{30,6},{31,7}} | collective-permute-start | bytes 3612680 | tf_op jit(solution)/shard_map/ppermute | solution.py:187
  942.7 108.0 %collective-permute-start.14 = (bf16[294,2048]{1,0:T(8,128)(2,1)}, bf16[294,2048]{1,0:T(8,128)(2,1)}, u32[]{:S(2)}, u32[]{:S(2)}) collective-permute-start(bf16[294,2048]{1,0:T(8,128)(2,1)} %get-tuple-element.68), channel_id=1, source_target_pairs={{16,0},{17,1},{18,2},{19,3},{20,4},{21,5},{22,6},{23,7}} | collective-permute-start | bytes 3612680 | tf_op jit(solution)/shard_map/ppermute | solution.py:187
  944.0 106.7 %collective-permute-start.13 = (bf16[294,2048]{1,0:T(8,128)(2,1)}, bf16[294,2048]{1,0:T(8,128)(2,1)}, u32[]{:S(2)}, u32[]{:S(2)}) collective-permute-start(bf16[294,2048]{1,0:T(8,128)(2,1)} %get-tuple-element.68), channel_id=1, source_target_pairs={{8,0},{9,1},{10,2},{11,3},{12,4},{13,5},{14,6},{15,7}} | collective-permute-start | bytes 3612680 | tf_op jit(solution)/shard_map/ppermute | solution.py:187
  956.9 127.1 %all-to-all-start.1 = ((bf16[4,6,49,2048]{3,2,1,0:T(8,128)(2,1)}), bf16[4,6,49,2048]{3,2,1,0:T(8,128)(2,1)}, u32[]{:S(2)}, u32[]{:S(2)}) async-start(bf16[4,6,49,2048]{3,2,1,0:T(8,128)(2,1)} %pad_maximum_fusion.1), calls=%async_computation.1 | async-start | bytes 11010048 | tf_op jit(solution)/shard_map/all_to_all | solution.py:359
  963.7 85.6 %all-reduce.22.cloned.1.call-start = ((), (), s32[]{:S(2)}) async-start(), calls=%async_computation.14 | async-start | bytes 131072 | tf_op jit(solution)/shard_map/psum | solution.py:384
  964.6 86.1 %copy-start.13 = (bf16[294,2048]{1,0:T(8,128)(2,1)S(1)}, bf16[294,2048]{1,0:T(8,128)(2,1)}, u32[]{:S(2)}) copy-start(bf16[294,2048]{1,0:T(8,128)(2,1)} %get-tuple-element.68) | copy-start | bytes 3612676
  1115.7 12.0 %slice-start = ((bf16[2,4,1856,512]{3,2,1,0:T(8,128)(2,1)}), bf16[2,4,256,512]{3,2,1,0:T(8,128)(2,1)S(1)}, s32[]{:S(2)}) async-start(bf16[2,4,1856,512]{3,2,1,0:T(8,128)(2,1)} %copy-done.1), calls=%async_computation.15 | async-start | bytes 4194304 | tf_op jit(solution)/shard_map/slice | solution.py:439
  (87 other events, 384.9 us)
Sparse Core Ops, SparseCore 0:
  18.5 121.8 all-gather.3
  703.3 63.9 reduce-scatter.1
  768.8 65.7 all-gather.5
  967.6 81.6 all-reduce.21

commit v2 on v1

v2 whole, which is shorter than its diff:
```python
import functools

import jax
import jax.numpy as jnp
import numpy as np
from jax import lax
from jax.experimental import pallas as pl
from jax.experimental.pallas import tpu as pltpu
from jax.sharding import PartitionSpec as P

MAP = 7
EPSILON = 1e-05
OFFSETS = ((-1, -1), (-1, 0), (-1, 1), (0, -1), (0, 0), (0, 1), (1, -1), (1, 0), (1, 1))
MESH = pl.DeviceIdType.MESH
F32 = jnp.float32
BF16 = jnp.bfloat16
VMEM_BYTES = 58 * 2**20
TILE = 256


def greet(count):
    segment, me = lax.axis_index("segment"), lax.axis_index("dp")
    barrier = pltpu.get_barrier_semaphore()

    def one(k, carry):
        pl.semaphore_signal(
            barrier, inc=1, device_id=(segment, lax.rem(me + k, count)), device_id_type=MESH
        )
        return carry

    lax.fori_loop(1, count, one, 0)


def greeted(count):
    pl.semaphore_wait(pltpu.get_barrier_semaphore(), count - 1)


def exchange(count, slots, send_sem, recv_sem):
    segment, me = lax.axis_index("segment"), lax.axis_index("dp")

    def copy(k):
        return pltpu.make_async_remote_copy(
            src_ref=slots.at[me],
            dst_ref=slots.at[me],
            send_sem=send_sem.at[k],
            recv_sem=recv_sem.at[k],
            device_id=(segment, lax.rem(me + k, count)),
            device_id_type=MESH,
        )

    def start(k, carry):
        copy(k).start()
        return carry

    def finish(k, carry):
        copy(k).wait_recv()
        copy(k).wait_send()
        return carry

    lax.fori_loop(1, count, start, 0)
    lax.fori_loop(1, count, finish, 0)
    total = slots[0]
    for k in range(1, count):
        total = total + slots[k]
    return total


def sync_scratch(count, shapes):
    out = []
    for shape in shapes:
        out += [
            pltpu.VMEM((count,) + shape, F32),
            pltpu.SemaphoreType.DMA((count,)),
            pltpu.SemaphoreType.DMA((count,)),
        ]
    return out


def kernel_call(kernel, outs, args, scratch, ident, flops, moved, spaces=None):
    params = dict(has_side_effects=True, vmem_limit_bytes=VMEM_BYTES)
    if ident is not None:
        params["collective_id"] = ident
    return pl.pallas_call(
        kernel,
        out_shape=outs,
        in_specs=[pl.BlockSpec(memory_space=pltpu.VMEM) for _ in args],
        out_specs=[pl.BlockSpec(memory_space=pltpu.VMEM) for _ in outs],
        scratch_shapes=scratch,
        compiler_params=pltpu.CompilerParams(**params),
        cost_estimate=pl.CostEstimate(flops=flops, bytes_accessed=moved, transcendentals=0),
    )(*args)


def shape_of(shape, dtype):
    return jax.ShapeDtypeStruct(shape, dtype)


def dot(a, b):
    return jnp.dot(a, b, preferred_element_type=F32)


def dot_t(a, b):
    return lax.dot_general(a, b, (((1,), (1,)), ((), ())), preferred_element_type=F32)


def sigmoid(v):
    return 1.0 / (1.0 + jnp.exp(-v))


def slope(v):
    s = sigmoid(v)
    return s * (1.0 + v * (1.0 - s))


def over(width, step, body):
    def one(j, carry):
        body(pl.ds(pl.multiple_of(j * step, step), step))
        return carry

    lax.fori_loop(0, width // step, one, 0)


def lane(at):
    return lax.div(at.start, 128)


def unrolled_shift(ref_value, shift):
    rows = ref_value.shape[0]
    return ref_value if shift % rows == 0 else pltpu.roll(ref_value, (-shift) % rows, 0)


def by_batch(values):
    rows, width = values.shape
    part = jnp.sum(values.reshape(rows // 8, 8, width), axis=0)
    return part[:4] + part[4:]


def spread8(values):
    return jnp.concatenate([values, values], axis=0)[None]


def first_kernel(
    count, x, w, k, gb, pack, tiles, a2_out, cols, h1n, h2n, stats_out, count_out, act, *sync
):
    s1, send1, recv1, s2, send2, recv2 = sync
    rows, narrow = h1n.shape
    me = lax.axis_index("dp")
    greet(count)
    full = act.shape[1]

    def tile8(v):
        return v.reshape(rows // 8, 8, v.shape[1])

    def project(at):
        h = dot(x[...], w[:, at])
        h1n[:, at] = h
        m = pack[:, 0:1] * h
        s1[me, 0:4, at] = by_batch(m)
        s1[me, 4:8, at] = by_batch(m * h)

    over(narrow, TILE, project)
    s1[me, 0:4, narrow:] = jnp.broadcast_to(by_batch(pack[:, 0:1]), (4, 128))
    s1[me, 4:8, narrow:] = jnp.broadcast_to(by_batch(tiles[:, 0:1]), (4, 128))
    greeted(count)
    total = exchange(count, s1, send1, recv1)
    counts = total[:, narrow:]
    count_out[...] = counts
    valid = counts[0:4, 0:1]
    average = total[0:4, :narrow] / valid
    inverse = lax.rsqrt(total[4:8, :narrow] / valid - average * average + EPSILON)
    stats_out[0:4, :] = average
    stats_out[4:8, :] = inverse

    def activate(stat_at, gain_at, source):
        def body(at):
            mean = spread8(stats_out[stat_at : stat_at + 4, at])
            inv = spread8(stats_out[stat_at + 4 : stat_at + 8, at])
            hn = (tile8(source[:, at]) - mean) * inv
            source[:, at] = hn.reshape(rows, hn.shape[2])
            n = gb[gain_at : gain_at + 1, at][None] * hn + gb[gain_at + 1 : gain_at + 2, at][None]
            n = n.reshape(rows, n.shape[2])
            act[lane(at), 0:rows, :] = pack[:, 0:1] * (n * sigmoid(n))

        return body

    over(narrow, 128, activate(0, 0, h1n))

    for t, (vertical, lateral) in enumerate(OFFSETS):
        shift = 4 * (7 * vertical + lateral)

        def place(j, carry, t=t, shift=shift):
            at = pl.ds(pl.multiple_of(j * 128, 128), 128)
            to = pl.ds(pl.multiple_of(t * narrow + j * 128, 128), 128)
            moved = unrolled_shift(act[j, 0:rows, :], shift)
            cols[:, to] = (pack[:, 1 + t : 2 + t] * moved).astype(BF16)
            return carry

        lax.fori_loop(0, narrow // 128, place, 0)

    def convolve(at):
        h = dot(cols[...], k[:, at])
        h2n[:, at] = h
        m = pack[:, 0:1] * h
        s2[me, 0:4, at] = by_batch(m)
        s2[me, 4:8, at] = by_batch(m * h)

    over(narrow, TILE, convolve)
    total = exchange(count, s2, send2, recv2)
    average = total[0:4] / valid
    stats_out[8:12, :] = average
    stats_out[12:16, :] = lax.rsqrt(total[4:8] / valid - average * average + EPSILON)
    over(narrow, 128, activate(8, 2, h2n))
    act[:, rows:, :] = jnp.zeros((narrow // 128, full - rows, 128), F32)
    for m in range(4):

        def pick(j, carry, m=m):
            at = pl.ds(pl.multiple_of(j * 128, 128), 128)
            a2_out[m, :, at] = act[j, pl.ds(m, full // 4, stride=4), :].astype(BF16)
            return carry

        lax.fori_loop(0, narrow // 128, pick, 0)


def residual_kernel(x, wa, wb, out, hold):
    rows, depth = x.shape[0], wa.shape[0]
    full, quarter = hold.shape[1], out.shape[2]
    core = lax.rem(lax.axis_index("dp"), 2)
    first = pl.ds(pl.multiple_of(core * depth, depth), depth)
    second = pl.ds(pl.multiple_of((1 - core) * depth, depth), depth)
    hold[:, rows:, :] = jnp.zeros((quarter // 128, full - rows, 128), F32)

    def body(at):
        value = dot(x[:, first], wa[:, at]) + dot(x[:, second], wb[:, at])
        for part in range(TILE // 128):
            hold[lane(at) + part, 0:rows, :] = value[:, part * 128 : part * 128 + 128]

    over(quarter, TILE, body)
    for m in range(4):

        def pick(j, carry, m=m):
            at = pl.ds(pl.multiple_of(j * 128, 128), 128)
            out[m, :, at] = hold[j, pl.ds(m, full // 4, stride=4), :].astype(BF16)
            return carry

        lax.fori_loop(0, quarter // 128, pick, 0)


def norm_sums(slots, me, at, masked, h):
    slots[me, 0:1, at] = jnp.sum(masked, axis=0, keepdims=True)
    slots[me, 1:2, at] = jnp.sum(masked * h, axis=0, keepdims=True)


def finish_stats(total, valid, stats_out, at_row):
    average = total[0:1] / valid
    width = average.shape[1]
    stats_out[at_row : at_row + 1, 0:width] = average
    stats_out[at_row + 1 : at_row + 2, 0:width] = lax.rsqrt(
        total[1:2] / valid - average * average + EPSILON
    )


def second_kernel(
    count, a2, w1, res, pack, gb, valid_in, moves, y_out, u_out, h3n, stats_out, s1, send1, recv1
):
    wide = h3n.shape[1]
    quarter = res.shape[2]
    me = lax.axis_index("dp")
    greet(count)

    def project(at):
        h = dot_t(a2[...], w1[at, :])
        h3n[:, at] = h
        norm_sums(s1, me, at, pack[:, 0:1] * h, h)

    over(wide, TILE, project)
    greeted(count)
    valid = valid_in[0:1, 0:1]
    finish_stats(exchange(count, s1, send1, recv1), valid, stats_out, 0)
    for q in range(wide // quarter):

        def body(j, carry, q=q):
            at = pl.ds(pl.multiple_of(q * quarter + j * 128, 128), 128)
            own = pl.ds(pl.multiple_of(j * 128, 128), 128)
            hn = (h3n[:, at] - stats_out[0:1, at]) * stats_out[1:2, at]
            h3n[:, at] = hn
            z = gb[0:1, at] * hn + gb[1:2, at] + res[q, :, own].astype(F32)
            y_out[:, at] = (pack[:, 0:1] * (z * sigmoid(z))).astype(BF16)
            return carry

        lax.fori_loop(0, quarter // 128, body, 0)

    def permute(at):
        u_out[:, at] = dot(moves[...], y_out[:, at]).astype(BF16)

    over(wide, TILE, permute)


def back_sums(slots, me, at, grad, hn):
    slots[me, 0:1, at] = jnp.sum(grad, axis=0, keepdims=True)
    slots[me, 1:2, at] = jnp.sum(grad * hn, axis=0, keepdims=True)


def tile_kernel(
    count,
    u,
    w2,
    k2,
    w3,
    og,
    pack,
    gb2,
    gb3,
    valid_in,
    back,
    y_out,
    a2,
    cols,
    dh3,
    dh2,
    dh1,
    dy,
    sums_out,
    h1n,
    h2n,
    h3n,
    act,
    dz,
    stats,
    *sync,
):
    s1, send1, recv1, s2, send2, recv2, s3, send3, recv3 = sync[:9]
    b3, bsend3, brecv3, b2, bsend2, brecv2, b1, bsend1, brecv1 = sync[9:]
    rows, wide = u.shape
    narrow = h1n.shape[1]
    me = lax.axis_index("dp")
    valid = valid_in[0:1, 0:1]
    greet(count)

    def project(at):
        h = dot(u[...], w2[:, at])
        h1n[:, at] = h
        norm_sums(s1, me, at, pack[:, 0:1] * h, h)

    over(narrow, TILE, project)
    greeted(count)
    finish_stats(exchange(count, s1, send1, recv1), valid, stats, 0)

    def activate(row, gain, source, store):
        def body(at):
            hn = (source[:, at] - stats[row : row + 1, at]) * stats[row + 1 : row + 2, at]
            source[:, at] = hn
            n = gb2[gain : gain + 1, at] * hn + gb2[gain + 1 : gain + 2, at]
            store(at, pack[:, 0:1] * (n * sigmoid(n)))

        return body

    def to_act(at, value):
        act[:, at] = value

    def to_a2(at, value):
        a2[:, at] = value.astype(BF16)

    over(narrow, 128, activate(0, 0, h1n, to_act))
    for t, (vertical, lateral) in enumerate(OFFSETS):
        shift = 7 * vertical + lateral

        def place(j, carry, t=t, shift=shift):
            at = pl.ds(pl.multiple_of(j * 128, 128), 128)
            to = pl.ds(pl.multiple_of(t * narrow + j * 128, 128), 128)
            moved = unrolled_shift(act[:, at], shift)
            cols[:, to] = (pack[:, 1 + t : 2 + t] * moved).astype(BF16)
            return carry

        lax.fori_loop(0, narrow // 128, place, 0)

    def convolve(at):
        h = dot(cols[...], k2[:, at])
        h2n[:, at] = h
        norm_sums(s2, me, at, pack[:, 0:1] * h, h)

    over(narrow, TILE, convolve)
    finish_stats(exchange(count, s2, send2, recv2), valid, stats, 2)
    over(narrow, 128, activate(2, 2, h2n, to_a2))

    def expand(at):
        h = dot_t(a2[...], w3[at, :])
        h3n[:, at] = h
        norm_sums(s3, me, at, pack[:, 0:1] * h, h)

    over(wide, TILE, expand)
    finish_stats(exchange(count, s3, send3, recv3), valid, stats, 4)

    def result(at):
        hn = (h3n[:, at] - stats[4:5, at]) * stats[5:6, at]
        h3n[:, at] = hn
        z = gb3[0:1, at] * hn + gb3[1:2, at] + u[:, at].astype(F32)
        s = sigmoid(z)
        m = pack[:, 0:1]
        y_out[:, at] = (m * (z * s)).astype(BF16)
        grad = (og[:, at].astype(F32) * m * (s * (1.0 + z * (1.0 - s)))).astype(BF16)
        dz[:, at] = grad
        grad = grad.astype(F32)
        back_sums(b3, me, at, grad, hn)

    over(wide, 128, result)
    total = exchange(count, b3, bsend3, brecv3)
    sums_out[0:2, :] = total

    def through(at):
        offset, scale = sums_out[0:1, at], sums_out[1:2, at]
        dh3[:, at] = (
            pack[:, 0:1]
            * gb3[0:1, at]
            * stats[5:6, at]
            * (dz[:, at].astype(F32) - (offset + h3n[:, at] * scale) / valid)
        ).astype(BF16)

    over(wide, 128, through)

    def into_two(at):
        grad = dot(dh3[...], w3[:, at]).astype(BF16).astype(F32)
        hn = h2n[:, at]
        n = gb2[2:3, at] * hn + gb2[3:4, at]
        grad = grad * pack[:, 0:1] * slope(n)
        act[:, at] = grad
        back_sums(b2, me, at, grad, hn)

    over(narrow, TILE, into_two)
    total = exchange(count, b2, bsend2, brecv2)
    sums_out[2:4, 0:narrow] = total

    def through_two(at):
        offset, scale = sums_out[2:3, at], sums_out[3:4, at]
        grad = (
            pack[:, 0:1]
            * gb2[2:3, at]
            * stats[3:4, at]
            * (act[:, at] - (offset + h2n[:, at] * scale) / valid)
        )
        dh2[:, at] = grad.astype(BF16)
        act[:, at] = dh2[:, at].astype(F32)

    over(narrow, 128, through_two)
    h2n[...] = jnp.zeros((rows, narrow), F32)
    for t, (vertical, lateral) in enumerate(OFFSETS):
        shift = -(7 * vertical + lateral)
        other = 8 - t

        def place_back(j, carry, t=t, shift=shift, other=other):
            at = pl.ds(pl.multiple_of(j * 128, 128), 128)
            moved = unrolled_shift(act[:, at], shift)
            dy[:, at] = (pack[:, 1 + other : 2 + other] * moved).astype(BF16)
            return carry

        lax.fori_loop(0, narrow // 128, place_back, 0)

        def gather(at, t=t):
            row = pl.ds(pl.multiple_of(t * narrow + at.start, TILE), TILE)
            h2n[:, at] += dot_t(dy[:, 0:narrow], k2[row, :])

        over(narrow, TILE, gather)

    def into_one(at):
        hn = h1n[:, at]
        n = gb2[0:1, at] * hn + gb2[1:2, at]
        grad = h2n[:, at] * pack[:, 0:1] * slope(n)
        act[:, at] = grad
        back_sums(b1, me, at, grad, hn)

    over(narrow, 128, into_one)
    total = exchange(count, b1, bsend1, brecv1)
    sums_out[4:6, 0:narrow] = total

    def through_one(at):
        offset, scale = sums_out[4:5, at], sums_out[5:6, at]
        dh1[:, at] = (
            pack[:, 0:1]
            * gb2[0:1, at]
            * stats[1:2, at]
            * (act[:, at] - (offset + h1n[:, at] * scale) / valid)
        ).astype(BF16)

    over(narrow, 128, through_one)

    def into_input(at):
        grad = dot_t(dh1[...], w2[at, :]) + dz[:, at].astype(F32)
        dy[:, at] = dot(back[...], grad.astype(BF16)).astype(BF16)

    over(wide, TILE, into_input)


def image_back_kernel(
    count, dy, res, h3n, pack, gb, stats, valid_in, w1, dz, dh3, da2, sums_out, b3, send3, recv3
):
    wide = dy.shape[1]
    quarter = res.shape[2]
    narrow = da2.shape[1]
    me = lax.axis_index("dp")
    valid = valid_in[0:1, 0:1]
    greet(count)
    for q in range(wide // quarter):

        def body(j, carry, q=q):
            at = pl.ds(pl.multiple_of(q * quarter + j * 128, 128), 128)
            own = pl.ds(pl.multiple_of(j * 128, 128), 128)
            hn = h3n[:, at]
            z = gb[0:1, at] * hn + gb[1:2, at] + res[q, :, own].astype(F32)
            grad = (dy[:, at].astype(F32) * pack[:, 0:1] * slope(z)).astype(BF16)
            dz[:, at] = grad
            back_sums(b3, me, at, grad.astype(F32), hn)
            return carry

        lax.fori_loop(0, quarter // 128, body, 0)
    greeted(count)
    total = exchange(count, b3, send3, recv3)
    sums_out[...] = total

    def through(at):
        offset, scale = sums_out[0:1, at], sums_out[1:2, at]
        dh3[:, at] = (
            pack[:, 0:1]
            * gb[0:1, at]
            * stats[1:2, at]
            * (dz[:, at].astype(F32) - (offset + h3n[:, at] * scale) / valid)
        ).astype(BF16)

    over(wide, 128, through)

    def into(at):
        da2[:, at] = dot(dh3[...], w1[:, at]).astype(BF16)

    over(narrow, TILE, into)


def last_kernel(
    count, da2, k, gb, pack, h1n, h2n, stats, counts, dh2, dh1, sums_out, act, acc, hold, *sync
):
    b2, send2, recv2, b1, send1, recv1 = sync
    rows, narrow = h1n.shape
    full = act.shape[1]
    me = lax.axis_index("dp")
    greet(count)
    valid = counts[0:4, 0:1]

    def tile8(v):
        return v.reshape(rows // 8, 8, v.shape[1])

    for m in range(4):

        def put(j, carry, m=m):
            at = pl.ds(pl.multiple_of(j * 128, 128), 128)
            act[j, pl.ds(m, full // 4, stride=4), :] = da2[m, :, at].astype(F32)
            return carry

        lax.fori_loop(0, narrow // 128, put, 0)

    def into(gain, source, hidden, slots):
        def body(at):
            hn = hidden[:, at]
            n = gb[gain : gain + 1, at] * hn + gb[gain + 1 : gain + 2, at]
            grad = source(at) * pack[:, 0:1] * slope(n)
            act[lane(at), 0:rows, :] = grad
            slots[me, 0:4, at] = by_batch(grad)
            slots[me, 4:8, at] = by_batch(grad * hn)

        return body

    def through(gain, stat_at, row, hidden, out):
        def body(at):
            offset = spread8(sums_out[row : row + 4, at] / valid)
            scale = spread8(sums_out[row + 4 : row + 8, at] / valid)
            inv = spread8(stats[stat_at : stat_at + 4, at])
            g = tile8(act[lane(at), 0:rows, :])
            value = inv * gb[gain : gain + 1, at][None] * (g - (offset + tile8(hidden[:, at]) * scale))
            value = (pack[:, 0:1] * value.reshape(rows, value.shape[2])).astype(BF16)
            out[:, at] = value
            act[lane(at), 0:rows, :] = value.astype(F32)

        return body

    over(narrow, 128, into(2, lambda at: act[lane(at), 0:rows, :], h2n, b2))
    greeted(count)
    sums_out[0:8, :] = exchange(count, b2, send2, recv2)
    over(narrow, 128, through(2, 12, 0, h2n, dh2))
    acc[...] = jnp.zeros((rows, narrow), F32)
    for t, (vertical, lateral) in enumerate(OFFSETS):
        shift = -4 * (7 * vertical + lateral)
        other = 8 - t

        def place_back(j, carry, t=t, shift=shift, other=other):
            at = pl.ds(pl.multiple_of(j * 128, 128), 128)
            moved = unrolled_shift(act[j, 0:rows, :], shift)
            hold[:, at] = (pack[:, 1 + other : 2 + other] * moved).astype(BF16)
            return carry

        lax.fori_loop(0, narrow // 128, place_back, 0)

        def gather(at, t=t):
            row = pl.ds(pl.multiple_of(t * narrow + at.start, TILE), TILE)
            acc[:, at] += dot_t(hold[...], k[row, :])

        over(narrow, TILE, gather)
    over(narrow, 128, into(0, lambda at: acc[:, at], h1n, b1))
    sums_out[8:16, :] = exchange(count, b1, send1, recv1)
    over(narrow, 128, through(0, 4, 8, h1n, dh1))


def input_kernel(dh1, dz, w, short, out):
    def body(at):
        out[:, at] = (dot_t(dh1[...], w[at, :]) + dot_t(dz[...], short[at, :])).astype(BF16)

    over(out.shape[1], TILE, body)


def layouts(resolution_ids, order_ids):
    pixels = jnp.arange(MAP * MAP, dtype=jnp.int32)
    row_of = pixels // MAP
    column_of = pixels % MAP
    extent = 5 + resolution_ids[:, None]
    image_mask = ((row_of[None, :] < extent) & (column_of[None, :] < extent)).astype(F32)
    inside = (row_of < 6) & (column_of < 6)
    position = jnp.where(inside, row_of // 2 * 3 + column_of // 2, 0)
    onehot_tile = (position[:, None] == jnp.arange(9)[None, :]).astype(jnp.int32)
    picked = jnp.sum(onehot_tile[None] * order_ids[:, None, :], axis=2)
    row_to = 2 * (picked // 3) + row_of % 2
    column_to = 2 * (picked % 3) + column_of % 2
    target = row_to * MAP + column_to
    tile_mask = (inside & (row_to < extent) & (column_to < extent)).astype(F32)
    return image_mask, tile_mask, jnp.where(inside, target, -1)


def tap_tables(tiled):
    lattice = np.arange(MAP)
    tables = []
    for vertical, lateral in OFFSETS:
        row, column = lattice + vertical, lattice + lateral
        in_row = (row >= 0) & (row < MAP)
        in_column = (column >= 0) & (column < MAP)
        if tiled:
            in_row &= row // 2 == lattice // 2
            in_column &= column // 2 == lattice // 2
        tables.append((in_row[:, None] & in_column[None, :]).reshape(-1))
    return np.stack(tables, axis=1).astype(np.float32)


def mm(a, b, dims="rk,kn->rn"):
    return jnp.einsum(dims, a, b, preferred_element_type=F32)


def core_swap(value):
    count = lax.axis_size("dp")
    return lax.ppermute(value, "dp", [(d, d ^ 1) for d in range(count)])


def from_section(value, source, section):
    out = value[source]
    for t in range(value.shape[0]):
        if t != source:
            got = lax.ppermute(value[t], "segment", [(source, t)])
            out = jnp.where(section == t, got, out)
    return out


def to_section_zero(value):
    sections = lax.axis_size("segment")
    parts = [value] + [lax.ppermute(value, "segment", [(t, 0)]) for t in range(1, sections)]
    return jnp.stack(parts)


def body(
    layer_input,
    output_grad,
    resolution,
    tile_order,
    proj_weight,
    spatial_weight,
    shortcut_weight,
    bn_gain,
    bn_bias,
):
    micro, images, pixels, wide = layer_input.shape
    narrow = proj_weight.shape[2]
    rows = images * pixels
    padded = -(-rows // 16) * 16
    sections = lax.axis_size("segment")
    count = lax.axis_size("dp")
    section = lax.axis_index("segment")
    place = lax.axis_index("dp")
    core = place % 2
    first = section == 0
    proj, spatial, shortcut = proj_weight[0], spatial_weight[0], shortcut_weight[0]
    pick = lambda a: lax.dynamic_index_in_dim(a, section, 0, keepdims=False)

    half_rows = wide // 2
    w1_half = lax.dynamic_slice_in_dim(proj, core * half_rows, half_rows)
    w1_half = from_section(jnp.broadcast_to(w1_half, (sections,) + w1_half.shape), 1, section)
    w1_other = core_swap(w1_half)
    w1 = jnp.where(
        core == 0,
        jnp.concatenate([w1_half, w1_other]),
        jnp.concatenate([w1_other, w1_half]),
    )

    quarter = wide // sections
    own_half = lax.dynamic_slice_in_dim(shortcut, core * half_rows, half_rows)
    short_half = from_section(
        jnp.stack([own_half[:, t * quarter : (t + 1) * quarter] for t in range(sections)]),
        0,
        section,
    )
    short_other = core_swap(short_half)

    slice_rows = wide // count
    tap_rows = spatial.shape[0] // count
    own_proj = lax.dynamic_slice_in_dim(proj, place * slice_rows, slice_rows)
    own_taps = lax.dynamic_slice_in_dim(spatial, place * tap_rows, tap_rows)
    fine = tap_rows // sections
    taps_piece = from_section(own_taps.reshape(sections, fine, narrow), 2, section)
    packed = jnp.concatenate([own_proj, taps_piece])
    everyone = lax.all_gather(packed, ("segment", "dp"), axis=0, tiled=True)
    everyone = everyone.reshape(sections, count, slice_rows + fine, narrow)
    w2 = everyone[2, :, :slice_rows].reshape(wide, narrow)
    w3 = everyone[3, :, :slice_rows].reshape(wide, narrow)
    k2 = jnp.swapaxes(everyone[:, :, slice_rows:], 0, 1).reshape(9 * narrow, narrow)

    gains = lax.all_gather(jnp.concatenate([bn_gain[0], bn_bias[0]]), "segment", axis=0)
    gain, bias = gains[:, :wide], gains[:, wide:]

    image_masks, tile_masks, targets = layouts(
        resolution.reshape(-1), tile_order.reshape(micro * images, -1)
    )
    interleave = lambda a: jnp.transpose(a.reshape(micro, rows), (1, 0)).reshape(rows * micro, 1)
    taps_image = np.tile(np.repeat(tap_tables(False), micro, axis=0), (images, 1))
    pack_all = jnp.concatenate(
        [interleave(image_masks), jnp.asarray(taps_image), jnp.zeros((rows * micro, 6), F32)], axis=1
    )
    tiles_all = interleave(tile_masks)
    pad_rows = lambda a: jnp.pad(a, ((0, padded - rows), (0, 0)))
    image_mask = pad_rows(pick(image_masks.reshape(micro, rows, 1)))
    tile_mask = pad_rows(pick(tile_masks.reshape(micro, rows, 1)))
    taps_tile = np.pad(np.tile(tap_tables(True), (images, 1)), ((0, padded - rows), (0, 6)))
    pack_tile = jnp.concatenate([tile_mask, jnp.asarray(taps_tile)], axis=1)
    target = pick(targets.reshape(micro, images, pixels))
    base = (jnp.arange(images) * pixels)[:, None]
    target = jnp.where(target >= 0, target + base, -1).reshape(rows)
    target = jnp.pad(target, (0, padded - rows), constant_values=-1)
    index = jnp.arange(padded)
    moves = (target[:, None] == index[None, :]).astype(BF16)
    moves_back = (target[None, :] == index[:, None]).astype(BF16)

    x_all = jnp.transpose(layer_input, (1, 2, 0, 3)).reshape(rows * micro, wide)
    gb_first = jnp.stack(
        [bn_gain[0, :narrow], bn_bias[0, :narrow]]
        + [bn_gain[0, narrow : 2 * narrow], bn_bias[0, narrow : 2 * narrow]]
    )
    total = rows * micro
    a2_all, cols_all, h1n_all, h2n_all, stats_all, counts = kernel_call(
        functools.partial(first_kernel, count),
        [
            shape_of((micro, padded, narrow), BF16),
            shape_of((total, 9 * narrow), BF16),
            shape_of((total, narrow), F32),
            shape_of((total, narrow), F32),
            shape_of((16, narrow), F32),
            shape_of((8, 128), F32),
        ],
        [x_all, proj, spatial, gb_first, pack_all, tiles_all],
        [pltpu.VMEM((narrow // 128, 4 * padded, 128), F32)]
        + sync_scratch(count, [(8, narrow + 128), (8, narrow)]),
        0,
        2 * total * narrow * (wide + 9 * narrow),
        40 * 2**20,
    )
    a2 = from_section(a2_all, 0, section)
    [res_quarter] = kernel_call(
        residual_kernel,
        [shape_of((micro, padded, quarter), BF16)],
        [x_all, short_half, short_other],
        [pltpu.VMEM((quarter // 128, 4 * padded, 128), F32)],
        None,
        2 * total * wide * quarter,
        10 * 2**20,
    )
    residual = lax.all_to_all(res_quarter, "segment", 0, 0, tiled=True)

    valid_image = pick(counts[:4])[None]
    valid_tile = pick(counts[4:])[None]
    gb_one = jnp.stack([gain[1], bias[1]])
    y1, u, h3n, stats_three = kernel_call(
        functools.partial(second_kernel, count),
        [
            shape_of((padded, wide), BF16),
            shape_of((padded, wide), BF16),
            shape_of((padded, wide), F32),
            shape_of((2, wide), F32),
        ],
        [a2, w1, residual, image_mask, gb_one, valid_image, moves],
        sync_scratch(count, [(2, wide)]),
        1,
        2 * padded * wide * (narrow + padded),
        10 * 2**20,
    )
    gb_two = jnp.stack(
        [gain[2, :narrow], bias[2, :narrow]]
        + [gain[2, narrow : 2 * narrow], bias[2, narrow : 2 * narrow]]
    )
    gb_three = jnp.stack([gain[3], bias[3]])
    og = jnp.transpose(output_grad, (1, 2, 0, 3)).reshape(rows, micro, wide)
    og = pad_rows(lax.dynamic_index_in_dim(og, section, 1, keepdims=False))
    y2, t_a2, t_cols, t_dh3, t_dh2, t_dh1, dy1, t_sums = kernel_call(
        functools.partial(tile_kernel, count),
        [
            shape_of((padded, wide), BF16),
            shape_of((padded, narrow), BF16),
            shape_of((padded, 9 * narrow), BF16),
            shape_of((padded, wide), BF16),
            shape_of((padded, narrow), BF16),
            shape_of((padded, narrow), BF16),
            shape_of((padded, wide), BF16),
            shape_of((6, wide), F32),
        ],
        [u, w2, k2, w3, og, pack_tile, gb_two, gb_three, valid_tile, moves_back],
        [
            pltpu.VMEM((padded, narrow), F32),
            pltpu.VMEM((padded, narrow), F32),
            pltpu.VMEM((padded, wide), F32),
            pltpu.VMEM((padded, narrow), F32),
            pltpu.VMEM((padded, wide), BF16),
            pltpu.VMEM((6, wide), F32),
        ]
        + sync_scratch(
            count, [(2, narrow), (2, narrow), (2, wide), (2, wide), (2, narrow), (2, narrow)]
        ),
        2,
        4 * padded * narrow * (2 * wide + 9 * narrow),
        30 * 2**20,
    )
    dz, dh3, da2, i_sums = kernel_call(
        functools.partial(image_back_kernel, count),
        [
            shape_of((padded, wide), BF16),
            shape_of((padded, wide), BF16),
            shape_of((padded, narrow), BF16),
            shape_of((2, wide), F32),
        ],
        [dy1, residual, h3n, image_mask, gb_one, stats_three, valid_image, w1],
        sync_scratch(count, [(2, wide)]),
        3,
        2 * padded * narrow * wide,
        12 * 2**20,
    )
    da2_all = to_section_zero(da2)
    dh2_all, dh1_all, f_sums = kernel_call(
        functools.partial(last_kernel, count),
        [
            shape_of((total, narrow), BF16),
            shape_of((total, narrow), BF16),
            shape_of((16, narrow), F32),
        ],
        [da2_all, spatial, gb_first, pack_all, h1n_all, h2n_all, stats_all, counts],
        [
            pltpu.VMEM((narrow // 128, 4 * padded, 128), F32),
            pltpu.VMEM((total, narrow), F32),
            pltpu.VMEM((total, narrow), BF16),
        ]
        + sync_scratch(count, [(8, narrow), (8, narrow)]),
        4,
        2 * total * narrow * 9 * narrow,
        20 * 2**20,
    )
    weave = lambda a: jnp.swapaxes(a[:, :rows], 0, 1).reshape(total, a.shape[2])
    dz_all = weave(to_section_zero(dz))
    dz_quarter = weave(
        lax.all_to_all(dz.reshape(padded, sections, quarter), "segment", 1, 0, tiled=True).reshape(
            micro, padded, quarter
        )
    )
    [grad_input] = kernel_call(
        input_kernel,
        [shape_of((total, wide), BF16)],
        [dh1_all, dz_all, proj, shortcut],
        [],
        None,
        2 * total * wide * (wide + narrow),
        30 * 2**20,
    )

    proj_term_3 = mm(t_dh3, t_a2, "rd,rk->dk")
    taps_term_2 = mm(t_cols, t_dh2, "rk,rn->kn")
    proj_term_2 = mm(u, t_dh1, "rc,rn->cn")
    proj_term_1 = mm(dh3, a2, "rd,rk->dk")
    short_term = mm(x_all, dz_quarter, "rc,rd->cd")
    taps_term_0 = mm(cols_all, dh2_all, "rk,rn->kn")
    proj_term_0 = mm(x_all, dh1_all, "rc,rn->cn")

    exchanged = lax.all_to_all(jnp.stack([y1, y1, dy1, y2]), "segment", 0, 0)
    exchanged = jnp.swapaxes(exchanged[:, :rows], 0, 1)
    maps = jnp.where(first, grad_input.reshape(rows, micro, wide), exchanged)
    maps = jnp.transpose(maps.reshape(images, pixels, micro, wide), (2, 0, 1, 3))

    blank = jnp.zeros((wide,), F32)
    pad = jnp.zeros((wide - 2 * narrow,), F32)
    of_batches = lambda at: jnp.sum(f_sums[at : at + 4], axis=0)
    zero_gain = jnp.where(first, jnp.concatenate([of_batches(12), of_batches(4), pad]), blank)
    zero_bias = jnp.where(first, jnp.concatenate([of_batches(8), of_batches(0), pad]), blank)
    vectors = jnp.stack(
        [
            zero_gain,
            zero_bias,
            i_sums[1],
            i_sums[0],
            jnp.concatenate([t_sums[5, :narrow], t_sums[3, :narrow], pad]),
            jnp.concatenate([t_sums[4, :narrow], t_sums[2, :narrow], pad]),
            t_sums[1],
            t_sums[0],
        ]
    )
    vectors = pick(lax.psum(vectors, "segment").reshape(sections, 2, wide))

    groups = [[d for d in range(count) if d % 2 == c] for c in range(2)]
    depth = count // 2

    def halved(term):
        rows_half = term.shape[0] // 2
        mine = lax.dynamic_slice_in_dim(term, core * rows_half, rows_half)
        theirs = lax.dynamic_slice_in_dim(term, (1 - core) * rows_half, rows_half)
        return (mine + core_swap(theirs.astype(BF16)).astype(F32)).astype(BF16)

    def planar(terms):
        part = jnp.concatenate(
            [a.reshape(sections, a.shape[0] // sections, narrow) for a in terms], axis=1
        )
        part = lax.all_to_all(part, "segment", 0, 0)
        return jnp.sum(part.astype(F32), axis=0).astype(BF16)

    def over_z(joined):
        shape = joined.shape
        part = joined.reshape(depth, shape[0] // depth, narrow)
        part = lax.psum_scatter(
            part, "dp", scatter_dimension=0, tiled=False, axis_index_groups=groups
        )
        return lax.all_gather(part, "dp", axis=0, axis_index_groups=groups, tiled=True).reshape(shape)

    hp, ht = wide // 8, 9 * narrow // 8
    early = over_z(
        planar([halved(proj_term_1), halved(proj_term_2), halved(taps_term_2), halved(proj_term_3)])
    )
    early_of = {
        1: jnp.pad(early[:hp], ((0, ht), (0, 0))),
        2: early[hp : 2 * hp + ht],
        3: jnp.pad(early[2 * hp + ht :], ((0, ht), (0, 0))),
    }
    keep = jnp.stack([early_of[1], early_of[1], early_of[2], early_of[3]])
    early_parts = lax.all_to_all(keep, "segment", 0, 0)

    scattered = from_section(
        jnp.concatenate(
            [
                halved(a).reshape(sections, a.shape[0] // 2 // sections, narrow)
                for a in (proj_term_0, taps_term_0)
            ],
            axis=1,
        ),
        0,
        section,
    )
    late = over_z(jnp.concatenate([scattered, halved(short_term)]))
    late_parts = to_section_zero(late)

    parts = jnp.where(first, late_parts[:, : hp + ht], early_parts)
    other = core_swap(parts)
    both = jnp.where(core == 0, jnp.stack([parts, other]), jnp.stack([other, parts]))
    short_parts = late_parts[:, hp + ht :]
    short_swap = core_swap(short_parts)
    short_both = jnp.where(
        core == 0, jnp.stack([short_parts, short_swap]), jnp.stack([short_swap, short_parts])
    )
    short_both = jnp.where(first, short_both, jnp.zeros_like(short_both))
    proj_grad = both[:, :, :hp].reshape(wide, narrow).astype(F32)
    spatial_grad = both[:, :, hp:].reshape(9 * narrow, narrow).astype(F32)
    has_taps = (section % 2) == 0
    spatial_grad = jnp.where(has_taps, spatial_grad, jnp.zeros_like(spatial_grad))
    short_grad = jnp.swapaxes(short_both, 1, 2).reshape(wide, wide).astype(F32)
    return (
        maps[None],
        proj_grad[None],
        spatial_grad[None],
        short_grad[None],
        vectors[:1],
        vectors[1:],
    )


def solution(mesh):
    return jax.shard_map(
        body,
        mesh=mesh,
        in_specs=(
            P(None, "dp", None, None),
            P(None, "dp", None, None),
            P(None, "dp"),
            P(None, "dp", None),
            P("segment", None, None),
            P("segment", None, None),
            P("segment", None, None),
            P("segment", None),
            P("segment", None),
        ),
        out_specs=(
            P("segment", None, "dp", None, None),
            P("segment", None, None),
            P("segment", None, None),
            P("segment", None, None),
            P("segment", None),
            P("segment", None),
        ),
        check_vma=False,
    )
```

time: 1200 us -> 996 us (0.83)
  local copies, waits for them, and re-layouts: 289 us -> 171 us
  other arithmetic: 212 us -> 106 us
  matrix products: 134 us -> 28.1 us
  Pallas kernels: 115 us -> 205 us
  waiting for transfers between devices: 252 us -> 306 us
  blocking collectives: 95.4 us -> 51.9 us
  starting transfers between devices: 72.9 us -> 102 us
    ppermute x6 -> x9, waiting for transfers between devices: 0.02 us -> 123 us  [to_section_zero(): lax.ppermute(value, 'segment', [(t, 0)])]
    dot_general x23 -> x7, matrix products: 134 us -> 28.1 us  [mm(): return jnp.einsum(dims, a, b, preferred_element_type=F32)]
    pallas_call x12 -> x7, Pallas kernels: 115 us -> 205 us  [kernel_call(): pl.pallas_call(kernel, out_shape=outs, in_specs=[pl.BlockSpec(memory_spac...]
    all_to_all x1 -> x0, blocking collectives: 88.3 us -> none  [body(): parcels = lax.all_to_all(parcels, 'segment', 0, 0)]
    convert_element_type x24 -> x9, other arithmetic: 84 us -> 25 us  [the longest x7 18.4 us: halved(): return (mine + core_swap(theirs.astype(BF16)).astype(F32)).astype(BF16)]
    all_gather x1, blocking collectives: 7.11 us -> 51.9 us  [body(): lax.all_gather(jnp.concatenate([bn_gain[0], bn_bias[0]]), 'segment', axis=0)]
    reshape x21 -> x11, local copies, waits for them, and re-layouts: 77.8 us -> 33.3 us  [the longest x1 9.12 us: body(): maps = jnp.where(first, grad_input.reshape(rows, micro, wide), exchanged)]
    psum x1, waiting for transfers between devices: 78.1 us -> 38.4 us  [body(): vectors = pick(lax.psum(vectors, 'segment').reshape(sections, 2, wide))]
  transfers between devices with their start and end apart: 37 -> 46, of which waited for: 8 -> 11; matrix products, arithmetic and copies ran while one was open for 33% -> 27% of each run, Pallas kernels for 4% -> 13%
where the time goes in v2:
time: 996 us; the launch traced here: 986 us
  waiting for transfers between devices  306 us (31%)
  Pallas kernels  205 us (21%)
  local copies, waits for them, and re-layouts  171 us (17%)
  other arithmetic  106 us (11%)
  starting transfers between devices  102 us (10%)
  blocking collectives  51.9 us (5%)
  matrix products  28.1 us (3%)
  between operations  15.7 us (2%)
    pallas_call x7, Pallas kernels, kernel_call(): pl.pallas_call(kernel, out_shape=outs, in_specs=[pl.BlockSpec(memory_spac...  205 us
    ppermute x9, waiting for transfers between devices, to_section_zero(): lax.ppermute(value, 'segment', [(t, 0)])  123 us
    all_gather x2, waiting for transfers between devices, over_z(): lax.all_gather(part, 'dp', axis=0, axis_index_groups=groups, tiled=True)  70 us
    all_gather x1, blocking collectives, body(): lax.all_gather(jnp.concatenate([bn_gain[0], bn_bias[0]]), 'segment', axis=0)  51.9 us
    convert_element_type x2, local copies, waits for them, and re-layouts, body(): short_grad = jnp.swapaxes(short_both, 1, 2).reshape(wide, wide).astype(F32)  46.8 us
    ppermute x15, starting transfers between devices, from_section(): got = lax.ppermute(value[t], 'segment', [(source, t)])  41 us
    reduce_scatter x2, waiting for transfers between devices, over_z(): lax.psum_scatter(part, 'dp', scatter_dimension=0, tiled=False, axis_index...  40.6 us
    psum x1, waiting for transfers between devices, body(): vectors = pick(lax.psum(vectors, 'segment').reshape(sections, 2, wide))  38.4 us
  transfers between devices with their start and end apart: 46, of which 11 were waited for; matrix products, arithmetic and copies ran while one was open for 27% of the time, Pallas kernels for 13%

profile of v2, /device:TPU:0, one launch (start us, length us, event | category | flops | bytes accessed | tf_op | source)
XLA Modules:
  0.0 985.9 jit_solution(17525129658782521806)
XLA Ops:
  12.1 4.5 collective-permute-done.13
  20.5 2.5 dynamic-slice_bitcast_fusion
  26.8 10.2 %collective-permute-start.9 = (bf16[1024,512]{1,0:T(8,128)(2,1)}, bf16[1024,512]{1,0:T(8,128)(2,1)}, u32[]{:S(2)}, u32[]{:S(2)}) collective-permute-start(bf16[1024,512]{1,0:T(8,128)(2,1)} %get-tuple-element.67), channel_id=1, source_target_pairs={{0,8},{1,9},{2,10},{3,11},{4,12},{5,13},{6,14},{7,15}} | collective-permute-start | bytes 3145736 | tf_op jit(solution)/shard_map/ppermute | solution.py:659
  45.7 51.9 %all-gather = f32[16384]{0:T(1024)S(1)} all-gather(f32[4096]{0:T(1024)S(1)} %pad_maximum_fusion.13), channel_id=2, replica_groups=mesh['segment'=4,'dp'=8] {'segment'}, dimensions={0}, use_global_device_ids=true | all-gather | bytes 81920 | tf_op jit(solution)/shard_map/all_gather | solution.py:726
  101.3 8.6 reshape.694.x
  111.9 44.8 %shard_map.154 = (bf16[4,304,512]{2,1,0:T(8,128)(2,1)}, bf16[1176,4608]{1,0:T(8,128)(2,1)}, f32[1176,512]{1,0:T(8,128)}, f32[1176,512]{1,0:T(8,128)}, f32[16,512]{1,0:T(8,128)}, /*index=5*/f32[8,128]{1,0:T(8,128)}) custom-call(bf16[1176,2048]{1,0:T(8,128)(2,1)} %reshape.694.x, bf16[2048,512]{1,0:T(8,128)(2,1)} %bitcast.215, bf16[4608,512]{1,0:T(8,128)(2,1)} %bitcast.224, ...), custom_call_target="tpu_custom_call" | custom-call | flops 8015314944 | bytes 41943040 | tf_op jit(solution)/shard_map/pallas_call | solution.py:83
  162.5 6.5 collective-permute-start.2
  171.2 6.6 constant_dynamic-slice_fusion.12
  184.4 7.2 shard_map.155
  191.6 17.0 %all-to-all-start = ((bf16[4,304,512]{2,1,0:T(8,128)(2,1)}), bf16[4,304,512]{2,1,0:T(8,128)(2,1)S(1)}, u32[]{:S(2)}, u32[]{:S(2)}) async-start(bf16[4,304,512]{2,1,0:T(8,128)(2,1)} %shard_map.155), calls=%async_computation | async-start | bytes 2490368 | tf_op jit(solution)/shard_map/all_to_all | solution.py:784
  218.2 3.4 maximum_select_fusion.3.w1
  221.7 3.3 all-to-all-done.res
  226.0 14.8 %shard_map.156 = (bf16[304,2048]{1,0:T(8,128)(2,1)}, bf16[304,2048]{1,0:T(8,128)(2,1)}, f32[304,2048]{1,0:T(8,128)}, f32[2,2048]{1,0:T(2,128)}) custom-call(bf16[304,512]{1,0:T(8,128)(2,1)} %fusion.24.a2, bf16[2048,512]{1,0:T(8,128)(2,1)} %maximum_select_fusion.3.w1, bf16[4,304,512]{2,1,0:T(8,128)(2,1)} %copy-done.10, f32[304,1]{1,0:T(8,128)} %pad.22.pack, ...), custom_call_target="tpu_custom_call" | custom-call | flops 1016070144 | bytes 10485760 | tf_op jit(solution)/shard_map/pallas_call | solution.py:83
  240.9 4.6 fusion.53
  245.5 2.6 slice_bitcast_fusion.1
  248.2 2.5 copy.121
  250.6 63.6 %shard_map.157 = (bf16[304,2048]{1,0:T(8,128)(2,1)}, bf16[304,512]{1,0:T(8,128)(2,1)}, bf16[304,4608]{1,0:T(8,128)(2,1)}, bf16[304,2048]{1,0:T(8,128)(2,1)}, bf1...) custom-call(bf16[304,2048]{1,0:T(8,128)(2,1)} %get-tuple-element.33.u, ...), custom_call_target="tpu_custom_call" | custom-call | flops 5419040768 | bytes 31457280 | tf_op jit(solution)/shard_map/pallas_call | solution.py:83
  314.3 14.1 %shard_map.158 = (bf16[304,2048]{1,0:T(8,128)(2,1)}, bf16[304,2048]{1,0:T(8,128)(2,1)}, bf16[304,512]{1,0:T(8,128)(2,1)}, f32[2,2048]{1,0:T(2,128)}) custom-call(bf16[304,2048]{1,0:T(8,128)(2,1)} %get-tuple-element.34.dy, bf16[4,304,512]{2,1,0:T(8,128)(2,1)} %copy-done.10, f32[304,2048]{1,0:T(8,128)} %get-tuple-element.35.h3n, f32[304,1]{1,0:T(8,128)} %pad.22.pack, ...), custom_call_target="tpu_custom_call" | custom-call | flops 637534208 | bytes 12582912 | tf_op jit(solution)/shard_map/pallas_call | solution.py:83
  329.7 9.8 collective-permute-start.15
  339.6 2.7 fusion.66
  342.3 2.7 fusion.68
  358.9 4.8 all-to-all-start.2
  363.6 5.2 collective-permute-done.14
  373.8 2.8 add_convert_fusion.2
  376.7 2.5 add_convert_fusion
  379.2 8.0 pad_maximum_fusion
  387.2 5.1 all-to-all-start.3
  392.6 38.0 %shard_map.159 = (bf16[1176,512]{1,0:T(8,128)(2,1)}, bf16[1176,512]{1,0:T(8,128)(2,1)}, f32[16,512]{1,0:T(8,128)}) custom-call(bf16[4,304,512]{2,1,0:T(8,128)(2,1)} %pad_maximum_fusion.10.da2, bf16[4608,512]{1,0:T(8,128)(2,1)} %bitcast.225, f32[4,512]{1,0:T(4,128)} %pad_maximum_fusion.16.gb, f32[1176,16]{1,0:T(8,128)} %copy.118.pack, ...), custom_call_target="tpu_custom_call" | custom-call | flops 5549064192 | bytes 20971520 | tf_op jit(solution)/shard_map/pallas_call | solution.py:83
  430.6 10.2 %fusion.64 = f32[4608,512]{1,0:T(8,128)S(1)} fusion(bf16[1176,4608]{1,0:T(8,128)(2,1)} %get-tuple-element.45, bf16[1176,512]{1,0:T(8,128)(2,1)} %get-tuple-element.46), kind=kOutput, calls=%fused_computation.198 | convolution fusion | flops 5549064192 | bytes 21479424 | tf_op jit(solution)/shard_map/rk,rn->kn/dot_general | solution.py:647
  442.9 3.0 fusion.63
  450.4 6.9 fusion.65
  457.3 4.9 reduce_sum.58
  462.2 2.7 fusion.6
  468.3 5.4 add_convert_fusion.1
  473.7 3.1 copy.129
  476.8 2.6 fusion.10
  483.8 4.8 collective-permute-start.23
  494.5 3.3 fusion.3
  497.7 8.7 collective-permute-done.23
  511.9 15.3 %collective-permute-done.24 = bf16[832,512]{1,0:T(8,128)(2,1)} collective-permute-done((bf16[832,512]{1,0:T(8,128)(2,1)}, bf16[832,512]{1,0:T(8,128)(2,1)}, u32[]{:S(2)}, u32[]{:S(2)}) %collective-permute-start.24) | collective-permute-done | bytes 852000 | tf_op jit(solution)/shard_map/ppermute | solution.py:659
  534.5 40.6 %reduce-scatter.3.cloned.1.call-done = bf16[1,464,512]{2,1,0:T(8,128)(2,1)} async-done(((bf16[4,464,512]{2,1,0:T(8,128)(2,1)}), bf16[1,464,512]{2,1,0:T(8,128)(2,1)}) %reduce-scatter.3.cloned.1.call-update) | async-done | bytes 475152 | tf_op jit(solution)/shard_map/reduce_scatter | solution.py:939
  575.2 34.4 %all-gather.11.cloned.1.call-done = bf16[1,1344,512]{2,1,0:T(8,128)(2,1)} async-done(((bf16[1,336,512]{2,1,0:T(8,128)(2,1)}), bf16[1,1344,512]{2,1,0:T(8,128)(2,1)}) %all-gather.11.cloned.1.call-update) | async-done | bytes 1376272 | tf_op jit(solution)/shard_map/all_gather | solution.py:942
  613.2 3.7 all-to-all-start.4
  617.0 35.5 %all-gather.9.cloned.1.call-done = bf16[1,1856,512]{2,1,0:T(8,128)(2,1)} async-done(((bf16[1,464,512]{2,1,0:T(8,128)(2,1)}), bf16[1,1856,512]{2,1,0:T(8,128)(2,1)}) %all-gather.9.cloned.1.call-update) | async-done | bytes 1900560 | tf_op jit(solution)/shard_map/all_gather | solution.py:942
  659.0 6.0 pad_maximum_fusion.1
  666.0 8.2 all-to-all-start.1
  675.0 118.0 %collective-permute-done.27 = bf16[1856,512]{1,0:T(8,128)(2,1)} collective-permute-done((bf16[1856,512]{1,0:T(8,128)(2,1)}, bf16[1856,512]{1,0:T(8,128)(2,1)}, u32[]{:S(2)}, u32[]{:S(2)}) %collective-permute-start.27) | collective-permute-done | bytes 1900576 | tf_op jit(solution)/shard_map/ppermute | solution.py:666
  795.3 3.7 pad_maximum_fusion.5
  799.0 38.4 %all-reduce.7.cloned.1.call-done = f32[4,2,2048]{2,1,0:T(2,128)} async-done(((f32[4,2,2048]{2,1,0:T(2,128)}), f32[4,2,2048]{2,1,0:T(2,128)}) %all-reduce.7.cloned.1.call-update) | async-done | bytes 65552 | tf_op jit(solution)/shard_map/psum | solution.py:918
  838.9 2.6 fusion.2
  841.5 5.9 copy.125
  847.5 8.6 reshape.702.dz
  856.0 4.5 maximum_select_fusion.2
  860.6 22.2 %shard_map.160 = bf16[1176,2048]{1,0:T(8,128)(2,1)} custom-call(bf16[1176,512]{1,0:T(8,128)(2,1)} %get-tuple-element.41.dh1, bf16[1176,2048]{1,0:T(8,128)(2,1)} %reshape.702.dz, bf16[2048,512]{1,0:T(8,128)(2,1)} %bitcast.216, bf16[2048,2048]{1,0:T(8,128)(2,1)} %bitcast.217), custom_call_target="tpu_custom_call" | custom-call | flops 12331253760 | bytes 31457280 | tf_op jit(solution)/shard_map/pallas_call | solution.py:83
  882.8 9.1 reshape.703
  891.9 9.2 fusion.1
  901.1 5.9 copy.127
  909.1 4.5 fusion.85
  913.6 5.7 convert_bitcast_fusion
  919.3 26.2 %copy.139 = f32[2,1024,4,512]{3,2,1,0:T(4,128)} copy(f32[2,1024,4,512]{3,1,2,0:T(8,128)S(1)} %convert_bitcast_fusion) | data formatting | bytes 33554432 | tf_op jit(solution)/shard_map/convert_element_type | solution.py:983
  945.5 20.7 %reshape.722 = f32[1,2048,2048]{2,1,0:T(8,128)} reshape(f32[2,1024,4,512]{3,2,1,0:T(4,128)} %copy.139) | data formatting | bytes 33554432 | tf_op jit(solution)/shard_map/convert_element_type | solution.py:983
  966.1 4.6 maximum_select_fusion.1
  970.9 2.6 convert.8
  973.5 5.1 convert_select_fusion
  (299 shorter events, 122.7 us)
Async XLA Ops:
  7.2 11.2 %copy-start.19 = (bf16[1,2048,512]{2,1,0:T(8,128)(2,1)S(1)}, bf16[1,2048,512]{2,1,0:T(8,128)(2,1)}, u32[]{:S(2)}) copy-start(bf16[1,2048,512]{2,1,0:T(8,128)(2,1)} %param.15) | copy-start | bytes 6291460
  7.2 233.7 %all-gather.7.cloned.1.call-start = ((), (), s32[]{:S(2)}) async-start(), calls=%async_computation.7 | async-start | bytes 13516800 | tf_op jit(solution)/shard_map/all_gather | solution.py:720
  8.5 8.1 collective-permute-start.13
  9.8 6.8 collective-permute-start.12
  10.4 6.1 collective-permute-start.11
  18.5 159.4 %collective-permute-start.5 = (bf16[1024,512]{1,0:T(8,128)(2,1)S(1)}, bf16[1024,512]{1,0:T(8,128)(2,1)S(1)}, u32[]{:S(2)}, u32[]{:S(2)}) collective-permute-start(bf16[1024,512]{1,0:T(8,128)(2,1)S(1)} %dynamic-slice_bitcast_fusion.1), channel_id=1, source_target_pairs={{8,0},{9,1},{10,2},{11,3},{12,4},{13,5},{14,6},{15,7}} | collective-permute-start | bytes 3145736 | tf_op jit(solution)/shard_map/ppermute | solution.py:659
  19.8 160.1 %collective-permute-start.4 = (bf16[1024,512]{1,0:T(8,128)(2,1)S(1)}, bf16[1024,512]{1,0:T(8,128)(2,1)S(1)}, u32[]{:S(2)}, u32[]{:S(2)}) collective-permute-start(bf16[1024,512]{1,0:T(8,128)(2,1)S(1)} %dynamic-slice_bitcast_fusion.1), channel_id=1, source_target_pairs={{8,16},{9,17},{10,18},{11,19},{12,20},{13,21},{14,22},{15,23}} | collective-permute-start | bytes 3145736 | tf_op jit(solution)/shard_map/ppermute | solution.py:659
  25.0 16.5 %copy-start.41 = (s32[4,6]{1,0:T(4,128)S(1)}, s32[4,6]{1,0:T(4,128)}, u32[]{:S(2)}) copy-start(s32[4,6]{1,0:T(4,128)} %param.13) | copy-start | bytes 292
  25.0 17.4 %copy-start.34 = (s32[4,6,9]{2,0,1:T(4,128)S(1)}, s32[4,6,9]{2,0,1:T(4,128)}, u32[]{:S(2)}) copy-start(s32[4,6,9]{2,0,1:T(4,128)} %param.14) | copy-start | bytes 2596
  25.0 20.7 %copy-start.29 = (f32[1,2048]{1,0:T(1,128)S(1)}, f32[1,2048]{1,0:T(1,128)}, u32[]{:S(2)}) copy-start(f32[1,2048]{1,0:T(1,128)} %param.18) | copy-start | bytes 24580
  25.0 20.7 %copy-start.31 = (f32[1,2048]{1,0:T(1,128)S(1)}, f32[1,2048]{1,0:T(1,128)}, u32[]{:S(2)}) copy-start(f32[1,2048]{1,0:T(1,128)} %param.19) | copy-start | bytes 24580
  26.8 134.0 %collective-permute-start.9 = (bf16[1024,512]{1,0:T(8,128)(2,1)}, bf16[1024,512]{1,0:T(8,128)(2,1)}, u32[]{:S(2)}, u32[]{:S(2)}) collective-permute-start(bf16[1024,512]{1,0:T(8,128)(2,1)} %get-tuple-element.67), channel_id=1, source_target_pairs={{0,8},{1,9},{2,10},{3,11},{4,12},{5,13},{6,14},{7,15}} | collective-permute-start | bytes 3145736 | tf_op jit(solution)/shard_map/ppermute | solution.py:659
  37.0 125.5 %collective-permute-start.8 = (bf16[1024,512]{1,0:T(8,128)(2,1)}, bf16[1024,512]{1,0:T(8,128)(2,1)}, u32[]{:S(2)}, u32[]{:S(2)}) collective-permute-start(bf16[1024,512]{1,0:T(8,128)(2,1)} %get-tuple-element.68), channel_id=1, source_target_pairs={{0,16},{1,17},{2,18},{3,19},{4,20},{5,21},{6,22},{7,23}} | collective-permute-start | bytes 3145736 | tf_op jit(solution)/shard_map/ppermute | solution.py:659
  39.3 129.8 %collective-permute-start.7 = (bf16[1024,512]{1,0:T(8,128)(2,1)}, bf16[1024,512]{1,0:T(8,128)(2,1)}, u32[]{:S(2)}, u32[]{:S(2)}) collective-permute-start(bf16[1024,512]{1,0:T(8,128)(2,1)} %get-tuple-element.69), channel_id=1, source_target_pairs={{0,24},{1,25},{2,26},{3,27},{4,28},{5,29},{6,30},{7,31}} | collective-permute-start | bytes 3145736 | tf_op jit(solution)/shard_map/ppermute | solution.py:659
  44.0 53.8 %copy-start.39 = (pred[294]{0:T(512)(128)(4,1)}, pred[294]{0:T(512)(128)(4,1)S(1)}, u32[]{:S(2)}) copy-start(pred[294]{0:T(512)(128)(4,1)S(1)} %and.243) | copy-start | bytes 886
  111.8 50.6 %copy-start.35 = (s32[294]{0:T(512)S(1)}, s32[294]{0:T(512)}, u32[]{:S(2)}) copy-start(s32[294]{0:T(512)} %add.322) | copy-start | bytes 3532
  111.8 50.6 %copy-start.36 = (s32[294]{0:T(512)S(1)}, s32[294]{0:T(512)}, u32[]{:S(2)}) copy-start(s32[294]{0:T(512)} %squeeze.96) | copy-start | bytes 3532
  156.7 13.9 %copy-start.28 = (f32[304,15]{0,1:T(8,128)S(1)}, f32[304,15]{0,1:T(8,128)}, u32[]{:S(2)}) copy-start(f32[304,15]{0,1:T(8,128)} %constant.157.clone) | copy-start | bytes 54724
  160.8 21.1 %collective-permute-start.3 = (bf16[1024,512]{1,0:T(8,128)(2,1)S(1)}, bf16[1024,512]{1,0:T(8,128)(2,1)}, u32[]{:S(2)}, u32[]{:S(2)}) collective-permute-start(bf16[1024,512]{1,0:T(8,128)(2,1)S(1)} %dynamic-slice_bitcast_fusion.1), channel_id=1, source_target_pairs={{8,24},{9,25},{10,26},{11,27},{12,28},{13,29},{14,30},{15,31}} | collective-permute-start | bytes 3145736 | tf_op jit(solution)/shard_map/ppermute | solution.py:659
  162.5 54.0 %collective-permute-start.2 = (bf16[304,512]{1,0:T(8,128)(2,1)}, bf16[304,512]{1,0:T(8,128)(2,1)}, u32[]{:S(2)}, u32[]{:S(2)}) collective-permute-start(bf16[304,512]{1,0:T(8,128)(2,1)} %get-tuple-element.73), channel_id=1, source_target_pairs={{0,8},{1,9},{2,10},{3,11},{4,12},{5,13},{6,14},{7,15}} | collective-permute-start | bytes 933896 | tf_op jit(solution)/shard_map/ppermute | solution.py:659
  170.5 12.0 %copy-start.22 = (bf16[1024,512]{1,0:T(8,128)(2,1)}, bf16[1024,512]{1,0:T(8,128)(2,1)S(1)}, u32[]{:S(2)}) copy-start(bf16[1024,512]{1,0:T(8,128)(2,1)S(1)} %fusion.8.wa) | copy-start | bytes 3145732
  170.5 11.4 %copy-start.20 = (bf16[1,2048,512]{2,1,0:T(8,128)(2,1)S(1)}, bf16[1,2048,512]{2,1,0:T(8,128)(2,1)}, u32[]{:S(2)}) copy-start(bf16[1,2048,512]{2,1,0:T(8,128)(2,1)} %param.15) | copy-start | bytes 6291460
  170.5 12.8 %collective-permute-start.10 = (bf16[1024,512]{1,0:T(8,128)(2,1)S(1)}, bf16[1024,512]{1,0:T(8,128)(2,1)S(1)}, u32[]{:S(2)}, u32[]{:S(2)}) collective-permute-start(bf16[1024,512]{1,0:T(8,128)(2,1)S(1)} %fusion.8.wa), channel_id=1, source_target_pairs={{0,1},{1,0},{2,3},{3,2},{4,5},{5,4},{6,7},{7,6},{8,9},{9,8},{10,11... | collective-permute-start | bytes 3145736 | tf_op jit(solution)/shard_map/ppermute | solution.py:652
  177.8 38.6 %collective-permute-start.1 = (bf16[304,512]{1,0:T(8,128)(2,1)}, bf16[304,512]{1,0:T(8,128)(2,1)}, u32[]{:S(2)}, u32[]{:S(2)}) collective-permute-start(bf16[304,512]{1,0:T(8,128)(2,1)} %get-tuple-element.74), channel_id=1, source_target_pairs={{0,16},{1,17},{2,18},{3,19},{4,20},{5,21},{6,22},{7,23}} | collective-permute-start | bytes 933896 | tf_op jit(solution)/shard_map/ppermute | solution.py:659
  179.9 36.6 %collective-permute-start = (bf16[304,512]{1,0:T(8,128)(2,1)}, bf16[304,512]{1,0:T(8,128)(2,1)}, u32[]{:S(2)}, u32[]{:S(2)}) collective-permute-start(bf16[304,512]{1,0:T(8,128)(2,1)} %get-tuple-element.75), channel_id=1, source_target_pairs={{0,24},{1,25},{2,26},{3,27},{4,28},{5,29},{6,30},{7,31}} | collective-permute-start | bytes 933896 | tf_op jit(solution)/shard_map/ppermute | solution.py:659
  182.5 35.8 %collective-permute-start.6 = (bf16[1024,512]{1,0:T(8,128)(2,1)S(1)}, bf16[1024,512]{1,0:T(8,128)(2,1)}, u32[]{:S(2)}, u32[]{:S(2)}) collective-permute-start(bf16[1024,512]{1,0:T(8,128)(2,1)S(1)} %select_select_fusion), channel_id=1, source_target_pairs={{0,1},{1,0},{2,3},{3,2},{4,5},{5,4},{6,7},{7,6},{8,9},{9,8},{10,11... | collective-permute-start | bytes 3145736 | tf_op jit(solution)/shard_map/ppermute | solution.py:652
  183.3 27.3 %copy-start.37 = (f32[294,1]{0,1:T(1,128)S(1)}, f32[294,1]{0,1:T(1,128)}, u32[]{:S(2)}) copy-start(f32[294,1]{0,1:T(1,128)} %get-tuple-element.104) | copy-start | bytes 3532
  191.6 33.4 %all-to-all-start = ((bf16[4,304,512]{2,1,0:T(8,128)(2,1)}), bf16[4,304,512]{2,1,0:T(8,128)(2,1)S(1)}, u32[]{:S(2)}, u32[]{:S(2)}) async-start(bf16[4,304,512]{2,1,0:T(8,128)(2,1)} %shard_map.155), calls=%async_computation | async-start | bytes 2490368 | tf_op jit(solution)/shard_map/all_to_all | solution.py:784
  314.3 25.3 %copy-start.18 = (bf16[304,512]{1,0:T(8,128)(2,1)S(1)}, bf16[304,512]{1,0:T(8,128)(2,1)}, u32[]{:S(2)}) copy-start(bf16[304,512]{1,0:T(8,128)(2,1)} %fusion.24.a2) | copy-start | bytes 933892
  328.4 26.9 %collective-permute-start.16 = (bf16[304,512]{1,0:T(8,128)(2,1)}, bf16[304,512]{1,0:T(8,128)(2,1)S(1)}, u32[]{:S(2)}, u32[]{:S(2)}) collective-permute-start(bf16[304,512]{1,0:T(8,128)(2,1)} %get-tuple-element.37), channel_id=1, source_target_pairs={{24,0},{25,1},{26,2},{27,3},{28,4},{29,5},{30,6},{31,7}} | collective-permute-start | bytes 933896 | tf_op jit(solution)/shard_map/ppermute | solution.py:666
  329.7 26.7 %collective-permute-start.15 = (bf16[304,512]{1,0:T(8,128)(2,1)}, bf16[304,512]{1,0:T(8,128)(2,1)}, u32[]{:S(2)}, u32[]{:S(2)}) collective-permute-start(bf16[304,512]{1,0:T(8,128)(2,1)} %get-tuple-element.37), channel_id=1, source_target_pairs={{16,0},{17,1},{18,2},{19,3},{20,4},{21,5},{22,6},{23,7}} | collective-permute-start | bytes 933896 | tf_op jit(solution)/shard_map/ppermute | solution.py:666
  346.8 29.8 %collective-permute-start.31 = (bf16[2304,512]{1,0:T(8,128)(2,1)}, bf16[2304,512]{1,0:T(8,128)(2,1)}, u32[]{:S(2)}, u32[]{:S(2)}) collective-permute-start(bf16[2304,512]{1,0:T(8,128)(2,1)} %dynamic-slice_convert_fusion), channel_id=1, source_target_pairs={{0,1},{1,0},{2,3},{3,2},{4,5},{5,4},{6,7},{7,6},{8,9},{9,8},{10,11... | collective-permute-start | bytes 7077896 | tf_op jit(solution)/shard_map/ppermute | solution.py:652
  348.0 23.3 %collective-permute-start.29 = (bf16[1024,512]{1,0:T(8,128)(2,1)}, bf16[1024,512]{1,0:T(8,128)(2,1)S(1)}, u32[]{:S(2)}, u32[]{:S(2)}) collective-permute-start(bf16[1024,512]{1,0:T(8,128)(2,1)} %dynamic-slice_convert_fusion.4), channel_id=1, source_target_pairs={{0,1},{1,0},{2,3},{3,2},{4,5},{5,4},{6,7},{7,6},{8,9},{9,8},{10,11... | collective-permute-start | bytes 3145736 | tf_op jit(solution)/shard_map/ppermute | solution.py:652
  351.5 21.9 %collective-permute-start.30 = (bf16[1024,512]{1,0:T(8,128)(2,1)}, bf16[1024,512]{1,0:T(8,128)(2,1)S(1)}, u32[]{:S(2)}, u32[]{:S(2)}) collective-permute-start(bf16[1024,512]{1,0:T(8,128)(2,1)} %dynamic-slice_convert_fusion.3), channel_id=1, source_target_pairs={{0,1},{1,0},{2,3},{3,2},{4,5},{5,4},{6,7},{7,6},{8,9},{9,8},{10,11... | collective-permute-start | bytes 3145736 | tf_op jit(solution)/shard_map/ppermute | solution.py:652
  356.0 17.8 %collective-permute-start.32 = (bf16[1024,512]{1,0:T(8,128)(2,1)}, bf16[1024,512]{1,0:T(8,128)(2,1)}, u32[]{:S(2)}, u32[]{:S(2)}) collective-permute-start(bf16[1024,512]{1,0:T(8,128)(2,1)} %dynamic-slice_convert_fusion.2), channel_id=1, source_target_pairs={{0,1},{1,0},{2,3},{3,2},{4,5},{5,4},{6,7},{7,6},{8,9},{9,8},{10,11... | collective-permute-start | bytes 3145736 | tf_op jit(solution)/shard_map/ppermute | solution.py:652
  356.4 12.4 %collective-permute-start.14 = (bf16[304,512]{1,0:T(8,128)(2,1)}, bf16[304,512]{1,0:T(8,128)(2,1)}, u32[]{:S(2)}, u32[]{:S(2)}) collective-permute-start(bf16[304,512]{1,0:T(8,128)(2,1)} %get-tuple-element.37), channel_id=1, source_target_pairs={{8,0},{9,1},{10,2},{11,3},{12,4},{13,5},{14,6},{15,7}} | collective-permute-start | bytes 933896 | tf_op jit(solution)/shard_map/ppermute | solution.py:666
  358.9 28.3 %all-to-all-start.2 = ((bf16[304,4,512]{2,0,1:T(8,128)(2,1)}), bf16[304,4,512]{2,0,1:T(8,128)(2,1)S(1)}, u32[]{:S(2)}, u32[]{:S(2)}) async-start(bf16[304,4,512]{2,0,1:T(8,128)(2,1)} %bitcast.185), calls=%async_computation.2 | async-start | bytes 2490368 | tf_op jit(solution)/shard_map/all_to_all | solution.py:874
  387.2 70.1 %all-to-all-start.3 = ((bf16[4,1344,512]{2,1,0:T(8,128)(2,1)}), bf16[4,1344,512]{2,1,0:T(8,128)(2,1)}, u32[]{:S(2)}, u32[]{:S(2)}) async-start(bf16[4,1344,512]{2,1,0:T(8,128)(2,1)} %pad_maximum_fusion), calls=%async_computation.4 | async-start | bytes 11010048 | tf_op jit(solution)/shard_map/all_to_all | solution.py:933
  392.3 141.7 %reduce-scatter.5.cloned.1.call-start = ((), (), s32[]{:S(2)}) async-start(), calls=%async_computation.9 | async-start | bytes 1720320 | tf_op jit(solution)/shard_map/reduce_scatter | solution.py:939
  392.6 50.1 %slice-start = ((s8[4816896]{0:T(1024)(128)(4,1)}), s8[622592]{0:T(1024)(128)(4,1)S(1)}, s32[]{:S(2)}) async-start(s8[4816896]{0:T(1024)(128)(4,1)} %bitcast.188), calls=%async_computation.13 | async-start | bytes 1245184
  430.6 12.1 %slice-start.1 = ((s8[4816896]{0:T(1024)(128)(4,1)}), s8[4194304]{0:T(1024)(128)(4,1)S(1)}, s32[]{:S(2)}) async-start(s8[4816896]{0:T(1024)(128)(4,1)} %bitcast.188), calls=%async_computation.14 | async-start | bytes 8388608
  442.6 25.7 %collective-permute-start.21 = (bf16[2304,512]{1,0:T(8,128)(2,1)}, bf16[2304,512]{1,0:T(8,128)(2,1)}, u32[]{:S(2)}, u32[]{:S(2)}) collective-permute-start(bf16[2304,512]{1,0:T(8,128)(2,1)} %dynamic-slice_convert_fusion.1), channel_id=1, source_target_pairs={{0,1},{1,0},{2,3},{3,2},{4,5},{5,4},{6,7},{7,6},{8,9},{9,8},{10,11... | collective-permute-start | bytes 7077896 | tf_op jit(solution)/shard_map/ppermute | solution.py:652
  449.1 16.1 %collective-permute-start.20 = (bf16[1024,512]{0,1:T(8,128)(2,1)}, bf16[1024,512]{0,1:T(8,128)(2,1)S(1)}, u32[]{:S(2)}, u32[]{:S(2)}) collective-permute-start(bf16[1024,512]{0,1:T(8,128)(2,1)} %fusion.5), channel_id=1, source_target_pairs={{0,1},{1,0},{2,3},{3,2},{4,5},{5,4},{6,7},{7,6},{8,9},{9,8},{10,11... | collective-permute-start | bytes 3145736 | tf_op jit(solution)/shard_map/ppermute | solution.py:652
  462.2 113.0 %reduce-scatter.3.cloned.1.call-start = ((), (), s32[]{:S(2)}) async-start(), calls=%async_computation.8 | async-start | bytes 2375680 | tf_op jit(solution)/shard_map/reduce_scatter | solution.py:939
  465.0 29.5 %collective-permute-start.25 = (bf16[1024,512]{0,1:T(8,128)(2,1)}, bf16[1024,512]{0,1:T(8,128)(2,1)}, u32[]{:S(2)}, u32[]{:S(2)}) collective-permute-start(bf16[1024,512]{0,1:T(8,128)(2,1)} %fusion.6), channel_id=1, source_target_pairs={{0,1},{1,0},{2,3},{3,2},{4,5},{5,4},{6,7},{7,6},{8,9},{9,8},{10,11... | collective-permute-start | bytes 3145736 | tf_op jit(solution)/shard_map/ppermute | solution.py:652
  483.8 22.7 %collective-permute-start.23 = (bf16[832,512]{1,0:T(8,128)(2,1)}, bf16[832,512]{1,0:T(8,128)(2,1)}, u32[]{:S(2)}, u32[]{:S(2)}) collective-permute-start(bf16[832,512]{1,0:T(8,128)(2,1)} %copy.131), channel_id=1, source_target_pairs={{0,16},{1,17},{2,18},{3,19},{4,20},{5,21},{6,22},{7,23}} | collective-permute-start | bytes 2555912 | tf_op jit(solution)/shard_map/ppermute | solution.py:659
  488.6 21.2 %collective-permute-start.22 = (bf16[832,512]{1,0:T(8,128)(2,1)}, bf16[832,512]{1,0:T(8,128)(2,1)}, u32[]{:S(2)}, u32[]{:S(2)}) collective-permute-start(bf16[832,512]{1,0:T(8,128)(2,1)} %copy.130), channel_id=1, source_target_pairs={{0,24},{1,25},{2,26},{3,27},{4,28},{5,29},{6,30},{7,31}} | collective-permute-start | bytes 2555912 | tf_op jit(solution)/shard_map/ppermute | solution.py:659
  492.3 35.0 %collective-permute-start.24 = (bf16[832,512]{1,0:T(8,128)(2,1)}, bf16[832,512]{1,0:T(8,128)(2,1)}, u32[]{:S(2)}, u32[]{:S(2)}) collective-permute-start(bf16[832,512]{1,0:T(8,128)(2,1)} %copy.132), channel_id=1, source_target_pairs={{0,8},{1,9},{2,10},{3,11},{4,12},{5,13},{6,14},{7,15}} | collective-permute-start | bytes 2555912 | tf_op jit(solution)/shard_map/ppermute | solution.py:659
  533.9 76.9 %copy-start.42 = (pred[832]{0:T(1024)(128)(4,1)S(1)}, pred[832]{0:T(1024)(128)(4,1)}, u32[]{:S(2)}) copy-start(pred[832]{0:T(1024)(128)(4,1)} %constant.155.clone.1) | copy-start | bytes 2500
  533.9 75.7 %all-gather.11.cloned.1.call-start = ((), (), s32[]{:S(2)}) async-start(), calls=%async_computation.12 | async-start | bytes 1720320 | tf_op jit(solution)/shard_map/all_gather | solution.py:942
  534.5 118.0 %all-gather.9.cloned.1.call-start = ((), (), s32[]{:S(2)}) async-start(), calls=%async_computation.11 | async-start | bytes 2375680 | tf_op jit(solution)/shard_map/all_gather | solution.py:942
  613.2 52.7 %all-to-all-start.4 = ((bf16[4,832,512]{2,1,0:T(8,128)(2,1)}), bf16[4,832,512]{2,1,0:T(8,128)(2,1)S(1)}, u32[]{:S(2)}, u32[]{:S(2)}) async-start(bf16[4,832,512]{2,1,0:T(8,128)(2,1)} %pad_maximum_fusion.8), calls=%async_computation.6 | async-start | bytes 6815744 | tf_op jit(solution)/shard_map/all_to_all | solution.py:954
  652.5 140.6 %collective-permute-start.27 = (bf16[1856,512]{1,0:T(8,128)(2,1)}, bf16[1856,512]{1,0:T(8,128)(2,1)}, u32[]{:S(2)}, u32[]{:S(2)}) collective-permute-start(bf16[1856,512]{1,0:T(8,128)(2,1)} %bitcast.190), channel_id=1, source_target_pairs={{16,0},{17,1},{18,2},{19,3},{20,4},{21,5},{22,6},{23,7}} | collective-permute-start | bytes 5701640 | tf_op jit(solution)/shard_map/ppermute | solution.py:666
  653.8 185.1 %collective-permute-start.19 = (bf16[304,2048]{1,0:T(8,128)(2,1)}, bf16[304,2048]{1,0:T(8,128)(2,1)}, u32[]{:S(2)}, u32[]{:S(2)}) collective-permute-start(bf16[304,2048]{1,0:T(8,128)(2,1)} %get-tuple-element.42), channel_id=1, source_target_pairs={{24,0},{25,1},{26,2},{27,3},{28,4},{29,5},{30,6},{31,7}} | collective-permute-start | bytes 3735560 | tf_op jit(solution)/shard_map/ppermute | solution.py:666
  655.1 183.8 %collective-permute-start.18 = (bf16[304,2048]{1,0:T(8,128)(2,1)}, bf16[304,2048]{1,0:T(8,128)(2,1)}, u32[]{:S(2)}, u32[]{:S(2)}) collective-permute-start(bf16[304,2048]{1,0:T(8,128)(2,1)} %get-tuple-element.42), channel_id=1, source_target_pairs={{16,0},{17,1},{18,2},{19,3},{20,4},{21,5},{22,6},{23,7}} | collective-permute-start | bytes 3735560 | tf_op jit(solution)/shard_map/ppermute | solution.py:666
  656.4 138.9 %collective-permute-start.26 = (bf16[1856,512]{1,0:T(8,128)(2,1)}, bf16[1856,512]{1,0:T(8,128)(2,1)}, u32[]{:S(2)}, u32[]{:S(2)}) collective-permute-start(bf16[1856,512]{1,0:T(8,128)(2,1)} %bitcast.191), channel_id=1, source_target_pairs={{8,0},{9,1},{10,2},{11,3},{12,4},{13,5},{14,6},{15,7}} | collective-permute-start | bytes 5701640 | tf_op jit(solution)/shard_map/ppermute | solution.py:666
  657.7 137.6 %collective-permute-start.28 = (bf16[1856,512]{1,0:T(8,128)(2,1)}, bf16[1856,512]{1,0:T(8,128)(2,1)}, u32[]{:S(2)}, u32[]{:S(2)}) collective-permute-start(bf16[1856,512]{1,0:T(8,128)(2,1)} %bitcast.192), channel_id=1, source_target_pairs={{24,0},{25,1},{26,2},{27,3},{28,4},{29,5},{30,6},{31,7}} | collective-permute-start | bytes 5701640 | tf_op jit(solution)/shard_map/ppermute | solution.py:666
  665.9 128.5 %copy-start.27 = (f32[16,512]{1,0:T(8,128)S(1)}, f32[16,512]{1,0:T(8,128)}, u32[]{:S(2)}) copy-start(f32[16,512]{1,0:T(8,128)} %get-tuple-element.53) | copy-start | bytes 98308
  666.0 226.0 %all-to-all-start.1 = ((bf16[4,304,2048]{2,1,0:T(8,128)(2,1)}), bf16[4,304,2048]{2,1,0:T(8,128)(2,1)}, u32[]{:S(2)}, u32[]{:S(2)}) async-start(bf16[4,304,2048]{2,1,0:T(8,128)(2,1)} %pad_maximum_fusion.1), calls=%async_computation.1 | async-start | bytes 9961472 | tf_op jit(solution)/shard_map/all_to_all | solution.py:896
  674.1 163.3 %all-reduce.7.cloned.1.call-start = ((), (), s32[]{:S(2)}) async-start(), calls=%async_computation.10 | async-start | bytes 131072 | tf_op jit(solution)/shard_map/psum | solution.py:918
  793.1 45.8 %collective-permute-start.17 = (bf16[304,2048]{1,0:T(8,128)(2,1)}, bf16[304,2048]{1,0:T(8,128)(2,1)}, u32[]{:S(2)}, u32[]{:S(2)}) collective-permute-start(bf16[304,2048]{1,0:T(8,128)(2,1)} %get-tuple-element.42), channel_id=1, source_target_pairs={{8,0},{9,1},{10,2},{11,3},{12,4},{13,5},{14,6},{15,7}} | collective-permute-start | bytes 3735560 | tf_op jit(solution)/shard_map/ppermute | solution.py:666
  799.0 114.6 %collective-permute-start.34 = (bf16[4,1024,512]{2,1,0:T(8,128)(2,1)}, bf16[4,1024,512]{2,1,0:T(8,128)(2,1)}, u32[]{:S(2)}, u32[]{:S(2)}) collective-permute-start(bf16[4,1024,512]{2,1,0:T(8,128)(2,1)} %pad_maximum_fusion.5), channel_id=1, source_target_pairs={{0,1},{1,0},{2,3},{3,2},{4,5},{5,4},{6,7},{7,6},{8,9},{9,8},{10,11... | collective-permute-start | bytes 12582920 | tf_op jit(solution)/shard_map/ppermute | solution.py:652
  860.6 105.6 %collective-permute-start.33 = (bf16[4,832,512]{2,1,0:T(8,128)(2,1)}, bf16[4,832,512]{2,1,0:T(8,128)(2,1)}, u32[]{:S(2)}, u32[]{:S(2)}) collective-permute-start(bf16[4,832,512]{2,1,0:T(8,128)(2,1)} %maximum_select_fusion.2), channel_id=1, source_target_pairs={{0,1},{1,0},{2,3},{3,2},{4,5},{5,4},{6,7},{7,6},{8,9},{9,8},{10,11... | collective-permute-start | bytes 10223624 | tf_op jit(solution)/shard_map/ppermute | solution.py:652
  945.5 20.7 %copy-start.8 = (bf16[1,4,832,512]{3,2,1,0:T(8,128)(2,1)S(1)}, bf16[1,4,832,512]{3,2,1,0:T(8,128)(2,1)}, u32[]{:S(2)}) copy-start(bf16[1,4,832,512]{3,2,1,0:T(8,128)(2,1)} %fusion.85) | copy-start | bytes 10223620
  (29 other events, 123.4 us)
Sparse Core Ops, SparseCore 0:
  18.5 124.6 all-gather.6
  462.3 32.8 reduce-scatter.4
  534.0 41.0 reduce-scatter.2
  576.6 32.9 all-gather.10
  611.0 41.4 all-gather.8
  795.4 42.0 all-reduce.6

commit v3 on v2

--- a/solution.py
+++ b/solution.py
@@ -612,6 +612,421 @@
     over(out.shape[1], TILE, body)
 
 
+def mesh_copy(src, dst, send_sem, recv_sem, segment, place):
+    return pltpu.make_async_remote_copy(
+        src_ref=src,
+        dst_ref=dst,
+        send_sem=send_sem,
+        recv_sem=recv_sem,
+        device_id=(segment, place),
+        device_id_type=MESH,
+    )
+
+
+def loop(low, high, body):
+    def one(k, carry):
+        body(k)
+        return carry
+
+    lax.fori_loop(low, high, one, 0)
+
+
+SUMS = (("k2", 2, True), ("p3", 3, True), ("p2", 2, True), ("p1", 1, True), ("k0", 0, False), ("p0", 0, False))
+
+
+def gradient_kernel(
+    sections, count, sh, k2, p3, p2, p1, k0, p0, vec, sh_out, p_out, k_out, vec_out, *scratch
+):
+    names = [name for name, _, _ in SUMS]
+    terms = dict(zip(names, (k2, p3, p2, p1, k0, p0)))
+    owner = {name: section for name, section, _ in SUMS}
+    spread = {name: part for name, _, part in SUMS}
+    depth = count // 2
+    me, place = lax.axis_index("segment"), lax.axis_index("dp")
+    core, z = lax.rem(place, 2), lax.div(place, 2)
+    sibling = place + 1 - 2 * core
+    scratch = list(scratch)
+    take = lambda: scratch.pop(0)
+    half, theirs, planes, total, others, whole = {}, {}, {}, {}, {}, {}
+    for name in names:
+        half[name], theirs[name] = take(), take()
+        if spread[name]:
+            planes[name] = take()
+        total[name], others[name], whole[name] = take(), take(), take()
+    sh_half, sh_theirs, sh_others, sh_whole, vec_slots = take(), take(), take(), take(), take()
+    load_sem, a_send, a_recv, b_send, b_recv, c_send, c_recv, d_send, d_recv = (take() for _ in range(9))
+    e_send, e_recv, e_own, f_send, f_recv, v_send, v_recv = (take() for _ in range(7))
+    slot = {name: i for i, name in enumerate(names)}
+    last = len(names)
+
+    def chip(k):
+        return 2 * lax.rem(z + k, depth) + core
+
+    barrier = pltpu.get_barrier_semaphore()
+    pl.semaphore_signal(barrier, inc=1, device_id=(me, sibling), device_id_type=MESH)
+    for k in range(1, sections):
+        pl.semaphore_signal(
+            barrier, inc=1, device_id=(jnp.bitwise_xor(me, k), place), device_id_type=MESH
+        )
+    loop(
+        1,
+        depth,
+        lambda k: pl.semaphore_signal(
+            barrier, inc=1, device_id=(me, chip(k)), device_id_type=MESH
+        ),
+    )
+    pl.semaphore_wait(barrier, 1 + sections - 1 + depth - 1)
+
+    def swap(name):
+        return mesh_copy(
+            terms[name].at[1 - core],
+            theirs[name],
+            a_send.at[slot[name]],
+            a_recv.at[slot[name]],
+            me,
+            sibling,
+        )
+
+    def load(name):
+        return pltpu.make_async_copy(terms[name].at[core], half[name], load_sem.at[slot[name]])
+
+    def when_held(name, body):
+        if spread[name]:
+            body()
+        else:
+            pl.when(me == owner[name])(body)
+
+    sh_rows = sh_half.shape[0]
+    sh_swap = mesh_copy(
+        sh.at[1 - core], sh_theirs, a_send.at[last], a_recv.at[last], me, sibling
+    )
+    sh_load = pltpu.make_async_copy(sh.at[core], sh_half, load_sem.at[last])
+    sh_swap.start()
+    sh_load.start()
+
+    def vec_copy(k):
+        other = jnp.bitwise_xor(me, k)
+        return mesh_copy(
+            vec.at[other], vec_slots.at[k], v_send.at[k], v_recv.at[k], other, place
+        )
+
+    for k in range(1, sections):
+        vec_copy(k).start()
+    for name in names:
+
+        def begin(name=name):
+            swap(name).start()
+            load(name).start()
+
+        when_held(name, begin)
+
+    piece = sh_rows // depth
+    step = 32
+
+    def sh_at(i):
+        return pl.ds(pl.multiple_of(i * piece, 16), piece)
+
+    def sh_send(k):
+        to = lax.rem(z + k, depth)
+        return mesh_copy(
+            sh_half.at[sh_at(to)],
+            sh_others.at[k],
+            c_send.at[last, k],
+            c_recv.at[last, k],
+            me,
+            2 * to + core,
+        )
+
+    sh_load.wait()
+    sh_swap.wait_recv()
+
+    def sh_add(i):
+        at = pl.ds(pl.multiple_of(i * step, step), step)
+        sh_half[at, :] = (sh_half[at, :].astype(F32) + sh_theirs[at, :].astype(F32)).astype(BF16)
+
+    loop(0, sh_rows // step, sh_add)
+    loop(1, depth, lambda k: sh_send(k).start())
+
+    def to_section(name, k):
+        other = jnp.bitwise_xor(me, k)
+        target = planes[name].at[k] if spread[name] else total[name]
+        return mesh_copy(
+            half[name].at[other],
+            target,
+            b_send.at[slot[name], k],
+            b_recv.at[slot[name], k],
+            other,
+            place,
+        )
+
+    for name in names:
+
+        def combine(name=name):
+            load(name).wait()
+            swap(name).wait_recv()
+
+            def add(i):
+                q, y = lax.div(i, depth), lax.rem(i, depth)
+                half[name][q, y] = (
+                    half[name][q, y].astype(F32) + theirs[name][q, y].astype(F32)
+                ).astype(BF16)
+
+            loop(0, sections * depth, add)
+            for k in range(1, sections):
+                to_section(name, k).start()
+
+        when_held(name, combine)
+
+    loop(1, depth, lambda k: sh_send(k).wait_recv())
+    mine = sh_at(z)
+    acc = sh_half[mine, :].astype(F32)
+    for k in range(1, depth):
+        acc = acc + sh_others[k].astype(F32)
+    sh_whole[mine, :] = acc.astype(BF16)
+
+    def sh_share(k):
+        return mesh_copy(
+            sh_whole.at[mine],
+            sh_whole.at[mine],
+            d_send.at[last, k],
+            d_recv.at[last, k],
+            me,
+            chip(k),
+        )
+
+    loop(1, depth, lambda k: sh_share(k).start())
+
+    def to_chip(name, k):
+        to = lax.rem(z + k, depth)
+        return mesh_copy(
+            total[name].at[to],
+            others[name].at[k],
+            c_send.at[slot[name], k],
+            c_recv.at[slot[name], k],
+            me,
+            2 * to + core,
+        )
+
+    for name in names:
+        if spread[name]:
+            for k in range(1, sections):
+                to_section(name, k).wait_recv()
+
+            def plane_add(y, name=name):
+                acc = half[name][me, y].astype(F32)
+                for k in range(1, sections):
+                    acc = acc + planes[name][k, y].astype(F32)
+                total[name][y] = acc.astype(BF16)
+
+            loop(0, depth, plane_add)
+        else:
+
+            @pl.when(me == owner[name])
+            def _(name=name):
+                def keep(y):
+                    total[name][y] = half[name][owner[name], y]
+
+                loop(0, depth, keep)
+
+            for k in range(1, sections):
+
+                @pl.when(me == owner[name] ^ k)
+                def _(name=name, k=k):
+                    to_section(name, k).wait_recv()
+
+        loop(1, depth, lambda k, name=name: to_chip(name, k).start())
+
+    def sh_deliver(k):
+        at = pl.ds(pl.multiple_of(me * sh_whole.shape[1], 128), sh_whole.shape[1])
+        return mesh_copy(
+            sh_whole,
+            sh_out.at[core, :, at],
+            e_send.at[last],
+            e_recv.at[last, k],
+            0,
+            place,
+        )
+
+    loop(1, depth, lambda k: sh_share(k).wait_recv())
+    at_zero = pl.ds(0, sh_whole.shape[1])
+    sh_keep = pltpu.make_async_copy(sh_whole, sh_out.at[core, :, at_zero], e_own.at[last])
+
+    @pl.when(me == 0)
+    def _():
+        sh_keep.start()
+
+    for k in range(1, sections):
+
+        @pl.when(me == k)
+        def _(k=k):
+            sh_deliver(k).start()
+
+    def share(name, k):
+        return mesh_copy(
+            whole[name].at[z],
+            whole[name].at[z],
+            d_send.at[slot[name], k],
+            d_recv.at[slot[name], k],
+            me,
+            chip(k),
+        )
+
+    for name in names:
+        loop(1, depth, lambda k, name=name: to_chip(name, k).wait_recv())
+        acc = total[name][z].astype(F32)
+        for k in range(1, depth):
+            acc = acc + others[name][k].astype(F32)
+        whole[name][z] = acc.astype(BF16)
+        loop(1, depth, lambda k, name=name: share(name, k).start())
+
+    def final(name):
+        return k_out if name[0] == "k" else p_out
+
+    def deliver(name, k):
+        return mesh_copy(
+            whole[name],
+            final(name).at[core, me],
+            e_send.at[slot[name]],
+            e_recv.at[slot[name], k],
+            owner[name],
+            place,
+        )
+
+    def keep_own(name):
+        return pltpu.make_async_copy(whole[name], final(name).at[core, me], e_own.at[slot[name]])
+
+    for name in names:
+        loop(1, depth, lambda k, name=name: share(name, k).wait_recv())
+
+        @pl.when(me == owner[name])
+        def _(name=name):
+            keep_own(name).start()
+
+        for k in range(1, sections):
+
+            @pl.when(me == owner[name] ^ k)
+            def _(name=name, k=k):
+                deliver(name, k).start()
+
+    def cross(name):
+        return mesh_copy(
+            final(name).at[core],
+            final(name).at[core],
+            f_send.at[slot[name]],
+            f_recv.at[slot[name]],
+            me,
+            sibling,
+        )
+
+    sh_cross = mesh_copy(
+        sh_out.at[core], sh_out.at[core], f_send.at[last], f_recv.at[last], me, sibling
+    )
+
+    @pl.when(me == 0)
+    def _():
+        sh_keep.wait()
+        for k in range(1, sections):
+            sh_deliver(k).wait_recv()
+        sh_cross.start()
+
+    for name in names:
+
+        @pl.when(me == owner[name])
+        def _(name=name):
+            keep_own(name).wait()
+            for k in range(1, sections):
+                deliver(name, k).wait_recv()
+            cross(name).start()
+
+    for k in range(1, sections):
+        vec_copy(k).wait_recv()
+    sums = vec[me]
+    for k in range(1, sections):
+        sums = sums + vec_slots[k]
+    vec_out[...] = sums
+
+    for k in range(1, sections):
+        vec_copy(k).wait_send()
+    sh_swap.wait_send()
+    loop(1, depth, lambda k: sh_send(k).wait_send())
+    loop(1, depth, lambda k: sh_share(k).wait_send())
+
+    @pl.when(me == 0)
+    def _():
+        sh_cross.wait()
+
+    @pl.when(me != 0)
+    def _():
+        sh_deliver(0).wait_send()
+
+    for name in names:
+
+        def sent(name=name):
+            swap(name).wait_send()
+            for k in range(1, sections):
+                to_section(name, k).wait_send()
+
+        when_held(name, sent)
+        loop(1, depth, lambda k, name=name: to_chip(name, k).wait_send())
+        loop(1, depth, lambda k, name=name: share(name, k).wait_send())
+
+        @pl.when(me == owner[name])
+        def _(name=name):
+            cross(name).wait()
+
+        @pl.when(me != owner[name])
+        def _(name=name):
+            deliver(name, 0).wait_send()
+
+
+def sum_gradients(sections, count, short, terms, vectors):
+    narrow = short.shape[1]
+    depth = count // 2
+    args, scratch = [], []
+    for name, _, part in SUMS:
+        rows = terms[name].shape[0]
+        fine = rows // (2 * sections * depth)
+        args.append(terms[name].reshape(2, sections, depth, fine, narrow))
+        shapes = [(sections, depth, fine, narrow)] * 2
+        if part:
+            shapes.append((sections, depth, fine, narrow))
+        shapes += [(depth, fine, narrow)] * 3
+        scratch += [pltpu.VMEM(a, BF16) for a in shapes]
+    sh_rows = short.shape[0] // 2
+    scratch += [
+        pltpu.VMEM((sh_rows, narrow), BF16),
+        pltpu.VMEM((sh_rows, narrow), BF16),
+        pltpu.VMEM((depth, sh_rows // depth, narrow), BF16),
+        pltpu.VMEM((sh_rows, narrow), BF16),
+        pltpu.VMEM((sections,) + vectors.shape[1:], F32),
+    ]
+    kinds = len(SUMS) + 1
+    for shape in [(kinds,)] * 3 + [(kinds, sections)] * 2 + [(kinds, depth)] * 4:
+        scratch.append(pltpu.SemaphoreType.DMA(shape))
+    for shape in [(kinds,), (kinds, sections), (kinds,), (kinds,), (kinds,), (sections,), (sections,)]:
+        scratch.append(pltpu.SemaphoreType.DMA(shape))
+    hbm = pl.BlockSpec(memory_space=pl.ANY)
+    vmem = pl.BlockSpec(memory_space=pltpu.VMEM)
+    proj_shape = args[1].shape
+    taps_shape = args[0].shape
+    return pl.pallas_call(
+        functools.partial(gradient_kernel, sections, count),
+        out_shape=[
+            shape_of((2, sh_rows, narrow * sections), BF16),
+            shape_of(proj_shape, BF16),
+            shape_of(taps_shape, BF16),
+            shape_of(vectors.shape[1:], F32),
+        ],
+        in_specs=[hbm] * 7 + [vmem],
+        out_specs=[hbm, hbm, hbm, vmem],
+        scratch_shapes=scratch,
+        compiler_params=pltpu.CompilerParams(
+            has_side_effects=True, vmem_limit_bytes=VMEM_BYTES, collective_id=5
+        ),
+        cost_estimate=pl.CostEstimate(flops=0, bytes_accessed=400 * 2**20, transcendentals=0),
+    )(short.reshape(2, sh_rows, narrow), *args, vectors)
+
+
 def layouts(resolution_ids, order_ids):
     pixels = jnp.arange(MAP * MAP, dtype=jnp.int32)
     row_of = pixels // MAP
@@ -885,13 +1300,15 @@
         30 * 2**20,
     )
 
-    proj_term_3 = mm(t_dh3, t_a2, "rd,rk->dk")
-    taps_term_2 = mm(t_cols, t_dh2, "rk,rn->kn")
-    proj_term_2 = mm(u, t_dh1, "rc,rn->cn")
-    proj_term_1 = mm(dh3, a2, "rd,rk->dk")
-    short_term = mm(x_all, dz_quarter, "rc,rd->cd")
-    taps_term_0 = mm(cols_all, dh2_all, "rk,rn->kn")
-    proj_term_0 = mm(x_all, dh1_all, "rc,rn->cn")
+    terms = {
+        "p3": mm(t_dh3, t_a2, "rd,rk->dk").astype(BF16),
+        "k2": mm(t_cols, t_dh2, "rk,rn->kn").astype(BF16),
+        "p2": mm(u, t_dh1, "rc,rn->cn").astype(BF16),
+        "p1": mm(dh3, a2, "rd,rk->dk").astype(BF16),
+        "k0": mm(cols_all, dh2_all, "rk,rn->kn").astype(BF16),
+        "p0": mm(x_all, dh1_all, "rc,rn->cn").astype(BF16),
+    }
+    short_term = mm(x_all, dz_quarter, "rc,rd->cd").astype(BF16)
 
     exchanged = lax.all_to_all(jnp.stack([y1, y1, dy1, y2]), "segment", 0, 0)
     exchanged = jnp.swapaxes(exchanged[:, :rows], 0, 1)
@@ -915,72 +1332,14 @@
             t_sums[0],
         ]
     )
-    vectors = pick(lax.psum(vectors, "segment").reshape(sections, 2, wide))
-
-    groups = [[d for d in range(count) if d % 2 == c] for c in range(2)]
-    depth = count // 2
-
-    def halved(term):
-        rows_half = term.shape[0] // 2
-        mine = lax.dynamic_slice_in_dim(term, core * rows_half, rows_half)
-        theirs = lax.dynamic_slice_in_dim(term, (1 - core) * rows_half, rows_half)
-        return (mine + core_swap(theirs.astype(BF16)).astype(F32)).astype(BF16)
-
-    def planar(terms):
-        part = jnp.concatenate(
-            [a.reshape(sections, a.shape[0] // sections, narrow) for a in terms], axis=1
-        )
-        part = lax.all_to_all(part, "segment", 0, 0)
-        return jnp.sum(part.astype(F32), axis=0).astype(BF16)
-
-    def over_z(joined):
-        shape = joined.shape
-        part = joined.reshape(depth, shape[0] // depth, narrow)
-        part = lax.psum_scatter(
-            part, "dp", scatter_dimension=0, tiled=False, axis_index_groups=groups
-        )
-        return lax.all_gather(part, "dp", axis=0, axis_index_groups=groups, tiled=True).reshape(shape)
-
-    hp, ht = wide // 8, 9 * narrow // 8
-    early = over_z(
-        planar([halved(proj_term_1), halved(proj_term_2), halved(taps_term_2), halved(proj_term_3)])
-    )
-    early_of = {
-        1: jnp.pad(early[:hp], ((0, ht), (0, 0))),
-        2: early[hp : 2 * hp + ht],
-        3: jnp.pad(early[2 * hp + ht :], ((0, ht), (0, 0))),
-    }
-    keep = jnp.stack([early_of[1], early_of[1], early_of[2], early_of[3]])
-    early_parts = lax.all_to_all(keep, "segment", 0, 0)
-
-    scattered = from_section(
-        jnp.concatenate(
-            [
-                halved(a).reshape(sections, a.shape[0] // 2 // sections, narrow)
-                for a in (proj_term_0, taps_term_0)
-            ],
-            axis=1,
-        ),
-        0,
-        section,
-    )
-    late = over_z(jnp.concatenate([scattered, halved(short_term)]))
-    late_parts = to_section_zero(late)
-
-    parts = jnp.where(first, late_parts[:, : hp + ht], early_parts)
-    other = core_swap(parts)
-    both = jnp.where(core == 0, jnp.stack([parts, other]), jnp.stack([other, parts]))
-    short_parts = late_parts[:, hp + ht :]
-    short_swap = core_swap(short_parts)
-    short_both = jnp.where(
-        core == 0, jnp.stack([short_parts, short_swap]), jnp.stack([short_swap, short_parts])
-    )
-    short_both = jnp.where(first, short_both, jnp.zeros_like(short_both))
-    proj_grad = both[:, :, :hp].reshape(wide, narrow).astype(F32)
-    spatial_grad = both[:, :, hp:].reshape(9 * narrow, narrow).astype(F32)
-    has_taps = (section % 2) == 0
-    spatial_grad = jnp.where(has_taps, spatial_grad, jnp.zeros_like(spatial_grad))
-    short_grad = jnp.swapaxes(short_both, 1, 2).reshape(wide, wide).astype(F32)
+    short_sum, proj_sum, taps_sum, vectors = sum_gradients(
+        sections, count, short_term, terms, vectors.reshape(sections, 2, wide)
+    )
+    proj_grad = proj_sum.reshape(wide, narrow).astype(F32)
+    spatial_grad = taps_sum.reshape(9 * narrow, narrow).astype(F32)
+    spatial_grad = jnp.where((section % 2) == 0, spatial_grad, jnp.zeros_like(spatial_grad))
+    short_grad = short_sum.reshape(wide, wide).astype(F32)
+    short_grad = jnp.where(first, short_grad, jnp.zeros_like(short_grad))
     return (
         maps[None],
         proj_grad[None],

time: 996 us -> 785 us (0.79)
  waiting for transfers between devices: 306 us -> 18.5 us
  Pallas kernels: 205 us -> 428 us
  local copies, waits for them, and re-layouts: 171 us -> 92.9 us
  other arithmetic: 106 us -> 50.6 us
  starting transfers between devices: 102 us -> 76.7 us
  matrix products: 28.1 us -> 38.7 us
    pallas_call x0 -> x1, Pallas kernels: none -> 223 us  [sum_gradients(): pl.pallas_call(functools.partial(gradient_kernel, sections, count), out_s...]
    ppermute x9 -> x6, waiting for transfers between devices: 123 us -> 8.36 us  [to_section_zero(): lax.ppermute(value, 'segment', [(t, 0)])]
    all_gather x2 -> x0, waiting for transfers between devices: 70 us -> none  [over_z(): lax.all_gather(part, 'dp', axis=0, axis_index_groups=groups, tiled=True)]
    convert_element_type x9 -> x2, local copies, waits for them, and re-layouts: 58 us -> 6.42 us  [the longest x1 3.92 us: body(): mm(x_all, dh1_all, 'rc,rn->cn').astype(BF16)]
    reduce_scatter x2 -> x0, waiting for transfers between devices: 40.6 us -> none  [over_z(): lax.psum_scatter(part, 'dp', scatter_dimension=0, tiled=False, axis_index...]
    psum x1 -> x0, waiting for transfers between devices: 38.4 us -> none  [body(): vectors = pick(lax.psum(vectors, 'segment').reshape(sections, 2, wide))]
    ppermute x15 -> x12, waiting for transfers between devices: 30.1 us -> 4.48 us  [from_section(): got = lax.ppermute(value[t], 'segment', [(source, t)])]
    convert_element_type x9 -> x1, other arithmetic: 26.7 us -> 2.6 us  [body(): proj_grad = proj_sum.reshape(wide, narrow).astype(F32)]
  transfers between devices with their start and end apart: 46 -> 24, of which waited for: 11 -> 3; matrix products, arithmetic and copies ran while one was open for 27% -> 19% of each run, Pallas kernels for 13% -> 45%
where the time goes in v3:
time: 785 us; the launch traced here: 775 us
  Pallas kernels  428 us (55%)
  local copies, waits for them, and re-layouts  92.9 us (12%)
  starting transfers between devices  76.7 us (10%)
  blocking collectives  54.9 us (7%)
  other arithmetic  50.6 us (6%)
  matrix products  38.7 us (5%)
  waiting for transfers between devices  18.5 us (2%)
  between operations  14.9 us (2%)
    pallas_call x1, Pallas kernels, sum_gradients(): pl.pallas_call(functools.partial(gradient_kernel, sections, count), out_s...  223 us
    pallas_call x7, Pallas kernels, kernel_call(): pl.pallas_call(kernel, out_shape=outs, in_specs=[pl.BlockSpec(memory_spac...  205 us
    all_gather x1, blocking collectives, body(): lax.all_gather(jnp.concatenate([bn_gain[0], bn_bias[0]]), 'segment', axis=0)  54.9 us
    dot_general x7, matrix products, mm(): return jnp.einsum(dims, a, b, preferred_element_type=F32)  38.7 us
    ppermute x12, starting transfers between devices, from_section(): got = lax.ppermute(value[t], 'segment', [(source, t)])  29.7 us
    ppermute x6, starting transfers between devices, to_section_zero(): lax.ppermute(value, 'segment', [(t, 0)])  18.3 us
    all_to_all x1, starting transfers between devices, body(): residual = lax.all_to_all(res_quarter, 'segment', 0, 0, tiled=True)  17.3 us
  transfers between devices with their start and end apart: 24, of which 3 were waited for; matrix products, arithmetic and copies ran while one was open for 19% of the time, Pallas kernels for 45%

profile of v3, /device:TPU:0, one launch (start us, length us, event | category | flops | bytes accessed | tf_op | source)
XLA Modules:
  0.0 775.3 jit_solution(11227848928449306038)
XLA Ops:
  7.2 1.2 dynamic-slice_bitcast_fusion.4
  8.5 1.3 collective-permute-start.13
  12.1 4.5 collective-permute-done.13
  19.4 1.3 collective-permute-start.5
  21.5 2.5 dynamic-slice_bitcast_fusion
  24.0 1.8 fusion.35
  26.9 9.2 %collective-permute-start.9 = (bf16[1024,512]{1,0:T(8,128)(2,1)}, bf16[1024,512]{1,0:T(8,128)(2,1)S(1)}, u32[]{:S(2)}, u32[]{:S(2)}) collective-permute-start(bf16[1024,512]{1,0:T(8,128)(2,1)} %get-tuple-element.75), channel_id=1, source_target_pairs={{0,8},{1,9},{2,10},{3,11},{4,12},{5,13},{6,14},{7,15}} | collective-permute-start | bytes 3145736 | tf_op jit(solution)/shard_map/ppermute | solution.py:1074
  36.2 2.3 collective-permute-start.8
  38.4 2.3 collective-permute-start.7
  42.7 54.9 %all-gather = f32[16384]{0:T(1024)S(1)} all-gather(f32[4096]{0:T(1024)S(1)} %pad_maximum_fusion.6), channel_id=2, replica_groups=mesh['segment'=4,'dp'=8] {'segment'}, dimensions={0}, use_global_device_ids=true | all-gather | bytes 81920 | tf_op jit(solution)/shard_map/all_gather | solution.py:1141
  101.9 8.7 %reshape.694.x = bf16[1176,2048]{1,0:T(8,128)(2,1)} reshape(bf16[6,49,4,2048]{3,2,1,0:T(4,128)(2,1)} %bitcast.146) | data formatting | bytes 9633792 | tf_op jit(solution)/shard_map/reshape | solution.py:1166
  111.2 45.1 %shard_map.154 = (bf16[4,304,512]{2,1,0:T(8,128)(2,1)}, bf16[1176,4608]{1,0:T(8,128)(2,1)}, f32[1176,512]{1,0:T(8,128)}, f32[1176,512]{1,0:T(8,128)}, f32[16,512]{1,0:T(8,128)}, /*index=5*/f32[8,128]{1,0:T(8,128)}) custom-call(bf16[1176,2048]{1,0:T(8,128)(2,1)} %reshape.694.x, bf16[2048,512]{1,0:T(8,128)(2,1)} %bitcast.151, bf16[4608,512]{1,0:T(8,128)(2,1)} %bitcast.167, ...), custom_call_target="tpu_custom_call" | custom-call | flops 8015314944 | bytes 41943040 | tf_op jit(solution)/shard_map/pallas_call | solution.py:83
  157.8 2.1 slice_bitcast_fusion.3
  159.9 1.8 collective-permute-start.3
  161.7 5.5 collective-permute-start.2
  167.2 1.4 fusion.5.wa
  169.3 6.6 constant_dynamic-slice_fusion.9
  175.9 2.0 collective-permute-start.1
  178.0 2.0 collective-permute-start
  182.4 7.2 shard_map.155
  189.7 17.3 %all-to-all-start = ((bf16[4,304,512]{2,1,0:T(8,128)(2,1)}), bf16[4,304,512]{2,1,0:T(8,128)(2,1)S(1)}, u32[]{:S(2)}, u32[]{:S(2)}) async-start(bf16[4,304,512]{2,1,0:T(8,128)(2,1)} %shard_map.155), calls=%async_computation | async-start | bytes 2490368 | tf_op jit(solution)/shard_map/all_to_all | solution.py:1199
  209.1 2.4 copy.111
  214.0 1.8 fusion.9.a2
  215.8 1.9 maximum_select_fusion.w1
  217.7 5.6 all-to-all-done.res
  224.4 14.7 %shard_map.156 = (bf16[304,2048]{1,0:T(8,128)(2,1)}, bf16[304,2048]{1,0:T(8,128)(2,1)}, f32[304,2048]{1,0:T(8,128)}, f32[2,2048]{1,0:T(2,128)}) custom-call(bf16[304,512]{1,0:T(8,128)(2,1)} %fusion.9.a2, bf16[2048,512]{1,0:T(8,128)(2,1)} %maximum_select_fusion.w1, bf16[4,304,512]{2,1,0:T(8,128)(2,1)} %copy-done.1, f32[304,1]{1,0:T(8,128)} %pad.15.pack, ...), custom_call_target="tpu_custom_call" | custom-call | flops 1016070144 | bytes 10485760 | tf_op jit(solution)/shard_map/pallas_call | solution.py:83
  239.2 4.6 fusion.34
  243.8 2.6 slice_bitcast_fusion.1
  246.4 2.5 copy.94
  248.9 63.5 %shard_map.157 = (bf16[304,2048]{1,0:T(8,128)(2,1)}, bf16[304,512]{1,0:T(8,128)(2,1)}, bf16[304,4608]{1,0:T(8,128)(2,1)}, bf16[304,2048]{1,0:T(8,128)(2,1)}, bf1...) custom-call(bf16[304,2048]{1,0:T(8,128)(2,1)} %get-tuple-element.37.u, ...), custom_call_target="tpu_custom_call" | custom-call | flops 5419040768 | bytes 31457280 | tf_op jit(solution)/shard_map/pallas_call | solution.py:83
  314.3 14.1 %shard_map.158 = (bf16[304,2048]{1,0:T(8,128)(2,1)}, bf16[304,2048]{1,0:T(8,128)(2,1)}, bf16[304,512]{1,0:T(8,128)(2,1)}, f32[2,2048]{1,0:T(2,128)}) custom-call(bf16[304,2048]{1,0:T(8,128)(2,1)} %get-tuple-element.38.dy, bf16[4,304,512]{2,1,0:T(8,128)(2,1)} %copy-done.1, f32[304,2048]{1,0:T(8,128)} %get-tuple-element.39.h3n, f32[304,1]{1,0:T(8,128)} %pad.15.pack, ...), custom_call_target="tpu_custom_call" | custom-call | flops 637534208 | bytes 12582912 | tf_op jit(solution)/shard_map/pallas_call | solution.py:83
  328.4 1.4 collective-permute-start.16
  329.8 1.3 collective-permute-start.15
  331.1 1.3 collective-permute-start.14
  332.4 1.3 collective-permute-start.19
  333.7 11.7 %collective-permute-start.18 = (bf16[304,2048]{1,0:T(8,128)(2,1)}, bf16[304,2048]{1,0:T(8,128)(2,1)}, u32[]{:S(2)}, u32[]{:S(2)}) collective-permute-start(bf16[304,2048]{1,0:T(8,128)(2,1)} %get-tuple-element.46), channel_id=1, source_target_pairs={{16,0},{17,1},{18,2},{19,3},{20,4},{21,5},{22,6},{23,7}} | collective-permute-start | bytes 3735560 | tf_op jit(solution)/shard_map/ppermute | solution.py:1081
  346.3 3.9 convolution_convert_fusion.3
  351.4 6.0 all-to-all-start.2
  357.4 4.1 convolution_convert_fusion.4
  361.5 4.3 convolution_convert_fusion.1
  365.8 2.9 pad_maximum_fusion
  368.7 2.6 convolution_convert_fusion.5
  371.4 1.3 collective-permute-start.17
  372.6 8.3 %collective-permute-done.15 = bf16[304,512]{1,0:T(8,128)(2,1)S(1)} collective-permute-done((bf16[304,512]{1,0:T(8,128)(2,1)}, bf16[304,512]{1,0:T(8,128)(2,1)S(1)}, u32[]{:S(2)}, u32[]{:S(2)}) %collective-permute-start.15) | collective-permute-done | bytes 311328 | tf_op jit(solution)/shard_map/ppermute | solution.py:1081
  381.0 1.2 pad_maximum_fusion.4.da2
  382.2 38.0 %shard_map.159 = (bf16[1176,512]{1,0:T(8,128)(2,1)}, bf16[1176,512]{1,0:T(8,128)(2,1)}, f32[16,512]{1,0:T(8,128)}) custom-call(bf16[4,304,512]{2,1,0:T(8,128)(2,1)} %pad_maximum_fusion.4.da2, bf16[4608,512]{1,0:T(8,128)(2,1)} %bitcast.168, f32[4,512]{1,0:T(4,128)} %pad_maximum_fusion.9.gb, f32[1176,16]{1,0:T(8,128)} %copy.91.pack, ...), custom_call_target="tpu_custom_call" | custom-call | flops 5549064192 | bytes 20971520 | tf_op jit(solution)/shard_map/pallas_call | solution.py:83
  421.8 7.0 fusion.3
  428.8 3.9 copy.104
  432.7 11.1 %convolution_convert_fusion = bf16[4608,512]{1,0:T(8,128)(2,1)} fusion(bf16[1176,4608]{1,0:T(8,128)(2,1)} %get-tuple-element.55, bf16[1176,512]{1,0:T(8,128)(2,1)} %get-tuple-element.56), kind=kOutput, calls=%fused_computation.2 | convolution fusion | flops 5551423488 | bytes 16760832 | tf_op jit(solution)/shard_map/rk,rn->kn/dot_general | solution.py:1062
  443.8 5.0 all-to-all-start.1
  449.6 1.3 reshape.707
  450.9 5.7 fusion.2
  456.5 2.5 copy.103
  459.0 223.2 %shard_map.161 = (bf16[2,1024,2048]{2,1,0:T(8,128)(2,1)}, bf16[2,4,4,64,512]{4,3,2,1,0:T(8,128)(2,1)}, bf16[2,4,4,144,512]{4,3,2,1,0:T(8,128)(2,1)}, f32[2,2048]{1,0:T(2,128)}) custom-call(bf16[2,1024,512]{2,1,0:T(8,128)(2,1)} %bitcast.138, bf16[2,4,4,144,512]{4,3,2,1,0:T(8,128)(2,1)} %bitcast.148, bf16[2,4,4,64,512]{4,3,2,1,0:T(8,128)(2,1)} %bitcast.155, ...), custom_call_target="tpu_custom_call" | custom-call | bytes 419430400 | tf_op jit(solution)/shard_map/pallas_call | solution.py:1012
  682.3 7.5 convert_select_fusion.1
  690.5 2.6 convert.5
  693.1 12.0 %convert_select_fusion = f32[2,1024,2048]{2,1,0:T(8,128)} fusion(bf16[2,1024,2048]{2,1,0:T(8,128)(2,1)} %get-tuple-element.62, pred[]{:T(512)S(6)} %eq.79), kind=kLoop, calls=%fused_computation | loop fusion | flops 8388608 | bytes 25165824 | tf_op jit(solution)/shard_map/jit(_where)/select_n | solution.py:1342
  705.1 2.3 fusion.1
  707.3 5.9 copy.98
  713.3 8.6 %reshape.702.dz = bf16[1176,2048]{1,0:T(8,128)(2,1)} reshape(bf16[294,4,2048]{2,1,0:T(4,128)(2,1)} %copy.98) | data formatting | bytes 9633792 | tf_op jit(solution)/shard_map/reshape | solution.py:1286
  721.9 22.2 %shard_map.160 = bf16[1176,2048]{1,0:T(8,128)(2,1)} custom-call(bf16[1176,512]{1,0:T(8,128)(2,1)} %get-tuple-element.45.dh1, bf16[1176,2048]{1,0:T(8,128)(2,1)} %reshape.702.dz, bf16[2048,512]{1,0:T(8,128)(2,1)} %bitcast.152, bf16[2048,2048]{1,0:T(8,128)(2,1)} %bitcast.157), custom_call_target="tpu_custom_call" | custom-call | flops 12331253760 | bytes 31457280 | tf_op jit(solution)/shard_map/pallas_call | solution.py:83
  744.1 9.1 %reshape.703 = bf16[294,4,2048]{2,1,0:T(4,128)(2,1)} reshape(bf16[1176,2048]{1,0:T(8,128)(2,1)} %shard_map.160) | data formatting | bytes 9633792 | tf_op jit(solution)/shard_map/reshape | solution.py:1315
  753.2 9.2 %fusion = bf16[294,4,2048]{2,0,1:T(8,128)(2,1)S(1)} fusion(bf16[4,304,2048]{2,1,0:T(8,128)(2,1)} %all-to-all-done.1, bf16[294,4,2048]{2,1,0:T(4,128)(2,1)} %reshape.703, pred[]{:T(512)S(6)} %eq.79), kind=kLoop, calls=%fused_computation.6 | loop fusion | flops 2408448 | bytes 14450689 | tf_op jit(solution)/shard_map/jit(_where)/select_n | solution.py:1315
  762.3 5.9 copy.100
  (166 shorter events, 31.0 us)
Async XLA Ops:
  7.2 11.2 %copy-start.4 = (bf16[1,2048,512]{2,1,0:T(8,128)(2,1)S(1)}, bf16[1,2048,512]{2,1,0:T(8,128)(2,1)}, u32[]{:S(2)}) copy-start(bf16[1,2048,512]{2,1,0:T(8,128)(2,1)} %param.15) | copy-start | bytes 6291460
  7.2 232.0 %all-gather.3.cloned.1.call-start = ((), (), s32[]{:S(2)}) async-start(), calls=%async_computation.3 | async-start | bytes 13516800 | tf_op jit(solution)/shard_map/all_gather | solution.py:1135
  8.5 8.1 %collective-permute-start.13 = (bf16[144,512]{1,0:T(8,128)(2,1)S(1)}, bf16[144,512]{1,0:T(8,128)(2,1)S(1)}, u32[]{:S(2)}, u32[]{:S(2)}) collective-permute-start(bf16[144,512]{1,0:T(8,128)(2,1)S(1)} %get-tuple-element.72), channel_id=1, source_target_pairs={{16,0},{17,1},{18,2},{19,3},{20,4},{21,5},{22,6},{23,7}} | collective-permute-start | bytes 442376 | tf_op jit(solution)/shard_map/ppermute | solution.py:1074
  9.8 6.8 collective-permute-start.12
  10.4 6.1 collective-permute-start.11
  19.4 156.5 %collective-permute-start.5 = (bf16[1024,512]{1,0:T(8,128)(2,1)}, bf16[1024,512]{1,0:T(8,128)(2,1)S(1)}, u32[]{:S(2)}, u32[]{:S(2)}) collective-permute-start(bf16[1024,512]{1,0:T(8,128)(2,1)} %dynamic-slice_bitcast_fusion.1), channel_id=1, source_target_pairs={{8,0},{9,1},{10,2},{11,3},{12,4},{13,5},{14,6},{15,7}} | collective-permute-start | bytes 3145736 | tf_op jit(solution)/shard_map/ppermute | solution.py:1074
  20.7 157.2 %collective-permute-start.4 = (bf16[1024,512]{1,0:T(8,128)(2,1)}, bf16[1024,512]{1,0:T(8,128)(2,1)S(1)}, u32[]{:S(2)}, u32[]{:S(2)}) collective-permute-start(bf16[1024,512]{1,0:T(8,128)(2,1)} %dynamic-slice_bitcast_fusion.1), channel_id=1, source_target_pairs={{8,16},{9,17},{10,18},{11,19},{12,20},{13,21},{14,22},{15,23}} | collective-permute-start | bytes 3145736 | tf_op jit(solution)/shard_map/ppermute | solution.py:1074
  24.0 3.0 copy-start
  24.0 16.8 %copy-start.18 = (s32[4,6]{1,0:T(4,128)S(1)}, s32[4,6]{1,0:T(4,128)}, u32[]{:S(2)}) copy-start(s32[4,6]{1,0:T(4,128)} %param.13) | copy-start | bytes 292
  24.0 17.0 %copy-start.17 = (s32[4,6,9]{2,0,1:T(4,128)S(1)}, s32[4,6,9]{2,0,1:T(4,128)}, u32[]{:S(2)}) copy-start(s32[4,6,9]{2,0,1:T(4,128)} %param.14) | copy-start | bytes 2596
  24.0 18.7 %copy-start.14 = (f32[1,2048]{1,0:T(1,128)S(1)}, f32[1,2048]{1,0:T(1,128)}, u32[]{:S(2)}) copy-start(f32[1,2048]{1,0:T(1,128)} %param.18) | copy-start | bytes 24580
  24.0 18.7 %copy-start.15 = (f32[1,2048]{1,0:T(1,128)S(1)}, f32[1,2048]{1,0:T(1,128)}, u32[]{:S(2)}) copy-start(f32[1,2048]{1,0:T(1,128)} %param.19) | copy-start | bytes 24580
  26.9 133.0 %collective-permute-start.9 = (bf16[1024,512]{1,0:T(8,128)(2,1)}, bf16[1024,512]{1,0:T(8,128)(2,1)S(1)}, u32[]{:S(2)}, u32[]{:S(2)}) collective-permute-start(bf16[1024,512]{1,0:T(8,128)(2,1)} %get-tuple-element.75), channel_id=1, source_target_pairs={{0,8},{1,9},{2,10},{3,11},{4,12},{5,13},{6,14},{7,15}} | collective-permute-start | bytes 3145736 | tf_op jit(solution)/shard_map/ppermute | solution.py:1074
  36.2 125.5 %collective-permute-start.8 = (bf16[1024,512]{1,0:T(8,128)(2,1)}, bf16[1024,512]{1,0:T(8,128)(2,1)}, u32[]{:S(2)}, u32[]{:S(2)}) collective-permute-start(bf16[1024,512]{1,0:T(8,128)(2,1)} %get-tuple-element.76), channel_id=1, source_target_pairs={{0,16},{1,17},{2,18},{3,19},{4,20},{5,21},{6,22},{7,23}} | collective-permute-start | bytes 3145736 | tf_op jit(solution)/shard_map/ppermute | solution.py:1074
  38.4 128.7 %collective-permute-start.7 = (bf16[1024,512]{1,0:T(8,128)(2,1)}, bf16[1024,512]{1,0:T(8,128)(2,1)}, u32[]{:S(2)}, u32[]{:S(2)}) collective-permute-start(bf16[1024,512]{1,0:T(8,128)(2,1)} %get-tuple-element.77), channel_id=1, source_target_pairs={{0,24},{1,25},{2,26},{3,27},{4,28},{5,29},{6,30},{7,31}} | collective-permute-start | bytes 3145736 | tf_op jit(solution)/shard_map/ppermute | solution.py:1074
  101.9 9.3 %copy-start.12 = (f32[4,4096]{1,0:T(4,128)S(1)}, f32[4,4096]{1,0:T(4,128)}, u32[]{:S(2)}) copy-start(f32[4,4096]{1,0:T(4,128)} %reshape.723) | copy-start | bytes 196612
  159.9 8.8 %copy-start.13 = (f32[304,15]{0,1:T(8,128)S(1)}, f32[304,15]{0,1:T(8,128)}, u32[]{:S(2)}) copy-start(f32[304,15]{0,1:T(8,128)} %constant.148.clone) | copy-start | bytes 54724
  159.9 20.1 %collective-permute-start.3 = (bf16[1024,512]{1,0:T(8,128)(2,1)}, bf16[1024,512]{1,0:T(8,128)(2,1)}, u32[]{:S(2)}, u32[]{:S(2)}) collective-permute-start(bf16[1024,512]{1,0:T(8,128)(2,1)} %dynamic-slice_bitcast_fusion.1), channel_id=1, source_target_pairs={{8,24},{9,25},{10,26},{11,27},{12,28},{13,29},{14,30},{15,31}} | collective-permute-start | bytes 3145736 | tf_op jit(solution)/shard_map/ppermute | solution.py:1074
  161.7 52.4 %collective-permute-start.2 = (bf16[304,512]{1,0:T(8,128)(2,1)}, bf16[304,512]{1,0:T(8,128)(2,1)}, u32[]{:S(2)}, u32[]{:S(2)}) collective-permute-start(bf16[304,512]{1,0:T(8,128)(2,1)} %get-tuple-element.78), channel_id=1, source_target_pairs={{0,8},{1,9},{2,10},{3,11},{4,12},{5,13},{6,14},{7,15}} | collective-permute-start | bytes 933896 | tf_op jit(solution)/shard_map/ppermute | solution.py:1074
  168.6 12.0 %copy-start.10 = (bf16[1024,512]{1,0:T(8,128)(2,1)}, bf16[1024,512]{1,0:T(8,128)(2,1)S(1)}, u32[]{:S(2)}) copy-start(bf16[1024,512]{1,0:T(8,128)(2,1)S(1)} %fusion.5.wa) | copy-start | bytes 3145732
  168.6 11.4 %copy-start.5 = (bf16[1,2048,512]{2,1,0:T(8,128)(2,1)S(1)}, bf16[1,2048,512]{2,1,0:T(8,128)(2,1)}, u32[]{:S(2)}) copy-start(bf16[1,2048,512]{2,1,0:T(8,128)(2,1)} %param.15) | copy-start | bytes 6291460
  168.6 12.8 %collective-permute-start.10 = (bf16[1024,512]{1,0:T(8,128)(2,1)S(1)}, bf16[1024,512]{1,0:T(8,128)(2,1)S(1)}, u32[]{:S(2)}, u32[]{:S(2)}) collective-permute-start(bf16[1024,512]{1,0:T(8,128)(2,1)S(1)} %fusion.5.wa), channel_id=1, source_target_pairs={{0,1},{1,0},{2,3},{3,2},{4,5},{5,4},{6,7},{7,6},{8,9},{9,8},{10,11... | collective-permute-start | bytes 3145736 | tf_op jit(solution)/shard_map/ppermute | solution.py:1067
  175.9 38.1 %collective-permute-start.1 = (bf16[304,512]{1,0:T(8,128)(2,1)}, bf16[304,512]{1,0:T(8,128)(2,1)}, u32[]{:S(2)}, u32[]{:S(2)}) collective-permute-start(bf16[304,512]{1,0:T(8,128)(2,1)} %get-tuple-element.79), channel_id=1, source_target_pairs={{0,16},{1,17},{2,18},{3,19},{4,20},{5,21},{6,22},{7,23}} | collective-permute-start | bytes 933896 | tf_op jit(solution)/shard_map/ppermute | solution.py:1074
  178.0 36.1 %collective-permute-start = (bf16[304,512]{1,0:T(8,128)(2,1)}, bf16[304,512]{1,0:T(8,128)(2,1)}, u32[]{:S(2)}, u32[]{:S(2)}) collective-permute-start(bf16[304,512]{1,0:T(8,128)(2,1)} %get-tuple-element.80), channel_id=1, source_target_pairs={{0,24},{1,25},{2,26},{3,27},{4,28},{5,29},{6,30},{7,31}} | collective-permute-start | bytes 933896 | tf_op jit(solution)/shard_map/ppermute | solution.py:1074
  180.6 35.3 %collective-permute-start.6 = (bf16[1024,512]{1,0:T(8,128)(2,1)S(1)}, bf16[1024,512]{1,0:T(8,128)(2,1)S(1)}, u32[]{:S(2)}, u32[]{:S(2)}) collective-permute-start(bf16[1024,512]{1,0:T(8,128)(2,1)S(1)} %select_select_fusion), channel_id=1, source_target_pairs={{0,1},{1,0},{2,3},{3,2},{4,5},{5,4},{6,7},{7,6},{8,9},{9,8},{10,11... | collective-permute-start | bytes 3145736 | tf_op jit(solution)/shard_map/ppermute | solution.py:1067
  181.4 1.0 copy-start.19
  189.7 33.7 %all-to-all-start = ((bf16[4,304,512]{2,1,0:T(8,128)(2,1)}), bf16[4,304,512]{2,1,0:T(8,128)(2,1)S(1)}, u32[]{:S(2)}, u32[]{:S(2)}) async-start(bf16[4,304,512]{2,1,0:T(8,128)(2,1)} %shard_map.155), calls=%async_computation | async-start | bytes 2490368 | tf_op jit(solution)/shard_map/all_to_all | solution.py:1199
  223.4 1.0 copy-start.1
  314.3 32.0 %copy-start.7 = (bf16[304,512]{1,0:T(8,128)(2,1)S(1)}, bf16[304,512]{1,0:T(8,128)(2,1)}, u32[]{:S(2)}) copy-start(bf16[304,512]{1,0:T(8,128)(2,1)} %fusion.9.a2) | copy-start | bytes 933892
  328.4 21.8 %copy-start.2 = (bf16[304,2048]{1,0:T(8,128)(2,1)S(1)}, bf16[304,2048]{1,0:T(8,128)(2,1)}, u32[]{:S(2)}) copy-start(bf16[304,2048]{1,0:T(8,128)(2,1)} %get-tuple-element.46) | copy-start | bytes 3735556
  328.4 42.9 %collective-permute-start.16 = (bf16[304,512]{1,0:T(8,128)(2,1)}, bf16[304,512]{1,0:T(8,128)(2,1)S(1)}, u32[]{:S(2)}, u32[]{:S(2)}) collective-permute-start(bf16[304,512]{1,0:T(8,128)(2,1)} %get-tuple-element.41), channel_id=1, source_target_pairs={{24,0},{25,1},{26,2},{27,3},{28,4},{29,5},{30,6},{31,7}} | collective-permute-start | bytes 933896 | tf_op jit(solution)/shard_map/ppermute | solution.py:1081
  329.8 51.1 %collective-permute-start.15 = (bf16[304,512]{1,0:T(8,128)(2,1)}, bf16[304,512]{1,0:T(8,128)(2,1)S(1)}, u32[]{:S(2)}, u32[]{:S(2)}) collective-permute-start(bf16[304,512]{1,0:T(8,128)(2,1)} %get-tuple-element.41), channel_id=1, source_target_pairs={{16,0},{17,1},{18,2},{19,3},{20,4},{21,5},{22,6},{23,7}} | collective-permute-start | bytes 933896 | tf_op jit(solution)/shard_map/ppermute | solution.py:1081
  331.1 49.8 %collective-permute-start.14 = (bf16[304,512]{1,0:T(8,128)(2,1)}, bf16[304,512]{1,0:T(8,128)(2,1)S(1)}, u32[]{:S(2)}, u32[]{:S(2)}) collective-permute-start(bf16[304,512]{1,0:T(8,128)(2,1)} %get-tuple-element.41), channel_id=1, source_target_pairs={{8,0},{9,1},{10,2},{11,3},{12,4},{13,5},{14,6},{15,7}} | collective-permute-start | bytes 933896 | tf_op jit(solution)/shard_map/ppermute | solution.py:1081
  332.4 372.6 %collective-permute-start.19 = (bf16[304,2048]{1,0:T(8,128)(2,1)}, bf16[304,2048]{1,0:T(8,128)(2,1)}, u32[]{:S(2)}, u32[]{:S(2)}) collective-permute-start(bf16[304,2048]{1,0:T(8,128)(2,1)} %get-tuple-element.46), channel_id=1, source_target_pairs={{24,0},{25,1},{26,2},{27,3},{28,4},{29,5},{30,6},{31,7}} | collective-permute-start | bytes 3735560 | tf_op jit(solution)/shard_map/ppermute | solution.py:1081
  333.7 371.3 %collective-permute-start.18 = (bf16[304,2048]{1,0:T(8,128)(2,1)}, bf16[304,2048]{1,0:T(8,128)(2,1)}, u32[]{:S(2)}, u32[]{:S(2)}) collective-permute-start(bf16[304,2048]{1,0:T(8,128)(2,1)} %get-tuple-element.46), channel_id=1, source_target_pairs={{16,0},{17,1},{18,2},{19,3},{20,4},{21,5},{22,6},{23,7}} | collective-permute-start | bytes 3735560 | tf_op jit(solution)/shard_map/ppermute | solution.py:1081
  351.4 92.4 %all-to-all-start.2 = ((bf16[304,4,512]{2,0,1:T(8,128)(2,1)}), bf16[304,4,512]{2,0,1:T(8,128)(2,1)S(1)}, u32[]{:S(2)}, u32[]{:S(2)}) async-start(bf16[304,4,512]{2,0,1:T(8,128)(2,1)} %bitcast.133), calls=%async_computation.2 | async-start | bytes 2490368 | tf_op jit(solution)/shard_map/all_to_all | solution.py:1289
  357.4 4.1 copy-start.22
  357.4 4.1 copy-start.23
  361.5 4.3 copy-start.3
  361.5 4.3 copy-start.8
  361.5 4.3 copy-start.9
  365.8 2.9 copy-start.20
  365.8 2.9 copy-start.21
  368.7 12.3 %copy-start.11 = (bf16[304,512]{1,0:T(8,128)(2,1)S(1)}, bf16[304,512]{1,0:T(8,128)(2,1)}, u32[]{:S(2)}) copy-start(bf16[304,512]{1,0:T(8,128)(2,1)} %get-tuple-element.41) | copy-start | bytes 933892
  371.4 333.7 %collective-permute-start.17 = (bf16[304,2048]{1,0:T(8,128)(2,1)S(1)}, bf16[304,2048]{1,0:T(8,128)(2,1)}, u32[]{:S(2)}, u32[]{:S(2)}) collective-permute-start(bf16[304,2048]{1,0:T(8,128)(2,1)S(1)} %copy-done.2), channel_id=1, source_target_pairs={{8,0},{9,1},{10,2},{11,3},{12,4},{13,5},{14,6},{15,7}} | collective-permute-start | bytes 3735560 | tf_op jit(solution)/shard_map/ppermute | solution.py:1081
  443.8 309.4 %all-to-all-start.1 = ((bf16[4,304,2048]{2,1,0:T(8,128)(2,1)}), bf16[4,304,2048]{2,1,0:T(8,128)(2,1)}, u32[]{:S(2)}, u32[]{:S(2)}) async-start(bf16[4,304,2048]{2,1,0:T(8,128)(2,1)} %pad_maximum_fusion), calls=%async_computation.1 | async-start | bytes 9961472 | tf_op jit(solution)/shard_map/all_to_all | solution.py:1313
  682.3 7.6 copy-start.16
  682.3 8.2 %copy-start.6 = (bf16[2,4,4,64,512]{4,3,2,1,0:T(8,128)(2,1)S(1)}, bf16[2,4,4,64,512]{4,3,2,1,0:T(8,128)(2,1)}, u32[]{:S(2)}) copy-start(bf16[2,4,4,64,512]{4,3,2,1,0:T(8,128)(2,1)} %get-tuple-element.60) | copy-start | bytes 6291460
Sparse Core Ops, SparseCore 0:
  18.5 125.8 all-gather.2

commit v4 on v3

--- a/solution.py
+++ b/solution.py
@@ -18,7 +18,7 @@
 TILE = 256
 
 
-def greet(count):
+def greet(count, sections=0):
     segment, me = lax.axis_index("segment"), lax.axis_index("dp")
     barrier = pltpu.get_barrier_semaphore()
 
@@ -29,10 +29,14 @@
         return carry
 
     lax.fori_loop(1, count, one, 0)
-
-
-def greeted(count):
-    pl.semaphore_wait(pltpu.get_barrier_semaphore(), count - 1)
+    for k in range(1, sections):
+        pl.semaphore_signal(
+            barrier, inc=1, device_id=(jnp.bitwise_xor(segment, k), me), device_id_type=MESH
+        )
+
+
+def greeted(count, sections=1):
+    pl.semaphore_wait(pltpu.get_barrier_semaphore(), count - 1 + sections - 1)
 
 
 def exchange(count, slots, send_sem, recv_sem):
@@ -65,6 +69,25 @@
     return total
 
 
+def mesh_copy(src, dst, send_sem, recv_sem, segment, place):
+    return pltpu.make_async_remote_copy(
+        src_ref=src,
+        dst_ref=dst,
+        send_sem=send_sem,
+        recv_sem=recv_sem,
+        device_id=(segment, place),
+        device_id_type=MESH,
+    )
+
+
+def loop(low, high, body):
+    def one(k, carry):
+        body(k)
+        return carry
+
+    lax.fori_loop(low, high, one, 0)
+
+
 def sync_scratch(count, shapes):
     out = []
     for shape in shapes:
@@ -76,15 +99,19 @@
     return out
 
 
-def kernel_call(kernel, outs, args, scratch, ident, flops, moved, spaces=None):
+def kernel_call(kernel, outs, args, scratch, ident, flops, moved, far_in=(), far_out=()):
     params = dict(has_side_effects=True, vmem_limit_bytes=VMEM_BYTES)
     if ident is not None:
         params["collective_id"] = ident
     return pl.pallas_call(
         kernel,
         out_shape=outs,
-        in_specs=[pl.BlockSpec(memory_space=pltpu.VMEM) for _ in args],
-        out_specs=[pl.BlockSpec(memory_space=pltpu.VMEM) for _ in outs],
+        in_specs=[
+            pl.BlockSpec(memory_space=pl.ANY if i in far_in else pltpu.VMEM) for i in range(len(args))
+        ],
+        out_specs=[
+            pl.BlockSpec(memory_space=pl.ANY if i in far_out else pltpu.VMEM) for i in range(len(outs))
+        ],
         scratch_shapes=scratch,
         compiler_params=pltpu.CompilerParams(**params),
         cost_estimate=pl.CostEstimate(flops=flops, bytes_accessed=moved, transcendentals=0),
@@ -139,13 +166,12 @@
     return jnp.concatenate([values, values], axis=0)[None]
 
 
-def first_kernel(
-    count, x, w, k, gb, pack, tiles, a2_out, cols, h1n, h2n, stats_out, count_out, act, *sync
+def first_part(
+    count, ready, x, w, k, gb, pack, tiles, a2_out, cols, h1n, h2n, stats_out, count_out, act, *sync
 ):
     s1, send1, recv1, s2, send2, recv2 = sync
     rows, narrow = h1n.shape
     me = lax.axis_index("dp")
-    greet(count)
     full = act.shape[1]
 
     def tile8(v):
@@ -161,7 +187,7 @@
     over(narrow, TILE, project)
     s1[me, 0:4, narrow:] = jnp.broadcast_to(by_batch(pack[:, 0:1]), (4, 128))
     s1[me, 4:8, narrow:] = jnp.broadcast_to(by_batch(tiles[:, 0:1]), (4, 128))
-    greeted(count)
+    ready()
     total = exchange(count, s1, send1, recv1)
     counts = total[:, narrow:]
     count_out[...] = counts
@@ -221,16 +247,12 @@
         lax.fori_loop(0, narrow // 128, pick, 0)
 
 
-def residual_kernel(x, wa, wb, out, hold):
-    rows, depth = x.shape[0], wa.shape[0]
-    full, quarter = hold.shape[1], out.shape[2]
-    core = lax.rem(lax.axis_index("dp"), 2)
-    first = pl.ds(pl.multiple_of(core * depth, depth), depth)
-    second = pl.ds(pl.multiple_of((1 - core) * depth, depth), depth)
+def residual_part(x, w, out, hold):
+    rows, full, quarter = x.shape[0], hold.shape[1], out.shape[2]
     hold[:, rows:, :] = jnp.zeros((quarter // 128, full - rows, 128), F32)
 
     def body(at):
-        value = dot(x[:, first], wa[:, at]) + dot(x[:, second], wb[:, at])
+        value = dot(x[...], w[:, at])
         for part in range(TILE // 128):
             hold[lane(at) + part, 0:rows, :] = value[:, part * 128 : part * 128 + 128]
 
@@ -259,23 +281,21 @@
     )
 
 
-def second_kernel(
-    count, a2, w1, res, pack, gb, valid_in, moves, y_out, u_out, h3n, stats_out, s1, send1, recv1
+def second_part(
+    count, before, a2, w1, res, mask, gb, valid, moves, y_out, u_out, h3n, stats_out, s1, send1, recv1
 ):
     wide = h3n.shape[1]
     quarter = res.shape[2]
     me = lax.axis_index("dp")
-    greet(count)
 
     def project(at):
         h = dot_t(a2[...], w1[at, :])
         h3n[:, at] = h
-        norm_sums(s1, me, at, pack[:, 0:1] * h, h)
+        norm_sums(s1, me, at, mask[:, 0:1] * h, h)
 
     over(wide, TILE, project)
-    greeted(count)
-    valid = valid_in[0:1, 0:1]
     finish_stats(exchange(count, s1, send1, recv1), valid, stats_out, 0)
+    before()
     for q in range(wide // quarter):
 
         def body(j, carry, q=q):
@@ -283,8 +303,8 @@
             own = pl.ds(pl.multiple_of(j * 128, 128), 128)
             hn = (h3n[:, at] - stats_out[0:1, at]) * stats_out[1:2, at]
             h3n[:, at] = hn
-            z = gb[0:1, at] * hn + gb[1:2, at] + res[q, :, own].astype(F32)
-            y_out[:, at] = (pack[:, 0:1] * (z * sigmoid(z))).astype(BF16)
+            z = gb[1, 0:1, at] * hn + gb[1, 1:2, at] + res[q, :, own].astype(F32)
+            y_out[:, at] = (mask[:, 0:1] * (z * sigmoid(z))).astype(BF16)
             return carry
 
         lax.fori_loop(0, quarter // 128, body, 0)
@@ -293,6 +313,236 @@
         u_out[:, at] = dot(moves[...], y_out[:, at]).astype(BF16)
 
     over(wide, TILE, permute)
+
+
+def batch_valid(counts, row):
+    me = lax.axis_index("segment")
+    value = counts[row : row + 1, 0:1]
+    for m in range(1, 4):
+        value = jnp.where(me == m, counts[row + m : row + m + 1, 0:1], value)
+    return value
+
+
+def head_kernel(
+    sections,
+    count,
+    x3,
+    w,
+    short,
+    k,
+    gb,
+    vec,
+    pack,
+    tiles,
+    mask,
+    moves,
+    x,
+    cols,
+    h1n,
+    h2n,
+    stats_out,
+    count_out,
+    g_out,
+    y_out,
+    u_out,
+    h3n,
+    stats3,
+    a2_out,
+    w1_out,
+    res_out,
+    act,
+    a2_all,
+    a2,
+    wsc,
+    w1,
+    rq,
+    res,
+    gslots,
+    *rest,
+):
+    sync, rest = rest[:9], list(rest[9:])
+    short_send, short_recv, short_relay_send, short_relay_recv = rest[:4]
+    w1_send, w1_recv, w1_relay_send, w1_relay_recv = rest[4:8]
+    g_send, g_recv, a2_send, a2_recv, res_send, res_recv, own_sem, out_sem = rest[8:]
+    me, place = lax.axis_index("segment"), lax.axis_index("dp")
+    core = lax.rem(place, 2)
+    sibling = place + 1 - 2 * core
+    wide = x.shape[1]
+    quarter = wide // sections
+    half_rows = wide // 2
+    mine = pl.ds(pl.multiple_of(core * half_rows, 16), half_rows)
+    greet(count, sections)
+
+    def short_copy(t):
+        src = short.at[mine, pl.ds(t * quarter, quarter)]
+        return mesh_copy(src, wsc.at[mine], short_send.at[t], short_recv, t, place)
+
+    def w1_copy(t):
+        return mesh_copy(w.at[mine], w1.at[mine], w1_send.at[t], w1_recv, t, place)
+
+    short_own = pltpu.make_async_copy(short.at[:, pl.ds(0, quarter)], wsc, own_sem.at[0])
+    w1_own = pltpu.make_async_copy(w, w1, own_sem.at[1])
+    short_relay = mesh_copy(
+        wsc.at[mine], wsc.at[mine], short_relay_send, short_relay_recv, me, sibling
+    )
+    w1_relay = mesh_copy(w1.at[mine], w1.at[mine], w1_relay_send, w1_relay_recv, me, sibling)
+
+    def g_copy(k_):
+        return mesh_copy(
+            gslots.at[me],
+            gslots.at[me],
+            g_send.at[k_],
+            g_recv.at[k_],
+            jnp.bitwise_xor(me, k_),
+            place,
+        )
+
+    gslots[me] = vec[...]
+    greeted(count, sections)
+
+    @pl.when(me == 0)
+    def _():
+        for t in (3, 1, 2):
+            short_copy(t).start()
+        short_own.start()
+
+    @pl.when(me == 1)
+    def _():
+        for t in (2, 0, 3):
+            w1_copy(t).start()
+        w1_own.start()
+
+    for k_ in range(1, sections):
+        g_copy(k_).start()
+
+    def relayout(j, carry):
+        at = pl.ds(pl.multiple_of(j * 128, 128), 128)
+        x[:, at] = x3[:, :, at].reshape(x.shape[0], 128)
+        return carry
+
+    lax.fori_loop(0, wide // 128, relayout, 0)
+    first_part(
+        count,
+        lambda: None,
+        x,
+        w,
+        k,
+        gb,
+        pack,
+        tiles,
+        a2_all,
+        cols,
+        h1n,
+        h2n,
+        stats_out,
+        count_out,
+        act,
+        *sync[:6],
+    )
+
+    def a2_copy(t):
+        return mesh_copy(a2_all.at[t], a2, a2_send.at[t], a2_recv, t, place)
+
+    @pl.when(me == 0)
+    def _():
+        for t in range(1, sections):
+            a2_copy(t).start()
+        a2[...] = a2_all[0]
+        short_own.wait()
+
+    @pl.when(me != 0)
+    def _():
+        short_copy(0).wait_recv()
+        short_relay.start()
+
+    @pl.when(me == 1)
+    def _():
+        w1_own.wait()
+
+    @pl.when(me != 1)
+    def _():
+        w1_copy(0).wait_recv()
+        w1_relay.start()
+
+    @pl.when(me != 0)
+    def _():
+        short_relay.wait_recv()
+
+    residual_part(x, wsc, rq, act)
+
+    def res_copy(k_):
+        other = jnp.bitwise_xor(me, k_)
+        return mesh_copy(
+            rq.at[other], res.at[me], res_send.at[k_], res_recv.at[k_], other, place
+        )
+
+    for k_ in range(1, sections):
+        res_copy(k_).start()
+    res[me] = rq[me]
+
+    @pl.when(me != 0)
+    def _():
+        a2_copy(0).wait_recv()
+
+    @pl.when(me != 1)
+    def _():
+        w1_relay.wait_recv()
+
+    for k_ in range(1, sections):
+        g_copy(k_).wait_recv()
+    g_out[...] = gslots[...]
+
+    def before():
+        for k_ in range(1, sections):
+            res_copy(k_).wait_recv()
+
+    second_part(
+        count,
+        before,
+        a2,
+        w1,
+        res,
+        mask,
+        gslots,
+        batch_valid(count_out, 0),
+        moves,
+        y_out,
+        u_out,
+        h3n,
+        stats3,
+        *sync[6:],
+    )
+    outs = [
+        pltpu.make_async_copy(src, dst, out_sem.at[i])
+        for i, (src, dst) in enumerate(((a2, a2_out), (w1, w1_out), (res, res_out)))
+    ]
+    for copy in outs:
+        copy.start()
+    for k_ in range(1, sections):
+        g_copy(k_).wait_send()
+        res_copy(k_).wait_send()
+
+    @pl.when(me == 0)
+    def _():
+        for t in range(1, sections):
+            short_copy(t).wait_send()
+            a2_copy(t).wait_send()
+
+    @pl.when(me != 0)
+    def _():
+        short_relay.wait_send()
+
+    @pl.when(me == 1)
+    def _():
+        for t in (0, 2, 3):
+            w1_copy(t).wait_send()
+
+    @pl.when(me != 1)
+    def _():
+        w1_relay.wait_send()
+
+    for copy in outs:
+        copy.wait()
 
 
 def back_sums(slots, me, at, grad, hn):
@@ -300,18 +550,51 @@
     slots[me, 1:2, at] = jnp.sum(grad * hn, axis=0, keepdims=True)
 
 
+def map_sender(sections, src, dst, owner, send_sem, recv_sem, own_sem):
+    me, place = lax.axis_index("segment"), lax.axis_index("dp")
+    own = pltpu.make_async_copy(src, dst.at[me], own_sem)
+
+    def copy(k):
+        return mesh_copy(src, dst.at[me], send_sem, recv_sem.at[k], owner, place)
+
+    def start():
+        @pl.when(me == owner)
+        def _():
+            own.start()
+
+        for k in range(1, sections):
+
+            @pl.when(me == owner ^ k)
+            def _(k=k):
+                copy(k).start()
+
+    def finish():
+        @pl.when(me == owner)
+        def _():
+            own.wait()
+            for k in range(1, sections):
+                copy(k).wait_recv()
+
+        @pl.when(me != owner)
+        def _():
+            copy(0).wait_send()
+
+    return start, finish
+
+
 def tile_kernel(
+    sections,
     count,
     u,
     w2,
     k2,
     w3,
-    og,
+    og3,
     pack,
-    gb2,
-    gb3,
-    valid_in,
+    gains,
+    counts,
     back,
+    y1,
     y_out,
     a2,
     cols,
@@ -320,12 +603,17 @@
     dh1,
     dy,
     sums_out,
+    map_one,
     h1n,
     h2n,
     h3n,
     act,
     dz,
     stats,
+    og,
+    map_send,
+    map_recv,
+    map_own,
     *sync,
 ):
     s1, send1, recv1, s2, send2, recv2, s3, send3, recv3 = sync[:9]
@@ -333,8 +621,14 @@
     rows, wide = u.shape
     narrow = h1n.shape[1]
     me = lax.axis_index("dp")
-    valid = valid_in[0:1, 0:1]
-    greet(count)
+    section = lax.axis_index("segment")
+    valid = batch_valid(counts, 4)
+    gb3 = gains.at[3]
+
+    def gb2(row, at):
+        return gains[2, row % 2 : row % 2 + 1, pl.ds(at.start + row // 2 * narrow, at.size)]
+
+    greet(count, sections)
 
     def project(at):
         h = dot(u[...], w2[:, at])
@@ -342,14 +636,29 @@
         norm_sums(s1, me, at, pack[:, 0:1] * h, h)
 
     over(narrow, TILE, project)
-    greeted(count)
+    greeted(count, sections)
+    send_map, wait_map = map_sender(sections, y1, map_one, 1, map_send, map_recv, map_own)
+    send_map()
+    real = og3.shape[0]
+    for m in range(sections):
+
+        @pl.when(section == m)
+        def _(m=m):
+            def one(j, carry):
+                at = pl.ds(pl.multiple_of(j * 128, 128), 128)
+                og[0:real, at] = og3[:, m, at].astype(F32)
+                return carry
+
+            lax.fori_loop(0, wide // 128, one, 0)
+
+    og[real:, :] = jnp.zeros((rows - real, wide), F32)
     finish_stats(exchange(count, s1, send1, recv1), valid, stats, 0)
 
     def activate(row, gain, source, store):
         def body(at):
             hn = (source[:, at] - stats[row : row + 1, at]) * stats[row + 1 : row + 2, at]
             source[:, at] = hn
-            n = gb2[gain : gain + 1, at] * hn + gb2[gain + 1 : gain + 2, at]
+            n = gb2(gain, at) * hn + gb2(gain + 1, at)
             store(at, pack[:, 0:1] * (n * sigmoid(n)))
 
         return body
@@ -397,7 +706,7 @@
         s = sigmoid(z)
         m = pack[:, 0:1]
         y_out[:, at] = (m * (z * s)).astype(BF16)
-        grad = (og[:, at].astype(F32) * m * (s * (1.0 + z * (1.0 - s)))).astype(BF16)
+        grad = (og[:, at] * m * (s * (1.0 + z * (1.0 - s)))).astype(BF16)
         dz[:, at] = grad
         grad = grad.astype(F32)
         back_sums(b3, me, at, grad, hn)
@@ -420,7 +729,7 @@
     def into_two(at):
         grad = dot(dh3[...], w3[:, at]).astype(BF16).astype(F32)
         hn = h2n[:, at]
-        n = gb2[2:3, at] * hn + gb2[3:4, at]
+        n = gb2(2, at) * hn + gb2(3, at)
         grad = grad * pack[:, 0:1] * slope(n)
         act[:, at] = grad
         back_sums(b2, me, at, grad, hn)
@@ -433,7 +742,7 @@
         offset, scale = sums_out[2:3, at], sums_out[3:4, at]
         grad = (
             pack[:, 0:1]
-            * gb2[2:3, at]
+            * gb2(2, at)
             * stats[3:4, at]
             * (act[:, at] - (offset + h2n[:, at] * scale) / valid)
         )
@@ -462,7 +771,7 @@
 
     def into_one(at):
         hn = h1n[:, at]
-        n = gb2[0:1, at] * hn + gb2[1:2, at]
+        n = gb2(0, at) * hn + gb2(1, at)
         grad = h2n[:, at] * pack[:, 0:1] * slope(n)
         act[:, at] = grad
         back_sums(b1, me, at, grad, hn)
@@ -475,7 +784,7 @@
         offset, scale = sums_out[4:5, at], sums_out[5:6, at]
         dh1[:, at] = (
             pack[:, 0:1]
-            * gb2[0:1, at]
+            * gb2(0, at)
             * stats[1:2, at]
             * (act[:, at] - (offset + h1n[:, at] * scale) / valid)
         ).astype(BF16)
@@ -487,17 +796,16 @@
         dy[:, at] = dot(back[...], grad.astype(BF16)).astype(BF16)
 
     over(wide, TILE, into_input)
-
-
-def image_back_kernel(
-    count, dy, res, h3n, pack, gb, stats, valid_in, w1, dz, dh3, da2, sums_out, b3, send3, recv3
+    wait_map()
+
+
+def image_back_part(
+    count, after, dy, res, h3n, mask, gb, stats, valid, w1, dz, dh3, da2, sums_out, b3, send3, recv3
 ):
     wide = dy.shape[1]
     quarter = res.shape[2]
     narrow = da2.shape[1]
     me = lax.axis_index("dp")
-    valid = valid_in[0:1, 0:1]
-    greet(count)
     for q in range(wide // quarter):
 
         def body(j, carry, q=q):
@@ -505,20 +813,20 @@
             own = pl.ds(pl.multiple_of(j * 128, 128), 128)
             hn = h3n[:, at]
             z = gb[0:1, at] * hn + gb[1:2, at] + res[q, :, own].astype(F32)
-            grad = (dy[:, at].astype(F32) * pack[:, 0:1] * slope(z)).astype(BF16)
+            grad = (dy[:, at].astype(F32) * mask[:, 0:1] * slope(z)).astype(BF16)
             dz[:, at] = grad
             back_sums(b3, me, at, grad.astype(F32), hn)
             return carry
 
         lax.fori_loop(0, quarter // 128, body, 0)
-    greeted(count)
+    after()
     total = exchange(count, b3, send3, recv3)
     sums_out[...] = total
 
     def through(at):
         offset, scale = sums_out[0:1, at], sums_out[1:2, at]
         dh3[:, at] = (
-            pack[:, 0:1]
+            mask[:, 0:1]
             * gb[0:1, at]
             * stats[1:2, at]
             * (dz[:, at].astype(F32) - (offset + h3n[:, at] * scale) / valid)
@@ -532,14 +840,13 @@
     over(narrow, TILE, into)
 
 
-def last_kernel(
+def last_part(
     count, da2, k, gb, pack, h1n, h2n, stats, counts, dh2, dh1, sums_out, act, acc, hold, *sync
 ):
     b2, send2, recv2, b1, send1, recv1 = sync
     rows, narrow = h1n.shape
     full = act.shape[1]
     me = lax.axis_index("dp")
-    greet(count)
     valid = counts[0:4, 0:1]
 
     def tile8(v):
@@ -579,7 +886,6 @@
         return body
 
     over(narrow, 128, into(2, lambda at: act[lane(at), 0:rows, :], h2n, b2))
-    greeted(count)
     sums_out[0:8, :] = exchange(count, b2, send2, recv2)
     over(narrow, 128, through(2, 12, 0, h2n, dh2))
     acc[...] = jnp.zeros((rows, narrow), F32)
@@ -605,37 +911,164 @@
     over(narrow, 128, through(0, 4, 8, h1n, dh1))
 
 
-def input_kernel(dh1, dz, w, short, out):
-    def body(at):
-        out[:, at] = (dot_t(dh1[...], w[at, :]) + dot_t(dz[...], short[at, :])).astype(BF16)
-
-    over(out.shape[1], TILE, body)
-
-
-def mesh_copy(src, dst, send_sem, recv_sem, segment, place):
-    return pltpu.make_async_remote_copy(
-        src_ref=src,
-        dst_ref=dst,
-        send_sem=send_sem,
-        recv_sem=recv_sem,
-        device_id=(segment, place),
-        device_id_type=MESH,
-    )
-
-
-def loop(low, high, body):
-    def one(k, carry):
-        body(k)
+def back_kernel(
+    sections,
+    count,
+    dy,
+    res,
+    h3n,
+    mask,
+    gains,
+    stats3,
+    w1,
+    k,
+    gb,
+    pack,
+    h1n,
+    h2n,
+    stats,
+    counts,
+    y2,
+    dz,
+    dh3,
+    dh2,
+    dh1,
+    sums3,
+    sums12,
+    dzq_out,
+    dz_all,
+    map_two,
+    map_three,
+    da2,
+    da2_all,
+    dzq,
+    act,
+    acc,
+    hold,
+    *rest,
+):
+    sync, rest = rest[:9], list(rest[9:])
+    a_send, a_recv, q_send, q_recv = rest[:4]
+    maps = [rest[4:7], rest[7:10], rest[10:13]]
+    me, place = lax.axis_index("segment"), lax.axis_index("dp")
+    quarter = dzq.shape[2]
+    greet(count, sections)
+    send_dz, wait_dz = map_sender(sections, dz, dz_all, 0, *maps[0])
+    send_two, wait_two = map_sender(sections, dy, map_two, 2, *maps[1])
+    send_three, wait_three = map_sender(sections, y2, map_three, 3, *maps[2])
+
+    def q_copy(k_):
+        other = jnp.bitwise_xor(me, k_)
+        at = pl.ds(pl.multiple_of(other * quarter, 128), quarter)
+        return mesh_copy(dz.at[:, at], dzq.at[me], q_send.at[k_], q_recv.at[k_], other, place)
+
+    def after():
+        greeted(count, sections)
+        for k_ in range(1, sections):
+            q_copy(k_).start()
+
+    image_back_part(
+        count,
+        after,
+        dy,
+        res,
+        h3n,
+        mask,
+        gains.at[1],
+        stats3,
+        batch_valid(counts, 0),
+        w1,
+        dz,
+        dh3,
+        da2,
+        sums3,
+        *sync[:3],
+    )
+
+    def a_copy(k_):
+        return mesh_copy(da2, da2_all.at[me], a_send, a_recv.at[k_], 0, place)
+
+    for k_ in range(1, sections):
+
+        @pl.when(me == k_)
+        def _(k_=k_):
+            a_copy(k_).start()
+
+    for k_ in range(1, sections):
+        q_copy(k_).wait_recv()
+    dzq[me] = dz[:, pl.ds(pl.multiple_of(me * quarter, 128), quarter)]
+    rows, full = dzq_out.shape[0], act.shape[1]
+    for m in range(4):
+
+        def put(j, carry, m=m):
+            at = pl.ds(pl.multiple_of(j * 128, 128), 128)
+            act[j, pl.ds(m, full // 4, stride=4), :] = dzq[m, :, at].astype(F32)
+            return carry
+
+        lax.fori_loop(0, quarter // 128, put, 0)
+
+    def weave(j, carry):
+        at = pl.ds(pl.multiple_of(j * 128, 128), 128)
+        dzq_out[:, at] = act[j, 0:rows, :].astype(BF16)
         return carry
 
-    lax.fori_loop(low, high, one, 0)
+    lax.fori_loop(0, quarter // 128, weave, 0)
+
+    @pl.when(me == 0)
+    def _():
+        for k_ in range(1, sections):
+            a_copy(k_).wait_recv()
+        da2_all[0] = da2[...]
+
+    @pl.when(me != 0)
+    def _():
+        da2_all[...] = jnp.zeros(da2_all.shape, BF16)
+
+    send_dz()
+    send_two()
+    send_three()
+    last_part(
+        count, da2_all, k, gb, pack, h1n, h2n, stats, counts, dh2, dh1, sums12, act, acc, hold, *sync[3:]
+    )
+    for k_ in range(1, sections):
+        q_copy(k_).wait_send()
+
+    @pl.when(me != 0)
+    def _():
+        a_copy(0).wait_send()
+
+    wait_dz()
+    wait_two()
+    wait_three()
 
 
 SUMS = (("k2", 2, True), ("p3", 3, True), ("p2", 2, True), ("p1", 1, True), ("k0", 0, False), ("p0", 0, False))
 
 
 def gradient_kernel(
-    sections, count, sh, k2, p3, p2, p1, k0, p0, vec, sh_out, p_out, k_out, vec_out, *scratch
+    sections,
+    count,
+    sh,
+    k2,
+    p3,
+    p2,
+    p1,
+    k0,
+    p0,
+    vec,
+    dh1,
+    w,
+    short,
+    map_zero,
+    map_one,
+    map_two,
+    map_three,
+    sh_out,
+    p_out,
+    k_out,
+    vec_out,
+    maps,
+    *scratch,
 ):
     names = [name for name, _, _ in SUMS]
     terms = dict(zip(names, (k2, p3, p2, p1, k0, p0)))
@@ -656,8 +1089,78 @@
     sh_half, sh_theirs, sh_others, sh_whole, vec_slots = take(), take(), take(), take(), take()
     load_sem, a_send, a_recv, b_send, b_recv, c_send, c_recv, d_send, d_recv = (take() for _ in range(9))
     e_send, e_recv, e_own, f_send, f_recv, v_send, v_recv = (take() for _ in range(7))
+    pages, s_rows, w_rows, hold, stage, page_sem, s_sem, w_sem, stage_sem = (take() for _ in range(9))
     slot = {name: i for i, name in enumerate(names)}
     last = len(names)
+
+    page_loads = [
+        pltpu.make_async_copy(source, pages, page_sem)
+        for source in (map_zero, map_one, map_two, map_three)
+    ]
+    for i, copy in enumerate(page_loads):
+        pl.when(me == i)(copy.start)
+    wide = pages.shape[2]
+    full_rows, map_rows = hold.shape[1], maps.shape[0] * maps.shape[1]
+
+    def tile_loads(j):
+        at = pl.ds(pl.multiple_of(j * TILE, TILE), TILE)
+        at_slot = lax.rem(j, 2)
+        return (
+            pltpu.make_async_copy(short.at[at], s_rows.at[at_slot], s_sem.at[at_slot]),
+            pltpu.make_async_copy(w.at[at], w_rows.at[at_slot], w_sem.at[at_slot]),
+        )
+
+    def tile_store(j):
+        at = pl.ds(pl.multiple_of(j * TILE, TILE), TILE)
+        at_slot = lax.rem(j, 2)
+        return pltpu.make_async_copy(stage.at[at_slot], maps.at[:, :, at], stage_sem.at[at_slot])
+
+    @pl.when(me == 0)
+    def _():
+        for copy in tile_loads(0):
+            copy.start()
+
+    def map_tile(j):
+        at = pl.ds(pl.multiple_of(j * TILE, TILE), TILE)
+        at_slot = lax.rem(j, 2)
+
+        def weave(m, value):
+            for part in range(TILE // 128):
+                hold[part, pl.ds(m, full_rows // 4, stride=4), :] = value[
+                    :, part * 128 : part * 128 + 128
+                ]
+
+        @pl.when(j >= 2)
+        def _():
+            tile_store(j - 2).wait()
+
+        @pl.when(me == 0)
+        def _():
+            @pl.when(j + 1 < wide // TILE)
+            def _():
+                for copy in tile_loads(j + 1):
+                    copy.start()
+
+            for copy in tile_loads(j):
+                copy.wait()
+            for m in range(4):
+                weave(m, dot_t(pages[m], s_rows[at_slot]))
+            extra = dot_t(dh1[...], w_rows[at_slot])
+            for part in range(TILE // 128):
+                cols = slice(part * 128, part * 128 + 128)
+                value = (hold[part, 0:map_rows, :] + extra[:, cols]).astype(BF16)
+                stage[at_slot, :, :, cols] = value.reshape(map_rows // 4, 4, 128)
+
+        @pl.when(me != 0)
+        def _():
+            for m in range(4):
+                weave(m, pages[m, :, at].astype(F32))
+            for part in range(TILE // 128):
+                cols = slice(part * 128, part * 128 + 128)
+                value = hold[part, 0:map_rows, :].astype(BF16)
+                stage[at_slot, :, :, cols] = value.reshape(map_rows // 4, 4, 128)
+
+        tile_store(j).start()
 
     def chip(k):
         return 2 * lax.rem(z + k, depth) + core
@@ -777,6 +1280,10 @@
 
         when_held(name, combine)
 
+    for i, copy in enumerate(page_loads):
+        pl.when(me == i)(copy.wait)
+    loop(0, 2, map_tile)
+
     loop(1, depth, lambda k: sh_send(k).wait_recv())
     mine = sh_at(z)
     acc = sh_half[mine, :].astype(F32)
@@ -795,6 +1302,7 @@
         )
 
     loop(1, depth, lambda k: sh_share(k).start())
+    loop(2, wide // TILE, map_tile)
 
     def to_chip(name, k):
         to = lax.rem(z + k, depth)
@@ -945,6 +1453,8 @@
         sums = sums + vec_slots[k]
     vec_out[...] = sums
 
+    tile_store(wide // TILE - 2).wait()
+    tile_store(wide // TILE - 1).wait()
     for k in range(1, sections):
         vec_copy(k).wait_send()
     sh_swap.wait_send()
@@ -979,7 +1489,7 @@
             deliver(name, 0).wait_send()
 
 
-def sum_gradients(sections, count, short, terms, vectors):
+def sum_gradients(sections, count, short, terms, vectors, dh1, w, weights, map_sources, real):
     narrow = short.shape[1]
     depth = count // 2
     args, scratch = [], []
@@ -1005,6 +1515,19 @@
         scratch.append(pltpu.SemaphoreType.DMA(shape))
     for shape in [(kinds,), (kinds, sections), (kinds,), (kinds,), (kinds,), (sections,), (sections,)]:
         scratch.append(pltpu.SemaphoreType.DMA(shape))
+    wide = w.shape[0]
+    padded = map_sources[0].shape[1]
+    scratch += [
+        pltpu.VMEM(map_sources[0].shape, BF16),
+        pltpu.VMEM((2, TILE, wide), BF16),
+        pltpu.VMEM((2, TILE, narrow), BF16),
+        pltpu.VMEM((TILE // 128, 4 * padded, 128), F32),
+        pltpu.VMEM((2, real, 4, TILE), BF16),
+        pltpu.SemaphoreType.DMA,
+        pltpu.SemaphoreType.DMA((2,)),
+        pltpu.SemaphoreType.DMA((2,)),
+        pltpu.SemaphoreType.DMA((2,)),
+    ]
     hbm = pl.BlockSpec(memory_space=pl.ANY)
     vmem = pl.BlockSpec(memory_space=pltpu.VMEM)
     proj_shape = args[1].shape
@@ -1016,15 +1539,16 @@
             shape_of(proj_shape, BF16),
             shape_of(taps_shape, BF16),
             shape_of(vectors.shape[1:], F32),
+            shape_of((real, 4, wide), BF16),
         ],
-        in_specs=[hbm] * 7 + [vmem],
-        out_specs=[hbm, hbm, hbm, vmem],
+        in_specs=[hbm] * 7 + [vmem, vmem] + [hbm] * 6,
+        out_specs=[hbm, hbm, hbm, vmem, hbm],
         scratch_shapes=scratch,
         compiler_params=pltpu.CompilerParams(
             has_side_effects=True, vmem_limit_bytes=VMEM_BYTES, collective_id=5
         ),
         cost_estimate=pl.CostEstimate(flops=0, bytes_accessed=400 * 2**20, transcendentals=0),
-    )(short.reshape(2, sh_rows, narrow), *args, vectors)
+    )(short.reshape(2, sh_rows, narrow), *args, vectors, dh1, w, weights, *map_sources)
 
 
 def layouts(resolution_ids, order_ids):
@@ -1062,11 +1586,6 @@
     return jnp.einsum(dims, a, b, preferred_element_type=F32)
 
 
-def core_swap(value):
-    count = lax.axis_size("dp")
-    return lax.ppermute(value, "dp", [(d, d ^ 1) for d in range(count)])
-
-
 def from_section(value, source, section):
     out = value[source]
     for t in range(value.shape[0]):
@@ -1076,10 +1595,10 @@
     return out
 
 
-def to_section_zero(value):
-    sections = lax.axis_size("segment")
-    parts = [value] + [lax.ppermute(value, "segment", [(t, 0)]) for t in range(1, sections)]
-    return jnp.stack(parts)
+def by_share(weights, sections, count, place):
+    rows, width = weights.shape
+    blocks = weights.reshape(sections, count, rows // (sections * count), width)
+    return lax.dynamic_index_in_dim(blocks, place, 1, keepdims=False)
 
 
 def body(
@@ -1101,45 +1620,16 @@
     count = lax.axis_size("dp")
     section = lax.axis_index("segment")
     place = lax.axis_index("dp")
-    core = place % 2
     first = section == 0
     proj, spatial, shortcut = proj_weight[0], spatial_weight[0], shortcut_weight[0]
     pick = lambda a: lax.dynamic_index_in_dim(a, section, 0, keepdims=False)
 
-    half_rows = wide // 2
-    w1_half = lax.dynamic_slice_in_dim(proj, core * half_rows, half_rows)
-    w1_half = from_section(jnp.broadcast_to(w1_half, (sections,) + w1_half.shape), 1, section)
-    w1_other = core_swap(w1_half)
-    w1 = jnp.where(
-        core == 0,
-        jnp.concatenate([w1_half, w1_other]),
-        jnp.concatenate([w1_other, w1_half]),
-    )
-
-    quarter = wide // sections
-    own_half = lax.dynamic_slice_in_dim(shortcut, core * half_rows, half_rows)
-    short_half = from_section(
-        jnp.stack([own_half[:, t * quarter : (t + 1) * quarter] for t in range(sections)]),
-        0,
-        section,
-    )
-    short_other = core_swap(short_half)
-
-    slice_rows = wide // count
-    tap_rows = spatial.shape[0] // count
-    own_proj = lax.dynamic_slice_in_dim(proj, place * slice_rows, slice_rows)
-    own_taps = lax.dynamic_slice_in_dim(spatial, place * tap_rows, tap_rows)
-    fine = tap_rows // sections
-    taps_piece = from_section(own_taps.reshape(sections, fine, narrow), 2, section)
-    packed = jnp.concatenate([own_proj, taps_piece])
-    everyone = lax.all_gather(packed, ("segment", "dp"), axis=0, tiled=True)
-    everyone = everyone.reshape(sections, count, slice_rows + fine, narrow)
-    w2 = everyone[2, :, :slice_rows].reshape(wide, narrow)
-    w3 = everyone[3, :, :slice_rows].reshape(wide, narrow)
-    k2 = jnp.swapaxes(everyone[:, :, slice_rows:], 0, 1).reshape(9 * narrow, narrow)
-
-    gains = lax.all_gather(jnp.concatenate([bn_gain[0], bn_bias[0]]), "segment", axis=0)
-    gain, bias = gains[:, :wide], gains[:, wide:]
+    taps_share = from_section(by_share(spatial, sections, count, place), 2, section)
+    two_share = from_section(by_share(proj, sections, count, place), 2, section)
+    three_share = from_section(by_share(proj, sections, count, place), 3, section)
+    k2 = lax.all_gather(taps_share, ("segment", "dp"), axis=0, tiled=True)
+    w2 = lax.all_gather(two_share, ("segment", "dp"), axis=0, tiled=True)
+    w3 = lax.all_gather(three_share, ("segment", "dp"), axis=0, tiled=True)
 
     image_masks, tile_masks, targets = layouts(
         resolution.reshape(-1), tile_order.reshape(micro * images, -1)
@@ -1163,67 +1653,61 @@
     moves = (target[:, None] == index[None, :]).astype(BF16)
     moves_back = (target[None, :] == index[:, None]).astype(BF16)
 
-    x_all = jnp.transpose(layer_input, (1, 2, 0, 3)).reshape(rows * micro, wide)
+    x_in = jnp.transpose(layer_input, (1, 2, 0, 3)).reshape(rows, micro, wide)
+    og_in = jnp.transpose(output_grad, (1, 2, 0, 3)).reshape(rows, micro, wide)
     gb_first = jnp.stack(
         [bn_gain[0, :narrow], bn_bias[0, :narrow]]
         + [bn_gain[0, narrow : 2 * narrow], bn_bias[0, narrow : 2 * narrow]]
     )
+    gains_here = jnp.concatenate([bn_gain, bn_bias])
     total = rows * micro
-    a2_all, cols_all, h1n_all, h2n_all, stats_all, counts = kernel_call(
-        functools.partial(first_kernel, count),
-        [
-            shape_of((micro, padded, narrow), BF16),
-            shape_of((total, 9 * narrow), BF16),
-            shape_of((total, narrow), F32),
-            shape_of((total, narrow), F32),
-            shape_of((16, narrow), F32),
-            shape_of((8, 128), F32),
-        ],
-        [x_all, proj, spatial, gb_first, pack_all, tiles_all],
-        [pltpu.VMEM((narrow // 128, 4 * padded, 128), F32)]
-        + sync_scratch(count, [(8, narrow + 128), (8, narrow)]),
-        0,
-        2 * total * narrow * (wide + 9 * narrow),
-        40 * 2**20,
-    )
-    a2 = from_section(a2_all, 0, section)
-    [res_quarter] = kernel_call(
-        residual_kernel,
-        [shape_of((micro, padded, quarter), BF16)],
-        [x_all, short_half, short_other],
-        [pltpu.VMEM((quarter // 128, 4 * padded, 128), F32)],
-        None,
-        2 * total * wide * quarter,
-        10 * 2**20,
-    )
-    residual = lax.all_to_all(res_quarter, "segment", 0, 0, tiled=True)
-
-    valid_image = pick(counts[:4])[None]
-    valid_tile = pick(counts[4:])[None]
-    gb_one = jnp.stack([gain[1], bias[1]])
-    y1, u, h3n, stats_three = kernel_call(
-        functools.partial(second_kernel, count),
-        [
-            shape_of((padded, wide), BF16),
-            shape_of((padded, wide), BF16),
-            shape_of((padded, wide), F32),
-            shape_of((2, wide), F32),
-        ],
-        [a2, w1, residual, image_mask, gb_one, valid_image, moves],
-        sync_scratch(count, [(2, wide)]),
-        1,
-        2 * padded * wide * (narrow + padded),
-        10 * 2**20,
-    )
-    gb_two = jnp.stack(
-        [gain[2, :narrow], bias[2, :narrow]]
-        + [gain[2, narrow : 2 * narrow], bias[2, narrow : 2 * narrow]]
-    )
-    gb_three = jnp.stack([gain[3], bias[3]])
-    og = jnp.transpose(output_grad, (1, 2, 0, 3)).reshape(rows, micro, wide)
-    og = pad_rows(lax.dynamic_index_in_dim(og, section, 1, keepdims=False))
-    y2, t_a2, t_cols, t_dh3, t_dh2, t_dh1, dy1, t_sums = kernel_call(
-        functools.partial(tile_kernel, count),
+    quarter = wide // sections
+    dma = pltpu.SemaphoreType.DMA
+    x_all, cols_all, h1n_all, h2n_all, stats_all, counts, gains, y1, u, h3n, stats3, a2, w1, res = (
+        kernel_call(
+            functools.partial(head_kernel, sections, count),
+            [
+                shape_of((total, wide), BF16),
+                shape_of((total, 9 * narrow), BF16),
+                shape_of((total, narrow), F32),
+                shape_of((total, narrow), F32),
+                shape_of((16, narrow), F32),
+                shape_of((8, 128), F32),
+                shape_of((sections, 2, wide), F32),
+                shape_of((padded, wide), BF16),
+                shape_of((padded, wide), BF16),
+                shape_of((padded, wide), F32),
+                shape_of((2, wide), F32),
+                shape_of((padded, narrow), BF16),
+                shape_of((wide, narrow), BF16),
+                shape_of((sections, padded, quarter), BF16),
+            ],
+            [x_in, proj, shortcut, spatial, gb_first, gains_here, pack_all, tiles_all, image_mask, moves],
+            [
+                pltpu.VMEM((narrow // 128, 4 * padded, 128), F32),
+                pltpu.VMEM((micro, padded, narrow), BF16),
+                pltpu.VMEM((padded, narrow), BF16),
+                pltpu.VMEM((wide, quarter), BF16),
+                pltpu.VMEM((wide, narrow), BF16),
+                pltpu.VMEM((micro, padded, quarter), BF16),
+                pltpu.VMEM((sections, padded, quarter), BF16),
+                pltpu.VMEM((sections, 2, wide), F32),
+            ]
+            + sync_scratch(count, [(8, narrow + 128), (8, narrow), (2, wide)])
+            + [dma((sections,)), dma, dma, dma]
+            + [dma((sections,)), dma, dma, dma]
+            + [dma((sections,)), dma((sections,)), dma((sections,)), dma]
+            + [dma((sections,)), dma((sections,)), dma((2,)), dma((3,))],
+            0,
+            2 * total * (narrow * (wide + 9 * narrow) + wide * quarter),
+            60 * 2**20,
+            far_in=(2,),
+            far_out=(11, 12, 13),
+        )
+    )
+    paged = shape_of((sections, padded, wide), BF16)
+    y2, t_a2, t_cols, t_dh3, t_dh2, t_dh1, dy1, t_sums, map_one = kernel_call(
+        functools.partial(tile_kernel, sections, count),
         [
             shape_of((padded, wide), BF16),
             shape_of((padded, narrow), BF16),
@@ -1233,8 +1717,9 @@
             shape_of((padded, narrow), BF16),
             shape_of((padded, wide), BF16),
             shape_of((6, wide), F32),
+            paged,
         ],
-        [u, w2, k2, w3, og, pack_tile, gb_two, gb_three, valid_tile, moves_back],
+        [u, w2, k2, w3, og_in, pack_tile, gains, counts, moves_back, y1],
         [
             pltpu.VMEM((padded, narrow), F32),
             pltpu.VMEM((padded, narrow), F32),
@@ -1242,62 +1727,52 @@
             pltpu.VMEM((padded, narrow), F32),
             pltpu.VMEM((padded, wide), BF16),
             pltpu.VMEM((6, wide), F32),
+            pltpu.VMEM((padded, wide), F32),
+            dma,
+            dma((sections,)),
+            dma,
         ]
         + sync_scratch(
             count, [(2, narrow), (2, narrow), (2, wide), (2, wide), (2, narrow), (2, narrow)]
         ),
-        2,
+        1,
         4 * padded * narrow * (2 * wide + 9 * narrow),
         30 * 2**20,
-    )
-    dz, dh3, da2, i_sums = kernel_call(
-        functools.partial(image_back_kernel, count),
+        far_in=(9,),
+        far_out=(8,),
+    )
+    dz, dh3, dh2_all, dh1_all, i_sums, f_sums, dz_quarter, map_zero, map_two, map_three = kernel_call(
+        functools.partial(back_kernel, sections, count),
         [
             shape_of((padded, wide), BF16),
             shape_of((padded, wide), BF16),
-            shape_of((padded, narrow), BF16),
-            shape_of((2, wide), F32),
-        ],
-        [dy1, residual, h3n, image_mask, gb_one, stats_three, valid_image, w1],
-        sync_scratch(count, [(2, wide)]),
-        3,
-        2 * padded * narrow * wide,
-        12 * 2**20,
-    )
-    da2_all = to_section_zero(da2)
-    dh2_all, dh1_all, f_sums = kernel_call(
-        functools.partial(last_kernel, count),
-        [
             shape_of((total, narrow), BF16),
             shape_of((total, narrow), BF16),
+            shape_of((2, wide), F32),
             shape_of((16, narrow), F32),
+            shape_of((total, quarter), BF16),
+            paged,
+            paged,
+            paged,
         ],
-        [da2_all, spatial, gb_first, pack_all, h1n_all, h2n_all, stats_all, counts],
+        [dy1, res, h3n, image_mask, gains, stats3, w1, spatial, gb_first, pack_all]
+        + [h1n_all, h2n_all, stats_all, counts, y2],
         [
+            pltpu.VMEM((padded, narrow), BF16),
+            pltpu.VMEM((micro, padded, narrow), BF16),
+            pltpu.VMEM((micro, padded, quarter), BF16),
             pltpu.VMEM((narrow // 128, 4 * padded, 128), F32),
             pltpu.VMEM((total, narrow), F32),
             pltpu.VMEM((total, narrow), BF16),
         ]
-        + sync_scratch(count, [(8, narrow), (8, narrow)]),
-        4,
+        + sync_scratch(count, [(2, wide), (8, narrow), (8, narrow)])
+        + [dma, dma((sections,)), dma((sections,)), dma((sections,))]
+        + [dma, dma((sections,)), dma] * 3,
+        2,
         2 * total * narrow * 9 * narrow,
-        20 * 2**20,
-    )
-    weave = lambda a: jnp.swapaxes(a[:, :rows], 0, 1).reshape(total, a.shape[2])
-    dz_all = weave(to_section_zero(dz))
-    dz_quarter = weave(
-        lax.all_to_all(dz.reshape(padded, sections, quarter), "segment", 1, 0, tiled=True).reshape(
-            micro, padded, quarter
-        )
-    )
-    [grad_input] = kernel_call(
-        input_kernel,
-        [shape_of((total, wide), BF16)],
-        [dh1_all, dz_all, proj, shortcut],
-        [],
-        None,
-        2 * total * wide * (wide + narrow),
-        30 * 2**20,
+        40 * 2**20,
+        far_in=(14,),
+        far_out=(7, 8, 9),
     )
 
     terms = {
@@ -1309,11 +1784,6 @@
         "p0": mm(x_all, dh1_all, "rc,rn->cn").astype(BF16),
     }
     short_term = mm(x_all, dz_quarter, "rc,rd->cd").astype(BF16)
-
-    exchanged = lax.all_to_all(jnp.stack([y1, y1, dy1, y2]), "segment", 0, 0)
-    exchanged = jnp.swapaxes(exchanged[:, :rows], 0, 1)
-    maps = jnp.where(first, grad_input.reshape(rows, micro, wide), exchanged)
-    maps = jnp.transpose(maps.reshape(images, pixels, micro, wide), (2, 0, 1, 3))
 
     blank = jnp.zeros((wide,), F32)
     pad = jnp.zeros((wide - 2 * narrow,), F32)
@@ -1332,9 +1802,19 @@
             t_sums[0],
         ]
     )
-    short_sum, proj_sum, taps_sum, vectors = sum_gradients(
-        sections, count, short_term, terms, vectors.reshape(sections, 2, wide)
-    )
+    short_sum, proj_sum, taps_sum, vectors, maps = sum_gradients(
+        sections,
+        count,
+        short_term,
+        terms,
+        vectors.reshape(sections, 2, wide),
+        dh1_all,
+        proj,
+        shortcut,
+        (map_zero, map_one, map_two, map_three),
+        rows,
+    )
+    maps = jnp.transpose(maps.reshape(images, pixels, micro, wide), (2, 0, 1, 3))
     proj_grad = proj_sum.reshape(wide, narrow).astype(F32)
     spatial_grad = taps_sum.reshape(9 * narrow, narrow).astype(F32)
     spatial_grad = jnp.where((section % 2) == 0, spatial_grad, jnp.zeros_like(spatial_grad))

time: 785 us -> 677 us (0.86)
  local copies, waits for them, and re-layouts: 92.9 us -> 13.3 us
  waiting for transfers between devices: 18.5 us -> 96 us
  starting transfers between devices: 76.7 us -> 7.99 us
  blocking collectives: 54.9 us -> 0 us
  Pallas kernels: 428 us -> 469 us
  other arithmetic: 50.6 us -> 27.7 us
    all_gather x1 -> x3, waiting for transfers between devices: 0.02 us -> 75.1 us  [the longest x1 65.6 us: body(): k2 = lax.all_gather(taps_share, ('segment', 'dp'), axis=0, tiled=True)]
    pallas_call x7 -> x3, Pallas kernels: 205 us -> 278 us  [kernel_call(): pl.pallas_call(kernel, out_shape=outs, in_specs=[pl.BlockSpec(memory_spac...]
    all_gather x1 -> x0, blocking collectives: 54.9 us -> none  [body(): lax.all_gather(jnp.concatenate([bn_gain[0], bn_bias[0]]), 'segment', axis=0)]
    pallas_call x1, Pallas kernels: 223 us -> 191 us  [sum_gradients(): pl.pallas_call(functools.partial(gradient_kernel, sections, count), out_s...]
    reshape x5 -> x0, local copies, waits for them, and re-layouts: 28.8 us -> none  [the longest x2 9.89 us: body(): weave = lambda a: jnp.swapaxes(a[:, :rows], 0, 1).reshape(total, a.shape[2])]
    all_to_all x3 -> x0, starting transfers between devices: 28.3 us -> none  [the longest x1 17.3 us: body(): residual = lax.all_to_all(res_quarter, 'segment', 0, 0, tiled=True)]
    ppermute x12 -> x9, starting transfers between devices: 29.7 us -> 7.88 us  [from_section(): got = lax.ppermute(value[t], 'segment', [(source, t)])]
    ppermute x8 -> x0, starting transfers between devices: 18.6 us -> none  [the longest x6 18.3 us: to_section_zero(): lax.ppermute(value, 'segment', [(t, 0)])]
  transfers between devices with their start and end apart: 24 -> 12, of which waited for: 3 -> 5; matrix products, arithmetic and copies ran while one was open for 19% -> 2% of each run, Pallas kernels for 45% -> 15%
where the time goes in v4:
time: 677 us; the launch traced here: 666 us
  Pallas kernels  469 us (69%)
  waiting for transfers between devices  96 us (14%)
  matrix products  37.7 us (6%)
  other arithmetic  27.7 us (4%)
  between operations  14.5 us (2%)
  local copies, waits for them, and re-layouts  13.3 us (2%)
  starting transfers between devices  7.99 us (1%)
    pallas_call x3, Pallas kernels, kernel_call(): pl.pallas_call(kernel, out_shape=outs, in_specs=[pl.BlockSpec(memory_spac...  278 us
    pallas_call x1, Pallas kernels, sum_gradients(): pl.pallas_call(functools.partial(gradient_kernel, sections, count), out_s...  191 us
    all_gather x1, waiting for transfers between devices, body(): k2 = lax.all_gather(taps_share, ('segment', 'dp'), axis=0, tiled=True)  65.6 us
    dot_general x7, matrix products, mm(): return jnp.einsum(dims, a, b, preferred_element_type=F32)  37.7 us
    ppermute x9, waiting for transfers between devices, from_section(): got = lax.ppermute(value[t], 'segment', [(source, t)])  20.9 us
  transfers between devices with their start and end apart: 12, of which 5 were waited for; matrix products, arithmetic and copies ran while one was open for 2% of the time, Pallas kernels for 15%

profile of v4, /device:TPU:0, one launch (start us, length us, event | category | flops | bytes accessed | tf_op | source)
XLA Modules:
  0.0 666.2 jit_solution(976540910957187859)
XLA Ops:
  7.2 0.9 dynamic-slice_bitcast_fusion.5
  8.2 0.7 collective-permute-start.6
  8.8 0.7 collective-permute-start.7
  9.5 1.3 collective-permute-start.8
  10.9 8.5 %collective-permute-done.8 = bf16[64,512]{1,0:T(8,128)(2,1)S(1)} collective-permute-done((bf16[64,512]{1,0:T(8,128)(2,1)S(1)}, bf16[64,512]{1,0:T(8,128)(2,1)S(1)}, u32[]{:S(2)}, u32[]{:S(2)}) %collective-permute-start.8) | collective-permute-done | bytes 65568 | tf_op jit(solution)/shard_map/ppermute | solution.py:1593
  19.3 1.5 select_select_fusion
  20.9 0.7 collective-permute-start.1
  21.6 1.3 collective-permute-start.2
  22.9 0.7 collective-permute-start
  23.6 4.1 collective-permute-done.2
  27.7 0.6 select_select_fusion.1
  28.4 1.1 dynamic-slice_bitcast_fusion.1
  29.5 0.7 collective-permute-start.3
  30.2 0.7 collective-permute-start.4
  30.9 1.3 collective-permute-start.5
  32.2 8.3 %collective-permute-done.5 = bf16[144,512]{1,0:T(8,128)(2,1)S(1)} collective-permute-done((bf16[144,512]{1,0:T(8,128)(2,1)S(1)}, bf16[144,512]{1,0:T(8,128)(2,1)S(1)}, u32[]{:S(2)}, u32[]{:S(2)}) %collective-permute-start.5) | collective-permute-done | bytes 147488 | tf_op jit(solution)/shard_map/ppermute | solution.py:1593
  40.5 1.6 fusion.4
  42.1 0.1 copy.42
  42.2 0.1 mul.74
  42.4 0.1 multiply_reduce_fusion
  42.5 0.1 rem.235
  42.6 0.1 rem.240
  42.6 0.1 div.84
  42.8 0.1 ne.265
  42.9 0.1 ne.271
  43.1 0.1 lt.206
  43.2 0.1 lt.221
  43.4 0.1 add.239
  43.5 0.1 and.239
  43.7 0.1 lt.203
  43.8 0.1 copy.41
  44.0 0.1 reshape.690
  44.3 1.1 copy.45.pack
  45.3 0.1 copy.43
  45.5 1.0 reshape.696.tiles
  46.6 0.1 copy.44
  46.7 0.7 pad.11.mask
  47.6 0.1 add.256
  47.7 0.8 copy.47.pack
  48.5 0.6 pad_maximum_fusion.1.gb
  49.1 0.6 pad_maximum_fusion.vec
  49.7 0.9 fusion.1
  50.6 97.0 %shard_map.154 = (bf16[1176,2048]{1,0:T(8,128)(2,1)}, bf16[1176,4608]{1,0:T(8,128)(2,1)}, f32[1176,512]{1,0:T(8,128)}, f32[1176,512]{1,0:T(8,128)}, f32[16,512]{...) custom-call(bf16[294,4,2048]{2,1,0:T(4,128)(2,1)} %bitcast.121, ...), custom_call_target="tpu_custom_call" | custom-call | flops 10481565696 | bytes 62914560 | tf_op jit(solution)/shard_map/pallas_call | solution.py:106
  147.6 9.5 %all-gather.4.cloned.1.call-done.w2 = bf16[2048,512]{1,0:T(8,128)(2,1)} async-done(((bf16[64,512]{1,0:T(8,128)(2,1)}), bf16[2048,512]{1,0:T(8,128)(2,1)}) %all-gather.4.cloned.1.call-update) | async-done | bytes 2097168 | tf_op jit(solution)/shard_map/all_gather | solution.py:1631
  157.1 65.6 %all-gather.6.cloned.1.call-done.k2 = bf16[4608,512]{1,0:T(8,128)(2,1)} async-done(((bf16[144,512]{1,0:T(8,128)(2,1)}), bf16[4608,512]{1,0:T(8,128)(2,1)}) %all-gather.6.cloned.1.call-update) | async-done | bytes 4718608 | tf_op jit(solution)/shard_map/all_gather | solution.py:1630
  222.7 67.6 %shard_map.155 = (bf16[304,2048]{1,0:T(8,128)(2,1)}, bf16[304,512]{1,0:T(8,128)(2,1)}, bf16[304,4608]{1,0:T(8,128)(2,1)}, bf16[304,2048]{1,0:T(8,128)(2,1)}, bf1...) custom-call(bf16[304,2048]{1,0:T(8,128)(2,1)} %get-tuple-element.44., ...), custom_call_target="tpu_custom_call" | custom-call | flops 5419040768 | bytes 31457280 | tf_op jit(solution)/shard_map/pallas_call | solution.py:106
  290.3 0.9 fusion.27
  291.2 0.9 fusion.26
  292.2 3.6 convolution_convert_fusion.4
  295.8 113.8 %shard_map.156 = (bf16[304,2048]{1,0:T(8,128)(2,1)}, bf16[304,2048]{1,0:T(8,128)(2,1)}, bf16[1176,512]{1,0:T(8,128)(2,1)}, bf16[1176,512]{1,0:T(8,128)(2,1)}, f3...) custom-call(bf16[304,2048]{1,0:T(8,128)(2,1)} %get-tuple-element.48., ...), custom_call_target="tpu_custom_call" | custom-call | flops 5549064192 | bytes 41943040 | tf_op jit(solution)/shard_map/pallas_call | solution.py:106
  409.6 7.1 %convolution_convert_fusion.6 = bf16[2048,512]{1,0:T(8,128)(2,1)} fusion(bf16[1176,2048]{1,0:T(8,128)(2,1)} %get-tuple-element.43, bf16[1176,512]{1,0:T(8,128)(2,1)} %get-tuple-element.57), kind=kOutput, calls=%fused_computation.8 | convolution fusion | flops 2467299328 | bytes 8118272 | tf_op jit(solution)/shard_map/rc,rd->cd/dot_general | solution.py:1586
  416.7 7.0 %convolution_convert_fusion.2 = bf16[2048,512]{1,0:T(8,128)(2,1)} fusion(bf16[1176,2048]{1,0:T(8,128)(2,1)} %get-tuple-element.43, bf16[1176,512]{1,0:T(8,128)(2,1)S(1)} %copy-done), kind=kOutput, calls=%fused_computation.4 | convolution fusion | flops 2467299328 | bytes 8118272 | tf_op jit(solution)/shard_map/rc,rn->cn/dot_general | solution.py:1586
  423.9 0.1 stack.17
  424.0 0.7 reshape.687.vec
  424.6 4.5 convolution_convert_fusion.1
  429.1 2.6 convolution_convert_fusion.5
  431.7 2.6 convolution_convert_fusion.3
  434.4 10.3 %convolution_convert_fusion = bf16[4608,512]{1,0:T(8,128)(2,1)} fusion(bf16[1176,4608]{1,0:T(8,128)(2,1)} %get-tuple-element.65, bf16[1176,512]{1,0:T(8,128)(2,1)S(1)} %copy-done.16), kind=kOutput, calls=%fused_computation.2 | convolution fusion | flops 5551423488 | bytes 16760832 | tf_op jit(solution)/shard_map/rk,rn->kn/dot_general | solution.py:1586
  444.7 190.6 %shard_map.157 = (bf16[2,1024,2048]{2,1,0:T(8,128)(2,1)}, bf16[2,4,4,64,512]{4,3,2,1,0:T(8,128)(2,1)}, bf16[2,4,4,144,512]{4,3,2,1,0:T(8,128)(2,1)}, f32[2,2048]{1,0:T(2,128)}, bf16[294,4,2048]{2,1,0:T(4,128)(2,1)}) custom-call(bf16[2,1024,512]{2,1,0:T(8,128)(2,1)} %bitcast.101, bf16[2,4,4,144,512]{4,3,2,1,0:T(8,128)(2,1)} %bitcast.92, ...), custom_call_target="tpu_custom_call" | custom-call | bytes 419430400 | tf_op jit(solution)/shard_map/pallas_call | solution.py:1535
  635.2 4.2 convert.5
  639.4 12.1 %convert_select_fusion = f32[2,1024,2048]{2,1,0:T(8,128)} fusion(bf16[2,1024,2048]{2,1,0:T(8,128)(2,1)} %get-tuple-element.78, pred[]{:T(512)S(6)} %eq.80), kind=kLoop, calls=%fused_computation | loop fusion | flops 8388608 | bytes 25165824 | tf_op jit(solution)/shard_map/jit(_where)/select_n | solution.py:1822
  651.6 0.6 fusion.28
  652.2 5.1 convert_select_fusion.1
  657.3 2.2 copy.50
  (101 shorter events, 1.2 us)
Async XLA Ops:
  7.2 37.0 %copy-start.1 = (f32[1176,9]{0,1:T(8,128)S(1)}, f32[1176,9]{0,1:T(8,128)}, u32[]{:S(2)}) copy-start(f32[1176,9]{0,1:T(8,128)} %constant.128.clone) | copy-start | bytes 127012
  7.2 34.9 %copy-start.8 = (s32[4,6,9]{2,0,1:T(4,128)S(1)}, s32[4,6,9]{2,0,1:T(4,128)}, u32[]{:S(2)}) copy-start(s32[4,6,9]{2,0,1:T(4,128)} %param.14) | copy-start | bytes 2596
  7.2 35.8 %copy-start.9 = (s32[4,6]{1,0:T(4,128)S(1)}, s32[4,6]{1,0:T(4,128)}, u32[]{:S(2)}) copy-start(s32[4,6]{1,0:T(4,128)} %param.13) | copy-start | bytes 292
  7.2 140.4 %all-gather.8.cloned.1.call-start = ((), (), s32[]{:S(2)}) async-start(), calls=%async_computation.2 | async-start | bytes 2162688 | tf_op jit(solution)/shard_map/all_gather | solution.py:1632
  8.2 2.7 collective-permute-start.6
  8.8 2.0 collective-permute-start.7
  9.5 9.8 %collective-permute-start.8 = (bf16[64,512]{1,0:T(8,128)(2,1)S(1)}, bf16[64,512]{1,0:T(8,128)(2,1)S(1)}, u32[]{:S(2)}, u32[]{:S(2)}) collective-permute-start(bf16[64,512]{1,0:T(8,128)(2,1)S(1)} %get-tuple-element.91), channel_id=1, source_target_pairs={{24,0},{25,1},{26,2},{27,3},{28,4},{29,5},{30,6},{31,7}} | collective-permute-start | bytes 196616 | tf_op jit(solution)/shard_map/ppermute | solution.py:1593
  20.8 26.8 %copy-start.3 = (f32[304,15]{0,1:T(8,128)S(1)}, f32[304,15]{0,1:T(8,128)}, u32[]{:S(2)}) copy-start(f32[304,15]{0,1:T(8,128)} %constant.129.clone) | copy-start | bytes 54724
  20.8 136.3 %all-gather.4.cloned.1.call-start = ((), (), s32[]{:S(2)}) async-start(), calls=%async_computation | async-start | bytes 2162688 | tf_op jit(solution)/shard_map/all_gather | solution.py:1631
  20.9 2.7 collective-permute-start.1
  21.6 6.2 collective-permute-start.2
  22.9 4.9 collective-permute-start
  23.5 24.9 %copy-start.4 = (f32[1,2048]{1,0:T(1,128)S(1)}, f32[1,2048]{1,0:T(1,128)}, u32[]{:S(2)}) copy-start(f32[1,2048]{1,0:T(1,128)} %param.18) | copy-start | bytes 24580
  23.6 24.9 %copy-start.5 = (f32[1,2048]{1,0:T(1,128)S(1)}, f32[1,2048]{1,0:T(1,128)}, u32[]{:S(2)}) copy-start(f32[1,2048]{1,0:T(1,128)} %param.19) | copy-start | bytes 24580
  28.4 194.3 %all-gather.6.cloned.1.call-start = ((), (), s32[]{:S(2)}) async-start(), calls=%async_computation.1 | async-start | bytes 4866048 | tf_op jit(solution)/shard_map/all_gather | solution.py:1630
  29.5 2.7 collective-permute-start.3
  30.2 2.0 collective-permute-start.4
  30.9 9.6 %collective-permute-start.5 = (bf16[144,512]{1,0:T(8,128)(2,1)S(1)}, bf16[144,512]{1,0:T(8,128)(2,1)S(1)}, u32[]{:S(2)}, u32[]{:S(2)}) collective-permute-start(bf16[144,512]{1,0:T(8,128)(2,1)S(1)} %get-tuple-element.88), channel_id=1, source_target_pairs={{16,0},{17,1},{18,2},{19,3},{20,4},{21,5},{22,6},{23,7}} | collective-permute-start | bytes 442376 | tf_op jit(solution)/shard_map/ppermute | solution.py:1593
  222.7 69.5 %copy-start.12 = (bf16[304,2048]{1,0:T(8,128)(2,1)S(1)}, bf16[304,2048]{1,0:T(8,128)(2,1)}, u32[]{:S(2)}) copy-start(bf16[304,2048]{1,0:T(8,128)(2,1)} %get-tuple-element.44.u) | copy-start | bytes 3735556
  409.6 7.1 %copy-start = (bf16[1176,512]{1,0:T(8,128)(2,1)S(1)}, bf16[1176,512]{1,0:T(8,128)(2,1)}, u32[]{:S(2)}) copy-start(bf16[1176,512]{1,0:T(8,128)(2,1)} %get-tuple-element.67.dh1) | copy-start | bytes 3612676
  416.7 7.0 %copy-start.2 = (f32[16,512]{1,0:T(8,128)S(1)}, f32[16,512]{1,0:T(8,128)}, u32[]{:S(2)}) copy-start(f32[16,512]{1,0:T(8,128)} %get-tuple-element.68) | copy-start | bytes 98308
  416.7 7.1 %copy-start.6 = (f32[2,2048]{1,0:T(2,128)S(1)}, f32[2,2048]{1,0:T(2,128)}, u32[]{:S(2)}) copy-start(f32[2,2048]{1,0:T(2,128)} %get-tuple-element.69) | copy-start | bytes 49156
  416.7 7.9 %copy-start.15 = (bf16[304,4608]{1,0:T(8,128)(2,1)S(1)}, bf16[304,4608]{1,0:T(8,128)(2,1)}, u32[]{:S(2)}) copy-start(bf16[304,4608]{1,0:T(8,128)(2,1)} %get-tuple-element.58) | copy-start | bytes 8404996
  416.7 7.9 %copy-start.17 = (bf16[304,512]{1,0:T(8,128)(2,1)S(1)}, bf16[304,512]{1,0:T(8,128)(2,1)}, u32[]{:S(2)}) copy-start(bf16[304,512]{1,0:T(8,128)(2,1)} %get-tuple-element.59) | copy-start | bytes 933892
  424.6 4.5 copy-start.10
  424.6 4.5 copy-start.14
  429.1 2.6 copy-start.11
  429.1 2.6 copy-start.13
  431.7 2.6 copy-start.16
  639.4 12.7 %slice-start.2 = ((s8[4718592]{0:T(1024)(128)(4,1)}), s8[4194304]{0:T(1024)(128)(4,1)S(1)}, s32[]{:S(2)}) async-start(s8[4718592]{0:T(1024)(128)(4,1)} %bitcast.94), calls=%async_computation.5 | async-start | bytes 8388608
  639.4 12.1 %copy-start.7 = (f32[2,2048]{1,0:T(2,128)S(1)}, f32[2,2048]{1,0:T(2,128)}, u32[]{:S(2)}) copy-start(f32[2,2048]{1,0:T(2,128)} %get-tuple-element.79) | copy-start | bytes 49156
  639.4 12.7 %slice-start.3 = ((s8[4718592]{0:T(1024)(128)(4,1)}), s8[524288]{0:T(1024)(128)(4,1)S(1)}, s32[]{:S(2)}) async-start(s8[4718592]{0:T(1024)(128)(4,1)} %bitcast.94), calls=%async_computation.6 | async-start | bytes 1048576
  652.2 5.1 slice-start
  652.2 5.1 slice-start.1
Sparse Core Ops, SparseCore 0:
  21.0 68.4 all-gather.7
  92.4 64.6 all-gather.3
  160.1 62.5 all-gather.5

commit v5 on v4

--- a/solution.py
+++ b/solution.py
@@ -167,7 +167,7 @@
 
 
 def first_part(
-    count, ready, x, w, k, gb, pack, tiles, a2_out, cols, h1n, h2n, stats_out, count_out, act, *sync
+    count, ready, writes, x, w, k, gb, pack, tiles, a2_out, cols, h1n, h2n, stats_out, count_out, act, *sync
 ):
     s1, send1, recv1, s2, send2, recv2 = sync
     rows, narrow = h1n.shape
@@ -187,7 +187,7 @@
     over(narrow, TILE, project)
     s1[me, 0:4, narrow:] = jnp.broadcast_to(by_batch(pack[:, 0:1]), (4, 128))
     s1[me, 4:8, narrow:] = jnp.broadcast_to(by_batch(tiles[:, 0:1]), (4, 128))
-    ready()
+    ready[0]()
     total = exchange(count, s1, send1, recv1)
     counts = total[:, narrow:]
     count_out[...] = counts
@@ -230,7 +230,10 @@
         s2[me, 0:4, at] = by_batch(m)
         s2[me, 4:8, at] = by_batch(m * h)
 
+    for write in writes:
+        write.start()
     over(narrow, TILE, convolve)
+    ready[1]()
     total = exchange(count, s2, send2, recv2)
     average = total[0:4] / valid
     stats_out[8:12, :] = average
@@ -336,10 +339,6 @@
     tiles,
     mask,
     moves,
-    x,
-    cols,
-    h1n,
-    h2n,
     stats_out,
     count_out,
     g_out,
@@ -350,6 +349,17 @@
     a2_out,
     w1_out,
     res_out,
+    x_out,
+    cols_out,
+    h1n_out,
+    h2n_out,
+    w3_out,
+    w2_out,
+    k2_out,
+    x,
+    cols,
+    h1n,
+    h2n,
     act,
     a2_all,
     a2,
@@ -363,7 +373,8 @@
     sync, rest = rest[:9], list(rest[9:])
     short_send, short_recv, short_relay_send, short_relay_recv = rest[:4]
     w1_send, w1_recv, w1_relay_send, w1_relay_recv = rest[4:8]
-    g_send, g_recv, a2_send, a2_recv, res_send, res_recv, own_sem, out_sem = rest[8:]
+    g_send, g_recv, a2_send, a2_recv, res_send, res_recv, own_sem, out_sem = rest[8:16]
+    spread_send, spread_recv, far_send, far_recv, near_send, near_recv, keep_sem = rest[16:]
     me, place = lax.axis_index("segment"), lax.axis_index("dp")
     core = lax.rem(place, 2)
     sibling = place + 1 - 2 * core
@@ -372,6 +383,59 @@
     half_rows = wide // 2
     mine = pl.ds(pl.multiple_of(core * half_rows, 16), half_rows)
     greet(count, sections)
+
+    odd = lax.rem(lax.div(place, 2), 2)
+    beside = place + 2 - 4 * odd
+    parts = [("w3", w, w3_out, 3, 0, 1), ("w2", w, w2_out, 2, 0, 1)]
+    parts += [("k2", k, k2_out, 2, i, 3) for i in range(3)]
+
+    def part_rows(i, at_odd):
+        _, src, _, _, piece, pieces = parts[i]
+        fine = src.shape[0] // (4 * pieces)
+        start = ((2 * at_odd + core) * pieces + piece) * fine
+        return pl.ds(pl.multiple_of(start, 16), fine)
+
+    def spread_copy(i, t):
+        _, src, dst, _, _, _ = parts[i]
+        at = part_rows(i, odd)
+        return mesh_copy(src.at[at], dst.at[at], spread_send.at[i, t], spread_recv.at[i], t, place)
+
+    def far_copy(i):
+        dst, at = parts[i][2], part_rows(i, odd)
+        return mesh_copy(dst.at[at], dst.at[at], far_send.at[i], far_recv.at[i], me, beside)
+
+    def near_copy(i, second):
+        dst = parts[i][2]
+        at = part_rows(i, 1 - odd if second else odd)
+        sems = near_send.at[i, second], near_recv.at[i, second]
+        return mesh_copy(dst.at[at], dst.at[at], *sems, me, sibling)
+
+    keeps = [
+        (3, pltpu.make_async_copy(w, w3_out, keep_sem.at[0])),
+        (2, pltpu.make_async_copy(w, w2_out, keep_sem.at[1])),
+        (2, pltpu.make_async_copy(k, k2_out, keep_sem.at[2])),
+    ]
+
+    def spread_start(i):
+        owner = parts[i][3]
+
+        @pl.when(me == owner)
+        def _():
+            for d in (3, 1, 2):
+                spread_copy(i, owner ^ d).start()
+
+    def spread_on(i):
+        @pl.when(me != parts[i][3])
+        def _():
+            spread_copy(i, 0).wait_recv()
+            far_copy(i).start()
+            near_copy(i, 0).start()
+
+    def far_on(i):
+        @pl.when(me != parts[i][3])
+        def _():
+            far_copy(i).wait_recv()
+            near_copy(i, 1).start()
 
     def short_copy(t):
         src = short.at[mine, pl.ds(t * quarter, quarter)]
@@ -414,6 +478,8 @@
 
     for k_ in range(1, sections):
         g_copy(k_).start()
+    spread_start(0)
+    spread_start(1)
 
     def relayout(j, carry):
         at = pl.ds(pl.multiple_of(j * 128, 128), 128)
@@ -421,9 +487,18 @@
         return carry
 
     lax.fori_loop(0, wide // 128, relayout, 0)
+    writes = [
+        pltpu.make_async_copy(src, dst, out_sem.at[i])
+        for i, (src, dst) in enumerate(
+            ((x, x_out), (h1n, h1n_out), (cols, cols_out), (h2n, h2n_out))
+            + ((a2, a2_out), (w1, w1_out), (res, res_out))
+        )
+    ]
+    writes[0].start()
     first_part(
         count,
-        lambda: None,
+        (lambda: spread_start(2), lambda: spread_start(3)),
+        writes[1:3],
         x,
         w,
         k,
@@ -440,6 +515,9 @@
         *sync[:6],
     )
 
+    writes[3].start()
+    spread_start(4)
+
     def a2_copy(t):
         return mesh_copy(a2_all.at[t], a2, a2_send.at[t], a2_recv, t, place)
 
@@ -463,6 +541,9 @@
     def _():
         w1_copy(0).wait_recv()
         w1_relay.start()
+
+    spread_on(0)
+    spread_on(1)
 
     @pl.when(me != 0)
     def _():
@@ -479,6 +560,7 @@
     for k_ in range(1, sections):
         res_copy(k_).start()
     res[me] = rq[me]
+    spread_on(2)
 
     @pl.when(me != 0)
     def _():
@@ -493,6 +575,9 @@
     g_out[...] = gslots[...]
 
     def before():
+        spread_on(3)
+        far_on(0)
+        far_on(1)
         for k_ in range(1, sections):
             res_copy(k_).wait_recv()
 
@@ -512,12 +597,13 @@
         stats3,
         *sync[6:],
     )
-    outs = [
-        pltpu.make_async_copy(src, dst, out_sem.at[i])
-        for i, (src, dst) in enumerate(((a2, a2_out), (w1, w1_out), (res, res_out)))
-    ]
-    for copy in outs:
+    spread_on(4)
+    for copy in writes[4:]:
         copy.start()
+    for owner, copy in keeps:
+        pl.when(me == owner)(copy.start)
+    for i in range(2, len(parts)):
+        far_on(i)
     for k_ in range(1, sections):
         g_copy(k_).wait_send()
         res_copy(k_).wait_send()
@@ -541,7 +627,23 @@
     def _():
         w1_relay.wait_send()
 
-    for copy in outs:
+    for i in range(len(parts)):
+        owner = parts[i][3]
+
+        @pl.when(me == owner)
+        def _(i=i, owner=owner):
+            for d in (1, 2, 3):
+                spread_copy(i, owner ^ d).wait_send()
+
+        @pl.when(me != owner)
+        def _(i=i):
+            far_copy(i).wait_send()
+            near_copy(i, 0).wait()
+            near_copy(i, 1).wait()
+
+    for owner, copy in keeps:
+        pl.when(me == owner)(copy.wait)
+    for copy in writes:
         copy.wait()
 
 
@@ -604,6 +706,7 @@
     dy,
     sums_out,
     map_one,
+    map_three,
     h1n,
     h2n,
     h3n,
@@ -614,6 +717,9 @@
     map_send,
     map_recv,
     map_own,
+    three_send,
+    three_recv,
+    three_own,
     *sync,
 ):
     s1, send1, recv1, s2, send2, recv2, s3, send3, recv3 = sync[:9]
@@ -712,6 +818,10 @@
         back_sums(b3, me, at, grad, hn)
 
     over(wide, 128, result)
+    send_three, wait_three = map_sender(
+        sections, y_out, map_three, 3, three_send, three_recv, three_own
+    )
+    send_three()
     total = exchange(count, b3, bsend3, brecv3)
     sums_out[0:2, :] = total
 
@@ -797,6 +907,7 @@
 
     over(wide, TILE, into_input)
     wait_map()
+    wait_three()
 
 
 def image_back_part(
@@ -928,7 +1039,6 @@
     h2n,
     stats,
     counts,
-    y2,
     dz,
     dh3,
     dh2,
@@ -938,7 +1048,6 @@
     dzq_out,
     dz_all,
     map_two,
-    map_three,
     da2,
     da2_all,
     dzq,
@@ -949,21 +1058,22 @@
 ):
     sync, rest = rest[:9], list(rest[9:])
     a_send, a_recv, q_send, q_recv = rest[:4]
-    maps = [rest[4:7], rest[7:10], rest[10:13]]
+    maps = [rest[4:7], rest[7:10]]
     me, place = lax.axis_index("segment"), lax.axis_index("dp")
     quarter = dzq.shape[2]
     greet(count, sections)
     send_dz, wait_dz = map_sender(sections, dz, dz_all, 0, *maps[0])
     send_two, wait_two = map_sender(sections, dy, map_two, 2, *maps[1])
-    send_three, wait_three = map_sender(sections, y2, map_three, 3, *maps[2])
 
     def q_copy(k_):
         other = jnp.bitwise_xor(me, k_)
         at = pl.ds(pl.multiple_of(other * quarter, 128), quarter)
         return mesh_copy(dz.at[:, at], dzq.at[me], q_send.at[k_], q_recv.at[k_], other, place)
 
+    greeted(count, sections)
+    send_two()
+
     def after():
-        greeted(count, sections)
         for k_ in range(1, sections):
             q_copy(k_).start()
 
@@ -994,6 +1104,7 @@
         def _(k_=k_):
             a_copy(k_).start()
 
+    send_dz()
     for k_ in range(1, sections):
         q_copy(k_).wait_recv()
     dzq[me] = dz[:, pl.ds(pl.multiple_of(me * quarter, 128), quarter)]
@@ -1024,9 +1135,6 @@
     def _():
         da2_all[...] = jnp.zeros(da2_all.shape, BF16)
 
-    send_dz()
-    send_two()
-    send_three()
     last_part(
         count, da2_all, k, gb, pack, h1n, h2n, stats, counts, dh2, dh1, sums12, act, acc, hold, *sync[3:]
     )
@@ -1039,7 +1147,6 @@
 
     wait_dz()
     wait_two()
-    wait_three()
 
 
 SUMS = (("k2", 2, True), ("p3", 3, True), ("p2", 2, True), ("p1", 1, True), ("k0", 0, False), ("p0", 0, False))
@@ -1586,21 +1693,6 @@
     return jnp.einsum(dims, a, b, preferred_element_type=F32)
 
 
-def from_section(value, source, section):
-    out = value[source]
-    for t in range(value.shape[0]):
-        if t != source:
-            got = lax.ppermute(value[t], "segment", [(source, t)])
-            out = jnp.where(section == t, got, out)
-    return out
-
-
-def by_share(weights, sections, count, place):
-    rows, width = weights.shape
-    blocks = weights.reshape(sections, count, rows // (sections * count), width)
-    return lax.dynamic_index_in_dim(blocks, place, 1, keepdims=False)
-
-
 def body(
     layer_input,
     output_grad,
@@ -1619,17 +1711,9 @@
     sections = lax.axis_size("segment")
     count = lax.axis_size("dp")
     section = lax.axis_index("segment")
-    place = lax.axis_index("dp")
     first = section == 0
     proj, spatial, shortcut = proj_weight[0], spatial_weight[0], shortcut_weight[0]
     pick = lambda a: lax.dynamic_index_in_dim(a, section, 0, keepdims=False)
-
-    taps_share = from_section(by_share(spatial, sections, count, place), 2, section)
-    two_share = from_section(by_share(proj, sections, count, place), 2, section)
-    three_share = from_section(by_share(proj, sections, count, place), 3, section)
-    k2 = lax.all_gather(taps_share, ("segment", "dp"), axis=0, tiled=True)
-    w2 = lax.all_gather(two_share, ("segment", "dp"), axis=0, tiled=True)
-    w3 = lax.all_gather(three_share, ("segment", "dp"), axis=0, tiled=True)
 
     image_masks, tile_masks, targets = layouts(
         resolution.reshape(-1), tile_order.reshape(micro * images, -1)
@@ -1663,50 +1747,58 @@
     total = rows * micro
     quarter = wide // sections
     dma = pltpu.SemaphoreType.DMA
-    x_all, cols_all, h1n_all, h2n_all, stats_all, counts, gains, y1, u, h3n, stats3, a2, w1, res = (
-        kernel_call(
-            functools.partial(head_kernel, sections, count),
-            [
-                shape_of((total, wide), BF16),
-                shape_of((total, 9 * narrow), BF16),
-                shape_of((total, narrow), F32),
-                shape_of((total, narrow), F32),
-                shape_of((16, narrow), F32),
-                shape_of((8, 128), F32),
-                shape_of((sections, 2, wide), F32),
-                shape_of((padded, wide), BF16),
-                shape_of((padded, wide), BF16),
-                shape_of((padded, wide), F32),
-                shape_of((2, wide), F32),
-                shape_of((padded, narrow), BF16),
-                shape_of((wide, narrow), BF16),
-                shape_of((sections, padded, quarter), BF16),
-            ],
-            [x_in, proj, shortcut, spatial, gb_first, gains_here, pack_all, tiles_all, image_mask, moves],
-            [
-                pltpu.VMEM((narrow // 128, 4 * padded, 128), F32),
-                pltpu.VMEM((micro, padded, narrow), BF16),
-                pltpu.VMEM((padded, narrow), BF16),
-                pltpu.VMEM((wide, quarter), BF16),
-                pltpu.VMEM((wide, narrow), BF16),
-                pltpu.VMEM((micro, padded, quarter), BF16),
-                pltpu.VMEM((sections, padded, quarter), BF16),
-                pltpu.VMEM((sections, 2, wide), F32),
-            ]
-            + sync_scratch(count, [(8, narrow + 128), (8, narrow), (2, wide)])
-            + [dma((sections,)), dma, dma, dma]
-            + [dma((sections,)), dma, dma, dma]
-            + [dma((sections,)), dma((sections,)), dma((sections,)), dma]
-            + [dma((sections,)), dma((sections,)), dma((2,)), dma((3,))],
-            0,
-            2 * total * (narrow * (wide + 9 * narrow) + wide * quarter),
-            60 * 2**20,
-            far_in=(2,),
-            far_out=(11, 12, 13),
-        )
-    )
+    stats_all, counts, gains, y1, u, h3n, stats3, *far = kernel_call(
+        functools.partial(head_kernel, sections, count),
+        [
+            shape_of((16, narrow), F32),
+            shape_of((8, 128), F32),
+            shape_of((sections, 2, wide), F32),
+            shape_of((padded, wide), BF16),
+            shape_of((padded, wide), BF16),
+            shape_of((padded, wide), F32),
+            shape_of((2, wide), F32),
+            shape_of((padded, narrow), BF16),
+            shape_of((wide, narrow), BF16),
+            shape_of((sections, padded, quarter), BF16),
+            shape_of((total, wide), BF16),
+            shape_of((total, 9 * narrow), BF16),
+            shape_of((total, narrow), F32),
+            shape_of((total, narrow), F32),
+            shape_of((wide, narrow), BF16),
+            shape_of((wide, narrow), BF16),
+            shape_of((9 * narrow, narrow), BF16),
+        ],
+        [x_in, proj, shortcut, spatial, gb_first, gains_here, pack_all, tiles_all, image_mask, moves],
+        [
+            pltpu.VMEM((total, wide), BF16),
+            pltpu.VMEM((total, 9 * narrow), BF16),
+            pltpu.VMEM((total, narrow), F32),
+            pltpu.VMEM((total, narrow), F32),
+            pltpu.VMEM((narrow // 128, 4 * padded, 128), F32),
+            pltpu.VMEM((micro, padded, narrow), BF16),
+            pltpu.VMEM((padded, narrow), BF16),
+            pltpu.VMEM((wide, quarter), BF16),
+            pltpu.VMEM((wide, narrow), BF16),
+            pltpu.VMEM((micro, padded, quarter), BF16),
+            pltpu.VMEM((sections, padded, quarter), BF16),
+            pltpu.VMEM((sections, 2, wide), F32),
+        ]
+        + sync_scratch(count, [(8, narrow + 128), (8, narrow), (2, wide)])
+        + [dma((sections,)), dma, dma, dma]
+        + [dma((sections,)), dma, dma, dma]
+        + [dma((sections,)), dma((sections,)), dma((sections,)), dma]
+        + [dma((sections,)), dma((sections,)), dma((2,)), dma((7,))]
+        + [dma((5, sections)), dma((5,)), dma((5,)), dma((5,))]
+        + [dma((5, 2)), dma((5, 2)), dma((3,))],
+        0,
+        2 * total * (narrow * (wide + 9 * narrow) + wide * quarter),
+        60 * 2**20,
+        far_in=(2,),
+        far_out=tuple(range(7, 17)),
+    )
+    a2, w1, res, x_all, cols_all, h1n_all, h2n_all, w3, w2, k2 = far
     paged = shape_of((sections, padded, wide), BF16)
-    y2, t_a2, t_cols, t_dh3, t_dh2, t_dh1, dy1, t_sums, map_one = kernel_call(
+    _, t_a2, t_cols, t_dh3, t_dh2, t_dh1, dy1, t_sums, map_one, map_three = kernel_call(
         functools.partial(tile_kernel, sections, count),
         [
             shape_of((padded, wide), BF16),
@@ -1718,6 +1810,7 @@
             shape_of((padded, wide), BF16),
             shape_of((6, wide), F32),
             paged,
+            paged,
         ],
         [u, w2, k2, w3, og_in, pack_tile, gains, counts, moves_back, y1],
         [
@@ -1728,10 +1821,8 @@
             pltpu.VMEM((padded, wide), BF16),
             pltpu.VMEM((6, wide), F32),
             pltpu.VMEM((padded, wide), F32),
-            dma,
-            dma((sections,)),
-            dma,
         ]
+        + [dma, dma((sections,)), dma] * 2
         + sync_scratch(
             count, [(2, narrow), (2, narrow), (2, wide), (2, wide), (2, narrow), (2, narrow)]
         ),
@@ -1739,9 +1830,9 @@
         4 * padded * narrow * (2 * wide + 9 * narrow),
         30 * 2**20,
         far_in=(9,),
-        far_out=(8,),
-    )
-    dz, dh3, dh2_all, dh1_all, i_sums, f_sums, dz_quarter, map_zero, map_two, map_three = kernel_call(
+        far_out=(8, 9),
+    )
+    dz, dh3, dh2_all, dh1_all, i_sums, f_sums, dz_quarter, map_zero, map_two = kernel_call(
         functools.partial(back_kernel, sections, count),
         [
             shape_of((padded, wide), BF16),
@@ -1753,10 +1844,9 @@
             shape_of((total, quarter), BF16),
             paged,
             paged,
-            paged,
         ],
         [dy1, res, h3n, image_mask, gains, stats3, w1, spatial, gb_first, pack_all]
-        + [h1n_all, h2n_all, stats_all, counts, y2],
+        + [h1n_all, h2n_all, stats_all, counts],
         [
             pltpu.VMEM((padded, narrow), BF16),
             pltpu.VMEM((micro, padded, narrow), BF16),
@@ -1767,12 +1857,11 @@
         ]
         + sync_scratch(count, [(2, wide), (8, narrow), (8, narrow)])
         + [dma, dma((sections,)), dma((sections,)), dma((sections,))]
-        + [dma, dma((sections,)), dma] * 3,
+        + [dma, dma((sections,)), dma] * 2,
         2,
         2 * total * narrow * 9 * narrow,
         40 * 2**20,
-        far_in=(14,),
-        far_out=(7, 8, 9),
+        far_out=(7, 8),
     )
 
     terms = {

time: 677 us -> 598 us (0.88)
  waiting for transfers between devices: 96 us -> 0 us
  Pallas kernels: 469 us -> 512 us
  between operations: 14.5 us -> 1.22 us
  starting transfers between devices: 7.99 us -> 0 us
    all_gather x3 -> x0, waiting for transfers between devices: 75.1 us -> none  [the longest x1 65.6 us: body(): k2 = lax.all_gather(taps_share, ('segment', 'dp'), axis=0, tiled=True)]
    pallas_call x3, Pallas kernels: 278 us -> 307 us  [kernel_call(): pl.pallas_call(kernel, out_shape=outs, in_specs=[pl.BlockSpec(memory_spac...]
    ppermute x9 -> x0, waiting for transfers between devices: 20.9 us -> none  [from_section(): got = lax.ppermute(value[t], 'segment', [(source, t)])]
    pallas_call x1, Pallas kernels: 191 us -> 206 us  [sum_gradients(): pl.pallas_call(functools.partial(gradient_kernel, sections, count), out_s...]
    ppermute x9 -> x0, starting transfers between devices: 7.88 us -> none  [from_section(): got = lax.ppermute(value[t], 'segment', [(source, t)])]
  transfers between devices with their start and end apart: 12 -> 0, of which waited for: 5 -> 0; matrix products, arithmetic and copies ran while one was open for 2% -> 0% of each run, Pallas kernels for 15% -> 0%
where the time goes in v5:
time: 598 us; the launch traced here: 588 us
  Pallas kernels  512 us (86%)
  matrix products  34.1 us (6%)
  other arithmetic  27.2 us (5%)
  local copies, waits for them, and re-layouts  13.3 us (2%)
    pallas_call x3, Pallas kernels, kernel_call(): pl.pallas_call(kernel, out_shape=outs, in_specs=[pl.BlockSpec(memory_spac...  307 us
    pallas_call x1, Pallas kernels, sum_gradients(): pl.pallas_call(functools.partial(gradient_kernel, sections, count), out_s...  206 us
    dot_general x7, matrix products, mm(): return jnp.einsum(dims, a, b, preferred_element_type=F32)  34.1 us

profile of v5, /device:TPU:0, one launch (start us, length us, event | category | flops | bytes accessed | tf_op | source)
XLA Modules:
  0.0 588.0 jit_solution(8011536443542260703)
XLA Ops:
  0.6 0.0 copy-start.3
  0.6 0.0 copy-start.4
  0.7 0.8 copy.42
  1.5 0.1 mul.74
  1.6 0.1 multiply_reduce_fusion
  1.7 0.1 rem.240
  1.8 0.1 div.86
  1.9 0.1 ne.271
  2.0 0.1 add.232
  2.1 0.1 add.238
  2.2 0.1 lt.196
  2.3 0.1 lt.203
  2.4 0.1 and.238
  2.5 0.7 broadcast_add_fusion.2
  3.2 0.1 lt.198
  3.3 0.1 lt.214
  3.4 0.1 copy.44
  3.5 0.7 pad.11.mask
  4.3 0.1 squeeze.36
  4.4 0.1 add.248
  4.4 0.1 add.249
  4.5 0.9 fusion.1
  5.4 0.1 div.84
  5.5 0.1 rem.235
  5.6 0.1 ne.265
  5.7 0.1 lt.199
  5.8 0.1 copy.41
  5.9 0.1 reshape.674
  6.1 0.1 pad.30.clone
  6.2 1.0 maximum_maximum_fusion
  7.1 1.1 copy.45.pack
  8.2 0.1 copy.43
  8.3 1.0 reshape.680.tiles
  9.4 0.0 copy-done.3
  9.4 0.0 copy-done.4
  9.4 0.6 pad_maximum_fusion.1.gb
  10.0 0.6 pad_maximum_fusion.vec
  10.6 115.7 %shard_map.154 = (f32[16,512]{1,0:T(8,128)}, f32[8,128]{1,0:T(8,128)}, f32[4,2,2048]{2,1,0:T(2,128)}, bf16[304,2048]{1,0:T(8,128)(2,1)}, bf16[304,2048]{1,0:T(8,...) custom-call(bf16[294,4,2048]{2,1,0:T(4,128)(2,1)} %bitcast.86, ...), custom_call_target="tpu_custom_call" | custom-call | flops 10481565696 | bytes 62914560 | tf_op jit(solution)/shard_map/pallas_call | solution.py:106
  126.4 0.8 copy.47.pack
  127.2 69.5 %shard_map.155 = (bf16[304,2048]{1,0:T(8,128)(2,1)}, bf16[304,512]{1,0:T(8,128)(2,1)}, bf16[304,4608]{1,0:T(8,128)(2,1)}, bf16[304,2048]{1,0:T(8,128)(2,1)}, bf1...) custom-call(bf16[304,2048]{1,0:T(8,128)(2,1)} %get-tuple-element.46., ...), custom_call_target="tpu_custom_call" | custom-call | flops 5419040768 | bytes 31457280 | tf_op jit(solution)/shard_map/pallas_call | solution.py:106
  196.7 0.9 fusion.22
  197.6 121.4 %shard_map.156 = (bf16[304,2048]{1,0:T(8,128)(2,1)}, bf16[304,2048]{1,0:T(8,128)(2,1)}, bf16[1176,512]{1,0:T(8,128)(2,1)}, bf16[1176,512]{1,0:T(8,128)(2,1)}, f3...) custom-call(bf16[304,2048]{1,0:T(8,128)(2,1)} %get-tuple-element.53., ...), custom_call_target="tpu_custom_call" | custom-call | flops 5549064192 | bytes 41943040 | tf_op jit(solution)/shard_map/pallas_call | solution.py:106
  319.0 0.8 slice_reduce_fusion.1
  319.8 0.8 fusion.24
  320.6 0.9 fusion.21
  321.6 0.1 stack.17
  321.7 0.7 reshape.671.vec
  322.3 7.1 %convolution_convert_fusion.2 = bf16[2048,512]{1,0:T(8,128)(2,1)} fusion(bf16[1176,2048]{1,0:T(8,128)(2,1)} %get-tuple-element.45, bf16[1176,512]{1,0:T(8,128)(2,1)} %get-tuple-element.71.dh1), kind=kOutput, calls=%fused_computation.4 | convolution fusion | flops 2467299328 | bytes 8118272 | tf_op jit(solution)/shard_map/rc,rn->cn/dot_general | solution.py:1693
  329.5 10.6 %convolution_convert_fusion = bf16[4608,512]{1,0:T(8,128)(2,1)} fusion(bf16[1176,4608]{1,0:T(8,128)(2,1)} %get-tuple-element.69, bf16[1176,512]{1,0:T(8,128)(2,1)S(1)} %copy-done.14), kind=kOutput, calls=%fused_computation.2 | convolution fusion | flops 5551423488 | bytes 16760832 | tf_op jit(solution)/shard_map/rk,rn->kn/dot_general | solution.py:1693
  340.1 2.7 convolution_convert_fusion.3
  342.8 2.6 convolution_convert_fusion.4
  345.4 0.0 copy-done.10
  345.4 0.0 slice-start
  345.5 2.6 convolution_convert_fusion.5
  348.1 4.3 convolution_convert_fusion.1
  352.4 0.0 copy-done.13
  352.4 4.1 convolution_convert_fusion.6
  356.5 205.7 %shard_map.157 = (bf16[2,1024,2048]{2,1,0:T(8,128)(2,1)}, bf16[2,4,4,64,512]{4,3,2,1,0:T(8,128)(2,1)}, bf16[2,4,4,144,512]{4,3,2,1,0:T(8,128)(2,1)}, f32[2,2048]{1,0:T(2,128)}, bf16[294,4,2048]{2,1,0:T(4,128)(2,1)}) custom-call(bf16[2,1024,512]{2,1,0:T(8,128)(2,1)} %bitcast.74, bf16[2,4,4,144,512]{4,3,2,1,0:T(8,128)(2,1)} %bitcast.66, ...), custom_call_target="tpu_custom_call" | custom-call | bytes 419430400 | tf_op jit(solution)/shard_map/pallas_call | solution.py:1642
  562.2 12.0 %convert_select_fusion = f32[2,1024,2048]{2,1,0:T(8,128)} fusion(bf16[2,1024,2048]{2,1,0:T(8,128)(2,1)} %get-tuple-element.82, pred[]{:T(512)S(6)} %eq.66), kind=kLoop, calls=%fused_computation | loop fusion | flops 8388608 | bytes 25165824 | tf_op jit(solution)/shard_map/jit(_where)/select_n | solution.py:1911
  574.1 7.5 %convert_select_fusion.1 = f32[2,4,4,144,512]{4,3,2,1,0:T(8,128)} fusion(bf16[2,4,4,144,512]{4,3,2,1,0:T(8,128)(2,1)} %get-tuple-element.81, pred[]{:T(512)S(6)} %eq.67), kind=kLoop, calls=%fused_computation.1 | loop fusion | flops 4718592 | bytes 14155777 | tf_op jit(solution)/shard_map/jit(_where)/select_n | solution.py:1909
  581.7 2.7 convert.5
  584.4 0.6 fusion.23
  585.0 0.6 copy-done
  585.6 2.2 copy.50
  (60 shorter events, 0.3 us)
Async XLA Ops:
  0.6 8.7 %copy-start.3 = (f32[1,2048]{1,0:T(1,128)S(1)}, f32[1,2048]{1,0:T(1,128)}, u32[]{:S(2)}) copy-start(f32[1,2048]{1,0:T(1,128)} %param.18) | copy-start | bytes 24580
  0.6 8.7 %copy-start.4 = (f32[1,2048]{1,0:T(1,128)S(1)}, f32[1,2048]{1,0:T(1,128)}, u32[]{:S(2)}) copy-start(f32[1,2048]{1,0:T(1,128)} %param.19) | copy-start | bytes 24580
  10.6 115.8 %copy-start.2 = (f32[304,15]{0,1:T(8,128)S(1)}, f32[304,15]{0,1:T(8,128)}, u32[]{:S(2)}) copy-start(f32[304,15]{0,1:T(8,128)} %constant.114.clone) | copy-start | bytes 54724
  322.3 7.1 %copy-start.14 = (bf16[1176,512]{1,0:T(8,128)(2,1)S(1)}, bf16[1176,512]{1,0:T(8,128)(2,1)}, u32[]{:S(2)}) copy-start(bf16[1176,512]{1,0:T(8,128)(2,1)} %get-tuple-element.70) | copy-start | bytes 3612676
  329.5 10.6 %copy-start.8 = (bf16[304,2048]{1,0:T(8,128)(2,1)S(1)}, bf16[304,2048]{1,0:T(8,128)(2,1)}, u32[]{:S(2)}) copy-start(bf16[304,2048]{1,0:T(8,128)(2,1)} %get-tuple-element.67) | copy-start | bytes 3735556
  329.5 10.6 %copy-start.9 = (bf16[304,512]{1,0:T(8,128)(2,1)S(1)}, bf16[304,512]{1,0:T(8,128)(2,1)}, u32[]{:S(2)}) copy-start(bf16[304,512]{1,0:T(8,128)(2,1)} %get-tuple-element.68) | copy-start | bytes 933892
  340.0 2.7 copy-start.6
  340.0 2.7 copy-start.11
  342.8 2.7 copy-start.7
  342.8 2.7 copy-start.10
  345.4 2.6 copy-start.12
  345.4 2.6 copy-start.15
  345.4 6.9 %slice-start = ((s8[4816896]{0:T(1024)(128)(4,1)}), s8[4194304]{0:T(1024)(128)(4,1)S(1)}, s32[]{:S(2)}) async-start(s8[4816896]{0:T(1024)(128)(4,1)} %bitcast.90), calls=%async_computation | async-start | bytes 8388608
  348.1 4.3 copy-start.13
  348.1 4.3 slice-start.1
  574.1 7.5 %copy-start.1 = (bf16[2,4,4,64,512]{4,3,2,1,0:T(8,128)(2,1)S(1)}, bf16[2,4,4,64,512]{4,3,2,1,0:T(8,128)(2,1)}, u32[]{:S(2)}) copy-start(bf16[2,4,4,64,512]{4,3,2,1,0:T(8,128)(2,1)} %get-tuple-element.80) | copy-start | bytes 6291460
  581.7 2.7 copy-start.5
  581.7 3.9 copy-start

commit v6 on v5

--- a/solution.py
+++ b/solution.py
@@ -167,7 +167,7 @@
 
 
 def first_part(
-    count, ready, writes, x, w, k, gb, pack, tiles, a2_out, cols, h1n, h2n, stats_out, count_out, act, *sync
+    count, writes, x, w, k, gb, pack, tiles, a2_out, cols, h1n, h2n, stats_out, count_out, act, *sync
 ):
     s1, send1, recv1, s2, send2, recv2 = sync
     rows, narrow = h1n.shape
@@ -187,7 +187,6 @@
     over(narrow, TILE, project)
     s1[me, 0:4, narrow:] = jnp.broadcast_to(by_batch(pack[:, 0:1]), (4, 128))
     s1[me, 4:8, narrow:] = jnp.broadcast_to(by_batch(tiles[:, 0:1]), (4, 128))
-    ready[0]()
     total = exchange(count, s1, send1, recv1)
     counts = total[:, narrow:]
     count_out[...] = counts
@@ -233,7 +232,6 @@
     for write in writes:
         write.start()
     over(narrow, TILE, convolve)
-    ready[1]()
     total = exchange(count, s2, send2, recv2)
     average = total[0:4] / valid
     stats_out[8:12, :] = average
@@ -424,6 +422,10 @@
             for d in (3, 1, 2):
                 spread_copy(i, owner ^ d).start()
 
+    def spread_sent(i):
+        for d in (1, 2, 3):
+            spread_copy(i, parts[i][3] ^ d).wait_send()
+
     def spread_on(i):
         @pl.when(me != parts[i][3])
         def _():
@@ -478,8 +480,10 @@
 
     for k_ in range(1, sections):
         g_copy(k_).start()
-    spread_start(0)
-    spread_start(1)
+    for i in range(3):
+        spread_start(i)
+    for owner, copy in keeps:
+        pl.when(me == owner)(copy.start)
 
     def relayout(j, carry):
         at = pl.ds(pl.multiple_of(j * 128, 128), 128)
@@ -495,34 +499,31 @@
         )
     ]
     writes[0].start()
-    first_part(
-        count,
-        (lambda: spread_start(2), lambda: spread_start(3)),
-        writes[1:3],
-        x,
-        w,
-        k,
-        gb,
-        pack,
-        tiles,
-        a2_all,
-        cols,
-        h1n,
-        h2n,
-        stats_out,
-        count_out,
-        act,
-        *sync[:6],
-    )
-
-    writes[3].start()
-    spread_start(4)
 
     def a2_copy(t):
         return mesh_copy(a2_all.at[t], a2, a2_send.at[t], a2_recv, t, place)
 
     @pl.when(me == 0)
     def _():
+        first_part(
+            count,
+            writes[1:3],
+            x,
+            w,
+            k,
+            gb,
+            pack,
+            tiles,
+            a2_all,
+            cols,
+            h1n,
+            h2n,
+            stats_out,
+            count_out,
+            act,
+            *sync[:6],
+        )
+        writes[3].start()
         for t in range(1, sections):
             a2_copy(t).start()
         a2[...] = a2_all[0]
@@ -530,6 +531,27 @@
 
     @pl.when(me != 0)
     def _():
+        slots, send1, recv1 = sync[:3]
+        narrow = h1n.shape[1]
+        stats_out[...] = jnp.zeros(stats_out.shape, F32)
+        slots[place, :, 0:narrow] = jnp.zeros((8, narrow), F32)
+        slots[place, 0:4, narrow:] = jnp.broadcast_to(by_batch(pack[:, 0:1]), (4, 128))
+        slots[place, 4:8, narrow:] = jnp.broadcast_to(by_batch(tiles[:, 0:1]), (4, 128))
+        count_out[...] = exchange(count, slots, send1, recv1)[:, narrow:]
+
+    def spread_paced(i, after):
+        @pl.when(me == parts[i][3])
+        def _():
+            spread_sent(after)
+            for d in (3, 1, 2):
+                spread_copy(i, parts[i][3] ^ d).start()
+
+    spread_on(0)
+    spread_paced(3, 1)
+    spread_on(1)
+
+    @pl.when(me != 0)
+    def _():
         short_copy(0).wait_recv()
         short_relay.start()
 
@@ -542,8 +564,7 @@
         w1_copy(0).wait_recv()
         w1_relay.start()
 
-    spread_on(0)
-    spread_on(1)
+    spread_on(2)
 
     @pl.when(me != 0)
     def _():
@@ -560,7 +581,7 @@
     for k_ in range(1, sections):
         res_copy(k_).start()
     res[me] = rq[me]
-    spread_on(2)
+    spread_paced(4, 2)
 
     @pl.when(me != 0)
     def _():
@@ -600,8 +621,6 @@
     spread_on(4)
     for copy in writes[4:]:
         copy.start()
-    for owner, copy in keeps:
-        pl.when(me == owner)(copy.start)
     for i in range(2, len(parts)):
         far_on(i)
     for k_ in range(1, sections):
@@ -630,10 +649,8 @@
     for i in range(len(parts)):
         owner = parts[i][3]
 
-        @pl.when(me == owner)
-        def _(i=i, owner=owner):
-            for d in (1, 2, 3):
-                spread_copy(i, owner ^ d).wait_send()
+        if i not in (1, 2):
+            pl.when(me == owner)(functools.partial(spread_sent, i))
 
         @pl.when(me != owner)
         def _(i=i):
@@ -643,8 +660,11 @@
 
     for owner, copy in keeps:
         pl.when(me == owner)(copy.wait)
-    for copy in writes:
-        copy.wait()
+    for i, copy in enumerate(writes):
+        if i in (1, 2, 3):
+            pl.when(me == 0)(copy.wait)
+        else:
+            copy.wait()
 
 
 def back_sums(slots, me, at, grad, hn):
@@ -706,7 +726,6 @@
     dy,
     sums_out,
     map_one,
-    map_three,
     h1n,
     h2n,
     h3n,
@@ -717,9 +736,6 @@
     map_send,
     map_recv,
     map_own,
-    three_send,
-    three_recv,
-    three_own,
     *sync,
 ):
     s1, send1, recv1, s2, send2, recv2, s3, send3, recv3 = sync[:9]
@@ -818,10 +834,6 @@
         back_sums(b3, me, at, grad, hn)
 
     over(wide, 128, result)
-    send_three, wait_three = map_sender(
-        sections, y_out, map_three, 3, three_send, three_recv, three_own
-    )
-    send_three()
     total = exchange(count, b3, bsend3, brecv3)
     sums_out[0:2, :] = total
 
@@ -907,7 +919,6 @@
 
     over(wide, TILE, into_input)
     wait_map()
-    wait_three()
 
 
 def image_back_part(
@@ -1039,6 +1050,10 @@
     h2n,
     stats,
     counts,
+    p3,
+    p2,
+    k2,
+    y2,
     dz,
     dh3,
     dh2,
@@ -1046,8 +1061,12 @@
     sums3,
     sums12,
     dzq_out,
+    p3_out,
+    p2_out,
+    k2_out,
     dz_all,
     map_two,
+    map_three,
     da2,
     da2_all,
     dzq,
@@ -1057,13 +1076,19 @@
     *rest,
 ):
     sync, rest = rest[:9], list(rest[9:])
+    halves, theirs, pieces, totals, chips, wholes = (
+        rest[:3], rest[3:6], rest[6:9], rest[9:11], rest[11:13], rest[13:16]
+    )
+    load_sem, swap_send, swap_recv, piece_send, piece_recv, next_send, next_recv, share_send, share_recv, out_sem = rest[16:26]
+    rest = rest[26:]
     a_send, a_recv, q_send, q_recv = rest[:4]
-    maps = [rest[4:7], rest[7:10]]
+    maps = [rest[4:7], rest[7:10], rest[10:13]]
     me, place = lax.axis_index("segment"), lax.axis_index("dp")
     quarter = dzq.shape[2]
     greet(count, sections)
     send_dz, wait_dz = map_sender(sections, dz, dz_all, 0, *maps[0])
     send_two, wait_two = map_sender(sections, dy, map_two, 2, *maps[1])
+    send_three, wait_three = map_sender(sections, y2, map_three, 3, *maps[2])
 
     def q_copy(k_):
         other = jnp.bitwise_xor(me, k_)
@@ -1071,11 +1096,63 @@
         return mesh_copy(dz.at[:, at], dzq.at[me], q_send.at[k_], q_recv.at[k_], other, place)
 
     greeted(count, sections)
-    send_two()
+    core, z = lax.rem(place, 2), lax.div(place, 2)
+    depth = count // 2
+    terms = (p3, p2, k2)
+    loads = [pltpu.make_async_copy(terms[i].at[core], halves[i], load_sem.at[i]) for i in range(3)]
+    swaps = [
+        mesh_copy(
+            terms[i].at[1 - core],
+            theirs[i],
+            swap_send.at[i],
+            swap_recv.at[i],
+            me,
+            place + 1 - 2 * core,
+        )
+        for i in range(3)
+    ]
+    for i in range(3):
+        swaps[i].start()
+        loads[i].start()
+
+    def to_section(i, k_):
+        other = jnp.bitwise_xor(me, k_)
+        return mesh_copy(
+            halves[i].at[other],
+            pieces[i].at[k_],
+            piece_send.at[i, k_],
+            piece_recv.at[i, k_],
+            other,
+            place,
+        )
+
+    def to_chip(k_):
+        to = lax.rem(z + k_, depth)
+        return mesh_copy(
+            halves[2].at[:, to],
+            pieces[2].at[k_],
+            piece_send.at[2, k_],
+            piece_recv.at[2, k_],
+            me,
+            2 * to + core,
+        )
+
+    def add_cores(i):
+        loads[i].wait()
+        swaps[i].wait_recv()
+
+        def add(n):
+            q, y = lax.div(n, depth), lax.rem(n, depth)
+            halves[i][q, y] = (
+                halves[i][q, y].astype(F32) + theirs[i][q, y].astype(F32)
+            ).astype(BF16)
+
+        loop(0, sections * depth, add)
+
+    send_three()
 
     def after():
-        for k_ in range(1, sections):
-            q_copy(k_).start()
+        return
 
     image_back_part(
         count,
@@ -1104,7 +1181,88 @@
         def _(k_=k_):
             a_copy(k_).start()
 
+    for i in range(2):
+        add_cores(i)
+        for k_ in range(1, sections):
+            to_section(i, k_).start()
+    for k_ in range(1, sections):
+        q_copy(k_).start()
     send_dz()
+    send_two()
+    add_cores(2)
+    loop(1, depth, lambda k_: to_chip(k_).start())
+
+    @pl.when(me == 0)
+    def _():
+        for k_ in range(1, sections):
+            a_copy(k_).wait_recv()
+        da2_all[0] = da2[...]
+        last_part(
+            count,
+            da2_all,
+            k,
+            gb,
+            pack,
+            h1n,
+            h2n,
+            stats,
+            counts,
+            dh2,
+            dh1,
+            sums12,
+            act,
+            acc,
+            hold,
+            *sync[3:],
+        )
+
+    @pl.when(me != 0)
+    def _():
+        a_copy(0).wait_send()
+        sums12[...] = jnp.zeros(sums12.shape, F32)
+
+    def next_chip(i, k_):
+        to = lax.rem(z + k_, depth)
+        return mesh_copy(
+            totals[i].at[to],
+            chips[i].at[k_],
+            next_send.at[i, k_],
+            next_recv.at[i, k_],
+            me,
+            2 * to + core,
+        )
+
+    def share(i, k_):
+        return mesh_copy(
+            wholes[i].at[z],
+            wholes[i].at[z],
+            share_send.at[i, k_],
+            share_recv.at[i, k_],
+            me,
+            2 * lax.rem(z + k_, depth) + core,
+        )
+
+    for i in range(2):
+        for k_ in range(1, sections):
+            to_section(i, k_).wait_recv()
+
+        def p_sum(y, i=i):
+            total = halves[i][me, y].astype(F32)
+            for k_ in range(1, sections):
+                total = total + pieces[i][k_, y].astype(F32)
+            totals[i][y] = total.astype(BF16)
+
+        loop(0, depth, p_sum)
+        loop(1, depth, lambda k_, i=i: next_chip(i, k_).start())
+    loop(1, depth, lambda k_: to_chip(k_).wait_recv())
+
+    def k2_sum(q):
+        total = halves[2][q, z].astype(F32)
+        for k_ in range(1, depth):
+            total = total + pieces[2][k_, q].astype(F32)
+        wholes[2][q] = total.astype(BF16)
+
+    loop(0, sections, k2_sum)
     for k_ in range(1, sections):
         q_copy(k_).wait_recv()
     dzq[me] = dz[:, pl.ds(pl.multiple_of(me * quarter, 128), quarter)]
@@ -1124,44 +1282,56 @@
         return carry
 
     lax.fori_loop(0, quarter // 128, weave, 0)
-
-    @pl.when(me == 0)
-    def _():
-        for k_ in range(1, sections):
-            a_copy(k_).wait_recv()
-        da2_all[0] = da2[...]
-
-    @pl.when(me != 0)
-    def _():
-        da2_all[...] = jnp.zeros(da2_all.shape, BF16)
-
-    last_part(
-        count, da2_all, k, gb, pack, h1n, h2n, stats, counts, dh2, dh1, sums12, act, acc, hold, *sync[3:]
-    )
+    for i in range(2):
+        loop(1, depth, lambda k_, i=i: next_chip(i, k_).wait_recv())
+        total = totals[i][z].astype(F32)
+        for k_ in range(1, depth):
+            total = total + chips[i][k_].astype(F32)
+        wholes[i][z] = total.astype(BF16)
+        loop(1, depth, lambda k_, i=i: share(i, k_).start())
+    outs = []
+    for i, out in enumerate((p3_out, p2_out, k2_out)):
+        if i < 2:
+            loop(1, depth, lambda k_, i=i: share(i, k_).wait_recv())
+        outs.append(pltpu.make_async_copy(wholes[i], out, out_sem.at[i]))
+        outs[i].start()
     for k_ in range(1, sections):
         q_copy(k_).wait_send()
-
-    @pl.when(me != 0)
-    def _():
-        a_copy(0).wait_send()
-
+        for i in range(2):
+            to_section(i, k_).wait_send()
+    loop(1, depth, lambda k_: to_chip(k_).wait_send())
+    for i in range(2):
+        loop(1, depth, lambda k_, i=i: next_chip(i, k_).wait_send())
+    for i in range(3):
+        swaps[i].wait_send()
+        if i < 2:
+            loop(1, depth, lambda k_, i=i: share(i, k_).wait_send())
+        outs[i].wait()
     wait_dz()
     wait_two()
-
-
-SUMS = (("k2", 2, True), ("p3", 3, True), ("p2", 2, True), ("p1", 1, True), ("k0", 0, False), ("p0", 0, False))
+    wait_three()
+
+
+SUMS = (
+    ("k0", 0, "owner"),
+    ("p0", 0, "owner"),
+    ("p1", 1, "each"),
+    ("p3", 3, "done"),
+    ("p2", 2, "done"),
+    ("k2", 2, "chips"),
+)
 
 
 def gradient_kernel(
     sections,
     count,
     sh,
-    k2,
+    k0,
+    p0,
+    p1,
     p3,
     p2,
-    p1,
-    k0,
-    p0,
+    k2,
     vec,
     dh1,
     w,
@@ -1178,9 +1348,10 @@
     *scratch,
 ):
     names = [name for name, _, _ in SUMS]
-    terms = dict(zip(names, (k2, p3, p2, p1, k0, p0)))
+    terms = dict(zip(names, (k0, p0, p1, p3, p2, k2)))
     owner = {name: section for name, section, _ in SUMS}
-    spread = {name: part for name, _, part in SUMS}
+    held = {name: kind for name, _, kind in SUMS}
+    fresh = [name for name in names if held[name] in ("owner", "each")]
     depth = count // 2
     me, place = lax.axis_index("segment"), lax.axis_index("dp")
     core, z = lax.rem(place, 2), lax.div(place, 2)
@@ -1189,13 +1360,19 @@
     take = lambda: scratch.pop(0)
     half, theirs, planes, total, others, whole = {}, {}, {}, {}, {}, {}
     for name in names:
-        half[name], theirs[name] = take(), take()
-        if spread[name]:
+        if name in fresh:
+            half[name], theirs[name] = take(), take()
+        if held[name] in ("each", "chips"):
             planes[name] = take()
-        total[name], others[name], whole[name] = take(), take(), take()
+        if name in fresh:
+            total[name], others[name] = take(), take()
+        whole[name] = terms[name] if held[name] == "done" else take()
+    relay = {name: take() for name in names if owner[name] == 0}
+    relay["sh"] = take()
     sh_half, sh_theirs, sh_others, sh_whole, vec_slots = take(), take(), take(), take(), take()
     load_sem, a_send, a_recv, b_send, b_recv, c_send, c_recv, d_send, d_recv = (take() for _ in range(9))
     e_send, e_recv, e_own, f_send, f_recv, v_send, v_recv = (take() for _ in range(7))
+    r_send, r_recv = take(), take()
     pages, s_rows, w_rows, hold, stage, page_sem, s_sem, w_sem, stage_sem = (take() for _ in range(9))
     slot = {name: i for i, name in enumerate(names)}
     last = len(names)
@@ -1301,7 +1478,7 @@
         return pltpu.make_async_copy(terms[name].at[core], half[name], load_sem.at[slot[name]])
 
     def when_held(name, body):
-        if spread[name]:
+        if held[name] == "each":
             body()
         else:
             pl.when(me == owner[name])(body)
@@ -1322,13 +1499,60 @@
 
     for k in range(1, sections):
         vec_copy(k).start()
-    for name in names:
+    for name in fresh:
 
         def begin(name=name):
             swap(name).start()
             load(name).start()
 
         when_held(name, begin)
+
+    def final(name):
+        return k_out if name[0] == "k" else p_out
+
+    def deliver(name, k):
+        return mesh_copy(
+            whole[name],
+            final(name).at[core, me],
+            e_send.at[slot[name]],
+            e_recv.at[slot[name], k],
+            owner[name],
+            place,
+        )
+
+    def keep_own(name):
+        return pltpu.make_async_copy(whole[name], final(name).at[core, me], e_own.at[slot[name]])
+
+    def to_plane(name, k):
+        other = jnp.bitwise_xor(me, k)
+        return mesh_copy(
+            terms[name].at[other],
+            planes[name].at[k],
+            b_send.at[slot[name], k],
+            b_recv.at[slot[name], k],
+            other,
+            place,
+        )
+
+    def load_plane(name):
+        return pltpu.make_async_copy(terms[name].at[me], planes[name].at[0], load_sem.at[slot[name]])
+
+    for name in names:
+        if held[name] == "chips":
+            for k in range(1, sections):
+                to_plane(name, k).start()
+            load_plane(name).start()
+        if held[name] == "done":
+
+            @pl.when(me == owner[name])
+            def _(name=name):
+                keep_own(name).start()
+
+            for k in range(1, sections):
+
+                @pl.when(me == owner[name] ^ k)
+                def _(name=name, k=k):
+                    deliver(name, k).start()
 
     piece = sh_rows // depth
     step = 32
@@ -1359,7 +1583,7 @@
 
     def to_section(name, k):
         other = jnp.bitwise_xor(me, k)
-        target = planes[name].at[k] if spread[name] else total[name]
+        target = planes[name].at[k] if held[name] == "each" else total[name]
         return mesh_copy(
             half[name].at[other],
             target,
@@ -1369,7 +1593,7 @@
             place,
         )
 
-    for name in names:
+    for name in fresh:
 
         def combine(name=name):
             load(name).wait()
@@ -1390,6 +1614,16 @@
     for i, copy in enumerate(page_loads):
         pl.when(me == i)(copy.wait)
     loop(0, 2, map_tile)
+
+    def share(name, k):
+        return mesh_copy(
+            whole[name].at[z],
+            whole[name].at[z],
+            d_send.at[slot[name], k],
+            d_recv.at[slot[name], k],
+            me,
+            chip(k),
+        )
 
     loop(1, depth, lambda k: sh_send(k).wait_recv())
     mine = sh_at(z)
@@ -1410,6 +1644,16 @@
 
     loop(1, depth, lambda k: sh_share(k).start())
     loop(2, wide // TILE, map_tile)
+
+    for name in names:
+        if held[name] == "chips":
+            load_plane(name).wait()
+            acc = planes[name][0].astype(F32)
+            for k in range(1, sections):
+                to_plane(name, k).wait_recv()
+                acc = acc + planes[name][k].astype(F32)
+            whole[name][z] = acc.astype(BF16)
+            loop(1, depth, lambda k, name=name: share(name, k).start())
 
     def to_chip(name, k):
         to = lax.rem(z + k, depth)
@@ -1422,8 +1666,8 @@
             2 * to + core,
         )
 
-    for name in names:
-        if spread[name]:
+    for name in fresh:
+        if held[name] == "each":
             for k in range(1, sections):
                 to_section(name, k).wait_recv()
 
@@ -1470,23 +1714,7 @@
     def _():
         sh_keep.start()
 
-    for k in range(1, sections):
-
-        @pl.when(me == k)
-        def _(k=k):
-            sh_deliver(k).start()
-
-    def share(name, k):
-        return mesh_copy(
-            whole[name].at[z],
-            whole[name].at[z],
-            d_send.at[slot[name], k],
-            d_recv.at[slot[name], k],
-            me,
-            chip(k),
-        )
-
-    for name in names:
+    for name in fresh:
         loop(1, depth, lambda k, name=name: to_chip(name, k).wait_recv())
         acc = total[name][z].astype(F32)
         for k in range(1, depth):
@@ -1494,34 +1722,51 @@
         whole[name][z] = acc.astype(BF16)
         loop(1, depth, lambda k, name=name: share(name, k).start())
 
-    def final(name):
-        return k_out if name[0] == "k" else p_out
-
-    def deliver(name, k):
-        return mesh_copy(
-            whole[name],
-            final(name).at[core, me],
-            e_send.at[slot[name]],
-            e_recv.at[slot[name], k],
-            owner[name],
-            place,
-        )
-
-    def keep_own(name):
-        return pltpu.make_async_copy(whole[name], final(name).at[core, me], e_own.at[slot[name]])
-
-    for name in names:
+    def relayed(name, onward):
+        index = last if name == "sh" else slot[name]
+        at = pl.ds(3 * sh_whole.shape[1], sh_whole.shape[1])
+        src, dst = (sh_whole, sh_out.at[core, :, at]) if name == "sh" else (whole[name], final(name).at[core, 3])
+        if onward:
+            return mesh_copy(relay[name], dst, r_send.at[index], e_recv.at[index, 3], 0, place)
+        return mesh_copy(src, relay[name], e_send.at[index], r_recv.at[index], 1, place)
+
+    def start_delivery(name):
+        index = last if name == "sh" else slot[name]
+        section = 0 if name == "sh" else owner[name]
+        copy = sh_deliver if name == "sh" else functools.partial(deliver, name)
+        for k in range(1, sections):
+            direct = me == section ^ k
+            if section == 0 and k == 3:
+                direct = direct & (core == 0)
+
+                @pl.when((me == 3) & (core == 1))
+                def _():
+                    relayed(name, False).start()
+
+            @pl.when(direct)
+            def _(k=k):
+                copy(k).start()
+
+    def pass_on(name):
+        @pl.when((me == 1) & (core == 1))
+        def _():
+            relayed(name, False).wait_recv()
+            relayed(name, True).start()
+
+    start_delivery("sh")
+    for name in ["k2"] + fresh:
+        if name == fresh[-1]:
+            pass_on("sh")
         loop(1, depth, lambda k, name=name: share(name, k).wait_recv())
 
         @pl.when(me == owner[name])
         def _(name=name):
             keep_own(name).start()
 
-        for k in range(1, sections):
-
-            @pl.when(me == owner[name] ^ k)
-            def _(name=name, k=k):
-                deliver(name, k).start()
+        start_delivery(name)
+    for name in fresh:
+        if owner[name] == 0:
+            pass_on(name)
 
     def cross(name):
         return mesh_copy(
@@ -1576,6 +1821,11 @@
     def _():
         sh_deliver(0).wait_send()
 
+    @pl.when((me == 1) & (core == 1))
+    def _():
+        for name in relay:
+            relayed(name, True).wait_send()
+
     for name in names:
 
         def sent(name=name):
@@ -1583,9 +1833,14 @@
             for k in range(1, sections):
                 to_section(name, k).wait_send()
 
-        when_held(name, sent)
-        loop(1, depth, lambda k, name=name: to_chip(name, k).wait_send())
-        loop(1, depth, lambda k, name=name: share(name, k).wait_send())
+        if name in fresh:
+            when_held(name, sent)
+            loop(1, depth, lambda k, name=name: to_chip(name, k).wait_send())
+        if held[name] == "chips":
+            for k in range(1, sections):
+                to_plane(name, k).wait_send()
+        if held[name] != "done":
+            loop(1, depth, lambda k, name=name: share(name, k).wait_send())
 
         @pl.when(me == owner[name])
         def _(name=name):
@@ -1600,15 +1855,25 @@
     narrow = short.shape[1]
     depth = count // 2
     args, scratch = [], []
-    for name, _, part in SUMS:
-        rows = terms[name].shape[0]
-        fine = rows // (2 * sections * depth)
-        args.append(terms[name].reshape(2, sections, depth, fine, narrow))
-        shapes = [(sections, depth, fine, narrow)] * 2
-        if part:
-            shapes.append((sections, depth, fine, narrow))
-        shapes += [(depth, fine, narrow)] * 3
+    relays = []
+    for name, section, kind in SUMS:
+        args.append(terms[name])
+        full = (sections, depth) + terms[name].shape[-2:]
+        shapes = []
+        if kind in ("owner", "each"):
+            shapes += [full, full]
+        if kind == "each":
+            shapes.append(full)
+        if kind == "chips":
+            shapes.append((sections,) + full[2:])
+        if kind in ("owner", "each"):
+            shapes += [full[1:]] * 2
+        if kind != "done":
+            shapes.append(full[1:])
+        if section == 0:
+            relays.append(pltpu.VMEM(full[1:], BF16))
         scratch += [pltpu.VMEM(a, BF16) for a in shapes]
+    scratch += relays + [pltpu.VMEM((short.shape[0] // 2, narrow), BF16)]
     sh_rows = short.shape[0] // 2
     scratch += [
         pltpu.VMEM((sh_rows, narrow), BF16),
@@ -1620,7 +1885,7 @@
     kinds = len(SUMS) + 1
     for shape in [(kinds,)] * 3 + [(kinds, sections)] * 2 + [(kinds, depth)] * 4:
         scratch.append(pltpu.SemaphoreType.DMA(shape))
-    for shape in [(kinds,), (kinds, sections), (kinds,), (kinds,), (kinds,), (sections,), (sections,)]:
+    for shape in [(kinds,), (kinds, sections), (kinds,), (kinds,), (kinds,), (sections,), (sections,), (kinds,), (kinds,)]:
         scratch.append(pltpu.SemaphoreType.DMA(shape))
     wide = w.shape[0]
     padded = map_sources[0].shape[1]
@@ -1637,8 +1902,7 @@
     ]
     hbm = pl.BlockSpec(memory_space=pl.ANY)
     vmem = pl.BlockSpec(memory_space=pltpu.VMEM)
-    proj_shape = args[1].shape
-    taps_shape = args[0].shape
+    taps_shape, proj_shape = args[0].shape, args[1].shape
     return pl.pallas_call(
         functools.partial(gradient_kernel, sections, count),
         out_shape=[
@@ -1798,7 +2062,7 @@
     )
     a2, w1, res, x_all, cols_all, h1n_all, h2n_all, w3, w2, k2 = far
     paged = shape_of((sections, padded, wide), BF16)
-    _, t_a2, t_cols, t_dh3, t_dh2, t_dh1, dy1, t_sums, map_one, map_three = kernel_call(
+    y2, t_a2, t_cols, t_dh3, t_dh2, t_dh1, dy1, t_sums, map_one = kernel_call(
         functools.partial(tile_kernel, sections, count),
         [
             shape_of((padded, wide), BF16),
@@ -1809,7 +2073,6 @@
             shape_of((padded, narrow), BF16),
             shape_of((padded, wide), BF16),
             shape_of((6, wide), F32),
-            paged,
             paged,
         ],
         [u, w2, k2, w3, og_in, pack_tile, gains, counts, moves_back, y1],
@@ -1822,7 +2085,7 @@
             pltpu.VMEM((6, wide), F32),
             pltpu.VMEM((padded, wide), F32),
         ]
-        + [dma, dma((sections,)), dma] * 2
+        + [dma, dma((sections,)), dma]
         + sync_scratch(
             count, [(2, narrow), (2, narrow), (2, wide), (2, wide), (2, narrow), (2, narrow)]
         ),
@@ -1830,47 +2093,73 @@
         4 * padded * narrow * (2 * wide + 9 * narrow),
         30 * 2**20,
         far_in=(9,),
-        far_out=(8, 9),
+        far_out=(8,),
     )
-    dz, dh3, dh2_all, dh1_all, i_sums, f_sums, dz_quarter, map_zero, map_two = kernel_call(
-        functools.partial(back_kernel, sections, count),
-        [
-            shape_of((padded, wide), BF16),
-            shape_of((padded, wide), BF16),
-            shape_of((total, narrow), BF16),
-            shape_of((total, narrow), BF16),
-            shape_of((2, wide), F32),
-            shape_of((16, narrow), F32),
-            shape_of((total, quarter), BF16),
-            paged,
-            paged,
-        ],
-        [dy1, res, h3n, image_mask, gains, stats3, w1, spatial, gb_first, pack_all]
-        + [h1n_all, h2n_all, stats_all, counts],
-        [
-            pltpu.VMEM((padded, narrow), BF16),
-            pltpu.VMEM((micro, padded, narrow), BF16),
-            pltpu.VMEM((micro, padded, quarter), BF16),
-            pltpu.VMEM((narrow // 128, 4 * padded, 128), F32),
-            pltpu.VMEM((total, narrow), F32),
-            pltpu.VMEM((total, narrow), BF16),
-        ]
-        + sync_scratch(count, [(2, wide), (8, narrow), (8, narrow)])
-        + [dma, dma((sections,)), dma((sections,)), dma((sections,))]
-        + [dma, dma((sections,)), dma] * 2,
-        2,
-        2 * total * narrow * 9 * narrow,
-        40 * 2**20,
-        far_out=(7, 8),
+    depth = count // 2
+
+    def split(term):
+        return term.astype(BF16).reshape(
+            2, sections, depth, term.shape[0] // (2 * sections * depth), narrow
+        )
+
+    p3_term = split(mm(t_dh3, t_a2, "rd,rk->dk"))
+    k2_term = split(mm(t_cols, t_dh2, "rk,rn->kn"))
+    p2_term = split(mm(u, t_dh1, "rc,rn->cn"))
+    proj_piece, taps_piece = p3_term.shape[3], k2_term.shape[3]
+    dz, dh3, dh2_all, dh1_all, i_sums, f_sums, dz_quarter, p3_part, p2_part, k2_part, map_zero, map_two, map_three = (
+        kernel_call(
+            functools.partial(back_kernel, sections, count),
+            [
+                shape_of((padded, wide), BF16),
+                shape_of((padded, wide), BF16),
+                shape_of((total, narrow), BF16),
+                shape_of((total, narrow), BF16),
+                shape_of((2, wide), F32),
+                shape_of((16, narrow), F32),
+                shape_of((total, quarter), BF16),
+                shape_of((depth, proj_piece, narrow), BF16),
+                shape_of((depth, proj_piece, narrow), BF16),
+                shape_of((sections, taps_piece, narrow), BF16),
+                paged,
+                paged,
+                paged,
+            ],
+            [dy1, res, h3n, image_mask, gains, stats3, w1, spatial, gb_first, pack_all]
+            + [h1n_all, h2n_all, stats_all, counts, p3_term, p2_term, k2_term, y2],
+            [
+                pltpu.VMEM((padded, narrow), BF16),
+                pltpu.VMEM((micro, padded, narrow), BF16),
+                pltpu.VMEM((micro, padded, quarter), BF16),
+                pltpu.VMEM((narrow // 128, 4 * padded, 128), F32),
+                pltpu.VMEM((total, narrow), F32),
+                pltpu.VMEM((total, narrow), BF16),
+            ]
+            + sync_scratch(count, [(2, wide), (8, narrow), (8, narrow)])
+            + [pltpu.VMEM(a.shape[1:], BF16) for a in (p3_term, p2_term, k2_term)] * 2
+            + [pltpu.VMEM(p3_term.shape[1:], BF16)] * 2
+            + [pltpu.VMEM((depth, sections, taps_piece, narrow), BF16)]
+            + [pltpu.VMEM((depth, proj_piece, narrow), BF16)] * 6
+            + [pltpu.VMEM((sections, taps_piece, narrow), BF16)]
+            + [dma((3,))] * 3
+            + [dma((3, max(sections, depth)))] * 6
+            + [dma((3,))]
+            + [dma, dma((sections,)), dma((sections,)), dma((sections,))]
+            + [dma, dma((sections,)), dma] * 3,
+            2,
+            2 * total * narrow * 9 * narrow,
+            40 * 2**20,
+            far_in=(14, 15, 16, 17),
+            far_out=(7, 8, 9, 10, 11, 12),
+        )
     )
 
     terms = {
-        "p3": mm(t_dh3, t_a2, "rd,rk->dk").astype(BF16),
-        "k2": mm(t_cols, t_dh2, "rk,rn->kn").astype(BF16),
-        "p2": mm(u, t_dh1, "rc,rn->cn").astype(BF16),
-        "p1": mm(dh3, a2, "rd,rk->dk").astype(BF16),
-        "k0": mm(cols_all, dh2_all, "rk,rn->kn").astype(BF16),
-        "p0": mm(x_all, dh1_all, "rc,rn->cn").astype(BF16),
+        "p3": p3_part,
+        "k2": k2_part,
+        "p2": p2_part,
+        "p1": split(mm(dh3, a2, "rd,rk->dk")),
+        "k0": split(mm(cols_all, dh2_all, "rk,rn->kn")),
+        "p0": split(mm(x_all, dh1_all, "rc,rn->cn")),
     }
     short_term = mm(x_all, dz_quarter, "rc,rd->cd").astype(BF16)
 

time: 598 us -> 580 us (0.970)
  the two profiles are of different devices: /device:TPU:0 before, /device:TPU:25 now
where the time goes in v6:
time: 580 us; the launch traced here: 571 us
  Pallas kernels  492 us (85%)
  matrix products  37.8 us (7%)
  other arithmetic  27 us (5%)
  local copies, waits for them, and re-layouts  13.5 us (2%)
    pallas_call x3, Pallas kernels, kernel_call(): pl.pallas_call(kernel, out_shape=outs, in_specs=[pl.BlockSpec(memory_spac...  308 us
    pallas_call x1, Pallas kernels, sum_gradients(): pl.pallas_call(functools.partial(gradient_kernel, sections, count), out_s...  184 us
    dot_general x7, matrix products, mm(): return jnp.einsum(dims, a, b, preferred_element_type=F32)  37.8 us
    select_n x1, other arithmetic, body(): short_grad = jnp.where(first, short_grad, jnp.zeros_like(short_grad))  12 us

profile of v6, /device:TPU:25, one launch (start us, length us, event | category | flops | bytes accessed | tf_op | source)
XLA Modules:
  0.0 571.4 jit_solution(4043665811264335873)
XLA Ops:
  0.7 0.1 pad.30.clone
  0.8 0.1 and.238
  0.9 0.7 broadcast_add_fusion.2
  1.6 0.1 lt.203
  1.7 0.1 add.248
  1.8 0.1 add.249
  1.8 0.1 add.238
  1.9 0.1 add.232
  2.0 0.1 lt.196
  2.1 0.7 fusion.25
  2.8 0.6 pad_maximum_fusion.1.gb
  3.5 0.1 lt.198
  3.5 0.1 lt.214
  3.6 0.1 lt.199
  3.7 1.3 pad_maximum_fusion.vec
  5.0 0.8 copy.42
  5.8 0.1 mul.74
  5.9 0.1 multiply_reduce_fusion
  6.0 0.1 ne.271
  6.1 0.1 ne.265
  6.2 0.1 rem.240
  6.3 0.1 div.86
  6.5 0.1 div.84
  6.5 0.1 rem.235
  6.7 0.1 squeeze.36
  6.8 0.7 select_maximum_fusion
  7.6 0.8 copy.47.pack
  8.4 0.1 copy.43
  8.5 0.1 copy.41
  8.6 0.1 reshape.674
  8.8 1.0 maximum_maximum_fusion
  9.8 0.1 copy.44
  9.9 0.7 pad.11.mask
  10.6 1.0 reshape.680.tiles
  11.6 0.9 fusion.1
  12.5 1.1 copy.45.pack
  13.5 99.5 %shard_map.154 = (f32[16,512]{1,0:T(8,128)}, f32[8,128]{1,0:T(8,128)}, f32[4,2,2048]{2,1,0:T(2,128)}, bf16[304,2048]{1,0:T(8,128)(2,1)}, bf16[304,2048]{1,0:T(8,...) custom-call(bf16[294,4,2048]{2,1,0:T(4,128)(2,1)} %bitcast.90, ...), custom_call_target="tpu_custom_call" | custom-call | flops 10481565696 | bytes 62914560 | tf_op jit(solution)/shard_map/pallas_call | solution.py:106
  113.1 0.0 copy-start.6
  113.1 79.5 %shard_map.155 = (bf16[304,2048]{1,0:T(8,128)(2,1)}, bf16[304,512]{1,0:T(8,128)(2,1)}, bf16[304,4608]{1,0:T(8,128)(2,1)}, bf16[304,2048]{1,0:T(8,128)(2,1)}, bf1...) custom-call(bf16[304,2048]{1,0:T(8,128)(2,1)} %get-tuple-element.50., ...), custom_call_target="tpu_custom_call" | custom-call | flops 5419040768 | bytes 31457280 | tf_op jit(solution)/shard_map/pallas_call | solution.py:106
  192.6 0.0 copy-start.7
  192.6 0.0 copy-start.9
  192.6 0.9 fusion.22
  193.5 0.9 fusion.21
  194.4 0.0 copy-done.6
  194.4 3.6 convolution_convert_fusion.5
  198.0 2.6 convolution_convert_fusion.6
  200.7 4.3 convolution_convert_fusion.1
  204.9 129.3 %shard_map.156 = (bf16[304,2048]{1,0:T(8,128)(2,1)}, bf16[304,2048]{1,0:T(8,128)(2,1)}, bf16[1176,512]{1,0:T(8,128)(2,1)}, bf16[1176,512]{1,0:T(8,128)(2,1)}, f3...) custom-call(bf16[304,2048]{1,0:T(8,128)(2,1)} %get-tuple-element.57., ...), custom_call_target="tpu_custom_call" | custom-call | flops 5549064192 | bytes 41943040 | tf_op jit(solution)/shard_map/pallas_call | solution.py:106
  334.2 0.0 copy-start.2
  334.2 0.0 copy-start.3
  334.2 0.0 copy-start.5
  334.2 11.0 %convolution_convert_fusion = bf16[4608,512]{1,0:T(8,128)(2,1)} fusion(bf16[1176,4608]{1,0:T(8,128)(2,1)} %get-tuple-element.72, bf16[1176,512]{1,0:T(8,128)(2,1)} %get-tuple-element.73), kind=kOutput, calls=%fused_computation.2 | convolution fusion | flops 5551423488 | bytes 16760832 | tf_op jit(solution)/shard_map/rk,rn->kn/dot_general | solution.py:1957
  345.3 0.1 stack.17
  345.4 0.7 reshape.671.vec
  346.1 6.9 %convolution_convert_fusion.4 = bf16[2048,512]{1,0:T(8,128)(2,1)} fusion(bf16[1176,2048]{1,0:T(8,128)(2,1)} %get-tuple-element.49, bf16[1176,512]{1,0:T(8,128)(2,1)S(1)} %copy-done.5), kind=kOutput, calls=%fused_computation.6 | convolution fusion | flops 2467299328 | bytes 8118272 | tf_op jit(solution)/shard_map/rc,rd->cd/dot_general | solution.py:1957
  352.9 6.9 %convolution_convert_fusion.3 = bf16[2048,512]{1,0:T(8,128)(2,1)} fusion(bf16[1176,2048]{1,0:T(8,128)(2,1)} %get-tuple-element.49, bf16[1176,512]{1,0:T(8,128)(2,1)S(1)} %copy-done.1), kind=kOutput, calls=%fused_computation.5 | convolution fusion | flops 2467299328 | bytes 8118272 | tf_op jit(solution)/shard_map/rc,rn->cn/dot_general | solution.py:1957
  359.8 2.6 convolution_convert_fusion.2
  362.4 183.7 %shard_map.157 = (bf16[2,1024,2048]{2,1,0:T(8,128)(2,1)}, bf16[2,4,4,64,512]{4,3,2,1,0:T(8,128)(2,1)}, bf16[2,4,4,144,512]{4,3,2,1,0:T(8,128)(2,1)}, f32[2,2048]{1,0:T(2,128)}, bf16[294,4,2048]{2,1,0:T(4,128)(2,1)}) custom-call(bf16[2,1024,512]{2,1,0:T(8,128)(2,1)} %bitcast.74, bf16[2,4,4,144,512]{4,3,2,1,0:T(8,128)(2,1)} %bitcast.69, ...), custom_call_target="tpu_custom_call" | custom-call | bytes 419430400 | tf_op jit(solution)/shard_map/pallas_call | solution.py:1906
  546.1 1.4 fusion.23
  547.5 4.3 convert.5
  551.9 0.0 copy-done
  551.9 5.1 convert_select_fusion.1
  557.0 12.0 %convert_select_fusion = f32[2,1024,2048]{2,1,0:T(8,128)} fusion(bf16[2,1024,2048]{2,1,0:T(8,128)(2,1)} %get-tuple-element.90, pred[]{:T(512)S(6)} %eq.66), kind=kLoop, calls=%fused_computation | loop fusion | flops 8388608 | bytes 25165824 | tf_op jit(solution)/shard_map/jit(_where)/select_n | solution.py:2200
  569.0 2.2 copy.50
  (52 shorter events, 0.4 us)
Async XLA Ops:
  113.1 81.4 %copy-start.6 = (bf16[304,2048]{1,0:T(8,128)(2,1)S(1)}, bf16[304,2048]{1,0:T(8,128)(2,1)}, u32[]{:S(2)}) copy-start(bf16[304,2048]{1,0:T(8,128)(2,1)} %get-tuple-element.50.u) | copy-start | bytes 3735556
  192.6 5.5 copy-start.7
  192.6 5.5 copy-start.9
  198.0 2.6 copy-start.10
  198.0 2.6 copy-start.11
  334.2 11.0 %copy-start.2 = (f32[16,512]{1,0:T(8,128)S(1)}, f32[16,512]{1,0:T(8,128)}, u32[]{:S(2)}) copy-start(f32[16,512]{1,0:T(8,128)} %get-tuple-element.80) | copy-start | bytes 98308
  334.2 11.1 %copy-start.3 = (f32[2,2048]{1,0:T(2,128)S(1)}, f32[2,2048]{1,0:T(2,128)}, u32[]{:S(2)}) copy-start(f32[2,2048]{1,0:T(2,128)} %get-tuple-element.81) | copy-start | bytes 49156
  334.2 11.9 %copy-start.5 = (bf16[1176,512]{1,0:T(8,128)(2,1)S(1)}, bf16[1176,512]{1,0:T(8,128)(2,1)}, u32[]{:S(2)}) copy-start(bf16[1176,512]{1,0:T(8,128)(2,1)} %get-tuple-element.71) | copy-start | bytes 3612676
  346.1 6.9 %copy-start.1 = (bf16[1176,512]{1,0:T(8,128)(2,1)S(1)}, bf16[1176,512]{1,0:T(8,128)(2,1)}, u32[]{:S(2)}) copy-start(bf16[1176,512]{1,0:T(8,128)(2,1)} %get-tuple-element.74.dh1) | copy-start | bytes 3612676
  352.9 6.9 %copy-start.4 = (bf16[304,2048]{1,0:T(8,128)(2,1)S(1)}, bf16[304,2048]{1,0:T(8,128)(2,1)}, u32[]{:S(2)}) copy-start(bf16[304,2048]{1,0:T(8,128)(2,1)} %get-tuple-element.75) | copy-start | bytes 3735556
  352.9 6.9 %copy-start.8 = (bf16[304,512]{1,0:T(8,128)(2,1)S(1)}, bf16[304,512]{1,0:T(8,128)(2,1)}, u32[]{:S(2)}) copy-start(bf16[304,512]{1,0:T(8,128)(2,1)} %get-tuple-element.76) | copy-start | bytes 933892
  547.5 4.4 copy-start
  551.9 17.1 %slice-start = ((s8[4816896]{0:T(1024)(128)(4,1)}), s8[4194304]{0:T(1024)(128)(4,1)S(1)}, s32[]{:S(2)}) async-start(s8[4816896]{0:T(1024)(128)(4,1)} %bitcast.64), calls=%async_computation | async-start | bytes 8388608
  556.9 12.0 %slice-start.1 = ((s8[4816896]{0:T(1024)(128)(4,1)}), s8[622592]{0:T(1024)(128)(4,1)S(1)}, s32[]{:S(2)}) async-start(s8[4816896]{0:T(1024)(128)(4,1)} %bitcast.64), calls=%async_computation.1 | async-start | bytes 1245184

commit v7 on v6

--- a/solution.py
+++ b/solution.py
@@ -14,7 +14,7 @@
 MESH = pl.DeviceIdType.MESH
 F32 = jnp.float32
 BF16 = jnp.bfloat16
-VMEM_BYTES = 58 * 2**20
+VMEM_BYTES = 60 * 2**20
 TILE = 256
 
 
@@ -130,6 +130,36 @@
     return lax.dot_general(a, b, (((1,), (1,)), ((), ())), preferred_element_type=F32)
 
 
+def dot_0(a, b):
+    return lax.dot_general(a, b, (((0,), (0,)), ((), ())), preferred_element_type=F32)
+
+
+class Writer:
+    def __init__(self, stage, sems):
+        self.stage, self.sems, self.open, self.turn = stage, sems, [None, None], 0
+
+    def put(self, value, dst):
+        at = self.turn % 2
+        self.turn += 1
+        if self.open[at] is not None:
+            self.open[at].wait()
+        self.stage[at] = value.astype(BF16)
+        self.open[at] = pltpu.make_async_copy(self.stage.at[at], dst, self.sems.at[at])
+        self.open[at].start()
+
+    def rows_of_dot(self, left, right, out):
+        tall = self.stage.shape[1]
+        for j in range(out.shape[0] // tall):
+            at = pl.ds(j * tall, tall)
+            self.put(dot_0(left[:, at], right[...]), out.at[at])
+
+    def drain(self):
+        for at in range(2):
+            if self.open[at] is not None:
+                self.open[at].wait()
+        self.open = [None, None]
+
+
 def sigmoid(v):
     return 1.0 / (1.0 + jnp.exp(-v))
 
@@ -167,7 +197,7 @@
 
 
 def first_part(
-    count, writes, x, w, k, gb, pack, tiles, a2_out, cols, h1n, h2n, stats_out, count_out, act, *sync
+    count, hooks, writes, x, w, k, gb, pack, tiles, a2_out, cols, h1n, h2n, stats_out, count_out, act, *sync
 ):
     s1, send1, recv1, s2, send2, recv2 = sync
     rows, narrow = h1n.shape
@@ -195,6 +225,7 @@
     inverse = lax.rsqrt(total[4:8, :narrow] / valid - average * average + EPSILON)
     stats_out[0:4, :] = average
     stats_out[4:8, :] = inverse
+    hooks[0]()
 
     def activate(stat_at, gain_at, source):
         def body(at):
@@ -231,9 +262,11 @@
 
     for write in writes:
         write.start()
+    hooks[1]()
     over(narrow, TILE, convolve)
     total = exchange(count, s2, send2, recv2)
     average = total[0:4] / valid
+    hooks[2]()
     stats_out[8:12, :] = average
     stats_out[12:16, :] = lax.rsqrt(total[4:8] / valid - average * average + EPSILON)
     over(narrow, 128, activate(8, 2, h2n))
@@ -348,7 +381,7 @@
     w1_out,
     res_out,
     x_out,
-    cols_out,
+    a1_out,
     h1n_out,
     h2n_out,
     w3_out,
@@ -372,7 +405,8 @@
     short_send, short_recv, short_relay_send, short_relay_recv = rest[:4]
     w1_send, w1_recv, w1_relay_send, w1_relay_recv = rest[4:8]
     g_send, g_recv, a2_send, a2_recv, res_send, res_recv, own_sem, out_sem = rest[8:16]
-    spread_send, spread_recv, far_send, far_recv, near_send, near_recv, keep_sem = rest[16:]
+    spread_send, spread_recv, far_send, far_recv, near_send, near_recv, keep_sem = rest[16:23]
+    pass_send, kv, kv_sem = rest[23:]
     me, place = lax.axis_index("segment"), lax.axis_index("dp")
     core = lax.rem(place, 2)
     sibling = place + 1 - 2 * core
@@ -381,6 +415,8 @@
     half_rows = wide // 2
     mine = pl.ds(pl.multiple_of(core * half_rows, 16), half_rows)
     greet(count, sections)
+    k_load = pltpu.make_async_copy(k, kv, kv_sem)
+    k_load.start()
 
     odd = lax.rem(lax.div(place, 2), 2)
     beside = place + 2 - 4 * odd
@@ -411,7 +447,7 @@
     keeps = [
         (3, pltpu.make_async_copy(w, w3_out, keep_sem.at[0])),
         (2, pltpu.make_async_copy(w, w2_out, keep_sem.at[1])),
-        (2, pltpu.make_async_copy(k, k2_out, keep_sem.at[2])),
+        (2, pltpu.make_async_copy(kv, k2_out, keep_sem.at[2])),
     ]
 
     def spread_start(i):
@@ -419,17 +455,33 @@
 
         @pl.when(me == owner)
         def _():
-            for d in (3, 1, 2):
+            for d in (1, 2):
                 spread_copy(i, owner ^ d).start()
 
     def spread_sent(i):
-        for d in (1, 2, 3):
+        for d in (1, 2):
             spread_copy(i, parts[i][3] ^ d).wait_send()
 
+    def pass_copy(i):
+        dst, at = parts[i][2], part_rows(i, odd)
+        return mesh_copy(
+            dst.at[at], dst.at[at], pass_send.at[i], spread_recv.at[i], parts[i][3] ^ 3, place
+        )
+
     def spread_on(i):
-        @pl.when(me != parts[i][3])
+        owner = parts[i][3]
+
+        @pl.when(me == owner ^ 1)
         def _():
             spread_copy(i, 0).wait_recv()
+            pass_copy(i).start()
+
+        @pl.when((me != owner) & (me != owner ^ 1))
+        def _():
+            spread_copy(i, 0).wait_recv()
+
+        @pl.when(me != owner)
+        def _():
             far_copy(i).start()
             near_copy(i, 0).start()
 
@@ -482,7 +534,7 @@
         g_copy(k_).start()
     for i in range(3):
         spread_start(i)
-    for owner, copy in keeps:
+    for owner, copy in keeps[:2]:
         pl.when(me == owner)(copy.start)
 
     def relayout(j, carry):
@@ -494,7 +546,7 @@
     writes = [
         pltpu.make_async_copy(src, dst, out_sem.at[i])
         for i, (src, dst) in enumerate(
-            ((x, x_out), (h1n, h1n_out), (cols, cols_out), (h2n, h2n_out))
+            ((x, x_out), (h1n, h1n_out), (cols.at[:, pl.ds(4 * h1n.shape[1], h1n.shape[1])], a1_out), (h2n, h2n_out))
             + ((a2, a2_out), (w1, w1_out), (res, res_out))
         )
     ]
@@ -505,12 +557,17 @@
 
     @pl.when(me == 0)
     def _():
+        def between():
+            spread_on(0)
+            spread_on(1)
+
         first_part(
             count,
+            (lambda: spread_on(1), k_load.wait, lambda: spread_on(0)),
             writes[1:3],
             x,
             w,
-            k,
+            kv,
             gb,
             pack,
             tiles,
@@ -528,9 +585,13 @@
             a2_copy(t).start()
         a2[...] = a2_all[0]
         short_own.wait()
+        for i in (2, 3, 4):
+            spread_on(i)
 
     @pl.when(me != 0)
     def _():
+        k_load.wait()
+        pl.when(me == keeps[2][0])(keeps[2][1].start)
         slots, send1, recv1 = sync[:3]
         narrow = h1n.shape[1]
         stats_out[...] = jnp.zeros(stats_out.shape, F32)
@@ -543,12 +604,18 @@
         @pl.when(me == parts[i][3])
         def _():
             spread_sent(after)
-            for d in (3, 1, 2):
+            for d in (1, 2):
                 spread_copy(i, parts[i][3] ^ d).start()
 
-    spread_on(0)
+    def unless_zero(i):
+        pl.when(me != 0)(lambda: spread_on(i))
+
+    unless_zero(0)
     spread_paced(3, 1)
-    spread_on(1)
+    unless_zero(1)
+    spread_paced(4, 2)
+    unless_zero(2)
+    unless_zero(3)
 
     @pl.when(me != 0)
     def _():
@@ -564,8 +631,6 @@
         w1_copy(0).wait_recv()
         w1_relay.start()
 
-    spread_on(2)
-
     @pl.when(me != 0)
     def _():
         short_relay.wait_recv()
@@ -581,7 +646,7 @@
     for k_ in range(1, sections):
         res_copy(k_).start()
     res[me] = rq[me]
-    spread_paced(4, 2)
+    unless_zero(4)
 
     @pl.when(me != 0)
     def _():
@@ -596,7 +661,6 @@
     g_out[...] = gslots[...]
 
     def before():
-        spread_on(3)
         far_on(0)
         far_on(1)
         for k_ in range(1, sections):
@@ -618,7 +682,6 @@
         stats3,
         *sync[6:],
     )
-    spread_on(4)
     for copy in writes[4:]:
         copy.start()
     for i in range(2, len(parts)):
@@ -651,6 +714,7 @@
 
         if i not in (1, 2):
             pl.when(me == owner)(functools.partial(spread_sent, i))
+        pl.when(me == owner ^ 1)(lambda i=i: pass_copy(i).wait_send())
 
         @pl.when(me != owner)
         def _(i=i):
@@ -709,23 +773,32 @@
     count,
     u,
     w2,
-    k2,
-    w3,
-    og3,
+    k2_far,
+    w3_far,
+    og_far,
     pack,
     gains,
     counts,
     back,
     y1,
     y_out,
+    dy,
+    sums_out,
+    map_one,
+    p3_out,
+    p2_out,
+    k2_out,
     a2,
     cols,
     dh3,
     dh2,
     dh1,
-    dy,
-    sums_out,
-    map_one,
+    stage,
+    stage_sem,
+    k2,
+    w3,
+    og3,
+    load_sem,
     h1n,
     h2n,
     h3n,
@@ -746,6 +819,12 @@
     section = lax.axis_index("segment")
     valid = batch_valid(counts, 4)
     gb3 = gains.at[3]
+    loads = [
+        pltpu.make_async_copy(src, dst, load_sem.at[i])
+        for i, (src, dst) in enumerate(((og_far, og3), (k2_far, k2), (w3_far, w3)))
+    ]
+    for load in loads:
+        load.start()
 
     def gb2(row, at):
         return gains[2, row % 2 : row % 2 + 1, pl.ds(at.start + row // 2 * narrow, at.size)]
@@ -761,6 +840,7 @@
     greeted(count, sections)
     send_map, wait_map = map_sender(sections, y1, map_one, 1, map_send, map_recv, map_own)
     send_map()
+    loads[0].wait()
     real = og3.shape[0]
     for m in range(sections):
 
@@ -809,6 +889,7 @@
         h2n[:, at] = h
         norm_sums(s2, me, at, pack[:, 0:1] * h, h)
 
+    loads[1].wait()
     over(narrow, TILE, convolve)
     finish_stats(exchange(count, s2, send2, recv2), valid, stats, 2)
     over(narrow, 128, activate(2, 2, h2n, to_a2))
@@ -818,6 +899,7 @@
         h3n[:, at] = h
         norm_sums(s3, me, at, pack[:, 0:1] * h, h)
 
+    loads[2].wait()
     over(wide, TILE, expand)
     finish_stats(exchange(count, s3, send3, recv3), valid, stats, 4)
 
@@ -918,6 +1000,11 @@
         dy[:, at] = dot(back[...], grad.astype(BF16)).astype(BF16)
 
     over(wide, TILE, into_input)
+    writer = Writer(stage, stage_sem)
+    writer.rows_of_dot(dh3, a2, p3_out)
+    writer.rows_of_dot(cols, dh2, k2_out)
+    writer.rows_of_dot(u, dh1, p2_out)
+    writer.drain()
     wait_map()
 
 
@@ -963,7 +1050,7 @@
 
 
 def last_part(
-    count, da2, k, gb, pack, h1n, h2n, stats, counts, dh2, dh1, sums_out, act, acc, hold, *sync
+    count, between, taps_term, da2, k, gb, pack, h1n, h2n, stats, counts, dh2, dh1, sums_out, act, acc, hold, *sync
 ):
     b2, send2, recv2, b1, send1, recv1 = sync
     rows, narrow = h1n.shape
@@ -1009,6 +1096,7 @@
 
     over(narrow, 128, into(2, lambda at: act[lane(at), 0:rows, :], h2n, b2))
     sums_out[0:8, :] = exchange(count, b2, send2, recv2)
+    between()
     over(narrow, 128, through(2, 12, 0, h2n, dh2))
     acc[...] = jnp.zeros((rows, narrow), F32)
     for t, (vertical, lateral) in enumerate(OFFSETS):
@@ -1028,6 +1116,7 @@
             acc[:, at] += dot_t(hold[...], k[row, :])
 
         over(narrow, TILE, gather)
+        taps_term(t)
     over(narrow, 128, into(0, lambda at: acc[:, at], h1n, b1))
     sums_out[8:16, :] = exchange(count, b1, send1, recv1)
     over(narrow, 128, through(0, 4, 8, h1n, dh1))
@@ -1043,30 +1132,45 @@
     gains,
     stats3,
     w1,
-    k,
+    k_far,
     gb,
     pack,
-    h1n,
-    h2n,
+    h1n_far,
+    h2n_far,
     stats,
     counts,
     p3,
     p2,
     k2,
     y2,
-    dz,
-    dh3,
-    dh2,
+    a2,
+    a1_in,
+    x_in,
     dh1,
     sums3,
     sums12,
-    dzq_out,
     p3_out,
     p2_out,
     k2_out,
     dz_all,
     map_two,
     map_three,
+    p1_out,
+    k0_out,
+    p0_out,
+    sh_out,
+    dz,
+    dh3,
+    dh2,
+    dzq_out,
+    a1,
+    x,
+    k,
+    h1n,
+    h2n,
+    stage,
+    stage_sem,
+    x_sem,
     da2,
     da2_all,
     dzq,
@@ -1084,7 +1188,7 @@
     a_send, a_recv, q_send, q_recv = rest[:4]
     maps = [rest[4:7], rest[7:10], rest[10:13]]
     me, place = lax.axis_index("segment"), lax.axis_index("dp")
-    quarter = dzq.shape[2]
+    quarter, narrow = dzq.shape[2], da2.shape[1]
     greet(count, sections)
     send_dz, wait_dz = map_sender(sections, dz, dz_all, 0, *maps[0])
     send_two, wait_two = map_sender(sections, dy, map_two, 2, *maps[1])
@@ -1098,6 +1202,14 @@
     greeted(count, sections)
     core, z = lax.rem(place, 2), lax.div(place, 2)
     depth = count // 2
+    x_loads = [
+        pltpu.make_async_copy(src, dst, x_sem.at[i])
+        for i, (src, dst) in enumerate(
+            ((h2n_far, h2n), (k_far, k), (h1n_far, h1n), (a1_in, a1), (x_in, x))
+        )
+    ]
+    for copy in x_loads:
+        copy.start()
     terms = (p3, p2, k2)
     loads = [pltpu.make_async_copy(terms[i].at[core], halves[i], load_sem.at[i]) for i in range(3)]
     swaps = [
@@ -1190,15 +1302,29 @@
     send_dz()
     send_two()
     add_cores(2)
-    loop(1, depth, lambda k_: to_chip(k_).start())
+
+    def to_chips():
+        loop(1, depth, lambda k_: to_chip(k_).start())
+
+    pl.when(me != 0)(to_chips)
 
     @pl.when(me == 0)
     def _():
         for k_ in range(1, sections):
             a_copy(k_).wait_recv()
         da2_all[0] = da2[...]
+        for copy in x_loads:
+            copy.wait()
+        writer = Writer(stage, stage_sem)
+
+        def taps_term(t):
+            tall = narrow
+            writer.put(dot_0(a1[...], hold[...]), k0_out.at[pl.ds(t * tall, tall)])
+
         last_part(
             count,
+            to_chips,
+            taps_term,
             da2_all,
             k,
             gb,
@@ -1215,9 +1341,13 @@
             hold,
             *sync[3:],
         )
+        writer.rows_of_dot(x, dh1, p0_out)
+        writer.drain()
 
     @pl.when(me != 0)
     def _():
+        for copy in x_loads:
+            copy.wait()
         a_copy(0).wait_send()
         sums12[...] = jnp.zeros(sums12.shape, F32)
 
@@ -1282,6 +1412,10 @@
         return carry
 
     lax.fori_loop(0, quarter // 128, weave, 0)
+    writer = Writer(stage, stage_sem)
+    writer.rows_of_dot(x, dzq_out, sh_out)
+    writer.rows_of_dot(dh3, a2, p1_out)
+    writer.drain()
     for i in range(2):
         loop(1, depth, lambda k_, i=i: next_chip(i, k_).wait_recv())
         total = totals[i][z].astype(F32)
@@ -1922,6 +2056,37 @@
     )(short.reshape(2, sh_rows, narrow), *args, vectors, dh1, w, weights, *map_sources)
 
 
+def cast_kernel(proj, taps, short, proj_out, taps_out, short_out):
+    me = lax.axis_index("segment")
+    proj_out[...] = proj[...].astype(F32)
+    for held, src, out in (
+        ((me == 0) | (me == 2), taps, taps_out),
+        (me == 0, short, short_out),
+    ):
+
+        @pl.when(held)
+        def _(src=src, out=out):
+            out[...] = src[...].astype(F32)
+
+        @pl.when(jnp.logical_not(held))
+        def _(out=out):
+            out[...] = jnp.zeros(out.shape, F32)
+
+
+def cast_sums(*sums):
+    steps = 8
+    blocks = [pl.BlockSpec((a.shape[0] // steps, a.shape[1]), lambda i: (i, 0)) for a in sums]
+    return pl.pallas_call(
+        cast_kernel,
+        grid=(steps,),
+        out_shape=[shape_of(a.shape, F32) for a in sums],
+        in_specs=blocks,
+        out_specs=blocks,
+        compiler_params=pltpu.CompilerParams(vmem_limit_bytes=VMEM_BYTES),
+        cost_estimate=pl.CostEstimate(flops=0, bytes_accessed=45 * 2**20, transcendentals=0),
+    )(*sums)
+
+
 def layouts(resolution_ids, order_ids):
     pixels = jnp.arange(MAP * MAP, dtype=jnp.int32)
     row_of = pixels // MAP
@@ -1951,10 +2116,6 @@
             in_column &= column // 2 == lattice // 2
         tables.append((in_row[:, None] & in_column[None, :]).reshape(-1))
     return np.stack(tables, axis=1).astype(np.float32)
-
-
-def mm(a, b, dims="rk,kn->rn"):
-    return jnp.einsum(dims, a, b, preferred_element_type=F32)
 
 
 def body(
@@ -2025,7 +2186,7 @@
             shape_of((wide, narrow), BF16),
             shape_of((sections, padded, quarter), BF16),
             shape_of((total, wide), BF16),
-            shape_of((total, 9 * narrow), BF16),
+            shape_of((total, narrow), BF16),
             shape_of((total, narrow), F32),
             shape_of((total, narrow), F32),
             shape_of((wide, narrow), BF16),
@@ -2053,30 +2214,40 @@
         + [dma((sections,)), dma((sections,)), dma((sections,)), dma]
         + [dma((sections,)), dma((sections,)), dma((2,)), dma((7,))]
         + [dma((5, sections)), dma((5,)), dma((5,)), dma((5,))]
-        + [dma((5, 2)), dma((5, 2)), dma((3,))],
+        + [dma((5, 2)), dma((5, 2)), dma((3,))]
+        + [dma((5,)), pltpu.VMEM((9 * narrow, narrow), BF16), dma],
         0,
         2 * total * (narrow * (wide + 9 * narrow) + wide * quarter),
         60 * 2**20,
-        far_in=(2,),
+        far_in=(2, 3),
         far_out=tuple(range(7, 17)),
     )
-    a2, w1, res, x_all, cols_all, h1n_all, h2n_all, w3, w2, k2 = far
+    a2, w1, res, x_all, a1_all, h1n_all, h2n_all, w3, w2, k2 = far
     paged = shape_of((sections, padded, wide), BF16)
-    y2, t_a2, t_cols, t_dh3, t_dh2, t_dh1, dy1, t_sums, map_one = kernel_call(
+    y2, dy1, t_sums, map_one, p3_term, p2_term, k2_term = kernel_call(
         functools.partial(tile_kernel, sections, count),
         [
             shape_of((padded, wide), BF16),
-            shape_of((padded, narrow), BF16),
-            shape_of((padded, 9 * narrow), BF16),
-            shape_of((padded, wide), BF16),
-            shape_of((padded, narrow), BF16),
-            shape_of((padded, narrow), BF16),
             shape_of((padded, wide), BF16),
             shape_of((6, wide), F32),
             paged,
+            shape_of((wide, narrow), BF16),
+            shape_of((wide, narrow), BF16),
+            shape_of((9 * narrow, narrow), BF16),
         ],
         [u, w2, k2, w3, og_in, pack_tile, gains, counts, moves_back, y1],
         [
+            pltpu.VMEM((padded, narrow), BF16),
+            pltpu.VMEM((padded, 9 * narrow), BF16),
+            pltpu.VMEM((padded, wide), BF16),
+            pltpu.VMEM((padded, narrow), BF16),
+            pltpu.VMEM((padded, narrow), BF16),
+            pltpu.VMEM((2, 512, narrow), BF16),
+            dma((2,)),
+            pltpu.VMEM((9 * narrow, narrow), BF16),
+            pltpu.VMEM((wide, narrow), BF16),
+            pltpu.VMEM((rows, micro, wide), BF16),
+            dma((3,)),
             pltpu.VMEM((padded, narrow), F32),
             pltpu.VMEM((padded, narrow), F32),
             pltpu.VMEM((padded, wide), F32),
@@ -2092,76 +2263,82 @@
         1,
         4 * padded * narrow * (2 * wide + 9 * narrow),
         30 * 2**20,
-        far_in=(9,),
-        far_out=(8,),
+        far_in=(2, 3, 4, 9),
+        far_out=(3, 4, 5, 6),
     )
     depth = count // 2
 
     def split(term):
-        return term.astype(BF16).reshape(
-            2, sections, depth, term.shape[0] // (2 * sections * depth), narrow
-        )
-
-    p3_term = split(mm(t_dh3, t_a2, "rd,rk->dk"))
-    k2_term = split(mm(t_cols, t_dh2, "rk,rn->kn"))
-    p2_term = split(mm(u, t_dh1, "rc,rn->cn"))
+        return term.reshape(2, sections, depth, term.shape[0] // (2 * sections * depth), narrow)
+
+    p3_term, p2_term, k2_term = split(p3_term), split(p2_term), split(k2_term)
     proj_piece, taps_piece = p3_term.shape[3], k2_term.shape[3]
-    dz, dh3, dh2_all, dh1_all, i_sums, f_sums, dz_quarter, p3_part, p2_part, k2_part, map_zero, map_two, map_three = (
-        kernel_call(
-            functools.partial(back_kernel, sections, count),
-            [
-                shape_of((padded, wide), BF16),
-                shape_of((padded, wide), BF16),
-                shape_of((total, narrow), BF16),
-                shape_of((total, narrow), BF16),
-                shape_of((2, wide), F32),
-                shape_of((16, narrow), F32),
-                shape_of((total, quarter), BF16),
-                shape_of((depth, proj_piece, narrow), BF16),
-                shape_of((depth, proj_piece, narrow), BF16),
-                shape_of((sections, taps_piece, narrow), BF16),
-                paged,
-                paged,
-                paged,
-            ],
-            [dy1, res, h3n, image_mask, gains, stats3, w1, spatial, gb_first, pack_all]
-            + [h1n_all, h2n_all, stats_all, counts, p3_term, p2_term, k2_term, y2],
-            [
-                pltpu.VMEM((padded, narrow), BF16),
-                pltpu.VMEM((micro, padded, narrow), BF16),
-                pltpu.VMEM((micro, padded, quarter), BF16),
-                pltpu.VMEM((narrow // 128, 4 * padded, 128), F32),
-                pltpu.VMEM((total, narrow), F32),
-                pltpu.VMEM((total, narrow), BF16),
-            ]
-            + sync_scratch(count, [(2, wide), (8, narrow), (8, narrow)])
-            + [pltpu.VMEM(a.shape[1:], BF16) for a in (p3_term, p2_term, k2_term)] * 2
-            + [pltpu.VMEM(p3_term.shape[1:], BF16)] * 2
-            + [pltpu.VMEM((depth, sections, taps_piece, narrow), BF16)]
-            + [pltpu.VMEM((depth, proj_piece, narrow), BF16)] * 6
-            + [pltpu.VMEM((sections, taps_piece, narrow), BF16)]
-            + [dma((3,))] * 3
-            + [dma((3, max(sections, depth)))] * 6
-            + [dma((3,))]
-            + [dma, dma((sections,)), dma((sections,)), dma((sections,))]
-            + [dma, dma((sections,)), dma] * 3,
-            2,
-            2 * total * narrow * 9 * narrow,
-            40 * 2**20,
-            far_in=(14, 15, 16, 17),
-            far_out=(7, 8, 9, 10, 11, 12),
-        )
+    dh1_all, i_sums, f_sums, p3_part, p2_part, k2_part, *far = kernel_call(
+        functools.partial(back_kernel, sections, count),
+        [
+            shape_of((total, narrow), BF16),
+            shape_of((2, wide), F32),
+            shape_of((16, narrow), F32),
+            shape_of((depth, proj_piece, narrow), BF16),
+            shape_of((depth, proj_piece, narrow), BF16),
+            shape_of((sections, taps_piece, narrow), BF16),
+            paged,
+            paged,
+            paged,
+            shape_of((wide, narrow), BF16),
+            shape_of((9 * narrow, narrow), BF16),
+            shape_of((wide, narrow), BF16),
+            shape_of((wide, narrow), BF16),
+        ],
+        [dy1, res, h3n, image_mask, gains, stats3, w1, spatial, gb_first, pack_all]
+        + [h1n_all, h2n_all, stats_all, counts, p3_term, p2_term, k2_term, y2, a2, a1_all, x_all],
+        [
+            pltpu.VMEM((padded, wide), BF16),
+            pltpu.VMEM((padded, wide), BF16),
+            pltpu.VMEM((total, narrow), BF16),
+            pltpu.VMEM((total, quarter), BF16),
+            pltpu.VMEM((total, narrow), BF16),
+            pltpu.VMEM((total, wide), BF16),
+            pltpu.VMEM((9 * narrow, narrow), BF16),
+            pltpu.VMEM((total, narrow), F32),
+            pltpu.VMEM((total, narrow), F32),
+            pltpu.VMEM((2, 512, narrow), BF16),
+            dma((2,)),
+            dma((5,)),
+            pltpu.VMEM((padded, narrow), BF16),
+            pltpu.VMEM((micro, padded, narrow), BF16),
+            pltpu.VMEM((micro, padded, quarter), BF16),
+            pltpu.VMEM((narrow // 128, 4 * padded, 128), F32),
+            pltpu.VMEM((total, narrow), F32),
+            pltpu.VMEM((total, narrow), BF16),
+        ]
+        + sync_scratch(count, [(2, wide), (8, narrow), (8, narrow)])
+        + [pltpu.VMEM(a.shape[1:], BF16) for a in (p3_term, p2_term, k2_term)] * 2
+        + [pltpu.VMEM(p3_term.shape[1:], BF16)] * 2
+        + [pltpu.VMEM((depth, sections, taps_piece, narrow), BF16)]
+        + [pltpu.VMEM((depth, proj_piece, narrow), BF16)] * 6
+        + [pltpu.VMEM((sections, taps_piece, narrow), BF16)]
+        + [dma((3,))] * 3
+        + [dma((3, max(sections, depth)))] * 6
+        + [dma((3,))]
+        + [dma, dma((sections,)), dma((sections,)), dma((sections,))]
+        + [dma, dma((sections,)), dma] * 3,
+        2,
+        2 * total * narrow * 9 * narrow,
+        40 * 2**20,
+        far_in=(7, 10, 11, 14, 15, 16, 17, 19, 20),
+        far_out=tuple(range(3, 13)),
     )
+    map_zero, map_two, map_three, p1_term, k0_term, p0_term, short_term = far
 
     terms = {
         "p3": p3_part,
         "k2": k2_part,
         "p2": p2_part,
-        "p1": split(mm(dh3, a2, "rd,rk->dk")),
-        "k0": split(mm(cols_all, dh2_all, "rk,rn->kn")),
-        "p0": split(mm(x_all, dh1_all, "rc,rn->cn")),
+        "p1": split(p1_term),
+        "k0": split(k0_term),
+        "p0": split(p0_term),
     }
-    short_term = mm(x_all, dz_quarter, "rc,rd->cd").astype(BF16)
 
     blank = jnp.zeros((wide,), F32)
     pad = jnp.zeros((wide - 2 * narrow,), F32)
@@ -2193,11 +2370,11 @@
         rows,
     )
     maps = jnp.transpose(maps.reshape(images, pixels, micro, wide), (2, 0, 1, 3))
-    proj_grad = proj_sum.reshape(wide, narrow).astype(F32)
-    spatial_grad = taps_sum.reshape(9 * narrow, narrow).astype(F32)
-    spatial_grad = jnp.where((section % 2) == 0, spatial_grad, jnp.zeros_like(spatial_grad))
-    short_grad = short_sum.reshape(wide, wide).astype(F32)
-    short_grad = jnp.where(first, short_grad, jnp.zeros_like(short_grad))
+    proj_grad, spatial_grad, short_grad = cast_sums(
+        proj_sum.reshape(wide, narrow),
+        taps_sum.reshape(9 * narrow, narrow),
+        short_sum.reshape(wide, wide),
+    )
     return (
         maps[None],
         proj_grad[None],

time: 580 us -> 543 us (0.936)
  matrix products: 37.8 us -> 0 us
  other arithmetic: 27 us -> 5.64 us
  Pallas kernels: 492 us -> 508 us
    dot_general x7 -> x0, matrix products: 37.8 us -> none  [mm(): return jnp.einsum(dims, a, b, preferred_element_type=F32)]
    select_n x2 -> x0, other arithmetic: 17.1 us -> none  [the longest x1 12 us: body(): short_grad = jnp.where(first, short_grad, jnp.zeros_like(short_grad))]
    pallas_call x0 -> x1, Pallas kernels: none -> 16.8 us  [cast_sums(): pl.pallas_call(cast_kernel, grid=(steps,), out_shape=[shape_of(a.shape, F...]
where the time goes in v7:
time: 543 us; the launch traced here: 534 us
  Pallas kernels  508 us (94%)
  local copies, waits for them, and re-layouts  18.6 us (3%)
  other arithmetic  5.64 us (1%)
    pallas_call x3, Pallas kernels, kernel_call(): pl.pallas_call(kernel, out_shape=outs, in_specs=[pl.BlockSpec(memory_spac...  307 us
    pallas_call x1, Pallas kernels, sum_gradients(): pl.pallas_call(functools.partial(gradient_kernel, sections, count), out_s...  184 us
    pallas_call x1, Pallas kernels, cast_sums(): pl.pallas_call(cast_kernel, grid=(steps,), out_shape=[shape_of(a.shape, F...  16.8 us

profile of v7, /device:TPU:25, one launch (start us, length us, event | category | flops | bytes accessed | tf_op | source)
XLA Modules:
  0.0 533.6 jit_solution(2294915238315350088)
XLA Ops:
  0.6 0.7 fusion.25
  1.4 0.6 pad_maximum_fusion.1.gb
  2.0 1.3 pad_maximum_fusion.vec
  3.3 0.7 broadcast_add_fusion.2
  4.0 0.1 lt.192
  4.1 0.1 lt.193
  4.2 0.8 copy.42
  5.0 0.1 mul.74
  5.1 0.1 multiply_reduce_fusion
  5.2 0.1 rem.223
  5.3 0.1 div.84
  5.4 0.1 ne.259
  5.5 0.1 add.234
  5.6 0.1 add.228
  5.7 0.1 and.233
  5.8 0.1 lt.197
  5.9 0.1 lt.190
  6.0 0.1 copy.41
  6.1 0.1 reshape.637
  6.3 0.1 pad.30.clone
  6.4 1.0 maximum_maximum_fusion
  7.3 1.1 copy.45.pack
  8.4 0.1 copy.43
  8.5 1.0 reshape.642.tiles
  9.6 0.1 rem.228
  9.6 0.1 div.86
  9.7 0.1 ne.265
  9.8 0.1 lt.208
  9.9 0.1 copy.44
  10.1 0.7 pad.11.mask
  10.8 0.1 squeeze.36
  10.9 0.1 add.244
  11.0 0.1 add.245
  11.1 0.9 fusion.1
  12.0 0.0 copy-start
  12.0 91.5 %shard_map.154 = (f32[16,512]{1,0:T(8,128)}, f32[8,128]{1,0:T(8,128)}, f32[4,2,2048]{2,1,0:T(2,128)}, bf16[304,2048]{1,0:T(8,128)(2,1)}, bf16[304,2048]{1,0:T(8,...) custom-call(bf16[294,4,2048]{2,1,0:T(4,128)(2,1)} %bitcast.78, ...), custom_call_target="tpu_custom_call" | custom-call | flops 10481565696 | bytes 62914560 | tf_op jit(solution)/shard_map/pallas_call | solution.py:106
  103.5 0.0 copy-done
  103.5 0.8 copy.47.pack
  104.3 83.7 %shard_map.155 = (bf16[304,2048]{1,0:T(8,128)(2,1)}, bf16[304,2048]{1,0:T(8,128)(2,1)}, f32[6,2048]{1,0:T(8,128)}, bf16[4,304,2048]{2,1,0:T(8,128)(2,1)}, bf16[2...) custom-call(bf16[304,2048]{1,0:T(8,128)(2,1)} %get-tuple-element.51.u, ...), custom_call_target="tpu_custom_call" | custom-call | flops 5419040768 | bytes 31457280 | tf_op jit(solution)/shard_map/pallas_call | solution.py:106
  188.0 132.2 %shard_map.156 = (bf16[1176,512]{1,0:T(8,128)(2,1)}, f32[2,2048]{1,0:T(2,128)}, f32[16,512]{1,0:T(8,128)}, bf16[4,64,512]{2,1,0:T(8,128)(2,1)}, bf16[4,64,512]{2...) custom-call(bf16[304,2048]{1,0:T(8,128)(2,1)} %get-tuple-element.58., ...), custom_call_target="tpu_custom_call" | custom-call | flops 5549064192 | bytes 41943040 | tf_op jit(solution)/shard_map/pallas_call | solution.py:106
  320.3 0.9 fusion.22
  321.2 0.8 slice_reduce_fusion.1
  322.1 0.8 fusion.24
  322.9 0.9 fusion.21
  323.8 0.1 stack.17
  323.9 0.7 reshape.631.vec
  324.6 183.8 %shard_map.157 = (bf16[2,1024,2048]{2,1,0:T(8,128)(2,1)}, bf16[2,4,4,64,512]{4,3,2,1,0:T(8,128)(2,1)}, bf16[2,4,4,144,512]{4,3,2,1,0:T(8,128)(2,1)}, f32[2,2048]{1,0:T(2,128)}, bf16[294,4,2048]{2,1,0:T(4,128)(2,1)}) custom-call(bf16[2,1024,512]{2,1,0:T(8,128)(2,1)} %bitcast.61, bf16[2,4,4,144,512]{4,3,2,1,0:T(8,128)(2,1)} %bitcast.54, ...), custom_call_target="tpu_custom_call" | custom-call | bytes 419430400 | tf_op jit(solution)/shard_map/pallas_call | solution.py:2040
  508.4 0.0 copy-start.1
  508.4 16.8 %shard_map.158 = (f32[2048,512]{1,0:T(8,128)}, f32[4608,512]{1,0:T(8,128)}, f32[2048,2048]{1,0:T(8,128)}) custom-call(bf16[2048,512]{1,0:T(8,128)(2,1)} %bitcast.64, bf16[4608,512]{1,0:T(8,128)(2,1)} %bitcast.56, bf16[2048,2048]{1,0:T(8,128)(2,1)} %bitcast.48), custom_call_target="tpu_custom_call" | custom-call | bytes 47185920 | tf_op jit(solution)/shard_map/pallas_call | solution.py:2079
  525.2 0.0 copy-done.1
  525.2 0.6 fusion.23
  525.8 7.4 %copy.50 = bf16[1,4,6,49,2048]{4,1,3,2,0:T(4,128)(2,1)} copy(bf16[1,4,6,49,2048]{4,1,3,2,0:T(4,128)(2,1)} %bitcast.51) | data formatting | bytes 9633792
  (30 shorter events, 0.3 us)
Async XLA Ops:
  12.0 91.5 %copy-start = (f32[304,15]{0,1:T(8,128)S(1)}, f32[304,15]{0,1:T(8,128)}, u32[]{:S(2)}) copy-start(f32[304,15]{0,1:T(8,128)} %constant.106.clone) | copy-start | bytes 54724
  508.4 16.8 %copy-start.1 = (f32[2,2048]{1,0:T(2,128)S(1)}, f32[2,2048]{1,0:T(2,128)}, u32[]{:S(2)}) copy-start(f32[2,2048]{1,0:T(2,128)} %get-tuple-element.95) | copy-start | bytes 49156

commit v8 on v7

--- a/solution.py
+++ b/solution.py
@@ -616,6 +616,7 @@
     spread_paced(4, 2)
     unless_zero(2)
     unless_zero(3)
+    pl.when(me == parts[4][3] ^ 1)(lambda: spread_on(4))
 
     @pl.when(me != 0)
     def _():
@@ -646,7 +647,7 @@
     for k_ in range(1, sections):
         res_copy(k_).start()
     res[me] = rq[me]
-    unless_zero(4)
+    pl.when((me != 0) & (me != parts[4][3] ^ 1))(lambda: spread_on(4))
 
     @pl.when(me != 0)
     def _():
@@ -1139,8 +1140,6 @@
     h2n_far,
     stats,
     counts,
-    p3,
-    p2,
     k2,
     y2,
     a2,
@@ -1149,8 +1148,6 @@
     dh1,
     sums3,
     sums12,
-    p3_out,
-    p2_out,
     k2_out,
     dz_all,
     map_two,
@@ -1180,11 +1177,9 @@
     *rest,
 ):
     sync, rest = rest[:9], list(rest[9:])
-    halves, theirs, pieces, totals, chips, wholes = (
-        rest[:3], rest[3:6], rest[6:9], rest[9:11], rest[11:13], rest[13:16]
-    )
-    load_sem, swap_send, swap_recv, piece_send, piece_recv, next_send, next_recv, share_send, share_recv, out_sem = rest[16:26]
-    rest = rest[26:]
+    half, theirs, pieces, whole = rest[:4]
+    load_sem, swap_send, swap_recv, piece_send, piece_recv, out_sem = rest[4:10]
+    rest = rest[10:]
     a_send, a_recv, q_send, q_recv = rest[:4]
     maps = [rest[4:7], rest[7:10], rest[10:13]]
     me, place = lax.axis_index("segment"), lax.axis_index("dp")
@@ -1210,54 +1205,29 @@
     ]
     for copy in x_loads:
         copy.start()
-    terms = (p3, p2, k2)
-    loads = [pltpu.make_async_copy(terms[i].at[core], halves[i], load_sem.at[i]) for i in range(3)]
-    swaps = [
-        mesh_copy(
-            terms[i].at[1 - core],
-            theirs[i],
-            swap_send.at[i],
-            swap_recv.at[i],
-            me,
-            place + 1 - 2 * core,
-        )
-        for i in range(3)
-    ]
-    for i in range(3):
-        swaps[i].start()
-        loads[i].start()
-
-    def to_section(i, k_):
-        other = jnp.bitwise_xor(me, k_)
-        return mesh_copy(
-            halves[i].at[other],
-            pieces[i].at[k_],
-            piece_send.at[i, k_],
-            piece_recv.at[i, k_],
-            other,
-            place,
-        )
+    load = pltpu.make_async_copy(k2.at[core], half, load_sem)
+    swap = mesh_copy(k2.at[1 - core], theirs, swap_send, swap_recv, me, place + 1 - 2 * core)
+    swap.start()
+    load.start()
 
     def to_chip(k_):
         to = lax.rem(z + k_, depth)
         return mesh_copy(
-            halves[2].at[:, to],
-            pieces[2].at[k_],
-            piece_send.at[2, k_],
-            piece_recv.at[2, k_],
+            half.at[:, to],
+            pieces.at[k_],
+            piece_send.at[k_],
+            piece_recv.at[k_],
             me,
             2 * to + core,
         )
 
-    def add_cores(i):
-        loads[i].wait()
-        swaps[i].wait_recv()
+    def add_cores():
+        load.wait()
+        swap.wait_recv()
 
         def add(n):
             q, y = lax.div(n, depth), lax.rem(n, depth)
-            halves[i][q, y] = (
-                halves[i][q, y].astype(F32) + theirs[i][q, y].astype(F32)
-            ).astype(BF16)
+            half[q, y] = (half[q, y].astype(F32) + theirs[q, y].astype(F32)).astype(BF16)
 
         loop(0, sections * depth, add)
 
@@ -1293,15 +1263,11 @@
         def _(k_=k_):
             a_copy(k_).start()
 
-    for i in range(2):
-        add_cores(i)
-        for k_ in range(1, sections):
-            to_section(i, k_).start()
     for k_ in range(1, sections):
         q_copy(k_).start()
     send_dz()
     send_two()
-    add_cores(2)
+    add_cores()
 
     def to_chips():
         loop(1, depth, lambda k_: to_chip(k_).start())
@@ -1351,48 +1317,17 @@
         a_copy(0).wait_send()
         sums12[...] = jnp.zeros(sums12.shape, F32)
 
-    def next_chip(i, k_):
-        to = lax.rem(z + k_, depth)
-        return mesh_copy(
-            totals[i].at[to],
-            chips[i].at[k_],
-            next_send.at[i, k_],
-            next_recv.at[i, k_],
-            me,
-            2 * to + core,
-        )
-
-    def share(i, k_):
-        return mesh_copy(
-            wholes[i].at[z],
-            wholes[i].at[z],
-            share_send.at[i, k_],
-            share_recv.at[i, k_],
-            me,
-            2 * lax.rem(z + k_, depth) + core,
-        )
-
-    for i in range(2):
-        for k_ in range(1, sections):
-            to_section(i, k_).wait_recv()
-
-        def p_sum(y, i=i):
-            total = halves[i][me, y].astype(F32)
-            for k_ in range(1, sections):
-                total = total + pieces[i][k_, y].astype(F32)
-            totals[i][y] = total.astype(BF16)
-
-        loop(0, depth, p_sum)
-        loop(1, depth, lambda k_, i=i: next_chip(i, k_).start())
     loop(1, depth, lambda k_: to_chip(k_).wait_recv())
 
     def k2_sum(q):
-        total = halves[2][q, z].astype(F32)
+        total = half[q, z].astype(F32)
         for k_ in range(1, depth):
-            total = total + pieces[2][k_, q].astype(F32)
-        wholes[2][q] = total.astype(BF16)
+            total = total + pieces[k_, q].astype(F32)
+        whole[q] = total.astype(BF16)
 
     loop(0, sections, k2_sum)
+    out = pltpu.make_async_copy(whole, k2_out, out_sem)
+    out.start()
     for k_ in range(1, sections):
         q_copy(k_).wait_recv()
     dzq[me] = dz[:, pl.ds(pl.multiple_of(me * quarter, 128), quarter)]
@@ -1416,31 +1351,11 @@
     writer.rows_of_dot(x, dzq_out, sh_out)
     writer.rows_of_dot(dh3, a2, p1_out)
     writer.drain()
-    for i in range(2):
-        loop(1, depth, lambda k_, i=i: next_chip(i, k_).wait_recv())
-        total = totals[i][z].astype(F32)
-        for k_ in range(1, depth):
-            total = total + chips[i][k_].astype(F32)
-        wholes[i][z] = total.astype(BF16)
-        loop(1, depth, lambda k_, i=i: share(i, k_).start())
-    outs = []
-    for i, out in enumerate((p3_out, p2_out, k2_out)):
-        if i < 2:
-            loop(1, depth, lambda k_, i=i: share(i, k_).wait_recv())
-        outs.append(pltpu.make_async_copy(wholes[i], out, out_sem.at[i]))
-        outs[i].start()
     for k_ in range(1, sections):
         q_copy(k_).wait_send()
-        for i in range(2):
-            to_section(i, k_).wait_send()
     loop(1, depth, lambda k_: to_chip(k_).wait_send())
-    for i in range(2):
-        loop(1, depth, lambda k_, i=i: next_chip(i, k_).wait_send())
-    for i in range(3):
-        swaps[i].wait_send()
-        if i < 2:
-            loop(1, depth, lambda k_, i=i: share(i, k_).wait_send())
-        outs[i].wait()
+    swap.wait_send()
+    out.wait()
     wait_dz()
     wait_two()
     wait_three()
@@ -1450,8 +1365,8 @@
     ("k0", 0, "owner"),
     ("p0", 0, "owner"),
     ("p1", 1, "each"),
-    ("p3", 3, "done"),
-    ("p2", 2, "done"),
+    ("p2", 2, "each"),
+    ("p3", 3, "each"),
     ("k2", 2, "chips"),
 )
 
@@ -1463,8 +1378,8 @@
     k0,
     p0,
     p1,
+    p2,
     p3,
-    p2,
     k2,
     vec,
     dh1,
@@ -1482,7 +1397,7 @@
     *scratch,
 ):
     names = [name for name, _, _ in SUMS]
-    terms = dict(zip(names, (k0, p0, p1, p3, p2, k2)))
+    terms = dict(zip(names, (k0, p0, p1, p2, p3, k2)))
     owner = {name: section for name, section, _ in SUMS}
     held = {name: kind for name, _, kind in SUMS}
     fresh = [name for name in names if held[name] in ("owner", "each")]
@@ -1779,15 +1694,14 @@
     loop(1, depth, lambda k: sh_share(k).start())
     loop(2, wide // TILE, map_tile)
 
-    for name in names:
-        if held[name] == "chips":
-            load_plane(name).wait()
-            acc = planes[name][0].astype(F32)
-            for k in range(1, sections):
-                to_plane(name, k).wait_recv()
-                acc = acc + planes[name][k].astype(F32)
-            whole[name][z] = acc.astype(BF16)
-            loop(1, depth, lambda k, name=name: share(name, k).start())
+    def planes_end(name):
+        load_plane(name).wait()
+        acc = planes[name][0].astype(F32)
+        for k in range(1, sections):
+            to_plane(name, k).wait_recv()
+            acc = acc + planes[name][k].astype(F32)
+        whole[name][z] = acc.astype(BF16)
+        loop(1, depth, lambda k: share(name, k).start())
 
     def to_chip(name, k):
         to = lax.rem(z + k, depth)
@@ -1800,7 +1714,7 @@
             2 * to + core,
         )
 
-    for name in fresh:
+    def b_end(name):
         if held[name] == "each":
             for k in range(1, sections):
                 to_section(name, k).wait_recv()
@@ -1828,6 +1742,9 @@
                     to_section(name, k).wait_recv()
 
         loop(1, depth, lambda k, name=name: to_chip(name, k).start())
+
+    for name in ("k0", "p0"):
+        b_end(name)
 
     def sh_deliver(k):
         at = pl.ds(pl.multiple_of(me * sh_whole.shape[1], 128), sh_whole.shape[1])
@@ -1848,14 +1765,6 @@
     def _():
         sh_keep.start()
 
-    for name in fresh:
-        loop(1, depth, lambda k, name=name: to_chip(name, k).wait_recv())
-        acc = total[name][z].astype(F32)
-        for k in range(1, depth):
-            acc = acc + others[name][k].astype(F32)
-        whole[name][z] = acc.astype(BF16)
-        loop(1, depth, lambda k, name=name: share(name, k).start())
-
     def relayed(name, onward):
         index = last if name == "sh" else slot[name]
         at = pl.ds(3 * sh_whole.shape[1], sh_whole.shape[1])
@@ -1888,19 +1797,39 @@
             relayed(name, True).start()
 
     start_delivery("sh")
-    for name in ["k2"] + fresh:
-        if name == fresh[-1]:
-            pass_on("sh")
-        loop(1, depth, lambda k, name=name: share(name, k).wait_recv())
+
+    def c_end(name):
+        loop(1, depth, lambda k: to_chip(name, k).wait_recv())
+        acc = total[name][z].astype(F32)
+        for k in range(1, depth):
+            acc = acc + others[name][k].astype(F32)
+        whole[name][z] = acc.astype(BF16)
+        loop(1, depth, lambda k: share(name, k).start())
+
+    def d_end(name):
+        loop(1, depth, lambda k: share(name, k).wait_recv())
 
         @pl.when(me == owner[name])
-        def _(name=name):
+        def _():
             keep_own(name).start()
 
         start_delivery(name)
-    for name in fresh:
-        if owner[name] == 0:
-            pass_on(name)
+
+    later = ("p1", "p2", "p3")
+    planes_end("k2")
+    for name in ("k0", "p0"):
+        c_end(name)
+    for name in later:
+        b_end(name)
+    pass_on("sh")
+    for name in ("k0", "p0", "k2"):
+        d_end(name)
+    for name in later:
+        c_end(name)
+    for name in ("k0", "p0"):
+        pass_on(name)
+    for name in later:
+        d_end(name)
 
     def cross(name):
         return mesh_copy(
@@ -2272,15 +2201,13 @@
         return term.reshape(2, sections, depth, term.shape[0] // (2 * sections * depth), narrow)
 
     p3_term, p2_term, k2_term = split(p3_term), split(p2_term), split(k2_term)
-    proj_piece, taps_piece = p3_term.shape[3], k2_term.shape[3]
-    dh1_all, i_sums, f_sums, p3_part, p2_part, k2_part, *far = kernel_call(
+    taps_piece = k2_term.shape[3]
+    dh1_all, i_sums, f_sums, k2_part, *far = kernel_call(
         functools.partial(back_kernel, sections, count),
         [
             shape_of((total, narrow), BF16),
             shape_of((2, wide), F32),
             shape_of((16, narrow), F32),
-            shape_of((depth, proj_piece, narrow), BF16),
-            shape_of((depth, proj_piece, narrow), BF16),
             shape_of((sections, taps_piece, narrow), BF16),
             paged,
             paged,
@@ -2291,7 +2218,7 @@
             shape_of((wide, narrow), BF16),
         ],
         [dy1, res, h3n, image_mask, gains, stats3, w1, spatial, gb_first, pack_all]
-        + [h1n_all, h2n_all, stats_all, counts, p3_term, p2_term, k2_term, y2, a2, a1_all, x_all],
+        + [h1n_all, h2n_all, stats_all, counts, k2_term, y2, a2, a1_all, x_all],
         [
             pltpu.VMEM((padded, wide), BF16),
             pltpu.VMEM((padded, wide), BF16),
@@ -2313,28 +2240,24 @@
             pltpu.VMEM((total, narrow), BF16),
         ]
         + sync_scratch(count, [(2, wide), (8, narrow), (8, narrow)])
-        + [pltpu.VMEM(a.shape[1:], BF16) for a in (p3_term, p2_term, k2_term)] * 2
-        + [pltpu.VMEM(p3_term.shape[1:], BF16)] * 2
+        + [pltpu.VMEM(k2_term.shape[1:], BF16)] * 2
         + [pltpu.VMEM((depth, sections, taps_piece, narrow), BF16)]
-        + [pltpu.VMEM((depth, proj_piece, narrow), BF16)] * 6
         + [pltpu.VMEM((sections, taps_piece, narrow), BF16)]
-        + [dma((3,))] * 3
-        + [dma((3, max(sections, depth)))] * 6
-        + [dma((3,))]
+        + [dma, dma, dma, dma((depth,)), dma((depth,)), dma]
         + [dma, dma((sections,)), dma((sections,)), dma((sections,))]
         + [dma, dma((sections,)), dma] * 3,
         2,
         2 * total * narrow * 9 * narrow,
         40 * 2**20,
-        far_in=(7, 10, 11, 14, 15, 16, 17, 19, 20),
-        far_out=tuple(range(3, 13)),
+        far_in=(7, 10, 11, 14, 15, 17, 18),
+        far_out=tuple(range(3, 11)),
     )
     map_zero, map_two, map_three, p1_term, k0_term, p0_term, short_term = far
 
     terms = {
-        "p3": p3_part,
+        "p3": p3_term,
         "k2": k2_part,
-        "p2": p2_part,
+        "p2": p2_term,
         "p1": split(p1_term),
         "k0": split(k0_term),
         "p0": split(p0_term),

time: 543 us -> 490 us (0.902)
  the two profiles are of different devices: /device:TPU:25 before, /device:TPU:29 now
where the time goes in v8:
time: 490 us; the launch traced here: 481 us
  Pallas kernels  454 us (93%)
  local copies, waits for them, and re-layouts  19.4 us (4%)
  other arithmetic  6.39 us (1%)
    pallas_call x3, Pallas kernels, kernel_call(): pl.pallas_call(kernel, out_shape=outs, in_specs=[pl.BlockSpec(memory_spac...  261 us
    pallas_call x1, Pallas kernels, sum_gradients(): pl.pallas_call(functools.partial(gradient_kernel, sections, count), out_s...  176 us
    pallas_call x1, Pallas kernels, cast_sums(): pl.pallas_call(cast_kernel, grid=(steps,), out_shape=[shape_of(a.shape, F...  16.8 us

profile of v8, /device:TPU:29, one launch (start us, length us, event | category | flops | bytes accessed | tf_op | source)
XLA Modules:
  0.0 481.0 jit_solution(13697775491404482596)
XLA Ops:
  0.7 0.1 pad.30.clone
  0.8 0.1 and.233
  0.9 0.7 broadcast_add_fusion.2
  1.6 0.1 lt.197
  1.7 0.1 add.244
  1.8 0.1 add.245
  1.8 0.1 add.234
  1.9 0.1 add.228
  2.0 0.1 lt.190
  2.1 0.7 fusion.25
  2.8 0.6 pad_maximum_fusion.1.gb
  3.4 0.1 lt.192
  3.5 0.1 lt.208
  3.6 0.1 lt.193
  3.7 1.3 pad_maximum_fusion.vec
  5.0 0.8 copy.42
  5.8 0.1 mul.74
  5.9 0.1 multiply_reduce_fusion
  6.0 0.1 ne.265
  6.1 0.1 ne.259
  6.2 0.1 rem.228
  6.3 0.1 div.86
  6.5 0.1 div.84
  6.5 0.1 rem.223
  6.7 0.1 squeeze.36
  6.8 0.7 select_maximum_fusion
  7.6 0.8 copy.47.pack
  8.3 0.1 copy.43
  8.5 0.1 copy.41
  8.6 0.1 reshape.637
  8.8 1.0 maximum_maximum_fusion
  9.7 0.1 copy.44
  9.9 0.7 pad.11.mask
  10.6 1.0 reshape.642.tiles
  11.6 0.9 fusion.1
  12.5 1.1 copy.45.pack
  13.5 81.7 %shard_map.154 = (f32[16,512]{1,0:T(8,128)}, f32[8,128]{1,0:T(8,128)}, f32[4,2,2048]{2,1,0:T(2,128)}, bf16[304,2048]{1,0:T(8,128)(2,1)}, bf16[304,2048]{1,0:T(8,...) custom-call(bf16[294,4,2048]{2,1,0:T(4,128)(2,1)} %bitcast.78, ...), custom_call_target="tpu_custom_call" | custom-call | flops 10481565696 | bytes 62914560 | tf_op jit(solution)/shard_map/pallas_call | solution.py:106
  95.2 82.0 %shard_map.155 = (bf16[304,2048]{1,0:T(8,128)(2,1)}, bf16[304,2048]{1,0:T(8,128)(2,1)}, f32[6,2048]{1,0:T(8,128)}, bf16[4,304,2048]{2,1,0:T(8,128)(2,1)}, bf16[2...) custom-call(bf16[304,2048]{1,0:T(8,128)(2,1)} %get-tuple-element.49.u, ...), custom_call_target="tpu_custom_call" | custom-call | flops 5419040768 | bytes 31457280 | tf_op jit(solution)/shard_map/pallas_call | solution.py:106
  177.2 0.9 fusion.22
  178.1 0.9 fusion.21
  179.0 97.4 %shard_map.156 = (bf16[1176,512]{1,0:T(8,128)(2,1)}, f32[2,2048]{1,0:T(2,128)}, f32[16,512]{1,0:T(8,128)}, bf16[4,144,512]{2,1,0:T(8,128)(2,1)}, bf16[4,304,2048...) custom-call(bf16[304,2048]{1,0:T(8,128)(2,1)} %get-tuple-element.56., ...), custom_call_target="tpu_custom_call" | custom-call | flops 5549064192 | bytes 41943040 | tf_op jit(solution)/shard_map/pallas_call | solution.py:106
  276.5 0.8 slice_reduce_fusion.1
  277.3 0.8 fusion.24
  278.1 0.1 stack.17
  278.2 0.7 reshape.631.vec
  278.9 176.1 %shard_map.157 = (bf16[2,1024,2048]{2,1,0:T(8,128)(2,1)}, bf16[2,4,4,64,512]{4,3,2,1,0:T(8,128)(2,1)}, bf16[2,4,4,144,512]{4,3,2,1,0:T(8,128)(2,1)}, f32[2,2048]{1,0:T(2,128)}, bf16[294,4,2048]{2,1,0:T(4,128)(2,1)}) custom-call(bf16[2,1024,512]{2,1,0:T(8,128)(2,1)} %bitcast.63, bf16[2,4,4,144,512]{4,3,2,1,0:T(8,128)(2,1)} %bitcast.52, ...), custom_call_target="tpu_custom_call" | custom-call | bytes 419430400 | tf_op jit(solution)/shard_map/pallas_call | solution.py:1969
  455.0 1.4 fusion.23
  456.4 16.8 %shard_map.158 = (f32[2048,512]{1,0:T(8,128)}, f32[4608,512]{1,0:T(8,128)}, f32[2048,2048]{1,0:T(8,128)}) custom-call(bf16[2048,512]{1,0:T(8,128)(2,1)} %bitcast.64, bf16[4608,512]{1,0:T(8,128)(2,1)} %bitcast.56, bf16[2048,2048]{1,0:T(8,128)(2,1)} %bitcast.48), custom_call_target="tpu_custom_call" | custom-call | bytes 47185920 | tf_op jit(solution)/shard_map/pallas_call | solution.py:2008
  473.2 7.4 %copy.50 = bf16[1,4,6,49,2048]{4,1,3,2,0:T(4,128)(2,1)} copy(bf16[1,4,6,49,2048]{4,1,3,2,0:T(4,128)(2,1)} %bitcast.51) | data formatting | bytes 9633792
  (29 shorter events, 0.3 us)

commit v9 on v8

--- a/solution.py
+++ b/solution.py
@@ -1156,6 +1156,7 @@
     k0_out,
     p0_out,
     sh_out,
+    piece_out,
     dz,
     dh3,
     dh2,
@@ -1179,7 +1180,9 @@
     sync, rest = rest[:9], list(rest[9:])
     half, theirs, pieces, whole = rest[:4]
     load_sem, swap_send, swap_recv, piece_send, piece_recv, out_sem = rest[4:10]
-    rest = rest[10:]
+    sh_half, sh_other, sh_theirs, sh_pieces, sh_sum = rest[10:15]
+    sh_swap_send, sh_swap_recv, sh_send, sh_recv, sh_sem = rest[15:20]
+    rest = rest[20:]
     a_send, a_recv, q_send, q_recv = rest[:4]
     maps = [rest[4:7], rest[7:10], rest[10:13]]
     me, place = lax.axis_index("segment"), lax.axis_index("dp")
@@ -1317,6 +1320,63 @@
         a_copy(0).wait_send()
         sums12[...] = jnp.zeros(sums12.shape, F32)
 
+    for k_ in range(1, sections):
+        q_copy(k_).wait_recv()
+    dzq[me] = dz[:, pl.ds(pl.multiple_of(me * quarter, 128), quarter)]
+    rows, full = dzq_out.shape[0], act.shape[1]
+    for m in range(4):
+
+        def put(j, carry, m=m):
+            at = pl.ds(pl.multiple_of(j * 128, 128), 128)
+            act[j, pl.ds(m, full // 4, stride=4), :] = dzq[m, :, at].astype(F32)
+            return carry
+
+        lax.fori_loop(0, quarter // 128, put, 0)
+
+    def weave(j, carry):
+        at = pl.ds(pl.multiple_of(j * 128, 128), 128)
+        dzq_out[:, at] = act[j, 0:rows, :].astype(BF16)
+        return carry
+
+    lax.fori_loop(0, quarter // 128, weave, 0)
+    tall = stage.shape[1]
+    sh_rows = sh_half.shape[0]
+    fine = sh_rows // depth
+    sh_swap = mesh_copy(
+        sh_other, sh_theirs, sh_swap_send, sh_swap_recv, me, place + 1 - 2 * core
+    )
+
+    def sh_to_chip(k_):
+        to = lax.rem(z + k_, depth)
+        return mesh_copy(
+            sh_half.at[pl.ds(pl.multiple_of(to * fine, 16), fine)],
+            sh_pieces.at[k_],
+            sh_send.at[k_],
+            sh_recv.at[k_],
+            me,
+            2 * to + core,
+        )
+
+    @pl.when(me != 0)
+    def _():
+        for half_of, target in ((1 - core, sh_other), (core, sh_half)):
+            for j in range(sh_rows // tall):
+                at = pl.ds(pl.multiple_of(half_of * sh_rows + j * tall, 128), tall)
+                target[j * tall : j * tall + tall, :] = dot_0(x[:, at], dzq_out[...]).astype(BF16)
+            if target is sh_other:
+                sh_swap.start()
+        sh_swap.wait_recv()
+
+        def add(n):
+            at = pl.ds(pl.multiple_of(n * 32, 32), 32)
+            sh_half[at, :] = (sh_half[at, :].astype(F32) + sh_theirs[at, :].astype(F32)).astype(BF16)
+
+        loop(0, sh_rows // 32, add)
+        loop(1, depth, lambda k_: sh_to_chip(k_).start())
+
+    writer = Writer(stage, stage_sem)
+    writer.rows_of_dot(dh3, a2, p1_out)
+    writer.drain()
     loop(1, depth, lambda k_: to_chip(k_).wait_recv())
 
     def k2_sum(q):
@@ -1328,29 +1388,26 @@
     loop(0, sections, k2_sum)
     out = pltpu.make_async_copy(whole, k2_out, out_sem)
     out.start()
-    for k_ in range(1, sections):
-        q_copy(k_).wait_recv()
-    dzq[me] = dz[:, pl.ds(pl.multiple_of(me * quarter, 128), quarter)]
-    rows, full = dzq_out.shape[0], act.shape[1]
-    for m in range(4):
-
-        def put(j, carry, m=m):
-            at = pl.ds(pl.multiple_of(j * 128, 128), 128)
-            act[j, pl.ds(m, full // 4, stride=4), :] = dzq[m, :, at].astype(F32)
-            return carry
-
-        lax.fori_loop(0, quarter // 128, put, 0)
-
-    def weave(j, carry):
-        at = pl.ds(pl.multiple_of(j * 128, 128), 128)
-        dzq_out[:, at] = act[j, 0:rows, :].astype(BF16)
-        return carry
-
-    lax.fori_loop(0, quarter // 128, weave, 0)
-    writer = Writer(stage, stage_sem)
-    writer.rows_of_dot(x, dzq_out, sh_out)
-    writer.rows_of_dot(dh3, a2, p1_out)
-    writer.drain()
+
+    @pl.when(me == 0)
+    def _():
+        writer = Writer(stage, stage_sem)
+        writer.rows_of_dot(x, dzq_out, sh_out)
+        writer.drain()
+
+    @pl.when(me != 0)
+    def _():
+        loop(1, depth, lambda k_: sh_to_chip(k_).wait_recv())
+        acc = sh_half[pl.ds(pl.multiple_of(z * fine, 16), fine), :].astype(F32)
+        for k_ in range(1, depth):
+            acc = acc + sh_pieces[k_].astype(F32)
+        sh_sum[...] = acc.astype(BF16)
+        written = pltpu.make_async_copy(sh_sum, piece_out, sh_sem)
+        written.start()
+        sh_swap.wait_send()
+        loop(1, depth, lambda k_: sh_to_chip(k_).wait_send())
+        written.wait()
+
     for k_ in range(1, sections):
         q_copy(k_).wait_send()
     loop(1, depth, lambda k_: to_chip(k_).wait_send())
@@ -1375,6 +1432,7 @@
     sections,
     count,
     sh,
+    sh_piece,
     k0,
     p0,
     p1,
@@ -1537,8 +1595,35 @@
         sh.at[1 - core], sh_theirs, a_send.at[last], a_recv.at[last], me, sibling
     )
     sh_load = pltpu.make_async_copy(sh.at[core], sh_half, load_sem.at[last])
-    sh_swap.start()
-    sh_load.start()
+    piece = sh_rows // depth
+
+    def sh_at(i):
+        return pl.ds(pl.multiple_of(i * piece, 16), piece)
+
+    mine = sh_at(z)
+    piece_load = pltpu.make_async_copy(sh_piece, sh_whole.at[mine], load_sem.at[last])
+
+    def sh_share(k):
+        return mesh_copy(
+            sh_whole.at[mine],
+            sh_whole.at[mine],
+            d_send.at[last, k],
+            d_recv.at[last, k],
+            me,
+            chip(k),
+        )
+
+    @pl.when(me == 0)
+    def _():
+        sh_swap.start()
+        sh_load.start()
+
+    @pl.when(me != 0)
+    def _():
+        piece_load.start()
+        piece_load.wait()
+        loop(1, depth, lambda k: sh_share(k).start())
+
 
     def vec_copy(k):
         other = jnp.bitwise_xor(me, k)
@@ -1603,11 +1688,7 @@
                 def _(name=name, k=k):
                     deliver(name, k).start()
 
-    piece = sh_rows // depth
     step = 32
-
-    def sh_at(i):
-        return pl.ds(pl.multiple_of(i * piece, 16), piece)
 
     def sh_send(k):
         to = lax.rem(z + k, depth)
@@ -1620,15 +1701,17 @@
             2 * to + core,
         )
 
-    sh_load.wait()
-    sh_swap.wait_recv()
-
-    def sh_add(i):
-        at = pl.ds(pl.multiple_of(i * step, step), step)
-        sh_half[at, :] = (sh_half[at, :].astype(F32) + sh_theirs[at, :].astype(F32)).astype(BF16)
-
-    loop(0, sh_rows // step, sh_add)
-    loop(1, depth, lambda k: sh_send(k).start())
+    @pl.when(me == 0)
+    def _():
+        sh_load.wait()
+        sh_swap.wait_recv()
+
+        def sh_add(i):
+            at = pl.ds(pl.multiple_of(i * step, step), step)
+            sh_half[at, :] = (sh_half[at, :].astype(F32) + sh_theirs[at, :].astype(F32)).astype(BF16)
+
+        loop(0, sh_rows // step, sh_add)
+        loop(1, depth, lambda k: sh_send(k).start())
 
     def to_section(name, k):
         other = jnp.bitwise_xor(me, k)
@@ -1642,6 +1725,15 @@
             place,
         )
 
+    def scattered(name, onward):
+        if onward:
+            return mesh_copy(
+                relay[name], total[name], r_send.at[slot[name]], b_recv.at[slot[name], 3], 3, place
+            )
+        return mesh_copy(
+            half[name].at[3], relay[name], b_send.at[slot[name], 3], r_recv.at[slot[name]], 2, place
+        )
+
     for name in fresh:
 
         def combine(name=name):
@@ -1656,13 +1748,13 @@
 
             loop(0, sections * depth, add)
             for k in range(1, sections):
-                to_section(name, k).start()
+                if held[name] == "owner" and k == 3:
+                    pl.when(core == 0)(to_section(name, k).start)
+                    pl.when(core == 1)(scattered(name, False).start)
+                else:
+                    to_section(name, k).start()
 
         when_held(name, combine)
-
-    for i, copy in enumerate(page_loads):
-        pl.when(me == i)(copy.wait)
-    loop(0, 2, map_tile)
 
     def share(name, k):
         return mesh_copy(
@@ -1674,26 +1766,6 @@
             chip(k),
         )
 
-    loop(1, depth, lambda k: sh_send(k).wait_recv())
-    mine = sh_at(z)
-    acc = sh_half[mine, :].astype(F32)
-    for k in range(1, depth):
-        acc = acc + sh_others[k].astype(F32)
-    sh_whole[mine, :] = acc.astype(BF16)
-
-    def sh_share(k):
-        return mesh_copy(
-            sh_whole.at[mine],
-            sh_whole.at[mine],
-            d_send.at[last, k],
-            d_recv.at[last, k],
-            me,
-            chip(k),
-        )
-
-    loop(1, depth, lambda k: sh_share(k).start())
-    loop(2, wide // TILE, map_tile)
-
     def planes_end(name):
         load_plane(name).wait()
         acc = planes[name][0].astype(F32)
@@ -1702,6 +1774,29 @@
             acc = acc + planes[name][k].astype(F32)
         whole[name][z] = acc.astype(BF16)
         loop(1, depth, lambda k: share(name, k).start())
+
+    planes_end("k2")
+    for i, copy in enumerate(page_loads):
+        pl.when(me == i)(copy.wait)
+    loop(0, 2, map_tile)
+
+    @pl.when((me == 2) & (core == 1))
+    def _():
+        for name in ("k0", "p0"):
+            scattered(name, False).wait_recv()
+            scattered(name, True).start()
+
+
+    @pl.when(me == 0)
+    def _():
+        loop(1, depth, lambda k: sh_send(k).wait_recv())
+        acc = sh_half[mine, :].astype(F32)
+        for k in range(1, depth):
+            acc = acc + sh_others[k].astype(F32)
+        sh_whole[mine, :] = acc.astype(BF16)
+        loop(1, depth, lambda k: sh_share(k).start())
+
+    loop(2, wide // TILE, map_tile)
 
     def to_chip(name, k):
         to = lax.rem(z + k, depth)
@@ -1816,7 +1911,6 @@
         start_delivery(name)
 
     later = ("p1", "p2", "p3")
-    planes_end("k2")
     for name in ("k0", "p0"):
         c_end(name)
     for name in later:
@@ -1872,8 +1966,12 @@
     tile_store(wide // TILE - 1).wait()
     for k in range(1, sections):
         vec_copy(k).wait_send()
-    sh_swap.wait_send()
-    loop(1, depth, lambda k: sh_send(k).wait_send())
+
+    @pl.when(me == 0)
+    def _():
+        sh_swap.wait_send()
+        loop(1, depth, lambda k: sh_send(k).wait_send())
+
     loop(1, depth, lambda k: sh_share(k).wait_send())
 
     @pl.when(me == 0)
@@ -1888,6 +1986,11 @@
     def _():
         for name in relay:
             relayed(name, True).wait_send()
+
+    @pl.when((me == 2) & (core == 1))
+    def _():
+        for name in ("k0", "p0"):
+            scattered(name, True).wait_send()
 
     for name in names:
 
@@ -1914,7 +2017,7 @@
             deliver(name, 0).wait_send()
 
 
-def sum_gradients(sections, count, short, terms, vectors, dh1, w, weights, map_sources, real):
+def sum_gradients(sections, count, short, piece, terms, vectors, dh1, w, weights, map_sources, real):
     narrow = short.shape[1]
     depth = count // 2
     args, scratch = [], []
@@ -1975,14 +2078,14 @@
             shape_of(vectors.shape[1:], F32),
             shape_of((real, 4, wide), BF16),
         ],
-        in_specs=[hbm] * 7 + [vmem, vmem] + [hbm] * 6,
+        in_specs=[hbm] * 8 + [vmem, vmem] + [hbm] * 6,
         out_specs=[hbm, hbm, hbm, vmem, hbm],
         scratch_shapes=scratch,
         compiler_params=pltpu.CompilerParams(
             has_side_effects=True, vmem_limit_bytes=VMEM_BYTES, collective_id=5
         ),
         cost_estimate=pl.CostEstimate(flops=0, bytes_accessed=400 * 2**20, transcendentals=0),
-    )(short.reshape(2, sh_rows, narrow), *args, vectors, dh1, w, weights, *map_sources)
+    )(short.reshape(2, sh_rows, narrow), piece, *args, vectors, dh1, w, weights, *map_sources)
 
 
 def cast_kernel(proj, taps, short, proj_out, taps_out, short_out):
@@ -2216,6 +2319,7 @@
             shape_of((9 * narrow, narrow), BF16),
             shape_of((wide, narrow), BF16),
             shape_of((wide, narrow), BF16),
+            shape_of((wide // count, narrow), BF16),
         ],
         [dy1, res, h3n, image_mask, gains, stats3, w1, spatial, gb_first, pack_all]
         + [h1n_all, h2n_all, stats_all, counts, k2_term, y2, a2, a1_all, x_all],
@@ -2244,15 +2348,18 @@
         + [pltpu.VMEM((depth, sections, taps_piece, narrow), BF16)]
         + [pltpu.VMEM((sections, taps_piece, narrow), BF16)]
         + [dma, dma, dma, dma((depth,)), dma((depth,)), dma]
+        + [pltpu.VMEM((wide // 2, narrow), BF16)] * 3
+        + [pltpu.VMEM((depth, wide // count, narrow), BF16), pltpu.VMEM((wide // count, narrow), BF16)]
+        + [dma, dma, dma((depth,)), dma((depth,)), dma]
         + [dma, dma((sections,)), dma((sections,)), dma((sections,))]
         + [dma, dma((sections,)), dma] * 3,
         2,
         2 * total * narrow * 9 * narrow,
         40 * 2**20,
         far_in=(7, 10, 11, 14, 15, 17, 18),
-        far_out=tuple(range(3, 11)),
+        far_out=tuple(range(3, 12)),
     )
-    map_zero, map_two, map_three, p1_term, k0_term, p0_term, short_term = far
+    map_zero, map_two, map_three, p1_term, k0_term, p0_term, short_term, short_piece = far
 
     terms = {
         "p3": p3_term,
@@ -2284,6 +2391,7 @@
         sections,
         count,
         short_term,
+        short_piece,
         terms,
         vectors.reshape(sections, 2, wide),
         dh1_all,

time: 490 us -> 478 us (0.976)
  the two profiles are of different devices: /device:TPU:29 before, /device:TPU:0 now
where the time goes in v9:
time: 478 us; the launch traced here: 468 us
  Pallas kernels  441 us (92%)
  local copies, waits for them, and re-layouts  19.4 us (4%)
  other arithmetic  6.39 us (1%)
    pallas_call x3, Pallas kernels, kernel_call(): pl.pallas_call(kernel, out_shape=outs, in_specs=[pl.BlockSpec(memory_spac...  274 us
    pallas_call x1, Pallas kernels, sum_gradients(): pl.pallas_call(functools.partial(gradient_kernel, sections, count), out_s...  150 us
    pallas_call x1, Pallas kernels, cast_sums(): pl.pallas_call(cast_kernel, grid=(steps,), out_shape=[shape_of(a.shape, F...  16.8 us

profile of v9, /device:TPU:0, one launch (start us, length us, event | category | flops | bytes accessed | tf_op | source)
XLA Modules:
  0.0 468.3 jit_solution(5304884433565830850)
XLA Ops:
  0.7 0.1 pad.30.clone
  0.8 0.1 and.233
  0.9 0.7 broadcast_add_fusion.2
  1.6 0.1 lt.197
  1.7 0.1 add.244
  1.8 0.1 add.245
  1.8 0.1 add.234
  1.9 0.1 add.228
  2.0 0.1 lt.190
  2.1 0.7 fusion.25
  2.8 0.6 pad_maximum_fusion.1.gb
  3.4 0.1 lt.192
  3.5 0.1 lt.208
  3.6 0.1 lt.193
  3.7 1.3 pad_maximum_fusion.vec
  5.0 0.8 copy.42
  5.8 0.1 mul.74
  5.9 0.1 multiply_reduce_fusion
  6.0 0.1 ne.265
  6.1 0.1 ne.259
  6.2 0.1 rem.228
  6.3 0.1 div.86
  6.5 0.1 div.84
  6.5 0.1 rem.223
  6.7 0.1 squeeze.36
  6.8 0.7 select_maximum_fusion
  7.6 0.8 copy.47.pack
  8.3 0.1 copy.43
  8.5 0.1 copy.41
  8.6 0.1 reshape.637
  8.8 1.0 maximum_maximum_fusion
  9.7 0.1 copy.44
  9.9 0.7 pad.11.mask
  10.6 1.0 reshape.642.tiles
  11.6 0.9 fusion.1
  12.5 1.1 copy.45.pack
  13.5 93.8 %shard_map.154 = (f32[16,512]{1,0:T(8,128)}, f32[8,128]{1,0:T(8,128)}, f32[4,2,2048]{2,1,0:T(2,128)}, bf16[304,2048]{1,0:T(8,128)(2,1)}, bf16[304,2048]{1,0:T(8,...) custom-call(bf16[294,4,2048]{2,1,0:T(4,128)(2,1)} %bitcast.78, ...), custom_call_target="tpu_custom_call" | custom-call | flops 10481565696 | bytes 62914560 | tf_op jit(solution)/shard_map/pallas_call | solution.py:106
  107.3 73.7 %shard_map.155 = (bf16[304,2048]{1,0:T(8,128)(2,1)}, bf16[304,2048]{1,0:T(8,128)(2,1)}, f32[6,2048]{1,0:T(8,128)}, bf16[4,304,2048]{2,1,0:T(8,128)(2,1)}, bf16[2...) custom-call(bf16[304,2048]{1,0:T(8,128)(2,1)} %get-tuple-element.50.u, ...), custom_call_target="tpu_custom_call" | custom-call | flops 5419040768 | bytes 31457280 | tf_op jit(solution)/shard_map/pallas_call | solution.py:106
  181.0 0.9 fusion.22
  181.9 0.9 fusion.21
  182.8 106.6 %shard_map.156 = (bf16[1176,512]{1,0:T(8,128)(2,1)}, f32[2,2048]{1,0:T(2,128)}, f32[16,512]{1,0:T(8,128)}, bf16[4,144,512]{2,1,0:T(8,128)(2,1)}, bf16[4,304,2048...) custom-call(bf16[304,2048]{1,0:T(8,128)(2,1)} %get-tuple-element.57., ...), custom_call_target="tpu_custom_call" | custom-call | flops 5549064192 | bytes 41943040 | tf_op jit(solution)/shard_map/pallas_call | solution.py:106
  289.5 0.8 slice_reduce_fusion.1
  290.3 0.8 fusion.24
  291.1 0.1 stack.17
  291.2 0.7 reshape.631.vec
  291.9 150.5 %shard_map.157 = (bf16[2,1024,2048]{2,1,0:T(8,128)(2,1)}, bf16[2,4,4,64,512]{4,3,2,1,0:T(8,128)(2,1)}, bf16[2,4,4,144,512]{4,3,2,1,0:T(8,128)(2,1)}, f32[2,2048]{1,0:T(2,128)}, bf16[294,4,2048]{2,1,0:T(4,128)(2,1)}) custom-call(bf16[2,1024,512]{2,1,0:T(8,128)(2,1)} %bitcast.63, bf16[256,512]{1,0:T(8,128)(2,1)} %get-tuple-element.71.sh_piece, ...), custom_call_target="tpu_custom_call" | custom-call | bytes 419430400 | tf_op jit(solution)/shard_map/pallas_call | solution.py:2072
  442.4 1.4 fusion.23
  443.8 16.8 %shard_map.158 = (f32[2048,512]{1,0:T(8,128)}, f32[4608,512]{1,0:T(8,128)}, f32[2048,2048]{1,0:T(8,128)}) custom-call(bf16[2048,512]{1,0:T(8,128)(2,1)} %bitcast.64, bf16[4608,512]{1,0:T(8,128)(2,1)} %bitcast.56, bf16[2048,2048]{1,0:T(8,128)(2,1)} %bitcast.48), custom_call_target="tpu_custom_call" | custom-call | bytes 47185920 | tf_op jit(solution)/shard_map/pallas_call | solution.py:2111
  460.5 7.4 %copy.50 = bf16[1,4,6,49,2048]{4,1,3,2,0:T(4,128)(2,1)} copy(bf16[1,4,6,49,2048]{4,1,3,2,0:T(4,128)(2,1)} %bitcast.51) | data formatting | bytes 9633792
  (29 shorter events, 0.3 us)

commit v10 on v9

--- a/solution.py
+++ b/solution.py
@@ -2088,8 +2088,9 @@
     )(short.reshape(2, sh_rows, narrow), piece, *args, vectors, dh1, w, weights, *map_sources)
 
 
-def cast_kernel(proj, taps, short, proj_out, taps_out, short_out):
+def cast_kernel(proj, taps, short, maps, proj_out, taps_out, short_out, maps_out):
     me = lax.axis_index("segment")
+    maps_out[...] = maps[...]
     proj_out[...] = proj[...].astype(F32)
     for held, src, out in (
         ((me == 0) | (me == 2), taps, taps_out),
@@ -2105,18 +2106,19 @@
             out[...] = jnp.zeros(out.shape, F32)
 
 
-def cast_sums(*sums):
+def cast_sums(maps, *sums):
     steps = 8
     blocks = [pl.BlockSpec((a.shape[0] // steps, a.shape[1]), lambda i: (i, 0)) for a in sums]
+    blocks.append(pl.BlockSpec(maps.shape[:2] + (maps.shape[2] // steps,), lambda i: (0, 0, i)))
     return pl.pallas_call(
         cast_kernel,
         grid=(steps,),
-        out_shape=[shape_of(a.shape, F32) for a in sums],
+        out_shape=[shape_of(a.shape, F32) for a in sums] + [shape_of(maps.shape, BF16)],
         in_specs=blocks,
         out_specs=blocks,
         compiler_params=pltpu.CompilerParams(vmem_limit_bytes=VMEM_BYTES),
-        cost_estimate=pl.CostEstimate(flops=0, bytes_accessed=45 * 2**20, transcendentals=0),
-    )(*sums)
+        cost_estimate=pl.CostEstimate(flops=0, bytes_accessed=54 * 2**20, transcendentals=0),
+    )(*sums, maps)
 
 
 def layouts(resolution_ids, order_ids):
@@ -2400,12 +2402,13 @@
         (map_zero, map_one, map_two, map_three),
         rows,
     )
-    maps = jnp.transpose(maps.reshape(images, pixels, micro, wide), (2, 0, 1, 3))
-    proj_grad, spatial_grad, short_grad = cast_sums(
+    proj_grad, spatial_grad, short_grad, maps = cast_sums(
+        maps,
         proj_sum.reshape(wide, narrow),
         taps_sum.reshape(9 * narrow, narrow),
         short_sum.reshape(wide, wide),
     )
+    maps = jnp.transpose(maps.reshape(images, pixels, micro, wide), (2, 0, 1, 3))
     return (
         maps[None],
         proj_grad[None],

time: 478 us -> 473 us (0.990)
  local copies, waits for them, and re-layouts: 19.4 us -> 12 us
    unnamed x2 -> x1, local copies, waits for them, and re-layouts: 8.16 us -> 0.81 us
where the time goes in v10:
time: 473 us; the launch traced here: 464 us
  Pallas kernels  444 us (94%)
  local copies, waits for them, and re-layouts  12 us (3%)
  other arithmetic  6.39 us (1%)
    pallas_call x3, Pallas kernels, kernel_call(): pl.pallas_call(kernel, out_shape=outs, in_specs=[pl.BlockSpec(memory_spac...  274 us
    pallas_call x1, Pallas kernels, sum_gradients(): pl.pallas_call(functools.partial(gradient_kernel, sections, count), out_s...  150 us
    pallas_call x1, Pallas kernels, cast_sums(): pl.pallas_call(cast_kernel, grid=(steps,), out_shape=[shape_of(a.shape, F...  19.8 us

profile of v10, /device:TPU:0, one launch (start us, length us, event | category | flops | bytes accessed | tf_op | source)
XLA Modules:
  0.0 463.9 jit_solution(14053482848411105143)
XLA Ops:
  0.7 0.1 pad.30.clone
  0.8 0.1 and.233
  0.9 0.7 broadcast_add_fusion.2
  1.6 0.1 lt.197
  1.7 0.1 add.244
  1.8 0.1 add.245
  1.8 0.1 add.234
  1.9 0.1 add.228
  2.0 0.1 lt.190
  2.1 0.7 fusion.25
  2.8 0.6 pad_maximum_fusion.1.gb
  3.4 0.1 lt.192
  3.5 0.1 lt.208
  3.6 0.1 lt.193
  3.7 1.3 pad_maximum_fusion.vec
  5.0 0.8 copy.42
  5.8 0.1 mul.74
  5.9 0.1 multiply_reduce_fusion
  6.0 0.1 ne.265
  6.1 0.1 ne.259
  6.2 0.1 rem.228
  6.3 0.1 div.86
  6.5 0.1 div.84
  6.5 0.1 rem.223
  6.7 0.1 squeeze.36
  6.8 0.7 select_maximum_fusion
  7.6 0.8 copy.47.pack
  8.3 0.1 copy.43
  8.5 0.1 copy.41
  8.6 0.1 reshape.637
  8.8 1.0 maximum_maximum_fusion
  9.7 0.1 copy.44
  9.9 0.7 pad.11.mask
  10.6 1.0 reshape.642.tiles
  11.6 0.9 fusion.1
  12.5 1.1 copy.45.pack
  13.5 93.8 %shard_map.154 = (f32[16,512]{1,0:T(8,128)}, f32[8,128]{1,0:T(8,128)}, f32[4,2,2048]{2,1,0:T(2,128)}, bf16[304,2048]{1,0:T(8,128)(2,1)}, bf16[304,2048]{1,0:T(8,...) custom-call(bf16[294,4,2048]{2,1,0:T(4,128)(2,1)} %bitcast.77, ...), custom_call_target="tpu_custom_call" | custom-call | flops 10481565696 | bytes 62914560 | tf_op jit(solution)/shard_map/pallas_call | solution.py:106
  107.3 73.7 %shard_map.155 = (bf16[304,2048]{1,0:T(8,128)(2,1)}, bf16[304,2048]{1,0:T(8,128)(2,1)}, f32[6,2048]{1,0:T(8,128)}, bf16[4,304,2048]{2,1,0:T(8,128)(2,1)}, bf16[2...) custom-call(bf16[304,2048]{1,0:T(8,128)(2,1)} %get-tuple-element.51.u, ...), custom_call_target="tpu_custom_call" | custom-call | flops 5419040768 | bytes 31457280 | tf_op jit(solution)/shard_map/pallas_call | solution.py:106
  181.0 0.9 fusion.22
  181.9 0.9 fusion.21
  182.8 106.6 %shard_map.156 = (bf16[1176,512]{1,0:T(8,128)(2,1)}, f32[2,2048]{1,0:T(2,128)}, f32[16,512]{1,0:T(8,128)}, bf16[4,144,512]{2,1,0:T(8,128)(2,1)}, bf16[4,304,2048...) custom-call(bf16[304,2048]{1,0:T(8,128)(2,1)} %get-tuple-element.58., ...), custom_call_target="tpu_custom_call" | custom-call | flops 5549064192 | bytes 41943040 | tf_op jit(solution)/shard_map/pallas_call | solution.py:106
  289.5 0.8 slice_reduce_fusion.1
  290.3 0.8 fusion.24
  291.1 0.1 stack.17
  291.2 0.7 reshape.631.vec
  291.9 150.5 %shard_map.157 = (bf16[2,1024,2048]{2,1,0:T(8,128)(2,1)}, bf16[2,4,4,64,512]{4,3,2,1,0:T(8,128)(2,1)}, bf16[2,4,4,144,512]{4,3,2,1,0:T(8,128)(2,1)}, f32[2,2048]{1,0:T(2,128)}, bf16[294,4,2048]{2,1,0:T(4,128)(2,1)}) custom-call(bf16[2,1024,512]{2,1,0:T(8,128)(2,1)} %bitcast.62, bf16[256,512]{1,0:T(8,128)(2,1)} %get-tuple-element.72.sh_piece, ...), custom_call_target="tpu_custom_call" | custom-call | bytes 419430400 | tf_op jit(solution)/shard_map/pallas_call | solution.py:2072
  442.4 1.4 fusion.23
  443.8 19.8 %shard_map.158 = (f32[2048,512]{1,0:T(8,128)}, f32[4608,512]{1,0:T(8,128)}, f32[2048,2048]{1,0:T(8,128)}, bf16[294,4,2048]{2,1,0:T(4,128)(2,1)}) custom-call(bf16[2048,512]{1,0:T(8,128)(2,1)} %bitcast.63, bf16[4608,512]{1,0:T(8,128)(2,1)} %bitcast.55, bf16[2048,2048]{1,0:T(8,128)(2,1)} %bitcast.48, bf16[294,4,2048]{2,1,0:T(4,128)(2,1)} %get-tuple-element.90.maps), custom_call_target="tpu_custom_call" | custom-call | bytes 56623104 | tf_op jit(solution)/shard_map/pallas_call | solution.py:2113
  (29 shorter events, 0.3 us)

commit v11 on v10

--- a/solution.py
+++ b/solution.py
@@ -1271,6 +1271,9 @@
     send_dz()
     send_two()
     add_cores()
+    writer = Writer(stage, stage_sem)
+    writer.rows_of_dot(dh3, a2, p1_out)
+    writer.drain()
 
     def to_chips():
         loop(1, depth, lambda k_: to_chip(k_).start())
@@ -1374,9 +1377,6 @@
         loop(0, sh_rows // 32, add)
         loop(1, depth, lambda k_: sh_to_chip(k_).start())
 
-    writer = Writer(stage, stage_sem)
-    writer.rows_of_dot(dh3, a2, p1_out)
-    writer.drain()
     loop(1, depth, lambda k_: to_chip(k_).wait_recv())
 
     def k2_sum(q):

time: 473 us -> 476 us (level)
  the two profiles are of different devices: /device:TPU:0 before, /device:TPU:29 now
where the time goes in v11:
time: 476 us; the launch traced here: 467 us
  Pallas kernels  447 us (94%)
  local copies, waits for them, and re-layouts  12 us (3%)
  other arithmetic  6.39 us (1%)
    pallas_call x3, Pallas kernels, kernel_call(): pl.pallas_call(kernel, out_shape=outs, in_specs=[pl.BlockSpec(memory_spac...  261 us
    pallas_call x1, Pallas kernels, sum_gradients(): pl.pallas_call(functools.partial(gradient_kernel, sections, count), out_s...  166 us
    pallas_call x1, Pallas kernels, cast_sums(): pl.pallas_call(cast_kernel, grid=(steps,), out_shape=[shape_of(a.shape, F...  19.7 us

profile of v11, /device:TPU:29, one launch (start us, length us, event | category | flops | bytes accessed | tf_op | source)
XLA Modules:
  0.0 466.9 jit_solution(16973263858643278390)
XLA Ops:
  0.7 0.1 pad.30.clone
  0.8 0.1 and.233
  0.9 0.7 broadcast_add_fusion.2
  1.6 0.1 lt.197
  1.7 0.1 add.244
  1.8 0.1 add.245
  1.8 0.1 add.234
  1.9 0.1 add.228
  2.0 0.1 lt.190
  2.1 0.7 fusion.25
  2.8 0.6 pad_maximum_fusion.1.gb
  3.4 0.1 lt.192
  3.5 0.1 lt.208
  3.6 0.1 lt.193
  3.7 1.3 pad_maximum_fusion.vec
  5.0 0.8 copy.42
  5.8 0.1 mul.74
  5.9 0.1 multiply_reduce_fusion
  6.0 0.1 ne.265
  6.1 0.1 ne.259
  6.2 0.1 rem.228
  6.3 0.1 div.86
  6.5 0.1 div.84
  6.5 0.1 rem.223
  6.7 0.1 squeeze.36
  6.8 0.7 select_maximum_fusion
  7.6 0.8 copy.47.pack
  8.3 0.1 copy.43
  8.5 0.1 copy.41
  8.6 0.1 reshape.637
  8.8 1.0 maximum_maximum_fusion
  9.7 0.1 copy.44
  9.9 0.7 pad.11.mask
  10.6 1.0 reshape.642.tiles
  11.6 0.9 fusion.1
  12.5 1.1 copy.45.pack
  13.5 81.7 %shard_map.154 = (f32[16,512]{1,0:T(8,128)}, f32[8,128]{1,0:T(8,128)}, f32[4,2,2048]{2,1,0:T(2,128)}, bf16[304,2048]{1,0:T(8,128)(2,1)}, bf16[304,2048]{1,0:T(8,...) custom-call(bf16[294,4,2048]{2,1,0:T(4,128)(2,1)} %bitcast.77, ...), custom_call_target="tpu_custom_call" | custom-call | flops 10481565696 | bytes 62914560 | tf_op jit(solution)/shard_map/pallas_call | solution.py:106
  95.2 81.7 %shard_map.155 = (bf16[304,2048]{1,0:T(8,128)(2,1)}, bf16[304,2048]{1,0:T(8,128)(2,1)}, f32[6,2048]{1,0:T(8,128)}, bf16[4,304,2048]{2,1,0:T(8,128)(2,1)}, bf16[2...) custom-call(bf16[304,2048]{1,0:T(8,128)(2,1)} %get-tuple-element.51.u, ...), custom_call_target="tpu_custom_call" | custom-call | flops 5419040768 | bytes 31457280 | tf_op jit(solution)/shard_map/pallas_call | solution.py:106
  176.9 0.9 fusion.22
  177.8 0.9 fusion.21
  178.7 97.6 %shard_map.156 = (bf16[1176,512]{1,0:T(8,128)(2,1)}, f32[2,2048]{1,0:T(2,128)}, f32[16,512]{1,0:T(8,128)}, bf16[4,144,512]{2,1,0:T(8,128)(2,1)}, bf16[4,304,2048...) custom-call(bf16[304,2048]{1,0:T(8,128)(2,1)} %get-tuple-element.58., ...), custom_call_target="tpu_custom_call" | custom-call | flops 5549064192 | bytes 41943040 | tf_op jit(solution)/shard_map/pallas_call | solution.py:106
  276.3 0.8 slice_reduce_fusion.1
  277.2 0.8 fusion.24
  278.0 0.1 stack.17
  278.1 0.7 reshape.631.vec
  278.8 166.5 %shard_map.157 = (bf16[2,1024,2048]{2,1,0:T(8,128)(2,1)}, bf16[2,4,4,64,512]{4,3,2,1,0:T(8,128)(2,1)}, bf16[2,4,4,144,512]{4,3,2,1,0:T(8,128)(2,1)}, f32[2,2048]{1,0:T(2,128)}, bf16[294,4,2048]{2,1,0:T(4,128)(2,1)}) custom-call(bf16[2,1024,512]{2,1,0:T(8,128)(2,1)} %bitcast.62, bf16[256,512]{1,0:T(8,128)(2,1)} %get-tuple-element.72.sh_piece, ...), custom_call_target="tpu_custom_call" | custom-call | bytes 419430400 | tf_op jit(solution)/shard_map/pallas_call | solution.py:2072
  445.3 1.4 fusion.23
  446.7 19.7 %shard_map.158 = (f32[2048,512]{1,0:T(8,128)}, f32[4608,512]{1,0:T(8,128)}, f32[2048,2048]{1,0:T(8,128)}, bf16[294,4,2048]{2,1,0:T(4,128)(2,1)}) custom-call(bf16[2048,512]{1,0:T(8,128)(2,1)} %bitcast.63, bf16[4608,512]{1,0:T(8,128)(2,1)} %bitcast.55, bf16[2048,2048]{1,0:T(8,128)(2,1)} %bitcast.48, bf16[294,4,2048]{2,1,0:T(4,128)(2,1)} %get-tuple-element.90.maps), custom_call_target="tpu_custom_call" | custom-call | bytes 56623104 | tf_op jit(solution)/shard_map/pallas_call | solution.py:2113
  (29 shorter events, 0.3 us)
